TPU v7x, 32 devices: a whole 2x2x4 slice. The times are simulated.
32 devices in a mesh: lat: 2 (over x), lon: 16 (over z, y, core).
Axes of the slice: x: 2, y: 2, z: 4, core: 2. Of those that a mesh axis runs over, the one named last changes fastest.
Arguments:
- tokens: bfloat16 [16, 32, 64, 768], P(None, 'lat', 'lon'), may hold values from -6 to 6
- channel_mask: int32 [16, 69], replicated, may hold values 0 or 1
- lead_index: int32 [16], replicated, may hold values from 0 to 31
- chan_embed: bfloat16 [69, 768], replicated, may hold values from -2 to 2
- lead_embed: bfloat16 [32, 768], replicated, may hold values from -6 to 6
- norm1_gain: bfloat16 [768], replicated, may hold values from 0.25 to 1.75
- norm1_bias: bfloat16 [768], replicated, may hold values from -3 to 3
- qkv_weight: bfloat16 [768, 2304], replicated, may hold values from -0.21875 to 0.21875
- out_weight: bfloat16 [768, 768], replicated, may hold values from -4 to 4
- out_bias: bfloat16 [768], replicated, may hold values from -3 to 3
- norm2_gain: bfloat16 [768], replicated, may hold values from 0.25 to 1.75
- norm2_bias: bfloat16 [768], replicated, may hold values from -3 to 3
- up_weight: bfloat16 [768, 3072], replicated, may hold values from -0.21875 to 0.21875
- up_bias: bfloat16 [3072], replicated, may hold values from -3 to 3
- down_weight: bfloat16 [3072, 768], replicated, may hold values from -0.109375 to 0.109375
- down_bias: bfloat16 [768], replicated, may hold values from -3 to 3
- cotangent: bfloat16 [16, 32, 64, 768], P(None, 'lat', 'lon'), may hold values from -6 to 6
Outputs:
- result: bfloat16 [16, 32, 64, 768], P(None, 'lat', 'lon')
- grad_tokens: bfloat16 [16, 32, 64, 768], P(None, 'lat', 'lon')
- grad_chan_embed: float32 [69, 768], P(None, 'lon')
- grad_lead_embed: float32 [32, 768], P(None, 'lon')
- grad_norm1_gain: float32 [768], P('lon')
- grad_norm1_bias: float32 [768], P('lon')
- grad_qkv_weight: float32 [768, 2304], P('lon')
- grad_out_weight: float32 [768, 768], P('lon')
- grad_out_bias: float32 [768], P('lon')
- grad_norm2_gain: float32 [768], P('lon')
- grad_norm2_bias: float32 [768], P('lon')
- grad_up_weight: float32 [768, 3072], P('lon')
- grad_up_bias: float32 [3072], P('lon')
- grad_down_weight: float32 [3072, 768], P('lon')
- grad_down_bias: float32 [768], P('lon')
All inputs are finite; a program needn't handle non-finite values.
Results may differ from a plain program's by a relative error of at most 0.017.
Values may be sent and summed in bfloat16 or wider, within the bound.
No kernel may reach another device: no remote copies, remote signals or barrier semaphores. Data moves between devices by JAX's collectives and lax.ppermute only.
A program may use at most 512 MiB of HBM per device.

v0:
```python
from functools import partial

import jax
import jax.numpy as jnp
from jax import lax
from jax.sharding import PartitionSpec as P

HEADS = 12


EPSILON = 1e-06
SCALING = 0.125
HIGHEST = lax.Precision.HIGHEST


def layer_norm(value):
    row_mean = jnp.mean(value, axis=-1, keepdims=True)
    centered = value - row_mean
    inverse = lax.rsqrt(jnp.mean(centered * centered, axis=-1, keepdims=True) + EPSILON)
    return (centered * inverse, inverse)


def norm_back(grad_hat, normed, inverse):
    first = jnp.mean(grad_hat, axis=-1, keepdims=True)
    second = jnp.mean(grad_hat * normed, axis=-1, keepdims=True)
    return inverse * (grad_hat - first - normed * second)


def frame_scores(queries, keyset):
    return (
        jnp.einsum("fqhd,fkhd->fhqk", queries, keyset, preferred_element_type=jnp.float32) * SCALING
    )


def attend_block(pieces):
    queries, keyset, valueset = pieces
    scores = frame_scores(queries, keyset)
    row_top = jnp.max(scores, axis=-1, keepdims=True)
    expo = jnp.exp(scores - row_top)
    row_total = jnp.sum(expo, axis=-1, keepdims=True)
    attn_probs = (expo / row_total).astype(jnp.bfloat16)
    attended = jnp.einsum(
        "fhqk,fkhd->fqhd", attn_probs, valueset, preferred_element_type=jnp.float32
    )
    return (attended, (row_top + jnp.log(row_total))[..., 0])


def query_back(with_keys, pieces):
    queries, keyset, valueset, grad_att, log_total = pieces
    scores = frame_scores(queries, keyset)
    attn_probs = jnp.exp(scores - log_total[..., None])
    grad_probs = jnp.einsum(
        "fqhd,fkhd->fhqk", grad_att, valueset, preferred_element_type=jnp.float32
    )
    row_delta = jnp.sum(attn_probs * grad_probs, axis=-1)
    grad_scores = (attn_probs * (grad_probs - row_delta[..., None])).astype(jnp.bfloat16)
    grad_queries = (
        jnp.einsum("fhqk,fkhd->fqhd", grad_scores, keyset, preferred_element_type=jnp.float32)
        * SCALING
    )
    grad_keys = (
        jnp.einsum("fhqk,fqhd->fkhd", grad_scores, queries, preferred_element_type=jnp.float32)
        * SCALING
    )
    grad_values = jnp.einsum(
        "fhqk,fqhd->fkhd",
        attn_probs.astype(jnp.bfloat16),
        grad_att,
        preferred_element_type=jnp.float32,
    )
    return (grad_queries, grad_keys, grad_values)


def on_device(
    tokens,
    channel_mask,
    lead_index,
    chan_embed,
    lead_embed,
    norm1_gain,
    norm1_bias,
    qkv_weight,
    out_weight,
    out_bias,
    norm2_gain,
    norm2_bias,
    up_weight,
    up_bias,
    down_weight,
    down_bias,
    cotangent,
):
    lon_count = lax.axis_size("lon")
    lat_count = lax.axis_size("lat")
    frames_all, rows_here, cols_here, width = tokens.shape
    frames_here = frames_all // lon_count
    head_size = width // HEADS
    local_in, local_cot = (
        lax.all_to_all(tokens, "lon", split_axis=0, concat_axis=2, tiled=True),
        lax.all_to_all(cotangent, "lon", split_axis=0, concat_axis=2, tiled=True),
    )
    cols_all = local_in.shape[2]
    rows_frame = rows_here * cols_all
    keys_frame = rows_frame * lat_count
    count_tok = frames_here * rows_frame
    frames_per = max(1, 512 // rows_frame)
    while frames_here % frames_per:
        frames_per -= 1
    group = frames_here // frames_per

    def split(value):
        return value.reshape((group, frames_per) + value.shape[1:])

    def join(value):
        return value.reshape((frames_here,) + value.shape[2:])

    first = lax.axis_index("lon") * frames_here
    mask_here = lax.dynamic_slice_in_dim(channel_mask, first, frames_here, 0).astype(jnp.float32)
    lead_here = lax.dynamic_slice_in_dim(lead_index, first, frames_here, 0)
    lead_onehot = (
        lead_here[:, None] == jnp.arange(lead_embed.shape[0], dtype=jnp.int32)[None, :]
    ).astype(jnp.float32)
    chan_add = jnp.dot(
        mask_here.astype(jnp.bfloat16), chan_embed, preferred_element_type=jnp.float32
    )
    lead_add = jnp.dot(
        lead_onehot.astype(jnp.bfloat16), lead_embed, preferred_element_type=jnp.float32
    )
    gain_one = norm1_gain.astype(jnp.float32)
    gain_two = norm2_gain.astype(jnp.float32)
    start = (
        local_in.astype(jnp.float32).reshape(frames_here, rows_frame, width) + chan_add[:, None, :]
    )
    normed1, inverse1 = layer_norm(start)
    hidden1 = normed1 * gain_one + norm1_bias.astype(jnp.float32) + lead_add[:, None, :]
    hidden1_low = hidden1.astype(jnp.bfloat16).reshape(count_tok, width)
    qkv = jnp.dot(hidden1_low, qkv_weight, preferred_element_type=jnp.float32).astype(jnp.bfloat16)
    qkv = qkv.reshape(frames_here, rows_here, cols_all, 3 * width)
    queries = qkv[..., :width].reshape(frames_here, rows_frame, HEADS, head_size)
    pairs = qkv[..., width:]
    pairs_whole = lax.all_gather(pairs, "lat", axis=1, tiled=True).reshape(
        frames_here, keys_frame, 2, HEADS, head_size
    )
    attended, log_total = lax.map(
        attend_block, (split(queries), split(pairs_whole[:, :, 0]), split(pairs_whole[:, :, 1]))
    )
    attended_low = join(attended).astype(jnp.bfloat16).reshape(count_tok, width)
    middle = (
        start.reshape(count_tok, width)
        + jnp.dot(attended_low, out_weight, preferred_element_type=jnp.float32)
        + out_bias.astype(jnp.float32)
    )
    normed2, inverse2 = layer_norm(middle)
    hidden2_low = (normed2 * gain_two + norm2_bias.astype(jnp.float32)).astype(jnp.bfloat16)
    pre_act = jnp.dot(hidden2_low, up_weight, preferred_element_type=jnp.float32) + up_bias.astype(
        jnp.float32
    )
    activ_low = jax.nn.gelu(pre_act).astype(jnp.bfloat16)
    result = (
        middle
        + jnp.dot(activ_low, down_weight, preferred_element_type=jnp.float32)
        + down_bias.astype(jnp.float32)
    )
    result_low = result.astype(jnp.bfloat16).reshape(frames_here, rows_here, cols_all, width)
    grad_low = local_cot.reshape(count_tok, width)
    grad_res = grad_low.astype(jnp.float32)
    grad_down_weight = jnp.dot(activ_low.T, grad_low, preferred_element_type=jnp.float32)
    grad_down_bias = jnp.sum(grad_res, axis=0)
    grad_activ = jnp.dot(grad_low, down_weight.T, preferred_element_type=jnp.float32)
    unused, gelu_pull = jax.vjp(jax.nn.gelu, pre_act)
    grad_pre = gelu_pull(grad_activ)[0].astype(jnp.bfloat16)
    grad_up_weight = jnp.dot(hidden2_low.T, grad_pre, preferred_element_type=jnp.float32)
    grad_up_bias = jnp.sum(grad_pre.astype(jnp.float32), axis=0)
    grad_hidden2 = jnp.dot(grad_pre, up_weight.T, preferred_element_type=jnp.float32)
    grad_gain2 = jnp.sum(grad_hidden2 * normed2, axis=0)
    grad_bias2 = jnp.sum(grad_hidden2, axis=0)
    grad_middle = grad_res + norm_back(grad_hidden2 * gain_two, normed2, inverse2)
    grad_branch = grad_middle.astype(jnp.bfloat16)
    grad_out_weight = jnp.dot(attended_low.T, grad_branch, preferred_element_type=jnp.float32)
    grad_out_bias = jnp.sum(grad_branch.astype(jnp.float32), axis=0)
    grad_att = jnp.dot(grad_branch, out_weight.T, preferred_element_type=jnp.float32).astype(
        jnp.bfloat16
    )
    grad_att = grad_att.reshape(frames_here, rows_frame, HEADS, head_size)
    pairs_back = lax.all_gather(pairs, "lat", axis=1, tiled=True).reshape(
        frames_here, keys_frame, 2, HEADS, head_size
    )
    keys_back = split(pairs_back[:, :, 0])
    values_back = split(pairs_back[:, :, 1])
    grad_queries, grad_keys, grad_values = lax.map(
        partial(query_back, True),
        (split(queries), keys_back, values_back, split(grad_att), log_total),
    )
    grad_keys = join(grad_keys).reshape(frames_here, lat_count * rows_here, cols_all, width)
    grad_values = join(grad_values).reshape(frames_here, lat_count * rows_here, cols_all, width)
    grad_pairs = lax.psum_scatter(
        jnp.concatenate([grad_keys, grad_values], axis=3).astype(jnp.bfloat16),
        "lat",
        scatter_dimension=1,
        tiled=True,
    ).astype(jnp.float32)
    grad_qkv = jnp.concatenate(
        [join(grad_queries).reshape(count_tok, width), grad_pairs.reshape(count_tok, 2 * width)],
        axis=1,
    ).astype(jnp.bfloat16)
    grad_qkv_weight = jnp.dot(hidden1_low.T, grad_qkv, preferred_element_type=jnp.float32)
    grad_hidden1 = jnp.dot(grad_qkv, qkv_weight.T, preferred_element_type=jnp.float32).reshape(
        frames_here, rows_frame, width
    )
    grad_gain1 = jnp.sum(grad_hidden1 * normed1, axis=(0, 1))
    grad_bias1 = jnp.sum(grad_hidden1, axis=(0, 1))
    grad_lead = jnp.dot(lead_onehot.T, jnp.sum(grad_hidden1, axis=1), precision=HIGHEST)
    grad_start = grad_middle.reshape(frames_here, rows_frame, width) + norm_back(
        grad_hidden1 * gain_one, normed1, inverse1
    )
    grad_chan = jnp.dot(mask_here.T, jnp.sum(grad_start, axis=1), precision=HIGHEST)
    grad_start_low = grad_start.astype(jnp.bfloat16).reshape(
        frames_here, rows_here, cols_all, width
    )
    out_patch, grad_patch = (
        lax.all_to_all(result_low, "lon", split_axis=2, concat_axis=0, tiled=True),
        lax.all_to_all(grad_start_low, "lon", split_axis=2, concat_axis=0, tiled=True),
    )
    partial_sums = (
        lax.psum_scatter(
            grad_chan.astype(jnp.bfloat16), "lon", scatter_dimension=1, tiled=True
        ).astype(jnp.float32),
        lax.psum_scatter(
            grad_lead.astype(jnp.bfloat16), "lon", scatter_dimension=1, tiled=True
        ).astype(jnp.float32),
        lax.psum_scatter(
            grad_gain1.astype(jnp.bfloat16), "lon", scatter_dimension=0, tiled=True
        ).astype(jnp.float32),
        lax.psum_scatter(
            grad_bias1.astype(jnp.bfloat16), "lon", scatter_dimension=0, tiled=True
        ).astype(jnp.float32),
        lax.psum_scatter(
            grad_qkv_weight.astype(jnp.bfloat16), "lon", scatter_dimension=0, tiled=True
        ).astype(jnp.float32),
        lax.psum_scatter(
            grad_out_weight.astype(jnp.bfloat16), "lon", scatter_dimension=0, tiled=True
        ).astype(jnp.float32),
        lax.psum_scatter(
            grad_out_bias.astype(jnp.bfloat16), "lon", scatter_dimension=0, tiled=True
        ).astype(jnp.float32),
        lax.psum_scatter(
            grad_gain2.astype(jnp.bfloat16), "lon", scatter_dimension=0, tiled=True
        ).astype(jnp.float32),
        lax.psum_scatter(
            grad_bias2.astype(jnp.bfloat16), "lon", scatter_dimension=0, tiled=True
        ).astype(jnp.float32),
        lax.psum_scatter(
            grad_up_weight.astype(jnp.bfloat16), "lon", scatter_dimension=0, tiled=True
        ).astype(jnp.float32),
        lax.psum_scatter(
            grad_up_bias.astype(jnp.bfloat16), "lon", scatter_dimension=0, tiled=True
        ).astype(jnp.float32),
        lax.psum_scatter(
            grad_down_weight.astype(jnp.bfloat16), "lon", scatter_dimension=0, tiled=True
        ).astype(jnp.float32),
        lax.psum_scatter(
            grad_down_bias.astype(jnp.bfloat16), "lon", scatter_dimension=0, tiled=True
        ).astype(jnp.float32),
    )
    full_sums = lax.psum(tuple(partial_sums), "lat")
    return (out_patch, grad_patch) + tuple(full_sums)


def solution(mesh):
    return jax.shard_map(
        on_device,
        mesh=mesh,
        in_specs=(
            P(None, "lat", "lon", None),
            P(),
            P(),
            P(),
            P(),
            P(),
            P(),
            P(),
            P(),
            P(),
            P(),
            P(),
            P(),
            P(),
            P(),
            P(),
            P(None, "lat", "lon", None),
        ),
        out_specs=(
            P(None, "lat", "lon", None),
            P(None, "lat", "lon", None),
            P(None, "lon"),
            P(None, "lon"),
            P("lon"),
            P("lon"),
            P("lon", None),
            P("lon", None),
            P("lon"),
            P("lon"),
            P("lon"),
            P("lon", None),
            P("lon"),
            P("lon", None),
            P("lon"),
        ),
        check_vma=False,
    )
```

profile of v0, /device:TPU:0, one launch (start us, length us, event | category | flops | bytes accessed | tf_op | source)
XLA Modules:
  0.0 1277.1 jit_solution(3150707313979500012)
XLA Ops:
  19.5 27.5 %all-to-all-done = bf16[16,16,4,768]{3,2,1,0:T(4,128)(2,1)} async-done(((bf16[16,16,4,768]{3,2,1,0:T(4,128)(2,1)}), bf16[16,16,4,768]{3,2,1,0:T(4,128)(2,1)}, u32[]{:S(2)}, u32[]{:S(2)}) %all-to-all-start) | async-done | bytes 1572896 | tf_op jit(solution)/shard_map/all_to_all | solution.py:99
  60.2 15.9 %fusion.18 = f32[1024]{0:T(1024)S(1)} fusion(f32[1,16,16,4,768]{4,0,3,2,1:T(1,128)} %copy.49, f32[1024]{0:T(1024)S(1)} %div.43, f32[768]{0:T(1024)S(1)} %convolution_reduce_fusion.1), kind=kLoop, calls=%fused_computation.49 | loop fusion | flops 3144704 | bytes 3156992 | tf_op jit(solution)/shard_map/reduce_sum | solution.py:19
  116.9 25.4 %all-to-all-done.2 = bf16[16,16,4,768]{3,2,1,0:T(4,128)(2,1)} async-done(((bf16[16,16,4,768]{3,2,1,0:T(4,128)(2,1)}), bf16[16,16,4,768]{3,2,1,0:T(4,128)(2,1)}, u32[]{:S(2)}, u32[]{:S(2)}) %all-to-all-start.2) | async-done | bytes 1572896 | tf_op jit(solution)/shard_map/all_to_all | solution.py:100
  160.0 98.0 %all-gather.2.cloned.1.call-done = bf16[1,32,64,1536]{2,1,3,0:T(8,128)(2,1)} async-done(((bf16[1,16,64,1536]{2,1,3,0:T(8,128)(2,1)}), bf16[1,32,64,1536]{2,1,3,0:T(8,128)(2,1)}) %all-gather.2.cloned.1.call-update) | async-done | bytes 6291472 | tf_op jit(solution)/shard_map/all_gather | solution.py:141
  258.0 17.9 %reshape.473 = bf16[1,2048,2,12,64]{1,4,3,2,0:T(8,128)(2,1)} reshape(bf16[1,32,64,1536]{2,1,3,0:T(8,128)(2,1)} %all-gather.2.cloned.1.call-done) | data formatting | bytes 12582912 | tf_op jit(solution)/shard_map/reshape | solution.py:141
  275.8 37.5 %multiply_reduce_fusion.1 = (f32[12,1024]{1,0:T(8,128)}, f32[12,1024,2048]{2,1,0:T(8,128)}) fusion(bf16[1024,12,64]{0,2,1:T(8,128)(2,1)} %reshape.475, bf16[1,2048,2,12,64]{1,4,3,2,0:T(8,128)(2,1)} %reshape.473), kind=kOutput, calls=%fused_computation.6 | convolution fusion | flops 3271544832 | bytes 105431040 | tf_op jit(solution)/shard_map/while/body/eval_jaxpr/fqhd,fkhd->fhqk/dot_general | solution.py:31
  313.4 31.9 %fusion = f32[12,1024]{1,0:T(8,128)} fusion(f32[12,1024,2048]{2,1,0:T(8,128)} %get-tuple-element.123, f32[12,1024]{1,0:T(8,128)} %get-tuple-element.122), kind=kLoop, calls=%fused_computation.5 | loop fusion | flops 75485184 | bytes 100761600 | tf_op jit(solution)/shard_map/while/body/eval_jaxpr/reduce_sum | solution.py:40
  346.7 36.0 %fusion.27 = bf16[12,64,1024]{2,1,0:T(8,128)(2,1)} fusion(f32[12,1024,2048]{2,1,0:T(8,128)} %get-tuple-element.123, f32[12,1024]{1,0:T(8,128)} %fusion, f32[12,1024]{1,0:T(8,128)} %get-tuple-element.122, bf16[1,2048,2,12,64]{1,4,3,2,0:T(8,128)(2,1)} %reshape.473), kind=kOutput, calls=%fused_computation.60 | convolution fusion | flops 3322675200 | bytes 105512960 | tf_op jit(solution)/shard_map/while/body/eval_jaxpr/fhqk,fkhd->fqhd/dot_general | solution.py:42
  396.3 16.8 %fusion.42 = (bf16[3072]{0:T(1024)(128)(2,1)}, bf16[1024,3072]{1,0:T(8,128)(2,1)}) fusion(f32[1024,3072]{1,0:T(8,128)} %fusion.39, f32[3072]{0:T(1024)S(1)} %copy-done.24, bf16[1024,768]{1,0:T(8,128)(2,1)S(1)} %copy-done.4, bf16[3072,768]{1,0:T(8,128)(2,1)S(1)} %bitcast.138), kind=kOutput, calls=%fused_computation.100 | convolution fusion | flops 4901041152 | bytes 25184256 | tf_op jit(solution)/shard_map/dot_general | solution.py:169
  426.5 35.2 %fusion.20 = bf16[1,2048,12,64]{1,3,2,0:T(8,128)(2,1)} fusion(bf16[1024,12,64]{0,2,1:T(8,128)(2,1)S(1)} %bitcast.126, f32[12,1024,2048]{2,1,0:T(8,128)} %get-tuple-element.123, f32[12,1024]{1,0:T(8,128)S(1)} %copy-done.3), kind=kOutput, calls=%fused_computation.51 | convolution fusion | flops 3298295808 | bytes 105431040 | tf_op jit(solution)/shard_map/while/body/eval_jaxpr/fhqk,fqhd->fkhd/dot_general | solution.py:65
  461.7 68.6 %multiply_reduce_fusion = (f32[12,1024]{1,0:T(8,128)}, f32[12,1024,2048]{2,1,0:T(8,128)}) fusion(f32[12,1024,2048]{2,1,0:T(8,128)} %get-tuple-element.123, f32[12,1024]{1,0:T(8,128)} %log_add_fusion, bf16[1024,12,64]{0,2,1:T(8,128)(2,1)} %bitcast.127, bf16[1,2048,2,12,64]{1,4,3,2,0:T(8,128)(2,1)} %reshape.473), kind=kOutput, calls=%fused_computation.1 | convolution fusion | flops 3321876480 | bytes 206159872 | tf_op jit(solution)/shard_map/while/body/eval_jaxpr/fqhd,fkhd->fhqk/dot_general | solution.py:52
  540.4 78.3 %multiply_convert_fusion = bf16[12,1024,2048]{2,1,0:T(8,128)(2,1)} fusion(f32[12,1024,2048]{2,1,0:T(8,128)} %get-tuple-element.128, f32[12,1024,2048]{2,1,0:T(8,128)} %get-tuple-element.123, f32[12,1024]{1,0:T(8,128)} %get-tuple-element.127, f32[12,1024]{1,0:T(8,128)} %log_add_fusion), kind=kLoop, calls=%fused_computation | loop fusion | flops 125829120 | bytes 251756544 | tf_op jit(solution)/shard_map/while/body/eval_jaxpr/convert_element_type | solution.py:56
  618.7 20.1 %fusion.23 = bf16[1,2048,12,64]{1,3,2,0:T(8,128)(2,1)} fusion(bf16[1024,12,64]{0,2,1:T(8,128)(2,1)} %reshape.475, bf16[12,1024,2048]{2,1,0:T(8,128)(2,1)} %multiply_convert_fusion), kind=kOutput, calls=%fused_computation.52 | convolution fusion | flops 3224371200 | bytes 55050240 | tf_op jit(solution)/shard_map/while/body/eval_jaxpr/fhqk,fqhd->fkhd/dot_general | solution.py:62
  648.9 13.3 %pad_maximum_fusion = bf16[1,32,64,1536]{2,1,3,0:T(8,128)(2,1)} fusion(bf16[1,32,64,768]{2,1,3,0:T(8,128)(2,1)} %concatenate.21, bf16[1,32,64,768]{2,1,3,0:T(8,128)(2,1)} %concatenate.20), kind=kLoop, calls=%fused_computation.19 | loop fusion | flops 3145728 | bytes 12582912 | tf_op jit(solution)/shard_map/concatenate | solution.py:197
  667.4 13.6 %convolution_convert_fusion.1 = bf16[3072,768]{1,0:T(8,128)(2,1)} fusion(bf16[1024,768]{1,0:T(8,128)(2,1)} %reshape.479, f32[1024,3072]{1,0:T(8,128)} %fusion.39, f32[3072]{0:T(1024)S(1)} %copy-done.25), kind=kOutput, calls=%fused_computation.23 | convolution fusion | flops 4865654784 | bytes 18886656 | tf_op jit(solution)/shard_map/dot_general | solution.py:167
  716.1 23.5 %multiply_convert_fusion.3 = bf16[12,64,1024]{2,1,0:T(8,128)(2,1)} fusion(bf16[12,1024,2048]{2,1,0:T(8,128)(2,1)} %multiply_convert_fusion, bf16[1,2048,2,12,64]{1,4,3,2,0:T(8,128)(2,1)} %reshape.473), kind=kOutput, calls=%fused_computation.40 | convolution fusion | flops 3222798336 | bytes 55050240 | tf_op jit(solution)/shard_map/while/body/eval_jaxpr/fhqk,fkhd->fqhd/dot_general | solution.py:58
  742.2 64.6 %reduce-scatter.10.cloned.1.call-done = bf16[1,16,64,1536]{2,1,3,0:T(8,128)(2,1)} async-done(((bf16[1,32,64,1536]{2,1,3,0:T(8,128)(2,1)}), bf16[1,16,64,1536]{2,1,3,0:T(8,128)(2,1)}) %reduce-scatter.10.cloned.1.call-update) | async-done | bytes 3145744 | tf_op jit(solution)/shard_map/reduce_scatter | solution.py:196
  857.6 19.0 %reduce-scatter.16.cloned.1.call-done = bf16[48,768]{1,0:T(8,128)(2,1)} async-done(((bf16[768,768]{1,0:T(8,128)(2,1)}), bf16[48,768]{1,0:T(8,128)(2,1)}) %reduce-scatter.16.cloned.1.call-update) | async-done | bytes 73744 | tf_op jit(solution)/shard_map/reduce_scatter | solution.py:240
  879.9 82.0 %reduce-scatter.20.cloned.1.call-done = bf16[192,768]{1,0:T(8,128)(2,1)} async-done(((bf16[3072,768]{1,0:T(8,128)(2,1)}), bf16[192,768]{1,0:T(8,128)(2,1)}) %reduce-scatter.20.cloned.1.call-update) | async-done | bytes 294928 | tf_op jit(solution)/shard_map/reduce_scatter | solution.py:258
  961.9 78.9 %reduce-scatter.18.cloned.1.call-done = bf16[48,3072]{1,0:T(8,128)(2,1)} async-done(((bf16[768,3072]{1,0:T(8,128)(2,1)}), bf16[48,3072]{1,0:T(8,128)(2,1)}) %reduce-scatter.18.cloned.1.call-update) | async-done | bytes 294928 | tf_op jit(solution)/shard_map/reduce_scatter | solution.py:252
  1040.8 58.1 %all-reduce.8 = (bf16[768]{0:T(1024)(128)(2,1)}, bf16[768]{0:T(1024)(128)(2,1)}, bf16[768]{0:T(1024)(128)(2,1)}, bf16[768]{0:T(1024)(128)(2,1)}, bf16[768]{0:T(1...) all-reduce(bf16[768]{0:T(1024)(128)(2,1)} %get-tuple-element.90, ...), channel_id=5, replica_groups=mesh['lat'=2,'lon'=16] {'lon'}, use_global_device_ids=true, to_apply=%region_19.20.clone | all-reduce | flops 7680 | bytes 30720
  1106.8 47.4 %reduce-scatter.12.cloned.1.call-done = bf16[69,48]{0,1:T(8,128)(2,1)} async-done(((bf16[69,768]{0,1:T(8,128)(2,1)}), bf16[69,48]{0,1:T(8,128)(2,1)}) %reduce-scatter.12.cloned.1.call-update) | async-done | bytes 6640 | tf_op jit(solution)/shard_map/reduce_scatter | solution.py:225
  1157.5 67.6 %reduce-scatter.14.cloned.1.call-done = bf16[48,2304]{1,0:T(8,128)(2,1)} async-done(((bf16[768,2304]{1,0:T(8,128)(2,1)}), bf16[48,2304]{1,0:T(8,128)(2,1)}) %reduce-scatter.14.cloned.1.call-update) | async-done | bytes 221200 | tf_op jit(solution)/shard_map/reduce_scatter | solution.py:237
  1225.1 44.7 %all-reduce.10 = (f32[69,48]{0,1:T(8,128)}, f32[32,48]{1,0:T(8,128)}, f32[48]{0:T(128)}, f32[48]{0:T(128)}, f32[48,2304]{1,0:T(8,128)}, /*index=5*/f32[48,768]{1...) all-reduce(bf16[69,48]{0,1:T(8,128)(2,1)} %reduce-scatter.12.cloned, ...), channel_id=1, replica_groups=mesh['lat'=2,'lon'=16] {'lat'}, use_global_device_ids=true, to_apply=%region_14.15 | all-reduce | flops 447696 | bytes 2687136 | tf_op jit(solution)/shard_map/psum | solution.py:265
  (186 shorter events, 239.0 us)
Async XLA Ops:
  7.2 73.9 %copy-start = (bf16[768,2304]{1,0:T(8,128)(2,1)S(1)}, bf16[768,2304]{1,0:T(8,128)(2,1)}, u32[]{:S(2)}) copy-start(bf16[768,2304]{1,0:T(8,128)(2,1)} %param.24) | copy-start | bytes 10616836
  7.2 39.8 %all-to-all-start = ((bf16[16,16,4,768]{3,2,1,0:T(4,128)(2,1)}), bf16[16,16,4,768]{3,2,1,0:T(4,128)(2,1)}, u32[]{:S(2)}, u32[]{:S(2)}) async-start(bf16[16,16,4,768]{3,2,1,0:T(4,128)(2,1)} %param.17), calls=%async_computation | async-start | bytes 3145728 | tf_op jit(solution)/shard_map/all_to_all | solution.py:99
  14.9 243.0 %all-gather.2.cloned.1.call-start = ((), (), s32[]{:S(2)}) async-start(), calls=%async_computation.11 | async-start | bytes 18874368 | tf_op jit(solution)/shard_map/all_gather | solution.py:141
  15.0 66.0 %copy-start.14 = (f32[768]{0:T(1024)}, f32[768]{0:T(1024)S(1)}, u32[]{:S(2)}) copy-start(f32[768]{0:T(1024)S(1)} %convert_element_type.231) | copy-start | bytes 9220
  19.4 61.6 %copy-start.7 = (f32[768]{0:T(1024)}, f32[768]{0:T(1024)S(1)}, u32[]{:S(2)}) copy-start(f32[768]{0:T(1024)S(1)} %convolution_reduce_fusion.1) | copy-start | bytes 9220
  100.9 41.3 %all-to-all-start.2 = ((bf16[16,16,4,768]{3,2,1,0:T(4,128)(2,1)}), bf16[16,16,4,768]{3,2,1,0:T(4,128)(2,1)}, u32[]{:S(2)}, u32[]{:S(2)}) async-start(bf16[16,16,4,768]{3,2,1,0:T(4,128)(2,1)} %param.33), calls=%async_computation.2 | async-start | bytes 3145728 | tf_op jit(solution)/shard_map/all_to_all | solution.py:100
  110.2 696.6 %reduce-scatter.10.cloned.1.call-start = ((), (), s32[]{:S(2)}) async-start(), calls=%async_computation.12 | async-start | bytes 18874368 | tf_op jit(solution)/shard_map/reduce_scatter | solution.py:196
  346.7 36.0 %copy-start.8 = (f32[768]{0:T(1024)S(1)}, f32[768]{0:T(1024)}, u32[]{:S(2)}) copy-start(f32[768]{0:T(1024)} %copy-done.7) | copy-start | bytes 9220
  346.7 36.0 %copy-start.31 = (f32[768]{0:T(1024)S(1)}, f32[768]{0:T(1024)}, u32[]{:S(2)}) copy-start(f32[768]{0:T(1024)} %convert_element_type.241) | copy-start | bytes 9220
  387.4 34.3 %copy-start.1 = (f32[1024,768]{1,0:T(8,128)}, f32[1024,768]{1,0:T(8,128)S(1)}, u32[]{:S(2)}) copy-start(f32[1024,768]{1,0:T(8,128)S(1)} %get-tuple-element.125) | copy-start | bytes 9437188
  662.2 214.4 %reduce-scatter.16.cloned.1.call-start = ((), (), s32[]{:S(2)}) async-start(), calls=%async_computation.15 | async-start | bytes 1253376 | tf_op jit(solution)/shard_map/reduce_scatter | solution.py:240
  667.3 294.6 %reduce-scatter.20.cloned.1.call-start = ((), (), s32[]{:S(2)}) async-start(), calls=%async_computation.17 | async-start | bytes 5013504 | tf_op jit(solution)/shard_map/reduce_scatter | solution.py:258
  681.0 359.8 %reduce-scatter.18.cloned.1.call-start = ((), (), s32[]{:S(2)}) async-start(), calls=%async_computation.16 | async-start | bytes 5013504 | tf_op jit(solution)/shard_map/reduce_scatter | solution.py:252
  710.1 137.8 %all-to-all-start.1 = ((bf16[1,16,64,768]{3,1,0,2:T(8,128)(2,1)}), bf16[1,16,64,768]{3,1,0,2:T(8,128)(2,1)}, u32[]{:S(2)}, u32[]{:S(2)}) async-start(bf16[1,16,64,768]{3,1,0,2:T(8,128)(2,1)} %copy.52), calls=%async_computation.1 | async-start | bytes 3145728 | tf_op jit(solution)/shard_map/all_to_all | solution.py:221
  715.8 390.1 %reduce-scatter.22.cloned.1.call-start = ((), (), s32[]{:S(2)}) async-start(), calls=%async_computation.18 | async-start | bytes 208896
  742.2 72.3 %copy-start.9 = (f32[768]{0:T(1024)S(1)}, f32[768]{0:T(1024)}, u32[]{:S(2)}) copy-start(f32[768]{0:T(1024)} %copy-done.7) | copy-start | bytes 9220
  742.2 72.3 %copy-start.11 = (f32[1024]{0:T(1024)S(1)}, f32[1024]{0:T(1024)}, u32[]{:S(2)}) copy-start(f32[1024]{0:T(1024)} %copy-done.10) | copy-start | bytes 12292
  742.2 72.3 %copy-start.15 = (f32[768]{0:T(1024)S(1)}, f32[768]{0:T(1024)}, u32[]{:S(2)}) copy-start(f32[768]{0:T(1024)} %copy-done.14) | copy-start | bytes 9220
  742.2 72.3 %copy-start.17 = (f32[1024]{0:T(1024)S(1)}, f32[1024]{0:T(1024)}, u32[]{:S(2)}) copy-start(f32[1024]{0:T(1024)} %copy-done.16) | copy-start | bytes 12292
  828.6 325.5 %reduce-scatter.12.cloned.1.call-start = ((), (), s32[]{:S(2)}) async-start(), calls=%async_computation.13 | async-start | bytes 208896 | tf_op jit(solution)/shard_map/reduce_scatter | solution.py:225
  835.0 390.1 %reduce-scatter.14.cloned.1.call-start = ((), (), s32[]{:S(2)}) async-start(), calls=%async_computation.14 | async-start | bytes 3760128 | tf_op jit(solution)/shard_map/reduce_scatter | solution.py:237
  847.9 306.3 %all-to-all-start.3 = ((bf16[1,16,64,768]{3,1,0,2:T(8,128)(2,1)}), bf16[1,16,64,768]{3,1,0,2:T(8,128)(2,1)}, u32[]{:S(2)}, u32[]{:S(2)}) async-start(bf16[1,16,64,768]{3,1,0,2:T(8,128)(2,1)} %copy.56), calls=%async_computation.4 | async-start | bytes 3145728 | tf_op jit(solution)/shard_map/all_to_all | solution.py:222
  853.5 187.3 %copy-start.23 = (f32[768]{0:T(1024)S(1)}, f32[768]{0:T(1024)}, u32[]{:S(2)}) copy-start(f32[768]{0:T(1024)} %copy-done.22) | copy-start | bytes 9220
  853.5 187.3 %copy-start.27 = (bf16[768]{0:T(1024)(128)(2,1)S(1)}, bf16[768]{0:T(1024)(128)(2,1)}, u32[]{:S(2)}) copy-start(bf16[768]{0:T(1024)(128)(2,1)} %get-tuple-element.118) | copy-start | bytes 4612
  (34 other events, 245.9 us)
Sparse Core Ops, SparseCore 0:
  101.0 156.8 all-gather.1
  662.3 144.4 reduce-scatter.9
  810.4 66.0 reduce-scatter.15
  880.3 81.6 reduce-scatter.19
  966.1 74.6 reduce-scatter.17
  1044.7 52.6 reduce-scatter.21
  1101.5 52.6 reduce-scatter.11
  1158.0 67.0 reduce-scatter.13
where the time goes:
time: 1290 us; the launch traced here: 1280 us
  waiting for transfers between devices  511 us (40%)
  matrix products  331 us (26%)
  other arithmetic  172 us (13%)
  local copies, waits for them, and re-layouts  115 us (9%)
  blocking collectives  103 us (8%)
  starting transfers between devices  29.4 us (2%)
  between operations  16.4 us (1%)
    all_gather x1, waiting for transfers between devices, on_device(): lax.all_gather(pairs, 'lat', axis=1, tiled=True)  98 us
    reduce_scatter x1, waiting for transfers between devices, on_device(): lax.psum_scatter(grad_down_weight.astype(jnp.bfloat16), 'lon', scatter_di...  82 us
    reduce_scatter x1, waiting for transfers between devices, on_device(): lax.psum_scatter(grad_up_weight.astype(jnp.bfloat16), 'lon', scatter_dime...  78.9 us
    convert_element_type x1, other arithmetic, query_back(): (attn_probs * (grad_probs - row_delta[..., None])).astype(jnp.bfloat16)  78.3 us
    dot_general x1, matrix products, query_back(): jnp.einsum('fqhd,fkhd->fhqk', grad_att, valueset, preferred_element_type=...  68.6 us
    reduce_scatter x1, waiting for transfers between devices, on_device(): lax.psum_scatter(grad_qkv_weight.astype(jnp.bfloat16), 'lon', scatter_dim...  67.6 us
    reduce_scatter x1, waiting for transfers between devices, on_device(): lax.psum_scatter(jnp.concatenate([grad_keys, grad_values], axis=3).astype...  64.6 us
    unnamed x1, blocking collectives  58.1 us
  transfers between devices with their start and end apart: 12, of which 9 were waited for; matrix products, arithmetic and copies ran while one was open for 12% of the time, Pallas kernels for 0%

commit v1 on v0

v1 whole, which is shorter than its diff:
```python
import functools
import math

import jax
import jax.numpy as jnp
from jax import lax
from jax.experimental import pallas as pl
from jax.experimental.pallas import tpu as pltpu
from jax.sharding import Mesh, PartitionSpec as P

HEADS = 12
EPSILON = 1e-06
SCALING = 0.125
LOG2E = math.log2(math.e)
F32 = jnp.float32
BF = jnp.bfloat16
NN = (((1,), (0,)), ((), ()))
NT = (((1,), (1,)), ((), ()))
TN = (((0,), (0,)), ((), ()))
VMEM_LIMIT = 56 << 20


def mm(a, b, dims=NN):
    return lax.dot_general(a, b, dims, preferred_element_type=F32)


def of_head(value, head, axis=1):
    lane = lax.broadcasted_iota(jnp.int32, value.shape, axis)
    return jnp.where((lane // 64) == head, value, jnp.zeros_like(value))


def attend_kernel(q_ref, k0, k1, v0, v1, o_ref, full_ref, lse_ref):
    q = q_ref[...]
    ones = jnp.ones(v0.shape, BF)
    val0 = jnp.concatenate([v0[...], ones], 1)
    val1 = jnp.concatenate([v1[...], ones], 1)
    outs, logs = [], []
    for head in range(2):
        qm = of_head(q, head)
        s0 = mm(qm, k0[...], NT)
        s1 = mm(qm, k1[...], NT)
        top = jnp.max(jnp.maximum(s0, s1), axis=1, keepdims=True)
        p0 = jnp.exp2(s0 - top).astype(BF)
        p1 = jnp.exp2(s1 - top).astype(BF)
        both = mm(p0, val0) + mm(p1, val1)
        total = both[:, 128:]
        outs.append(both[:, :128] / total)
        logs.append(top + jnp.log2(total))
    lane = lax.broadcasted_iota(jnp.int32, outs[0].shape, 1)
    both = jnp.where(lane < 64, outs[0], outs[1])
    o_ref[...] = both.astype(BF)
    full_ref[...] = both
    turned = jnp.where(lane < 64, logs[0], logs[1]).T
    lse_ref[0:4, :] = turned[0:4]
    lse_ref[4:8, :] = turned[64:68]


def attend(q, kv_own, kv_peer, frames):
    tokens, width = q.shape
    pairs = width // 128
    n = tokens // frames
    bq = min(512, n)
    nb = n // bq
    qs = pl.BlockSpec((bq, 128), lambda f, p, j: (f * nb + j, p))
    ks = pl.BlockSpec((n, 128), lambda f, p, j: (f, p))
    vs = pl.BlockSpec((n, 128), lambda f, p, j: (f, pairs + p))
    ls = pl.BlockSpec((8, bq), lambda f, p, j: (p, f * nb + j))
    return pl.pallas_call(
        attend_kernel,
        grid=(frames, pairs, nb),
        in_specs=[qs, ks, ks, vs, vs],
        out_specs=[qs, qs, ls],
        out_shape=[
            jax.ShapeDtypeStruct((tokens, width), BF),
            jax.ShapeDtypeStruct((tokens, width), F32),
            jax.ShapeDtypeStruct((pairs * 8, tokens), F32),
        ],
        compiler_params=pltpu.CompilerParams(vmem_limit_bytes=VMEM_LIMIT),
        cost_estimate=pl.CostEstimate(
            flops=50_000_000_000, bytes_accessed=12_000_000, transcendentals=0
        ),
        name="attend",
    )(q, kv_own, kv_peer, kv_own, kv_peer)


def attend_back_kernel(
    q_ref, k0, k1, v0, v1, go_ref, o_ref, lse_ref, dq_ref, dk0, dk1, dv0, dv1, dka, dva
):
    j = pl.program_id(2)
    q = q_ref[...]
    go = go_ref[...]
    prod = (go.astype(F32) * o_ref[...]).T
    dq = None
    for part, (k, v) in enumerate(((k0, v0), (k1, v1))):
        keys = k[...]
        vals = v[...]
        turned = keys.T
        acc_v = acc_k = None
        for head in range(2):
            qm = of_head(q, head)
            gom = of_head(go, head)
            lse = lse_ref[4 * head : 4 * head + 1, :]
            delta = jnp.sum(prod[64 * head : 64 * head + 64], axis=0, keepdims=True)
            probs = jnp.exp2(mm(keys, qm, NT) - lse)
            ds = (probs * (mm(vals, gom, NT) - delta)).astype(BF)
            probs = probs.astype(BF)
            a = mm(probs, gom)
            b = mm(ds, qm)
            c = mm(of_head(turned, head, 0), ds)
            dq = c if dq is None else dq + c
            acc_v = a if acc_v is None else acc_v + a
            acc_k = b if acc_k is None else acc_k + b

        @pl.when(j == 0)
        def _():
            dva[part] = acc_v
            dka[part] = acc_k

        @pl.when(j > 0)
        def _():
            dva[part] += acc_v
            dka[part] += acc_k

    dq_ref[...] = (dq * SCALING).T.astype(BF)

    @pl.when(j == pl.num_programs(2) - 1)
    def _():
        back = SCALING / (SCALING * LOG2E)
        dk0[...] = (dka[0] * back).astype(BF)
        dk1[...] = (dka[1] * back).astype(BF)
        dv0[...] = dva[0].astype(BF)
        dv1[...] = dva[1].astype(BF)


def attend_back(q, kv_own, kv_peer, go, att, lse, frames, first, count):
    tokens, width = q.shape
    pairs = width // 128
    n = tokens // frames
    bq = min(512, n)
    nb = n // bq
    qs = pl.BlockSpec((bq, 128), lambda f, p, j: (f * nb + j, first + p))
    ks = pl.BlockSpec((n, 128), lambda f, p, j: (f, first + p))
    vs = pl.BlockSpec((n, 128), lambda f, p, j: (f, pairs + first + p))
    ls = pl.BlockSpec((8, bq), lambda f, p, j: (first + p, f * nb + j))
    qo = pl.BlockSpec((bq, 128), lambda f, p, j: (f * nb + j, p))
    ko = pl.BlockSpec((n, 128), lambda f, p, j: (f, p))
    shape = jax.ShapeDtypeStruct((tokens, 128 * count), BF)
    return pl.pallas_call(
        attend_back_kernel,
        grid=(frames, count, nb),
        in_specs=[qs, ks, ks, vs, vs, qs, qs, ls],
        out_specs=[qo, ko, ko, ko, ko],
        out_shape=[shape] * 5,
        scratch_shapes=[pltpu.VMEM((2, n, 128), F32)] * 2,
        compiler_params=pltpu.CompilerParams(vmem_limit_bytes=VMEM_LIMIT),
        cost_estimate=pl.CostEstimate(
            flops=14_000_000_000 * count, bytes_accessed=3_000_000 * count, transcendentals=0
        ),
        name="attend_back",
    )(q, kv_own, kv_peer, kv_own, kv_peer, go, att, lse)


def swap_pairs(size, bit):
    return [(i, i ^ (1 << bit)) for i in range(size)]


def halve(value, axis, bit, dim):
    size = lax.axis_size(axis)
    mine = (lax.axis_index(axis) >> bit) & 1
    keep = lax.dynamic_index_in_dim(value, mine, dim, keepdims=False)
    send = lax.dynamic_index_in_dim(value, 1 - mine, dim, keepdims=False)
    return keep + lax.ppermute(send, axis, swap_pairs(size, bit))


def bits_of(size):
    return size.bit_length() - 1


def scatter_sum(value, lat_first):
    lat, chips = lax.axis_size("lat"), lax.axis_size("chip")
    lb, cb = bits_of(lat), bits_of(chips)
    _, rows, cols = value.shape
    value = halve(value.reshape((chips, 2, rows, cols)), "core", 0, 1)

    def over_lat(value):
        lead = value.shape[0]
        for bit in reversed(range(lb)):
            value = value.reshape((lead, 2, value.shape[-2] // 2, cols))
            value = halve(value, "lat", bit, 1)
        return value

    def over_chip(value, bit):
        lead, left, width = value.shape
        value = value.reshape((lead // 2, 2, left, width))
        return halve(value, "chip", bit, 1)

    order = list(range(cb))
    if lat_first:
        value = over_lat(value)
        for bit in order:
            value = over_chip(value, bit)
    else:
        for bit in order[:1]:
            value = over_chip(value, bit)
        value = over_lat(value)
        for bit in order[1:]:
            value = over_chip(value, bit)
    value = value.reshape(value.shape[-2:])
    for bit in range(lb):
        other = lax.ppermute(value, "lat", swap_pairs(lat, bit))
        high = ((lax.axis_index("lat") >> bit) & 1) == 1
        value = jnp.where(
            high,
            jnp.concatenate([other, value], 0),
            jnp.concatenate([value, other], 0),
        )
    return value


def layer_norm(value):
    row_mean = jnp.mean(value, axis=-1, keepdims=True)
    centered = value - row_mean
    inverse = lax.rsqrt(jnp.mean(centered * centered, axis=-1, keepdims=True) + EPSILON)
    return centered * inverse, inverse


def norm_back(grad_hat, normed, inverse):
    first = jnp.mean(grad_hat, axis=-1, keepdims=True)
    second = jnp.mean(grad_hat * normed, axis=-1, keepdims=True)
    return inverse * (grad_hat - first - normed * second)


def to_frames(value, chips):
    frames_all, rows, cols, width = value.shape
    frames = frames_all // chips
    value = value.reshape(frames_all, rows * cols, width)
    value = lax.all_to_all(value, ("lat", "chip"), 0, 0, tiled=True)
    if frames > 1:
        value = value.reshape(chips, frames, rows * cols, width).swapaxes(0, 1)
    return value.reshape(-1, width)


def to_places(value, chips, frames_all, rows, cols):
    width = value.shape[-1]
    frames = frames_all // chips
    if frames > 1:
        value = value.reshape(frames, chips, rows * cols, width).swapaxes(0, 1)
    value = value.reshape(frames_all, rows * cols, width)
    value = lax.all_to_all(value, ("lat", "chip"), 0, 0, tiled=True)
    return value.reshape(frames_all, rows, cols, width)


def on_device(
    tokens,
    channel_mask,
    lead_index,
    chan_embed,
    lead_embed,
    norm1_gain,
    norm1_bias,
    qkv_weight,
    out_weight,
    out_bias,
    norm2_gain,
    norm2_bias,
    up_weight,
    up_bias,
    down_weight,
    down_bias,
    cotangent,
):
    lat = lax.axis_size("lat")
    chips = lat * lax.axis_size("chip")
    lon = 2 * lax.axis_size("chip")
    frames_all, rows_here, cols_here, width = tokens.shape
    frames = frames_all // chips
    leads = lead_embed.shape[0]
    place = (lax.axis_index("chip") * 2) + lax.axis_index("core")
    core_swap = swap_pairs(2, 0)

    local_in = to_frames(tokens, chips)
    local_cot = to_frames(cotangent, chips)
    count = local_in.shape[0]
    n = count // frames

    first = lax.axis_index(("lat", "chip")) * frames
    mask_here = lax.dynamic_slice_in_dim(channel_mask, first, frames, 0).astype(BF)
    lead_here = lax.dynamic_slice_in_dim(lead_index, first, frames, 0)
    lead_onehot = (lead_here[:, None] == jnp.arange(leads, dtype=jnp.int32)[None, :]).astype(BF)
    chan_add = mm(mask_here, chan_embed)
    lead_add = mm(lead_onehot, lead_embed)
    gain_one = norm1_gain.astype(F32)
    gain_two = norm2_gain.astype(F32)

    start = local_in.astype(F32).reshape(frames, n, width) + chan_add[:, None, :]
    normed1, inverse1 = layer_norm(start)
    hidden1 = normed1 * gain_one + norm1_bias.astype(F32) + lead_add[:, None, :]
    start = start.reshape(count, width)
    hidden1 = hidden1.astype(BF).reshape(count, width)
    kv_own = mm(hidden1, qkv_weight[:, width:]).astype(BF)
    kv_peer = lax.ppermute(kv_own, "core", core_swap)
    queries = (mm(hidden1, qkv_weight[:, :width]) * (SCALING * LOG2E)).astype(BF)
    attended, attended32, lse = attend(queries, kv_own, kv_peer, frames)

    middle = start + mm(attended, out_weight) + out_bias.astype(F32)
    normed2, inverse2 = layer_norm(middle)
    hidden2 = (normed2 * gain_two + norm2_bias.astype(F32)).astype(BF)
    pre_act = mm(hidden2, up_weight) + up_bias.astype(F32)
    activ = jax.nn.gelu(pre_act).astype(BF)
    result = middle + mm(activ, down_weight) + down_bias.astype(F32)
    out_patch = to_places(result.astype(BF), chips, frames_all, rows_here, cols_here)

    grad_res = local_cot.astype(F32)
    grad_down = mm(activ, local_cot, TN).astype(BF)
    grad_down_bias = jnp.sum(grad_res, axis=0)
    grad_activ = mm(local_cot, down_weight, NT)
    unused, gelu_pull = jax.vjp(jax.nn.gelu, pre_act)
    grad_pre32 = gelu_pull(grad_activ)[0]
    grad_pre = grad_pre32.astype(BF)
    grad_up = mm(hidden2, grad_pre, TN).astype(BF)
    grad_up_bias = jnp.sum(grad_pre.astype(F32), axis=0)
    grad_hidden2 = mm(grad_pre, up_weight, NT)
    grad_gain2 = jnp.sum(grad_hidden2 * normed2, axis=0)
    grad_bias2 = jnp.sum(grad_hidden2, axis=0)
    grad_middle = grad_res + norm_back(grad_hidden2 * gain_two, normed2, inverse2)
    grad_branch = grad_middle.astype(BF)
    grad_out = mm(attended, grad_branch, TN).astype(BF)
    grad_out_bias = jnp.sum(grad_branch.astype(F32), axis=0)
    grad_att = mm(grad_branch, out_weight, NT).astype(BF)

    share = width // lon
    ff_parts = grad_up_bias.shape[0] // width
    early = jnp.stack(
        [grad_down_bias, grad_gain2, grad_bias2, grad_out_bias]
        + [x for x in grad_up_bias.reshape(lon, ff_parts, share).swapaxes(0, 1).reshape(ff_parts, -1)]
    )
    early = early.reshape(4 + ff_parts, lon, share).swapaxes(0, 1).astype(BF)
    early = jnp.pad(early, ((0, 0), (0, 16 - early.shape[1]), (0, width - share)))
    grad_out = jnp.concatenate([grad_out.reshape(lon, share, width), early], 1)

    sum_down = scatter_sum(grad_down.reshape(lon, -1, width), True)
    sum_up = scatter_sum(grad_up.reshape(lon, share, -1), False)
    sum_out = scatter_sum(grad_out, True)

    step = 2
    pairs = width // 128
    dqs, dks, dvs = [], [], []
    for pair in range(0, pairs, step):
        dq, dk0, dk1, dv0, dv1 = attend_back(
            queries, kv_own, kv_peer, grad_att, attended32, lse, frames, pair, step
        )
        got_k = lax.ppermute(dk1, "core", core_swap)
        got_v = lax.ppermute(dv1, "core", core_swap)
        dqs.append(dq)
        dks.append(dk0 + got_k)
        dvs.append(dv0 + got_v)
    grad_qkv = jnp.concatenate(dqs + dks + dvs, axis=1)

    grad_hidden1 = mm(grad_qkv, qkv_weight, NT).reshape(frames, n, width)
    normed1 = normed1.reshape(frames, n, width)
    grad_gain1 = jnp.sum(grad_hidden1 * normed1, axis=(0, 1))
    grad_bias1 = jnp.sum(grad_hidden1, axis=1)
    grad_start = grad_middle.reshape(frames, n, width) + norm_back(
        grad_hidden1 * gain_one, normed1, inverse1
    )
    grad_frame = jnp.sum(grad_start, axis=1)
    grad_patch = to_places(
        grad_start.astype(BF).reshape(count, width), chips, frames_all, rows_here, cols_here
    )
    grad_qkv_weight = mm(hidden1, grad_qkv, TN).astype(BF).reshape(lon, share, -1)
    half = grad_qkv_weight.shape[-1] // 2
    sum_qkv = jnp.concatenate(
        [
            scatter_sum(grad_qkv_weight[..., :half], True),
            scatter_sum(grad_qkv_weight[..., half:], False),
        ],
        axis=1,
    )
    late = jnp.concatenate([grad_bias1, grad_frame, grad_gain1[None]], 0)
    late = lax.all_gather(late, ("lat", "chip", "core"), axis=0)
    late = lax.dynamic_slice_in_dim(late, place * share, share, 2)
    bias_of = late[:, :frames].reshape(chips, 2, frames, share).sum(1).reshape(frames_all, share)
    start_of = late[:, frames : 2 * frames].reshape(chips, 2, frames, share).sum(1)
    start_of = start_of.reshape(frames_all, share)
    sum_gain1 = late[:, 2 * frames].sum(0)
    hot = (lead_index[:, None] == jnp.arange(leads, dtype=jnp.int32)[None, :]).astype(F32)
    sum_lead = jnp.dot(hot.T, bias_of, precision=lax.Precision.HIGHEST)
    sum_chan = jnp.dot(
        channel_mask.astype(F32).T, start_of, precision=lax.Precision.HIGHEST
    )
    small = sum_out[share:, :share].astype(F32)
    return (
        out_patch,
        grad_patch,
        sum_chan,
        sum_lead,
        sum_gain1,
        bias_of.sum(0),
        sum_qkv.astype(F32),
        sum_out[:share].astype(F32),
        small[3],
        small[1],
        small[2],
        sum_up.astype(F32),
        small[4 : 4 + ff_parts].reshape(-1),
        sum_down.astype(F32),
        small[0],
    )


def solution(mesh):
    lat, lon = mesh.shape["lat"], mesh.shape["lon"]
    fine = Mesh(mesh.devices.reshape(lat, lon // 2, 2), ("lat", "chip", "core"))
    places = P(None, "lat", ("chip", "core"), None)
    wide = ("chip", "core")
    return jax.shard_map(
        on_device,
        mesh=fine,
        in_specs=(places,) + (P(),) * 15 + (places,),
        out_specs=(
            places,
            places,
            P(None, wide),
            P(None, wide),
            P(wide),
            P(wide),
            P(wide, None),
            P(wide, None),
            P(wide),
            P(wide),
            P(wide),
            P(wide, None),
            P(wide),
            P(wide, None),
            P(wide),
        ),
        check_vma=False,
    )
```

time: 1290 us -> 538 us (0.42)
  waiting for transfers between devices: 511 us -> 163 us
  matrix products: 331 us -> 97.9 us
  other arithmetic: 172 us -> 24.2 us
  Pallas kernels: 0 us -> 121 us
  local copies, waits for them, and re-layouts: 115 us -> 29 us
  blocking collectives: 103 us -> 43 us
  starting transfers between devices: 29.4 us -> 46.8 us
  between operations: 16.4 us -> 2.34 us
    reduce_scatter x6 -> x0, waiting for transfers between devices: 359 us -> none  [the longest x1 82 us: on_device(): lax.psum_scatter(grad_down_weight.astype(jnp.bfloat16), 'lon', scatter_di...]
    dot_general x20 -> x17, matrix products: 331 us -> 97.9 us  [the longest x15 96.2 us: mm(): return lax.dot_general(a, b, dims, preferred_element_type=F32)]
    pallas_call x0 -> x4, Pallas kernels: none -> 121 us  [the longest x3 75.7 us: attend_back(): pl.pallas_call(attend_back_kernel, grid=(frames, count, nb), in_specs=[qs...]
    ppermute x0 -> x37, waiting for transfers between devices: none -> 103 us  [the longest x25 78 us: halve(): return keep + lax.ppermute(send, axis, swap_pairs(size, bit))]
    all_gather x1 -> x0, waiting for transfers between devices: 98 us -> none  [on_device(): lax.all_gather(pairs, 'lat', axis=1, tiled=True)]
    convert_element_type x20 -> x14, other arithmetic: 93.6 us -> 4.35 us  [the longest x1 0.86 us: on_device(): sum_down.astype(F32)]
    unnamed x1 -> x0, blocking collectives: 58.1 us -> none
    psum x1 -> x0, blocking collectives: 44.7 us -> none  [on_device(): full_sums = lax.psum(tuple(partial_sums), 'lat')]
  transfers between devices with their start and end apart: 12 -> 41, of which waited for: 9 -> 23; matrix products, arithmetic and copies ran while one was open for 12% -> 13% of each run, Pallas kernels for 0% -> 14%
where the time goes in v1:
time: 538 us; the launch traced here: 528 us
  waiting for transfers between devices  163 us (30%)
  Pallas kernels  121 us (22%)
  matrix products  97.9 us (18%)
  starting transfers between devices  46.8 us (9%)
  blocking collectives  43 us (8%)
  local copies, waits for them, and re-layouts  29 us (5%)
  other arithmetic  24.2 us (4%)
    dot_general x15, matrix products, mm(): return lax.dot_general(a, b, dims, preferred_element_type=F32)  96.2 us
    ppermute x25, waiting for transfers between devices, halve(): return keep + lax.ppermute(send, axis, swap_pairs(size, bit))  78 us
    pallas_call x3, Pallas kernels, attend_back(): pl.pallas_call(attend_back_kernel, grid=(frames, count, nb), in_specs=[qs...  75.7 us
    all_to_all x2, waiting for transfers between devices, to_frames(): value = lax.all_to_all(value, ('lat', 'chip'), 0, 0, tiled=True)  60.1 us
    pallas_call x1, Pallas kernels, attend(): pl.pallas_call(attend_kernel, grid=(frames, pairs, nb), in_specs=[qs, ks,...  45.3 us
    all_gather x1, blocking collectives, on_device(): late = lax.all_gather(late, ('lat', 'chip', 'core'), axis=0)  43 us
    ppermute x5, waiting for transfers between devices, scatter_sum(): other = lax.ppermute(value, 'lat', swap_pairs(lat, bit))  22.7 us
    ppermute x25, starting transfers between devices, halve(): return keep + lax.ppermute(send, axis, swap_pairs(size, bit))  17.7 us
  transfers between devices with their start and end apart: 41, of which 23 were waited for; matrix products, arithmetic and copies ran while one was open for 13% of the time, Pallas kernels for 14%

profile of v1, /device:TPU:0, one launch (start us, length us, event | category | flops | bytes accessed | tf_op | source)
XLA Modules:
  0.0 527.7 jit_solution(7276280841997871390)
XLA Ops:
  4.5 8.5 %all-to-all-start = ((bf16[16,64,768]{2,1,0:T(8,128)(2,1)}), bf16[16,64,768]{2,1,0:T(8,128)(2,1)S(1)}, u32[]{:S(2)}, u32[]{:S(2)}) async-start(bf16[16,64,768]{2,1,0:T(8,128)(2,1)} %reshape.440), calls=%async_computation | async-start | bytes 3145728 | tf_op jit(solution)/shard_map/all_to_all | solution.py:237
  19.0 30.7 %all-to-all-done = bf16[16,64,768]{2,1,0:T(8,128)(2,1)S(1)} async-done(((bf16[16,64,768]{2,1,0:T(8,128)(2,1)}), bf16[16,64,768]{2,1,0:T(8,128)(2,1)S(1)}, u32[]{:S(2)}, u32[]{:S(2)}) %all-to-all-start) | async-done | bytes 1572896 | tf_op jit(solution)/shard_map/all_to_all | solution.py:237
  61.1 29.4 %all-to-all-done.2 = bf16[16,64,768]{2,1,0:T(8,128)(2,1)} async-done(((bf16[16,64,768]{2,1,0:T(8,128)(2,1)}), bf16[16,64,768]{2,1,0:T(8,128)(2,1)}, u32[]{:S(2)}, u32[]{:S(2)}) %all-to-all-start.2) | async-done | bytes 1572896 | tf_op jit(solution)/shard_map/all_to_all | solution.py:237
  97.2 45.3 %attend.1 = (bf16[1024,768]{1,0:T(8,128)(2,1)}, f32[1024,768]{1,0:T(8,128)}, f32[48,1024]{1,0:T(8,128)}) custom-call(bf16[1024,768]{1,0:T(8,128)(2,1)} %multiply_convert_fusion.1.q_ref, bf16[1024,1536]{1,0:T(8,128)(2,1)} %convolution_convert_fusion.3.k0.v0, bf16[1024,1536]{1,0:T(8,128)(2,1)} %collective-permute-done.k1.v1, ...), custom_call_target="tpu_custom_call" | custom-call | flops 49999998976 | bytes 12000000 | tf_op jit(solution)/shard_map/attend/pallas_call | solution.py:68
  146.3 8.4 %fusion.31 = f32[1024,3072]{1,0:T(8,128)} fusion(bf16[768,3072]{1,0:T(8,128)(2,1)S(1)} %bitcast.250, f32[1024,768]{1,0:T(8,128)S(1)} %get-tuple-element.74, f32[768]{0:T(1024)S(1)} %convert_element_type.146, f32[768]{0:T(1024)S(1)} %convert_element_type.145, f32[1024]{0:T(1024)S(1)} %add_rsqrt_fusion, f32[1024]{0:T(1024)S(1)} %broadcast_multiply_fusion.5), kind=kOutput, calls=%fused_computation.149 | convolution fusion | flops 4835770368 | bytes 20461568 | tf_op jit(solution)/shard_map/dot_general | solution.py:24
  154.7 12.8 %convolution_convert_fusion = bf16[3072,768]{1,0:T(8,128)(2,1)} fusion(bf16[1024,768]{1,0:T(8,128)(2,1)} %bitcast.7, f32[1024,3072]{1,0:T(8,128)} %fusion.31, f32[3072]{0:T(1024)S(1)} %convert_element_type.148), kind=kOutput, calls=%fused_computation.10 | convolution fusion | flops 4865654784 | bytes 18886656 | tf_op jit(solution)/shard_map/dot_general | solution.py:24
  167.5 16.8 %fusion.36 = (bf16[3072]{0:T(1024)(128)(2,1)S(1)}, bf16[1024,3072]{1,0:T(8,128)(2,1)}) fusion(f32[1024,3072]{1,0:T(8,128)} %fusion.31, f32[3072]{0:T(1024)S(1)} %convert_element_type.148, bf16[1024,768]{1,0:T(8,128)(2,1)} %bitcast.7, bf16[3072,768]{1,0:T(8,128)(2,1)S(1)} %bitcast.252), kind=kOutput, calls=%fused_computation.154 | convolution fusion | flops 4901041152 | bytes 25184256 | tf_op jit(solution)/shard_map/dot_general | solution.py:24
  184.3 7.9 %multiply_reduce_fusion = (bf16[768]{0:T(1024)(128)(2,1)S(1)}, f32[1024]{0:T(1024)S(1)}, f32[1024]{0:T(1024)S(1)}, bf16[768]{0:T(1024)(128)(2,1)S(1)}, f32[1024,768]{1,0:T(8,128)S(1)}) fusion(f32[1024,768]{1,0:T(8,128)S(1)} %get-tuple-element.74, f32[1024]{0:T(1024)S(1)} %add_rsqrt_fusion, f32[1024]{0:T(1024)S(1)} %broadcast_multiply_fusion.5, ...), kind=kOutput, calls=%fused_computation.19 | convolution fusion | flops 4838912000 | bytes 17324032 | tf_op jit(solution)/shard_map/dot_general | solution.py:24
  192.2 10.4 %convolution_convert_fusion.1 = bf16[768,3072]{1,0:T(8,128)(2,1)} fusion(bf16[1024,3072]{1,0:T(8,128)(2,1)} %get-tuple-element.78, f32[1024,768]{1,0:T(8,128)S(1)} %get-tuple-element.74, f32[768]{0:T(1024)S(1)} %convert_element_type.146, f32[768]{0:T(1024)S(1)} %convert_element_type.145, f32[1024]{0:T(1024)S(1)} %add_rsqrt_fusion, ...), kind=kOutput, calls=%fused_computation.11 | convolution fusion | flops 4838129664 | bytes 14170112 | tf_op jit(solution)/shard_map/dot_general | solution.py:24
  210.4 11.8 %add_convert_fusion = bf16[1024,768]{1,0:T(8,128)(2,1)} fusion(f32[1024,768]{1,0:T(8,128)S(1)} %get-tuple-element.74, bf16[3072,768]{1,0:T(8,128)(2,1)S(1)} %bitcast.252, f32[768]{0:T(1024)S(1)} %convert_element_type.150, f32[1024,3072]{1,0:T(8,128)} %fusion.31, f32[3072]{0:T(1024)S(1)} %convert_element_type.148), kind=kOutput, calls=%fused_computation.25 | convolution fusion | flops 4865654784 | bytes 22035456 | tf_op jit(solution)/shard_map/dot_general | solution.py:24
  234.8 25.2 %attend_back.4 = (bf16[1024,256]{1,0:T(8,128)(2,1)}, bf16[1024,256]{1,0:T(8,128)(2,1)}, bf16[1024,256]{1,0:T(8,128)(2,1)}, bf16[1024,256]{1,0:T(8,128)(2,1)}, bf16[1024,256]{1,0:T(8,128)(2,1)}) custom-call(bf16[1024,768]{1,0:T(8,128)(2,1)} %multiply_convert_fusion.1.q_ref, bf16[1024,1536]{1,0:T(8,128)(2,1)} %convolution_convert_fusion.3.k0.v0, ...), custom_call_target="tpu_custom_call" | custom-call | flops 28000000000 | bytes 6000000 | tf_op jit(solution)/shard_map/attend_back/pallas_call | solution.py:148
  260.6 25.1 %attend_back.3 = (bf16[1024,256]{1,0:T(8,128)(2,1)}, bf16[1024,256]{1,0:T(8,128)(2,1)}, bf16[1024,256]{1,0:T(8,128)(2,1)}, bf16[1024,256]{1,0:T(8,128)(2,1)}, bf16[1024,256]{1,0:T(8,128)(2,1)}) custom-call(bf16[1024,768]{1,0:T(8,128)(2,1)} %multiply_convert_fusion.1.q_ref, bf16[1024,1536]{1,0:T(8,128)(2,1)} %convolution_convert_fusion.3.k0.v0, ...), custom_call_target="tpu_custom_call" | custom-call | flops 28000000000 | bytes 6000000 | tf_op jit(solution)/shard_map/attend_back/pallas_call | solution.py:148
  285.8 25.4 %attend_back.5 = (bf16[1024,256]{1,0:T(8,128)(2,1)}, bf16[1024,256]{1,0:T(8,128)(2,1)}, bf16[1024,256]{1,0:T(8,128)(2,1)}, bf16[1024,256]{1,0:T(8,128)(2,1)}, bf16[1024,256]{1,0:T(8,128)(2,1)}) custom-call(bf16[1024,768]{1,0:T(8,128)(2,1)} %multiply_convert_fusion.1.q_ref, bf16[1024,1536]{1,0:T(8,128)(2,1)} %convolution_convert_fusion.3.k0.v0, ...), custom_call_target="tpu_custom_call" | custom-call | flops 28000000000 | bytes 6000000 | tf_op jit(solution)/shard_map/attend_back/pallas_call | solution.py:148
  317.6 5.3 %convolution_convert_fusion.2 = bf16[768,2304]{1,0:T(8,128)(2,1)} fusion(bf16[1024,768]{1,0:T(8,128)(2,1)S(1)} %copy-done.9, bf16[1024,2304]{1,0:T(8,128)(2,1)S(1)} %add_dynamic-update-slice_fusion), kind=kOutput, calls=%fused_computation.12 | convolution fusion | flops 3625648128 | bytes 9830400 | tf_op jit(solution)/shard_map/dot_general | solution.py:24
  330.3 43.0 %all-gather.1 = f32[32,3,768]{2,1,0:T(4,128)S(1)} all-gather(f32[1,3,768]{2,1,0:T(4,128)S(1)} %maximum_bitcast_fusion), channel_id=2, replica_groups=mesh['lat'=2,'chip'=8,'core'=2] {'lat','chip','core'}, dimensions={0}, use_global_device_ids=true | all-gather | bytes 304128 | tf_op jit(solution)/shard_map/all_gather | solution.py:380
  379.8 9.7 %collective-permute-done.20 = bf16[8,32,768]{2,1,0:T(8,128)(2,1)S(1)} collective-permute-done((bf16[8,32,768]{2,1,0:T(8,128)(2,1)S(1)}, bf16[8,32,768]{2,1,0:T(8,128)(2,1)S(1)}, u32[]{:S(2)}, u32[]{:S(2)}) %collective-permute-start.20) | collective-permute-done | bytes 393248 | tf_op jit(solution)/shard_map/ppermute | solution.py:172
  390.5 5.3 %collective-permute-done.21 = bf16[4,32,768]{2,1,0:T(8,128)(2,1)S(1)} collective-permute-done((bf16[4,32,768]{2,1,0:T(8,128)(2,1)S(1)}, bf16[4,32,768]{2,1,0:T(8,128)(2,1)S(1)}, u32[]{:S(2)}, u32[]{:S(2)}) %collective-permute-start.21) | collective-permute-done | bytes 196640 | tf_op jit(solution)/shard_map/ppermute | solution.py:172
  400.8 4.8 collective-permute-done.23
  412.1 5.9 %collective-permute-done.14 = bf16[4,48,1152]{2,1,0:T(8,128)(2,1)} collective-permute-done((bf16[4,48,1152]{2,1,0:T(8,128)(2,1)}, bf16[4,48,1152]{2,1,0:T(8,128)(2,1)}, u32[]{:S(2)}, u32[]{:S(2)}) %collective-permute-start.14) | collective-permute-done | bytes 442400 | tf_op jit(solution)/shard_map/ppermute | solution.py:172
  439.5 20.3 %collective-permute-done.12 = bf16[24,1152]{1,0:T(8,128)(2,1)S(1)} collective-permute-done((bf16[24,1152]{1,0:T(8,128)(2,1)S(1)}, bf16[24,1152]{1,0:T(8,128)(2,1)S(1)}, u32[]{:S(2)}, u32[]{:S(2)}) %collective-permute-start.12) | collective-permute-done | bytes 55328 | tf_op jit(solution)/shard_map/ppermute | solution.py:210
  464.1 5.8 %collective-permute-done.33 = bf16[4,96,768]{2,1,0:T(8,128)(2,1)S(1)} collective-permute-done((bf16[4,96,768]{2,1,0:T(8,128)(2,1)S(1)}, bf16[4,96,768]{2,1,0:T(8,128)(2,1)S(1)}, u32[]{:S(2)}, u32[]{:S(2)}) %collective-permute-start.33) | collective-permute-done | bytes 589856 | tf_op jit(solution)/shard_map/ppermute | solution.py:172
  470.9 7.0 %collective-permute-done.27 = bf16[4,24,3072]{2,1,0:T(8,128)(2,1)S(1)} collective-permute-done((bf16[4,24,3072]{2,1,0:T(8,128)(2,1)S(1)}, bf16[4,24,3072]{2,1,0:T(8,128)(2,1)S(1)}, u32[]{:S(2)}, u32[]{:S(2)}) %collective-permute-start.27) | collective-permute-done | bytes 589856 | tf_op jit(solution)/shard_map/ppermute | solution.py:172
  487.3 19.4 %collective-permute-done.28 = bf16[2,24,3072]{2,1,0:T(8,128)(2,1)S(1)} collective-permute-done((bf16[2,24,3072]{2,1,0:T(8,128)(2,1)S(1)}, bf16[2,24,3072]{2,1,0:T(8,128)(2,1)S(1)}, u32[]{:S(2)}, u32[]{:S(2)}) %collective-permute-start.28) | collective-permute-done | bytes 294944 | tf_op jit(solution)/shard_map/ppermute | solution.py:172
  511.2 5.3 %collective-permute-done.35 = bf16[1,96,768]{2,1,0:T(8,128)(2,1)S(1)} collective-permute-done((bf16[1,96,768]{2,1,0:T(8,128)(2,1)S(1)}, bf16[1,96,768]{2,1,0:T(8,128)(2,1)S(1)}, u32[]{:S(2)}, u32[]{:S(2)}) %collective-permute-start.35) | collective-permute-done | bytes 147488 | tf_op jit(solution)/shard_map/ppermute | solution.py:172
  (302 shorter events, 135.9 us)
Async XLA Ops:
  4.5 45.2 %all-to-all-start = ((bf16[16,64,768]{2,1,0:T(8,128)(2,1)}), bf16[16,64,768]{2,1,0:T(8,128)(2,1)S(1)}, u32[]{:S(2)}, u32[]{:S(2)}) async-start(bf16[16,64,768]{2,1,0:T(8,128)(2,1)} %reshape.440), calls=%async_computation | async-start | bytes 3145728 | tf_op jit(solution)/shard_map/all_to_all | solution.py:237
  49.7 40.9 %all-to-all-start.2 = ((bf16[16,64,768]{2,1,0:T(8,128)(2,1)}), bf16[16,64,768]{2,1,0:T(8,128)(2,1)}, u32[]{:S(2)}, u32[]{:S(2)}) async-start(bf16[16,64,768]{2,1,0:T(8,128)(2,1)} %reshape.444), calls=%async_computation.2 | async-start | bytes 3145728 | tf_op jit(solution)/shard_map/all_to_all | solution.py:237
  61.0 36.2 %collective-permute-start = (bf16[1024,1536]{1,0:T(8,128)(2,1)}, bf16[1024,1536]{1,0:T(8,128)(2,1)}, u32[]{:S(2)}, u32[]{:S(2)}) collective-permute-start(bf16[1024,1536]{1,0:T(8,128)(2,1)} %convolution_convert_fusion.3.k0.v0), channel_id=1, source_target_pairs={{0,1},{1,0},{2,3},{3,2},{4,5},{5,4},{6,7},{7,6},{8,9},{9,8},{10,11... | collective-permute-start | bytes 9437192 | tf_op jit(solution)/shard_map/ppermute | solution.py:301
  222.2 255.9 %all-to-all-start.1 = ((bf16[16,64,768]{2,1,0:T(8,128)(2,1)}), bf16[16,64,768]{2,1,0:T(8,128)(2,1)S(1)}, u32[]{:S(2)}, u32[]{:S(2)}) async-start(bf16[16,64,768]{2,1,0:T(8,128)(2,1)} %bitcast.236), calls=%async_computation.1 | async-start | bytes 3145728 | tf_op jit(solution)/shard_map/all_to_all | solution.py:249
  229.7 200.6 %collective-permute-start.31 = (bf16[8,192,768]{2,1,0:T(8,128)(2,1)}, bf16[8,192,768]{2,1,0:T(8,128)(2,1)}, u32[]{:S(2)}, u32[]{:S(2)}) collective-permute-start(bf16[8,192,768]{2,1,0:T(8,128)(2,1)} %dynamic-slice_bitcast_fusion), channel_id=1, source_target_pairs={{0,1},{1,0},{2,3},{3,2},{4,5},{5,4},{6,7},{7,6},{8,9},{9,8},{10,11... | collective-permute-start | bytes 7077896 | tf_op jit(solution)/shard_map/ppermute | solution.py:172
  231.1 145.7 %collective-permute-start.19 = (bf16[8,64,768]{2,1,0:T(8,128)(2,1)}, bf16[8,64,768]{2,1,0:T(8,128)(2,1)}, u32[]{:S(2)}, u32[]{:S(2)}) collective-permute-start(bf16[8,64,768]{2,1,0:T(8,128)(2,1)} %fusion.13), channel_id=1, source_target_pairs={{0,1},{1,0},{2,3},{3,2},{4,5},{5,4},{6,7},{7,6},{8,9},{9,8},{10,11... | collective-permute-start | bytes 2359304 | tf_op jit(solution)/shard_map/ppermute | solution.py:172
  234.8 199.8 %collective-permute-start.25 = (bf16[8,48,3072]{2,1,0:T(8,128)(2,1)}, bf16[8,48,3072]{2,1,0:T(8,128)(2,1)}, u32[]{:S(2)}, u32[]{:S(2)}) collective-permute-start(bf16[8,48,3072]{2,1,0:T(8,128)(2,1)} %dynamic-slice_bitcast_fusion.1), channel_id=1, source_target_pairs={{0,1},{1,0},{2,3},{3,2},{4,5},{5,4},{6,7},{7,6},{8,9},{9,8},{10,11... | collective-permute-start | bytes 7077896 | tf_op jit(solution)/shard_map/ppermute | solution.py:172
  260.0 53.4 %collective-permute-start.2 = (bf16[1024,256]{1,0:T(8,128)(2,1)}, bf16[1024,256]{1,0:T(8,128)(2,1)S(1)}, u32[]{:S(2)}, u32[]{:S(2)}) collective-permute-start(bf16[1024,256]{1,0:T(8,128)(2,1)} %get-tuple-element.42), channel_id=1, source_target_pairs={{0,1},{1,0},{2,3},{3,2},{4,5},{5,4},{6,7},{7,6},{8,9},{9,8},{10,11... | collective-permute-start | bytes 1572872 | tf_op jit(solution)/shard_map/ppermute | solution.py:352
  285.7 26.9 %collective-permute-start.1 = (bf16[1024,256]{1,0:T(8,128)(2,1)}, bf16[1024,256]{1,0:T(8,128)(2,1)S(1)}, u32[]{:S(2)}, u32[]{:S(2)}) collective-permute-start(bf16[1024,256]{1,0:T(8,128)(2,1)} %get-tuple-element.40), channel_id=1, source_target_pairs={{0,1},{1,0},{2,3},{3,2},{4,5},{5,4},{6,7},{7,6},{8,9},{9,8},{10,11... | collective-permute-start | bytes 1572872 | tf_op jit(solution)/shard_map/ppermute | solution.py:352
  376.4 19.5 %collective-permute-start.7 = (bf16[8,48,1152]{2,1,0:T(8,128)(2,1)S(1)}, bf16[8,48,1152]{2,1,0:T(8,128)(2,1)S(1)}, u32[]{:S(2)}, u32[]{:S(2)}) collective-permute-start(bf16[8,48,1152]{2,1,0:T(8,128)(2,1)S(1)} %dynamic-slice_bitcast_fusion.5), channel_id=1, source_target_pairs={{0,1},{1,0},{2,3},{3,2},{4,5},{5,4},{6,7},{7,6},{8,9},{9,8},{10,11... | collective-permute-start | bytes 2654216 | tf_op jit(solution)/shard_map/ppermute | solution.py:172
  378.1 11.3 %collective-permute-start.20 = (bf16[8,32,768]{2,1,0:T(8,128)(2,1)S(1)}, bf16[8,32,768]{2,1,0:T(8,128)(2,1)S(1)}, u32[]{:S(2)}, u32[]{:S(2)}) collective-permute-start(bf16[8,32,768]{2,1,0:T(8,128)(2,1)S(1)} %dynamic-slice_bitcast_fusion.10), channel_id=1, source_target_pairs={{0,16},{16,0},{1,17},{17,1},{2,18},{18,2},{3,19},{19,3},{4,20},{20... | collective-permute-start | bytes 1179656 | tf_op jit(solution)/shard_map/ppermute | solution.py:172
  378.9 21.8 %collective-permute-start.13 = (bf16[8,48,1152]{2,1,0:T(8,128)(2,1)S(1)}, bf16[8,48,1152]{2,1,0:T(8,128)(2,1)S(1)}, u32[]{:S(2)}, u32[]{:S(2)}) collective-permute-start(bf16[8,48,1152]{2,1,0:T(8,128)(2,1)S(1)} %dynamic-slice_bitcast_fusion.4), channel_id=1, source_target_pairs={{0,1},{1,0},{2,3},{3,2},{4,5},{5,4},{6,7},{7,6},{8,9},{9,8},{10,11... | collective-permute-start | bytes 2654216 | tf_op jit(solution)/shard_map/ppermute | solution.py:172
  396.9 14.8 %collective-permute-start.8 = (bf16[8,24,1152]{2,1,0:T(8,128)(2,1)}, bf16[8,24,1152]{2,1,0:T(8,128)(2,1)S(1)}, u32[]{:S(2)}, u32[]{:S(2)}) collective-permute-start(bf16[8,24,1152]{2,1,0:T(8,128)(2,1)} %dynamic-slice_bitcast_fusion.9), channel_id=1, source_target_pairs={{0,16},{16,0},{1,17},{17,1},{2,18},{18,2},{3,19},{19,3},{4,20},{20... | collective-permute-start | bytes 1327112 | tf_op jit(solution)/shard_map/ppermute | solution.py:172
  426.2 11.1 %collective-permute-start.11 = (bf16[1,24,1152]{2,1,0:T(8,128)(2,1)S(1)}, bf16[1,24,1152]{2,1,0:T(8,128)(2,1)S(1)}, u32[]{:S(2)}, u32[]{:S(2)}) collective-permute-start(bf16[1,24,1152]{2,1,0:T(8,128)(2,1)S(1)} %constant_dynamic-slice_fusion.6), channel_id=1, source_target_pairs={{0,8},{2,10},{4,12},{6,14},{8,0},{10,2},{12,4},{14,6},{1,9},{3,11}... | collective-permute-start | bytes 165896 | tf_op jit(solution)/shard_map/ppermute | solution.py:172
  433.1 26.6 %collective-permute-start.32 = (bf16[8,96,768]{2,1,0:T(8,128)(2,1)S(1)}, bf16[8,96,768]{2,1,0:T(8,128)(2,1)S(1)}, u32[]{:S(2)}, u32[]{:S(2)}) collective-permute-start(bf16[8,96,768]{2,1,0:T(8,128)(2,1)S(1)} %dynamic-slice_bitcast_fusion.2), channel_id=1, source_target_pairs={{0,16},{16,0},{1,17},{17,1},{2,18},{18,2},{3,19},{19,3},{4,20},{20... | collective-permute-start | bytes 3538952 | tf_op jit(solution)/shard_map/ppermute | solution.py:172
  436.6 25.9 %collective-permute-start.26 = (bf16[4,48,3072]{2,1,0:T(8,128)(2,1)S(1)}, bf16[4,48,3072]{2,1,0:T(8,128)(2,1)S(1)}, u32[]{:S(2)}, u32[]{:S(2)}) collective-permute-start(bf16[4,48,3072]{2,1,0:T(8,128)(2,1)S(1)} %dynamic-slice_bitcast_fusion.3), channel_id=1, source_target_pairs={{0,2},{2,0},{4,6},{6,4},{8,10},{10,8},{12,14},{14,12},{1,3},{3,1},... | collective-permute-start | bytes 3538952 | tf_op jit(solution)/shard_map/ppermute | solution.py:172
  437.3 22.4 %collective-permute-start.12 = (bf16[24,1152]{1,0:T(8,128)(2,1)S(1)}, bf16[24,1152]{1,0:T(8,128)(2,1)S(1)}, u32[]{:S(2)}, u32[]{:S(2)}) collective-permute-start(bf16[24,1152]{1,0:T(8,128)(2,1)S(1)} %add_bitcast_fusion.3), channel_id=1, source_target_pairs={{0,16},{16,0},{1,17},{17,1},{2,18},{18,2},{3,19},{19,3},{4,20},{20... | collective-permute-start | bytes 165896 | tf_op jit(solution)/shard_map/ppermute | solution.py:210
  438.0 25.4 %collective-permute-start.18 = (bf16[24,1152]{1,0:T(8,128)(2,1)S(1)}, bf16[24,1152]{1,0:T(8,128)(2,1)S(1)}, u32[]{:S(2)}, u32[]{:S(2)}) collective-permute-start(bf16[24,1152]{1,0:T(8,128)(2,1)S(1)} %add_bitcast_fusion.2), channel_id=1, source_target_pairs={{0,16},{16,0},{1,17},{17,1},{2,18},{18,2},{3,19},{19,3},{4,20},{20... | collective-permute-start | bytes 165896 | tf_op jit(solution)/shard_map/ppermute | solution.py:210
  462.7 15.2 %collective-permute-start.27 = (bf16[4,24,3072]{2,1,0:T(8,128)(2,1)S(1)}, bf16[4,24,3072]{2,1,0:T(8,128)(2,1)S(1)}, u32[]{:S(2)}, u32[]{:S(2)}) collective-permute-start(bf16[4,24,3072]{2,1,0:T(8,128)(2,1)S(1)} %dynamic-slice_bitcast_fusion.7), channel_id=1, source_target_pairs={{0,16},{16,0},{1,17},{17,1},{2,18},{18,2},{3,19},{19,3},{4,20},{20... | collective-permute-start | bytes 1769480 | tf_op jit(solution)/shard_map/ppermute | solution.py:172
  470.0 15.6 %collective-permute-start.34 = (bf16[2,96,768]{2,1,0:T(8,128)(2,1)S(1)}, bf16[2,96,768]{2,1,0:T(8,128)(2,1)S(1)}, u32[]{:S(2)}, u32[]{:S(2)}) collective-permute-start(bf16[2,96,768]{2,1,0:T(8,128)(2,1)S(1)} %dynamic-slice_bitcast_fusion.11), channel_id=1, source_target_pairs={{0,4},{2,6},{4,0},{6,2},{8,12},{10,14},{12,8},{14,10},{1,5},{3,7},... | collective-permute-start | bytes 884744 | tf_op jit(solution)/shard_map/ppermute | solution.py:172
  478.0 43.6 %all-to-all-start.3 = ((bf16[16,64,768]{2,1,0:T(8,128)(2,1)}), bf16[16,64,768]{2,1,0:T(8,128)(2,1)}, u32[]{:S(2)}, u32[]{:S(2)}) async-start(bf16[16,64,768]{2,1,0:T(8,128)(2,1)} %bitcast.206), calls=%async_computation.3 | async-start | bytes 3145728 | tf_op jit(solution)/shard_map/all_to_all | solution.py:249
  482.5 24.2 %collective-permute-start.28 = (bf16[2,24,3072]{2,1,0:T(8,128)(2,1)S(1)}, bf16[2,24,3072]{2,1,0:T(8,128)(2,1)S(1)}, u32[]{:S(2)}, u32[]{:S(2)}) collective-permute-start(bf16[2,24,3072]{2,1,0:T(8,128)(2,1)S(1)} %dynamic-slice_bitcast_fusion.12), channel_id=1, source_target_pairs={{0,4},{2,6},{4,0},{6,2},{8,12},{10,14},{12,8},{14,10},{1,5},{3,7},... | collective-permute-start | bytes 884744 | tf_op jit(solution)/shard_map/ppermute | solution.py:172
  485.7 30.8 %collective-permute-start.35 = (bf16[1,96,768]{2,1,0:T(8,128)(2,1)S(1)}, bf16[1,96,768]{2,1,0:T(8,128)(2,1)S(1)}, u32[]{:S(2)}, u32[]{:S(2)}) collective-permute-start(bf16[1,96,768]{2,1,0:T(8,128)(2,1)S(1)} %constant_dynamic-slice_fusion.2), channel_id=1, source_target_pairs={{0,8},{2,10},{4,12},{6,14},{8,0},{10,2},{12,4},{14,6},{1,9},{3,11}... | collective-permute-start | bytes 442376 | tf_op jit(solution)/shard_map/ppermute | solution.py:172
  506.8 11.3 %collective-permute-start.29 = (bf16[1,24,3072]{2,1,0:T(8,128)(2,1)S(1)}, bf16[1,24,3072]{2,1,0:T(8,128)(2,1)S(1)}, u32[]{:S(2)}, u32[]{:S(2)}) collective-permute-start(bf16[1,24,3072]{2,1,0:T(8,128)(2,1)S(1)} %constant_dynamic-slice_fusion.3), channel_id=1, source_target_pairs={{0,8},{2,10},{4,12},{6,14},{8,0},{10,2},{12,4},{14,6},{1,9},{3,11}... | collective-permute-start | bytes 442376 | tf_op jit(solution)/shard_map/ppermute | solution.py:172
  (70 other events, 847.0 us)

commit v2 on v1

v2 whole, which is shorter than its diff:
```python
import functools
import math

import jax
import jax.numpy as jnp
from jax import lax
from jax.experimental import pallas as pl
from jax.experimental.pallas import tpu as pltpu
from jax.sharding import Mesh, PartitionSpec as P

HEADS = 12
EPSILON = 1e-06
SCALING = 0.125
LOG2E = math.log2(math.e)
F32 = jnp.float32
BF = jnp.bfloat16
NN = (((1,), (0,)), ((), ()))
NT = (((1,), (1,)), ((), ()))
TN = (((0,), (0,)), ((), ()))
VMEM_LIMIT = 56 << 20


def mm(a, b, dims=NN):
    return lax.dot_general(a, b, dims, preferred_element_type=F32)


def of_head(value, head, axis=1):
    lane = lax.broadcasted_iota(jnp.int32, value.shape, axis)
    return jnp.where((lane // 64) == head, value, jnp.zeros_like(value))


def sds(shape, dtype):
    return jax.ShapeDtypeStruct(shape, dtype)


def call(kernel, name, grid, ins, outs, scratch=(), flops=0, deps=()):
    given, skipped = len(ins), len(deps)

    def body(*refs):
        kernel(*refs[:given], *refs[given + skipped :])

    anywhere = pl.BlockSpec(memory_space=pl.ANY)
    moved = sum(math.prod(a.shape) * a.dtype.itemsize for a, spec in list(ins) + list(outs))
    return pl.pallas_call(
        body,
        grid=grid,
        in_specs=[spec for a, spec in ins] + [anywhere] * skipped,
        out_specs=[spec for a, spec in outs],
        out_shape=[a for a, spec in outs],
        scratch_shapes=list(scratch),
        compiler_params=pltpu.CompilerParams(vmem_limit_bytes=VMEM_LIMIT),
        cost_estimate=pl.CostEstimate(flops=flops, bytes_accessed=moved, transcendentals=0),
        name=name,
    )(*[a for a, spec in ins], *deps)


def attend_kernel(q_ref, k0, k1, v0, v1, o_ref, full_ref, lse_ref):
    q = q_ref[...]
    ones = jnp.ones(v0.shape, BF)
    val0 = jnp.concatenate([v0[...], ones], 1)
    val1 = jnp.concatenate([v1[...], ones], 1)
    outs, logs = [], []
    for head in range(2):
        qm = of_head(q, head)
        s0 = mm(qm, k0[...], NT)
        s1 = mm(qm, k1[...], NT)
        top = jnp.max(jnp.maximum(s0, s1), axis=1, keepdims=True)
        p0 = jnp.exp2(s0 - top).astype(BF)
        p1 = jnp.exp2(s1 - top).astype(BF)
        both = mm(p0, val0) + mm(p1, val1)
        total = both[:, 128:]
        outs.append(both[:, :128] / total)
        logs.append(top + jnp.log2(total))
    lane = lax.broadcasted_iota(jnp.int32, outs[0].shape, 1)
    both = jnp.where(lane < 64, outs[0], outs[1])
    o_ref[...] = both.astype(BF)
    full_ref[...] = both
    turned = jnp.where(lane < 64, logs[0], logs[1]).T
    lse_ref[0:4, :] = turned[0:4]
    lse_ref[4:8, :] = turned[64:68]


def attend(q, kv_own, kv_peer, frames):
    tokens, width = q.shape
    pairs = width // 128
    n = tokens // frames
    bq = min(512, n)
    nb = n // bq
    qs = pl.BlockSpec((bq, 128), lambda f, p, j: (f * nb + j, p))
    ks = pl.BlockSpec((n, 128), lambda f, p, j: (f, p))
    vs = pl.BlockSpec((n, 128), lambda f, p, j: (f, pairs + p))
    ls = pl.BlockSpec((8, bq), lambda f, p, j: (p, f * nb + j))
    return call(
        attend_kernel,
        "attend",
        (frames, pairs, nb),
        [(q, qs), (kv_own, ks), (kv_peer, ks), (kv_own, vs), (kv_peer, vs)],
        [
            (sds((tokens, width), BF), qs),
            (sds((tokens, width), F32), qs),
            (sds((pairs * 8, tokens), F32), ls),
        ],
        flops=50_000_000_000,
    )


def attend_back_kernel(
    q_ref, k0, k1, v0, v1, go_ref, o_ref, lse_ref, dq_ref, dk0, dk1, dv0, dv1, dka, dva
):
    j = pl.program_id(2)
    q = q_ref[...]
    go = go_ref[...]
    prod = (go.astype(F32) * o_ref[...]).T
    dq = None
    for part, (k, v) in enumerate(((k0, v0), (k1, v1))):
        keys = k[...]
        vals = v[...]
        turned = keys.T
        acc_v = acc_k = None
        for head in range(2):
            qm = of_head(q, head)
            gom = of_head(go, head)
            lse = lse_ref[4 * head : 4 * head + 1, :]
            delta = jnp.sum(prod[64 * head : 64 * head + 64], axis=0, keepdims=True)
            probs = jnp.exp2(mm(keys, qm, NT) - lse)
            ds = (probs * (mm(vals, gom, NT) - delta)).astype(BF)
            probs = probs.astype(BF)
            a = mm(probs, gom)
            b = mm(ds, qm)
            c = mm(of_head(turned, head, 0), ds)
            dq = c if dq is None else dq + c
            acc_v = a if acc_v is None else acc_v + a
            acc_k = b if acc_k is None else acc_k + b

        @pl.when(j == 0)
        def _():
            dva[part] = acc_v
            dka[part] = acc_k

        @pl.when(j > 0)
        def _():
            dva[part] += acc_v
            dka[part] += acc_k

    dq_ref[...] = (dq * SCALING).T.astype(BF)

    @pl.when(j == pl.num_programs(2) - 1)
    def _():
        back = SCALING / (SCALING * LOG2E)
        dk0[...] = (dka[0] * back).astype(BF)
        dk1[...] = (dka[1] * back).astype(BF)
        dv0[...] = dva[0].astype(BF)
        dv1[...] = dva[1].astype(BF)


def attend_back(q, kv_own, kv_peer, go, att, lse, frames, first, count, deps):
    tokens, width = q.shape
    pairs = width // 128
    n = tokens // frames
    bq = min(512, n)
    nb = n // bq
    qs = pl.BlockSpec((bq, 128), lambda f, p, j: (f * nb + j, first + p))
    ks = pl.BlockSpec((n, 128), lambda f, p, j: (f, first + p))
    vs = pl.BlockSpec((n, 128), lambda f, p, j: (f, pairs + first + p))
    ls = pl.BlockSpec((8, bq), lambda f, p, j: (first + p, f * nb + j))
    qo = pl.BlockSpec((bq, 128), lambda f, p, j: (f * nb + j, p))
    ko = pl.BlockSpec((n, 128), lambda f, p, j: (f, p))
    shape = jax.ShapeDtypeStruct((tokens, 128 * count), BF)
    return call(
        attend_back_kernel,
        "attend_back",
        (frames, count, nb),
        [(q, qs), (kv_own, ks), (kv_peer, ks), (kv_own, vs), (kv_peer, vs), (go, qs), (att, qs), (lse, ls)],
        [(shape, qo)] + [(shape, ko)] * 4,
        [pltpu.VMEM((2, n, 128), F32)] * 2,
        14_000_000_000 * count,
        deps,
    )


def normed_of(value):
    row_mean = jnp.mean(value, axis=-1, keepdims=True)
    centered = value - row_mean
    inverse = lax.rsqrt(jnp.mean(centered * centered, axis=-1, keepdims=True) + EPSILON)
    return centered * inverse, inverse


def norm_back(grad_hat, normed, inverse):
    first = jnp.mean(grad_hat, axis=-1, keepdims=True)
    second = jnp.mean(grad_hat * normed, axis=-1, keepdims=True)
    return inverse * (grad_hat - first - normed * second)


def rows_of(block, width):
    return pl.BlockSpec((block, width), lambda i: (i, 0))


def whole_of(shape):
    return pl.BlockSpec(shape, lambda i: (0,) * len(shape))


SMALL = pl.BlockSpec(memory_space=pltpu.SMEM)


def key_kernel(x_ref, chan_ref, shift_ref, gain_ref, wk, wv, h_ref, kv_ref):
    width = x_ref.shape[1]
    normed, inverse = normed_of(x_ref[...].astype(F32) + chan_ref[0])
    hidden = (normed * gain_ref[...] + shift_ref[0]).astype(BF)
    h_ref[...] = hidden
    kv_ref[:, :width] = mm(hidden, wk[...]).astype(BF)
    kv_ref[:, width:] = mm(hidden, wv[...]).astype(BF)


def keys_of(x, chan_add, shift, gain, weight, frames):
    count, width = x.shape
    block = 256
    per = count // frames // block
    frame = pl.BlockSpec((1, 1, width), lambda i: (i // per, 0, 0))
    return call(
        key_kernel,
        "keys",
        (count // block,),
        [
            (x, rows_of(block, width)),
            (chan_add, frame),
            (shift, frame),
            (gain, whole_of((1, width))),
            (weight, pl.BlockSpec((width, width), lambda i: (0, 1))),
            (weight, pl.BlockSpec((width, width), lambda i: (0, 2))),
        ],
        [
            (sds((count, width), BF), rows_of(block, width)),
            (sds((count, 2 * width), BF), rows_of(block, 2 * width)),
        ],
        flops=2_400_000_000,
    )


def query_kernel(h_ref, w, q_ref):
    q_ref[...] = (mm(h_ref[...], w[...]) * (SCALING * LOG2E)).astype(BF)


def queries_of(hidden, weight):
    count, width = hidden.shape
    block = 256
    return call(
        query_kernel,
        "queries",
        (count // block,),
        [(hidden, rows_of(block, width)), (weight, pl.BlockSpec((width, width), lambda i: (0, 0)))],
        [(sds((count, width), BF), rows_of(block, width))],
        flops=1_200_000_000,
    )[0]


ROOT = math.sqrt(2 / math.pi)
CUBE = ROOT * 0.044715


def gelu_both(x):
    square = x * x
    t = jnp.tanh(x * (ROOT + CUBE * square))
    half = 0.5 * t + 0.5
    slope = half + (0.5 * x) * (1.0 - t * t) * (ROOT + (3.0 * CUBE) * square)
    return x * half, slope


def mlp_kernel(
    x_ref,
    chan_ref,
    att_ref,
    g_ref,
    rows_ref,
    up_bias_ref,
    wo_any,
    wu_any,
    wd_any,
    res_ref,
    act_ref,
    gpre_ref,
    hid_ref,
    mid_ref,
    branch_ref,
    gatt_ref,
    sums_ref,
    wo,
    wu,
    wd,
    sems,
):
    step = pl.program_id(0)
    width = x_ref.shape[1]
    chunks = wu.shape[1] // width
    copies = [
        pltpu.make_async_copy(wo_any, wo, sems.at[0]),
        pltpu.make_async_copy(wu_any, wu, sems.at[1]),
        pltpu.make_async_copy(wd_any, wd, sems.at[2]),
    ]

    @pl.when(step == 0)
    def _():
        for c in copies:
            c.start()
        sums_ref[...] = jnp.zeros_like(sums_ref)
        copies[0].wait()

    out_bias, gain, shift, down_bias = [rows_ref[i : i + 1] for i in range(4)]
    middle = x_ref[...].astype(F32) + chan_ref[0] + mm(att_ref[...], wo[...]) + out_bias
    normed, inverse = normed_of(middle)
    hidden = (normed * gain + shift).astype(BF)
    hid_ref[...] = hidden
    g = g_ref[...]

    @pl.when(step == 0)
    def _():
        copies[1].wait()
        copies[2].wait()

    result = middle + down_bias
    grad_hidden = None
    for c in range(chunks):
        cols = pl.ds(c * width, width)
        act, slope = gelu_both(mm(hidden, wu[:, cols]) + up_bias_ref[:, cols])
        act = act.astype(BF)
        act_ref[:, cols] = act
        grad_pre = (mm(g, wd[cols, :], NT) * slope).astype(BF)
        gpre_ref[:, cols] = grad_pre
        sums_ref[4 + c : 5 + c] += jnp.sum(grad_pre.astype(F32), axis=0, keepdims=True)
        result = result + mm(act, wd[cols, :])
        part = mm(grad_pre, wu[:, cols], NT)
        grad_hidden = part if grad_hidden is None else grad_hidden + part
    res_ref[...] = result.astype(BF)
    g = g.astype(F32)
    sums_ref[0:1] += jnp.sum(g, axis=0, keepdims=True)
    sums_ref[1:2] += jnp.sum(grad_hidden * normed, axis=0, keepdims=True)
    sums_ref[2:3] += jnp.sum(grad_hidden, axis=0, keepdims=True)
    grad_middle = g + norm_back(grad_hidden * gain, normed, inverse)
    mid_ref[...] = grad_middle
    branch = grad_middle.astype(BF)
    branch_ref[...] = branch
    sums_ref[3:4] += jnp.sum(branch.astype(F32), axis=0, keepdims=True)
    gatt_ref[...] = mm(branch, wo[...], NT).astype(BF)


def mlp(x, chan_add, att, g, rows, up_bias, wo, wu, wd, frames):
    count, width = x.shape
    wide = wu.shape[1]
    block = 256
    per = count // frames // block
    narrow, broad = rows_of(block, width), rows_of(block, wide)
    anywhere = pl.BlockSpec(memory_space=pl.ANY)
    return call(
        mlp_kernel,
        "mlp",
        (count // block,),
        [
            (x, narrow),
            (chan_add, pl.BlockSpec((1, 1, width), lambda i: (i // per, 0, 0))),
            (att, narrow),
            (g, narrow),
            (rows, whole_of((4, width))),
            (up_bias, whole_of((1, wide))),
            (wo, anywhere),
            (wu, anywhere),
            (wd, anywhere),
        ],
        [
            (sds((count, width), BF), narrow),
            (sds((count, wide), BF), broad),
            (sds((count, wide), BF), broad),
            (sds((count, width), BF), narrow),
            (sds((count, width), F32), narrow),
            (sds((count, width), BF), narrow),
            (sds((count, width), BF), narrow),
            (sds((4 + wide // width, width), F32), whole_of((4 + wide // width, width))),
        ],
        [
            pltpu.VMEM(wo.shape, BF),
            pltpu.VMEM(wu.shape, BF),
            pltpu.VMEM(wd.shape, BF),
            pltpu.SemaphoreType.DMA((3,)),
        ],
        25_000_000_000,
    )


def down_grad_kernel(core_ref, act_ref, g_ref, send_ref, keep_ref, scr):
    core = core_ref[0]
    places, share, width = scr.shape[1:]
    scr[...] = mm(act_ref[...], g_ref[...], TN).reshape(scr.shape)
    keep_ref[...] = scr[:, core].astype(BF)
    send_ref[...] = scr[:, 1 - core].astype(BF)


def down_grad(core, act, g, lon):
    count, wide = act.shape
    width = g.shape[1]
    share = wide // lon
    tile = 384
    chips = tile // (2 * share)
    out = sds((lon // 2, share, width), BF)
    spec = pl.BlockSpec((chips, share, width), lambda i: (i, 0, 0))
    return call(
        down_grad_kernel,
        "down_grad",
        (wide // tile,),
        [(core, SMALL), (act, pl.BlockSpec((count, tile), lambda i: (0, i))), (g, whole_of((count, width)))],
        [(out, spec), (out, spec)],
        [pltpu.VMEM((chips, 2, share, width), F32)],
        4_800_000_000,
    )


def up_grad_kernel(core_ref, hid_ref, gpre_ref, att_ref, branch_ref, send_ref, keep_ref, turned, scr):
    core = core_ref[0]
    step = pl.program_id(0)
    last = pl.num_programs(0) - 1

    @pl.when(step == 0)
    def _():
        turned[...] = hid_ref[...].T

    @pl.when(step < last)
    def _():
        scr[...] = mm(turned[...], gpre_ref[...]).reshape(scr.shape)

    @pl.when(step == last)
    def _():
        scr[...] = mm(att_ref[...], branch_ref[...], TN).reshape(scr.shape)

    keep_ref[...] = scr[:, core].astype(BF)
    send_ref[...] = scr[:, 1 - core].astype(BF)


def up_grad(core, hidden, gpre, att, branch, lon):
    count, width = hidden.shape
    wide = gpre.shape[1]
    share = width // lon
    last = wide // width - 1
    out = sds((lon // 2, share, wide + width), BF)
    spec = pl.BlockSpec((lon // 2, share, width), lambda i: (0, 0, i))
    full = whole_of((count, width))
    return call(
        up_grad_kernel,
        "up_grad",
        (last + 2,),
        [
            (core, SMALL),
            (hidden, full),
            (gpre, pl.BlockSpec((count, width), lambda i: (0, jnp.minimum(i, last)))),
            (att, full),
            (branch, full),
        ],
        [(out, spec), (out, spec)],
        [pltpu.VMEM((width, count), BF), pltpu.VMEM((lon // 2, 2, share, width), F32)],
        6_000_000_000,
    )


def qkv_grad_kernel_of(start, stop):
    def kernel(core_ref, hid_ref, grad_ref, send_ref, keep_ref, scr):
        core = core_ref[0]
        scr[...] = mm(hid_ref[...], grad_ref[:, start:stop], TN).reshape(scr.shape)
        keep_ref[...] = scr[:, core].astype(BF)
        send_ref[...] = scr[:, 1 - core].astype(BF)

    return kernel


def qkv_grad(core, hidden, grad, start, stop, lon, deps=()):
    count, width = hidden.shape
    cols = stop - start
    share = width // lon
    out = sds((lon // 2, share, cols), BF)
    spec = whole_of((lon // 2, share, cols))
    return call(
        qkv_grad_kernel_of(start, stop),
        "qkv_grad",
        (1,),
        [(core, SMALL), (hidden, whole_of((count, width))), (grad, whole_of(grad.shape))],
        [(out, spec), (out, spec)],
        [pltpu.VMEM((lon // 2, 2, share, cols), F32)],
        1_800_000_000,
        deps,
    )


def first_back_kernel_of(groups, frame_blocks):
    def kernel(*refs):
        ins = refs[: 5 * groups]
        x_ref, chan_ref, gain_ref, mid_ref, w, patch_ref, qkv_ref, frame_ref, gain_sum = refs[5 * groups :]
        step = pl.program_id(0)
        width = x_ref.shape[1]
        at = 0
        for c in range(groups):
            dq, dk0, dv0, got_k, got_v = ins[5 * c : 5 * c + 5]
            size = dq.shape[1]
            qkv_ref[:, pl.ds(at, size)] = dq[...]
            qkv_ref[:, pl.ds(width + at, size)] = dk0[...] + got_k[...]
            qkv_ref[:, pl.ds(2 * width + at, size)] = dv0[...] + got_v[...]
            at += size
        grad_hidden = mm(qkv_ref[...], w[...], NT)
        normed, inverse = normed_of(x_ref[...].astype(F32) + chan_ref[0])
        grad_start = mid_ref[...] + norm_back(grad_hidden * gain_ref[...], normed, inverse)
        patch_ref[...] = grad_start.astype(BF)

        @pl.when(step == 0)
        def _():
            gain_sum[...] = jnp.zeros_like(gain_sum)

        @pl.when(lax.rem(step, frame_blocks) == 0)
        def _():
            frame_ref[...] = jnp.zeros_like(frame_ref)

        gain_sum[...] += jnp.sum(grad_hidden * normed, axis=0, keepdims=True)
        frame_ref[0, 0:1] += jnp.sum(grad_hidden, axis=0, keepdims=True)
        frame_ref[0, 1:2] += jnp.sum(grad_start, axis=0, keepdims=True)

    return kernel


def first_back(pieces, x, chan_add, gain, grad_middle, weight, frames):
    count, width = x.shape
    block = 256
    per = count // frames // block
    ins = [(a, rows_of(block, a.shape[1])) for group in pieces for a in group]
    return call(
        first_back_kernel_of(len(pieces), per),
        "first_back",
        (count // block,),
        ins
        + [
            (x, rows_of(block, width)),
            (chan_add, pl.BlockSpec((1, 1, width), lambda i: (i // per, 0, 0))),
            (gain, whole_of((1, width))),
            (grad_middle, rows_of(block, width)),
            (weight, whole_of(weight.shape)),
        ],
        [
            (sds((count, width), BF), rows_of(block, width)),
            (sds((count, 3 * width), BF), rows_of(block, 3 * width)),
            (sds((frames, 2, width), F32), pl.BlockSpec((1, 2, width), lambda i: (i // per, 0, 0))),
            (sds((1, width), F32), whole_of((1, width))),
        ],
        flops=3_600_000_000,
    )


def swap_pairs(size, bit):
    return [(i, i ^ (1 << bit)) for i in range(size)]


def bits_of(size):
    return size.bit_length() - 1


def my_bit(axis, bit):
    return ((lax.axis_index(axis) >> bit) & 1).astype(jnp.int32).reshape(1)


def swap(value, axis, bit):
    return lax.ppermute(value, axis, swap_pairs(lax.axis_size(axis), bit))


def add_kernel_of(kind):
    def kernel(mine_ref, kept_ref, got_ref, *outs):
        mine = mine_ref[0]

        def total(*at):
            return (kept_ref[at].astype(F32) + got_ref[at].astype(F32)).astype(BF)

        for which, ref in zip((1 - mine, mine), outs):
            if kind == "lead":
                ref[0] = total(which)
            elif kind == "rows":
                half = ref.shape[1]
                ref[...] = total(slice(None), pl.ds(pl.multiple_of(which * half, half), half))
            else:
                half = ref.shape[2]
                ref[...] = total(
                    slice(None), slice(None), pl.ds(pl.multiple_of(which * half, half), half)
                )

    return kernel


def add_split(kept, got, kind, mine, deps=()):
    lead, rows, cols = kept.shape
    size = 2 if lead > 1 else 1
    spec = pl.BlockSpec((size, rows, cols), lambda i: (i, 0, 0))
    if kind == "lead":
        part, half = (1, rows, cols), (lead // 2, rows, cols)
    elif kind == "rows":
        part, half = (size, rows // 2, cols), (lead, rows // 2, cols)
    else:
        part, half = (size, rows, cols // 2), (lead, rows, cols // 2)
    out = pl.BlockSpec(part, lambda i: (i, 0, 0))
    return call(
        add_kernel_of(kind),
        "add_" + kind,
        (lead // size,),
        [(mine, SMALL), (kept, spec), (got, spec)],
        [(sds(half, BF), out)] * 2,
        deps=deps,
    )


class Sum:
    def __init__(self, send, kept, stages, cut):
        self.kept, self.stages, self.cut = kept, list(stages), cut
        self.got = swap(send, "core", 0)
        self.final = None

    def advance(self, deps=()):
        if not self.stages:
            return ()
        axis, bit = self.stages.pop(0)
        kind = "lead" if axis == "chip" else self.cut
        send, self.kept = add_split(self.kept, self.got, kind, my_bit(axis, bit), deps)
        self.got = swap(send, axis, bit)
        return (self.kept,)

    def finish(self):
        while self.stages:
            self.advance()
        total = (self.kept.astype(F32) + self.got.astype(F32)).astype(BF)
        total = total.reshape(total.shape[-2:])
        lat = lax.axis_size("lat")
        if lat == 2:
            other = swap(total, "lat", 0)
            dim = 0 if self.cut == "rows" else 1
            total = jnp.where(
                lax.axis_index("lat") == 1,
                jnp.concatenate([other, total], dim),
                jnp.concatenate([total, other], dim),
            ).astype(F32)
        elif lat > 1:
            total = lax.psum(total.astype(F32), "lat")
        return total.astype(F32)


def stages_of(lat_at):
    chip = [("chip", bit) for bit in range(bits_of(lax.axis_size("chip")))]
    if lax.axis_size("lat") == 2:
        chip.insert(lat_at, ("lat", 0))
    return chip


def to_frames(value, chips):
    frames_all, patches, width = value.shape
    frames = frames_all // chips
    value = lax.all_to_all(value, ("lat", "chip"), 0, 0, tiled=True)
    if frames > 1:
        value = value.reshape(chips, frames, patches, width).swapaxes(0, 1)
    return value.reshape(-1, width)


def to_places(value, chips, frames_all):
    width = value.shape[-1]
    frames = frames_all // chips
    if frames > 1:
        value = value.reshape(frames, chips, -1, width).swapaxes(0, 1)
    value = value.reshape(frames_all, -1, width)
    return lax.all_to_all(value, ("lat", "chip"), 0, 0, tiled=True)


def on_device(
    tokens,
    channel_mask,
    lead_index,
    chan_embed,
    lead_embed,
    norm1_gain,
    norm1_bias,
    qkv_weight,
    out_weight,
    out_bias,
    norm2_gain,
    norm2_bias,
    up_weight,
    up_bias,
    down_weight,
    down_bias,
    cotangent,
):
    lat = lax.axis_size("lat")
    chips = lat * lax.axis_size("chip")
    lon = 2 * lax.axis_size("chip")
    frames_all, rows_here, cols_here, width = tokens.shape
    frames = frames_all // chips
    leads = lead_embed.shape[0]
    wide = up_weight.shape[1]
    share = width // lon
    place = (lax.axis_index("chip") * 2) + lax.axis_index("core")
    core = my_bit("core", 0)

    x = to_frames(tokens.reshape(frames_all, -1, width), chips)
    g = to_frames(cotangent.reshape(frames_all, -1, width), chips)
    count = x.shape[0]

    first = lax.axis_index(("lat", "chip")) * frames
    mask_here = lax.dynamic_slice_in_dim(channel_mask, first, frames, 0).astype(BF)
    lead_here = lax.dynamic_slice_in_dim(lead_index, first, frames, 0)
    lead_onehot = (lead_here[:, None] == jnp.arange(leads, dtype=jnp.int32)[None, :]).astype(BF)
    chan_add = mm(mask_here, chan_embed)[:, None, :]
    shift1 = (mm(lead_onehot, lead_embed) + norm1_bias.astype(F32))[:, None, :]
    gain1 = norm1_gain.astype(F32)[None]
    rows2 = jnp.stack([out_bias, norm2_gain, norm2_bias, down_bias]).astype(F32)

    hidden1, kv_own = keys_of(x, chan_add, shift1, gain1, qkv_weight, frames)
    kv_peer = swap(kv_own, "core", 0)
    queries = queries_of(hidden1, qkv_weight)
    attended, attended32, lse = attend(queries, kv_own, kv_peer, frames)

    result, activ, grad_pre, hidden2, grad_middle, grad_branch, grad_att, early = mlp(
        x,
        chan_add,
        attended,
        g,
        rows2,
        up_bias.astype(F32)[None],
        out_weight,
        up_weight,
        down_weight,
        frames,
    )
    out_patch = to_places(result, chips, frames_all)
    down_sum = Sum(*down_grad(core, activ, g, lon), stages_of(0), "rows")
    up_sum = Sum(*up_grad(core, hidden2, grad_pre, attended, grad_branch, lon), stages_of(1), "cols")

    pairs = width // 128
    plan = [2] + [1] * (pairs - 2)
    pieces, pair = [], 0
    marks = ()
    for size in plan:
        deps = down_sum.advance(marks) + up_sum.advance(marks)
        dq, dk0, dk1, dv0, dv1 = attend_back(
            queries, kv_own, kv_peer, grad_att, attended32, lse, frames, pair, size, deps
        )
        pieces.append((dq, dk0, dv0, swap(dk1, "core", 0), swap(dv1, "core", 0)))
        pair += size
        marks = (dq,)

    grad_start, grad_qkv, frame_sums, gain_sum = first_back(
        pieces, x, chan_add, gain1, grad_middle, qkv_weight, frames
    )
    grad_patch = to_places(grad_start, chips, frames_all)
    middle = 3 * width // 512 * 256
    first_half = qkv_grad(core, hidden1, grad_qkv, 0, middle, lon)
    other_half = qkv_grad(core, hidden1, grad_qkv, middle, 3 * width, lon)
    qkv_a = Sum(*first_half, stages_of(0), "cols")
    qkv_b = Sum(*other_half, stages_of(1), "cols")

    parts = wide // width
    early_up = early[4:].reshape(lon, parts, share).swapaxes(0, 1).reshape(parts, width)
    late = jnp.concatenate(
        [frame_sums.reshape(2 * frames, width), gain_sum, early[:4], early_up], 0
    )
    late = late.reshape(-1, lon // 2, 2, share)
    mine = core[0]
    late = lax.dynamic_index_in_dim(late, mine, 2, keepdims=False) + swap(
        lax.dynamic_index_in_dim(late, 1 - mine, 2, keepdims=False), "core", 0
    )
    late = late.reshape(1, late.shape[0], -1)
    for axis in ("chip", "lat"):
        for bit in range(bits_of(lax.axis_size(axis))):
            other = swap(late, axis, bit)
            high = my_bit(axis, bit)[0] == 1
            late = jnp.where(
                high, jnp.concatenate([other, late], 0), jnp.concatenate([late, other], 0)
            )
    late = lax.dynamic_slice_in_dim(late, lax.axis_index("chip") * share, share, 2)
    bias_of = late[:, 0 : 2 * frames : 2].reshape(frames_all, share)
    start_of = late[:, 1 : 2 * frames : 2].reshape(frames_all, share)
    rest = late[:, 2 * frames :].sum(0)
    hot = (lead_index[:, None] == jnp.arange(leads, dtype=jnp.int32)[None, :]).astype(F32)
    exact = lax.Precision.HIGHEST
    sum_lead = jnp.dot(hot.T, bias_of, precision=exact)
    sum_chan = jnp.dot(channel_mask.astype(F32).T, start_of, precision=exact)

    sum_down = down_sum.finish()
    sum_up = up_sum.finish()
    sum_qkv = jnp.concatenate([qkv_a.finish(), qkv_b.finish()], 1)
    shape = (frames_all, rows_here, cols_here, width)
    return (
        out_patch.reshape(shape),
        grad_patch.reshape(shape),
        sum_chan,
        sum_lead,
        rest[0],
        bias_of.sum(0),
        sum_qkv,
        sum_up[:, wide:],
        rest[4],
        rest[2],
        rest[3],
        sum_up[:, :wide],
        rest[5:].reshape(-1),
        sum_down,
        rest[1],
    )


def solution(mesh):
    lat, lon = mesh.shape["lat"], mesh.shape["lon"]
    fine = Mesh(mesh.devices.reshape(lat, lon // 2, 2), ("lat", "chip", "core"))
    places = P(None, "lat", ("chip", "core"), None)
    wide = ("chip", "core")
    return jax.shard_map(
        on_device,
        mesh=fine,
        in_specs=(places,) + (P(),) * 15 + (places,),
        out_specs=(
            places,
            places,
            P(None, wide),
            P(None, wide),
            P(wide),
            P(wide),
            P(wide, None),
            P(wide, None),
            P(wide),
            P(wide),
            P(wide),
            P(wide, None),
            P(wide),
            P(wide, None),
            P(wide),
        ),
        check_vma=False,
    )
```

time: 538 us -> 463 us (0.86); the launches traced: 528 us -> 459 us
  Pallas kernels: 121 us -> 264 us
  matrix products: 97.9 us -> 3.88 us
  waiting for transfers between devices: 163 us -> 99.1 us
  blocking collectives: 43 us -> 0 us
  other arithmetic: 24.2 us -> 7.22 us
  starting transfers between devices: 46.8 us -> 55.5 us
    pallas_call x4 -> x30, Pallas kernels: 121 us -> 264 us  [call(): pl.pallas_call(body, grid=grid, in_specs=[spec for a, spec in ins] + [any...]
    dot_general x15 -> x2, matrix products: 96.2 us -> 2.17 us  [mm(): return lax.dot_general(a, b, dims, preferred_element_type=F32)]
    all_gather x1 -> x0, blocking collectives: 43 us -> none  [on_device(): late = lax.all_gather(late, ('lat', 'chip', 'core'), axis=0)]
    ppermute x37 -> x40, waiting for transfers between devices: 103 us -> 66.4 us  [swap(): return lax.ppermute(value, axis, swap_pairs(lax.axis_size(axis), bit))]
    all_to_all x2, waiting for transfers between devices: 60.1 us -> 32.7 us  [to_frames(): value = lax.all_to_all(value, ('lat', 'chip'), 0, 0, tiled=True)]
    unnamed x109 -> x85, local copies, waits for them, and re-layouts: 2.07 us -> 13.6 us
    squeeze x25 -> x1, local copies, waits for them, and re-layouts: 9.42 us -> 0.53 us  [on_device(): rest[1]]
    reduce_sum x8 -> x1, other arithmetic: 8.4 us -> 0.03 us  [on_device(): rest = late[:, 2 * frames:].sum(0)]
  transfers between devices with their start and end apart: 41 -> 44, of which waited for: 23 -> 11; matrix products, arithmetic and copies ran while one was open for 13% -> 4% of each run, Pallas kernels for 14% -> 45%
where the time goes in v2:
time: 463 us; the launch traced here: 459 us
  Pallas kernels  264 us (57%)
  waiting for transfers between devices  99.1 us (21%)
  starting transfers between devices  55.5 us (12%)
  local copies, waits for them, and re-layouts  27.7 us (6%)
  other arithmetic  7.22 us (2%)
    pallas_call x30, Pallas kernels, call(): pl.pallas_call(body, grid=grid, in_specs=[spec for a, spec in ins] + [any...  264 us
    ppermute x40, waiting for transfers between devices, swap(): return lax.ppermute(value, axis, swap_pairs(lax.axis_size(axis), bit))  66.4 us
    all_to_all x2, waiting for transfers between devices, to_frames(): value = lax.all_to_all(value, ('lat', 'chip'), 0, 0, tiled=True)  32.7 us
    ppermute x40, starting transfers between devices, swap(): return lax.ppermute(value, axis, swap_pairs(lax.axis_size(axis), bit))  31.9 us
    unnamed x85, local copies, waits for them, and re-layouts  13.6 us
    all_to_all x2, starting transfers between devices, to_frames(): value = lax.all_to_all(value, ('lat', 'chip'), 0, 0, tiled=True)  12.7 us
    all_to_all x2, starting transfers between devices, to_places(): return lax.all_to_all(value, ('lat', 'chip'), 0, 0, tiled=True)  11 us
  transfers between devices with their start and end apart: 44, of which 11 were waited for; matrix products, arithmetic and copies ran while one was open for 4% of the time, Pallas kernels for 45%

profile of v2, /device:TPU:0, one launch (start us, length us, event | category | flops | bytes accessed | tf_op | source)
XLA Modules:
  0.0 458.8 jit_solution(5468951904716013432)
XLA Ops:
  4.4 8.5 %all-to-all-start = ((bf16[16,64,768]{2,1,0:T(8,128)(2,1)}), bf16[16,64,768]{2,1,0:T(8,128)(2,1)S(1)}, u32[]{:S(2)}, u32[]{:S(2)}) async-start(bf16[16,64,768]{2,1,0:T(8,128)(2,1)} %reshape.133), calls=%async_computation | async-start | bytes 3145728 | tf_op jit(solution)/shard_map/all_to_all | solution.py:652
  16.9 32.7 %all-to-all-done = bf16[16,64,768]{2,1,0:T(8,128)(2,1)S(1)} async-done(((bf16[16,64,768]{2,1,0:T(8,128)(2,1)}), bf16[16,64,768]{2,1,0:T(8,128)(2,1)S(1)}, u32[]{:S(2)}, u32[]{:S(2)}) %all-to-all-start) | async-done | bytes 1572896 | tf_op jit(solution)/shard_map/all_to_all | solution.py:652
  50.7 7.2 %keys.1 = (bf16[1024,768]{1,0:T(8,128)(2,1)}, bf16[1024,1536]{1,0:T(8,128)(2,1)}) custom-call(bf16[1024,768]{1,0:T(8,128)(2,1)} %bitcast.51, f32[1,1,768]{2,1,0:T(1,128)} %convolution_bitcast_fusion.1.refs_1_.refs_26_, f32[1,1,768]{2,1,0:T(1,128)} %broadcast_in_dim.22.refs_2_, f32[1,768]{1,0:T(1,128)} %reshape.156.refs_3_.refs_27_, ...), custom_call_target="tpu_custom_call" | custom-call | flops 2400000000 | bytes 13378560 | tf_op jit(solution)/shard_map/keys/pallas_call | solution.py:44
  59.3 4.2 all-to-all-start.1
  64.9 4.9 %queries.1.refs_0_ = bf16[1024,768]{1,0:T(8,128)(2,1)} custom-call(bf16[1024,768]{1,0:T(8,128)(2,1)} %get-tuple-element.97.refs_0_.refs_1_, bf16[768,2304]{1,0:T(8,128)(2,1)} %refs_29_.1), custom_call_target="tpu_custom_call" | custom-call | flops 1200000000 | bytes 6684672 | tf_op jit(solution)/shard_map/queries/pallas_call | solution.py:44
  69.8 45.3 %attend.1 = (bf16[1024,768]{1,0:T(8,128)(2,1)}, f32[1024,768]{1,0:T(8,128)}, f32[48,1024]{1,0:T(8,128)}) custom-call(bf16[1024,768]{1,0:T(8,128)(2,1)} %queries.1.refs_0_, bf16[1024,1536]{1,0:T(8,128)(2,1)} %get-tuple-element.98.refs_1_.refs_3_, bf16[1024,1536]{1,0:T(8,128)(2,1)} %collective-permute-done.refs_2_.refs_4_, ...), custom_call_target="tpu_custom_call" | custom-call | flops 49999998976 | bytes 19070976 | tf_op jit(solution)/shard_map/attend/pallas_call | solution.py:44
  116.2 35.2 %mlp.1 = (bf16[1024,768]{1,0:T(8,128)(2,1)}, bf16[1024,3072]{1,0:T(8,128)(2,1)}, bf16[1024,3072]{1,0:T(8,128)(2,1)}, bf16[1024,768]{1,0:T(8,128)(2,1)}, f32[1024...) custom-call(bf16[1024,768]{1,0:T(8,128)(2,1)} %bitcast.52, ...), custom_call_target="tpu_custom_call" | custom-call | flops 24999999488 | bytes 37407744 | tf_op jit(solution)/shard_map/mlp/pallas_call | solution.py:44
  151.4 12.9 %up_grad.1 = (bf16[8,48,3840]{2,1,0:T(8,128)(2,1)}, bf16[8,48,3840]{2,1,0:T(8,128)(2,1)}) custom-call(s32[1]{0:T(128)} %bitcast.10.refs_0_, bf16[1024,768]{1,0:T(8,128)(2,1)} %get-tuple-element.108.refs_1_, bf16[1024,3072]{1,0:T(8,128)(2,1)} %get-tuple-element.109.refs_2_, bf16[1024,768]{1,0:T(8,128)(2,1)} %get-tuple-element.99.refs_2_.refs_3_, ...), custom_call_target="tpu_custom_call" | custom-call | flops 6000000000 | bytes 16908292 | tf_op jit(solution)/shard_map/up_grad/pallas_call | solution.py:44
  164.6 11.1 %down_grad.1 = (bf16[8,192,768]{2,1,0:T(8,128)(2,1)}, bf16[8,192,768]{2,1,0:T(8,128)(2,1)}) custom-call(s32[1]{0:T(128)} %bitcast.10.refs_0_, bf16[1024,3072]{1,0:T(8,128)(2,1)} %get-tuple-element.104.refs_1_, bf16[1024,768]{1,0:T(8,128)(2,1)} %bitcast.55), custom_call_target="tpu_custom_call" | custom-call | flops 4800000000 | bytes 12582916 | tf_op jit(solution)/shard_map/down_grad/pallas_call | solution.py:44
  175.9 7.0 %all-to-all-start.2 = ((bf16[16,64,768]{2,1,0:T(8,128)(2,1)}), bf16[16,64,768]{2,1,0:T(8,128)(2,1)S(1)}, u32[]{:S(2)}, u32[]{:S(2)}) async-start(bf16[16,64,768]{2,1,0:T(8,128)(2,1)} %bitcast.8), calls=%async_computation.2 | async-start | bytes 3145728 | tf_op jit(solution)/shard_map/all_to_all | solution.py:664
  182.9 13.8 %attend_back.9 = (bf16[1024,128]{1,0:T(8,128)(2,1)}, bf16[1024,128]{1,0:T(8,128)(2,1)}, bf16[1024,128]{1,0:T(8,128)(2,1)}, bf16[1024,128]{1,0:T(8,128)(2,1)}, bf16[1024,128]{1,0:T(8,128)(2,1)}) custom-call(bf16[1024,768]{1,0:T(8,128)(2,1)} %queries.1.refs_0_, bf16[1024,1536]{1,0:T(8,128)(2,1)} %get-tuple-element.98.refs_1_.refs_3_, ...), custom_call_target="tpu_custom_call" | custom-call | flops 14000000000 | bytes 20381696 | tf_op jit(solution)/shard_map/attend_back/pallas_call | solution.py:44
  197.3 4.4 add_rows.1
  203.6 4.8 %add_lead.12 = (bf16[4,48,3840]{2,1,0:T(8,128)(2,1)}, bf16[4,48,3840]{2,1,0:T(8,128)(2,1)}) custom-call(s32[1]{0:T(128)} %bitcast.11.refs_0_, bf16[8,48,3840]{2,1,0:T(8,128)(2,1)} %get-tuple-element.111.refs_1_, bf16[8,48,3840]{2,1,0:T(8,128)(2,1)} %collective-permute-done.2.refs_2_), custom_call_target="tpu_custom_call" | custom-call | bytes 8847364 | tf_op jit(solution)/shard_map/add_lead/pallas_call | solution.py:44
  209.9 25.2 %attend_back.5 = (bf16[1024,256]{1,0:T(8,128)(2,1)}, bf16[1024,256]{1,0:T(8,128)(2,1)}, bf16[1024,256]{1,0:T(8,128)(2,1)}, bf16[1024,256]{1,0:T(8,128)(2,1)}, bf16[1024,256]{1,0:T(8,128)(2,1)}) custom-call(bf16[1024,768]{1,0:T(8,128)(2,1)} %queries.1.refs_0_, bf16[1024,1536]{1,0:T(8,128)(2,1)} %get-tuple-element.98.refs_1_.refs_3_, ...), custom_call_target="tpu_custom_call" | custom-call | flops 28000000000 | bytes 21692416 | tf_op jit(solution)/shard_map/attend_back/pallas_call | solution.py:44
  240.7 6.7 %collective-permute-done.6.refs_2_ = bf16[4,48,3840]{2,1,0:T(8,128)(2,1)S(1)} collective-permute-done((bf16[4,48,3840]{2,1,0:T(8,128)(2,1)}, bf16[4,48,3840]{2,1,0:T(8,128)(2,1)S(1)}, u32[]{:S(2)}, u32[]{:S(2)}) %collective-permute-start.6) | collective-permute-done | bytes 1474592 | tf_op jit(solution)/shard_map/ppermute | solution.py:562
  251.5 14.0 %attend_back.6 = (bf16[1024,128]{1,0:T(8,128)(2,1)}, bf16[1024,128]{1,0:T(8,128)(2,1)}, bf16[1024,128]{1,0:T(8,128)(2,1)}, bf16[1024,128]{1,0:T(8,128)(2,1)}, bf16[1024,128]{1,0:T(8,128)(2,1)}) custom-call(bf16[1024,768]{1,0:T(8,128)(2,1)} %queries.1.refs_0_, bf16[1024,1536]{1,0:T(8,128)(2,1)} %get-tuple-element.98.refs_1_.refs_3_, ...), custom_call_target="tpu_custom_call" | custom-call | flops 14000000000 | bytes 20381696 | tf_op jit(solution)/shard_map/attend_back/pallas_call | solution.py:44
  273.9 13.9 %attend_back.7 = (bf16[1024,128]{1,0:T(8,128)(2,1)}, bf16[1024,128]{1,0:T(8,128)(2,1)}, bf16[1024,128]{1,0:T(8,128)(2,1)}, bf16[1024,128]{1,0:T(8,128)(2,1)}, bf16[1024,128]{1,0:T(8,128)(2,1)}) custom-call(bf16[1024,768]{1,0:T(8,128)(2,1)} %queries.1.refs_0_, bf16[1024,1536]{1,0:T(8,128)(2,1)} %get-tuple-element.98.refs_1_.refs_3_, ...), custom_call_target="tpu_custom_call" | custom-call | flops 14000000000 | bytes 20381696 | tf_op jit(solution)/shard_map/attend_back/pallas_call | solution.py:44
  295.2 14.0 %attend_back.8 = (bf16[1024,128]{1,0:T(8,128)(2,1)}, bf16[1024,128]{1,0:T(8,128)(2,1)}, bf16[1024,128]{1,0:T(8,128)(2,1)}, bf16[1024,128]{1,0:T(8,128)(2,1)}, bf16[1024,128]{1,0:T(8,128)(2,1)}) custom-call(bf16[1024,768]{1,0:T(8,128)(2,1)} %queries.1.refs_0_, bf16[1024,1536]{1,0:T(8,128)(2,1)} %get-tuple-element.98.refs_1_.refs_3_, ...), custom_call_target="tpu_custom_call" | custom-call | flops 14000000000 | bytes 20381696 | tf_op jit(solution)/shard_map/attend_back/pallas_call | solution.py:44
  316.0 11.5 %first_back.1 = (bf16[1024,768]{1,0:T(8,128)(2,1)}, bf16[1024,2304]{1,0:T(8,128)(2,1)}, f32[1,2,768]{2,1,0:T(2,128)}, f32[1,768]{1,0:T(1,128)}) custom-call(bf16[1024,256]{1,0:T(8,128)(2,1)} %get-tuple-element.114.refs_3_.refs_0_, bf16[1024,256]{1,0:T(8,128)(2,1)} %get-tuple-element.115.refs_1_, bf16[1024,256]{1,0:T(8,128)(2,1)} %get-tuple-element.116.refs_2_, ...), custom_call_target="tpu_custom_call" | custom-call | flops 3600000000 | bytes 22428672 | tf_op jit(solution)/shard_map/first_back/pallas_call | solution.py:44
  332.1 6.5 %qkv_grad.3 = (bf16[8,48,1280]{2,1,0:T(8,128)(2,1)}, bf16[8,48,1280]{2,1,0:T(8,128)(2,1)}) custom-call(s32[1]{0:T(128)} %bitcast.10.refs_0_, bf16[1024,768]{1,0:T(8,128)(2,1)} %get-tuple-element.97.refs_0_.refs_1_, bf16[1024,2304]{1,0:T(8,128)(2,1)} %get-tuple-element.156.refs_2_), custom_call_target="tpu_custom_call" | custom-call | flops 1800000000 | bytes 8257540 | tf_op jit(solution)/shard_map/qkv_grad/pallas_call | solution.py:44
  340.7 5.9 %qkv_grad.2 = (bf16[8,48,1024]{2,1,0:T(8,128)(2,1)}, bf16[8,48,1024]{2,1,0:T(8,128)(2,1)}) custom-call(s32[1]{0:T(128)} %bitcast.10.refs_0_, bf16[1024,768]{1,0:T(8,128)(2,1)} %get-tuple-element.97.refs_0_.refs_1_, bf16[1024,2304]{1,0:T(8,128)(2,1)} %get-tuple-element.156.refs_2_), custom_call_target="tpu_custom_call" | custom-call | flops 1800000000 | bytes 7864324 | tf_op jit(solution)/shard_map/qkv_grad/pallas_call | solution.py:44
  354.5 37.8 %collective-permute-done.22 = f32[4,11,384]{2,1,0:T(8,128)S(1)} collective-permute-done((f32[4,11,384]{2,1,0:T(8,128)S(1)}, f32[4,11,384]{2,1,0:T(8,128)S(1)}, u32[]{:S(2)}, u32[]{:S(2)}) %collective-permute-start.22) | collective-permute-done | bytes 67616 | tf_op jit(solution)/shard_map/ppermute | solution.py:562
  408.0 8.2 %collective-permute-done.25.refs_2_ = bf16[8,48,512]{2,1,0:T(8,128)(2,1)S(1)} collective-permute-done((bf16[8,48,512]{2,1,0:T(8,128)(2,1)}, bf16[8,48,512]{2,1,0:T(8,128)(2,1)S(1)}, u32[]{:S(2)}, u32[]{:S(2)}) %collective-permute-start.25) | collective-permute-done | bytes 393248 | tf_op jit(solution)/shard_map/ppermute | solution.py:562
  428.4 4.8 %collective-permute-done.27.refs_2_ = bf16[2,48,512]{2,1,0:T(8,128)(2,1)S(1)} collective-permute-done((bf16[2,48,512]{2,1,0:T(8,128)(2,1)}, bf16[2,48,512]{2,1,0:T(8,128)(2,1)S(1)}, u32[]{:S(2)}, u32[]{:S(2)}) %collective-permute-start.27) | collective-permute-done | bytes 98336 | tf_op jit(solution)/shard_map/ppermute | solution.py:562
  (227 shorter events, 116.8 us)
Async XLA Ops:
  4.4 45.2 %all-to-all-start = ((bf16[16,64,768]{2,1,0:T(8,128)(2,1)}), bf16[16,64,768]{2,1,0:T(8,128)(2,1)S(1)}, u32[]{:S(2)}, u32[]{:S(2)}) async-start(bf16[16,64,768]{2,1,0:T(8,128)(2,1)} %reshape.133), calls=%async_computation | async-start | bytes 3145728 | tf_op jit(solution)/shard_map/all_to_all | solution.py:652
  59.3 55.7 %all-to-all-start.1 = ((bf16[16,64,768]{2,1,0:T(8,128)(2,1)}), bf16[16,64,768]{2,1,0:T(8,128)(2,1)S(1)}, u32[]{:S(2)}, u32[]{:S(2)}) async-start(bf16[16,64,768]{2,1,0:T(8,128)(2,1)} %reshape.136), calls=%async_computation.1 | async-start | bytes 3145728 | tf_op jit(solution)/shard_map/all_to_all | solution.py:652
  164.3 39.3 %collective-permute-start.2 = (bf16[8,48,3840]{2,1,0:T(8,128)(2,1)}, bf16[8,48,3840]{2,1,0:T(8,128)(2,1)}, u32[]{:S(2)}, u32[]{:S(2)}) collective-permute-start(bf16[8,48,3840]{2,1,0:T(8,128)(2,1)} %get-tuple-element.112), channel_id=1, source_target_pairs={{0,1},{1,0},{2,3},{3,2},{4,5},{5,4},{6,7},{7,6},{8,9},{9,8},{10,11... | collective-permute-start | bytes 8847368 | tf_op jit(solution)/shard_map/ppermute | solution.py:562
  175.7 21.6 %collective-permute-start.1 = (bf16[8,192,768]{2,1,0:T(8,128)(2,1)}, bf16[8,192,768]{2,1,0:T(8,128)(2,1)}, u32[]{:S(2)}, u32[]{:S(2)}) collective-permute-start(bf16[8,192,768]{2,1,0:T(8,128)(2,1)} %get-tuple-element.106), channel_id=1, source_target_pairs={{0,1},{1,0},{2,3},{3,2},{4,5},{5,4},{6,7},{7,6},{8,9},{9,8},{10,11... | collective-permute-start | bytes 7077896 | tf_op jit(solution)/shard_map/ppermute | solution.py:562
  175.9 135.4 %all-to-all-start.2 = ((bf16[16,64,768]{2,1,0:T(8,128)(2,1)}), bf16[16,64,768]{2,1,0:T(8,128)(2,1)S(1)}, u32[]{:S(2)}, u32[]{:S(2)}) async-start(bf16[16,64,768]{2,1,0:T(8,128)(2,1)} %bitcast.8), calls=%async_computation.2 | async-start | bytes 3145728 | tf_op jit(solution)/shard_map/all_to_all | solution.py:664
  196.8 96.2 %collective-permute-start.17 = (bf16[1024,128]{1,0:T(8,128)(2,1)}, bf16[1024,128]{1,0:T(8,128)(2,1)S(1)}, u32[]{:S(2)}, u32[]{:S(2)}) collective-permute-start(bf16[1024,128]{1,0:T(8,128)(2,1)} %get-tuple-element.149), channel_id=1, source_target_pairs={{0,1},{1,0},{2,3},{3,2},{4,5},{5,4},{6,7},{7,6},{8,9},{9,8},{10,11... | collective-permute-start | bytes 786440 | tf_op jit(solution)/shard_map/ppermute | solution.py:562
  196.8 112.4 %collective-permute-start.18 = (bf16[1024,128]{1,0:T(8,128)(2,1)}, bf16[1024,128]{1,0:T(8,128)(2,1)S(1)}, u32[]{:S(2)}, u32[]{:S(2)}) collective-permute-start(bf16[1024,128]{1,0:T(8,128)(2,1)} %get-tuple-element.150), channel_id=1, source_target_pairs={{0,1},{1,0},{2,3},{3,2},{4,5},{5,4},{6,7},{7,6},{8,9},{9,8},{10,11... | collective-permute-start | bytes 786440 | tf_op jit(solution)/shard_map/ppermute | solution.py:562
  201.7 33.5 %collective-permute-start.5 = (bf16[8,96,768]{2,1,0:T(8,128)(2,1)}, bf16[8,96,768]{2,1,0:T(8,128)(2,1)S(1)}, u32[]{:S(2)}, u32[]{:S(2)}) collective-permute-start(bf16[8,96,768]{2,1,0:T(8,128)(2,1)} %get-tuple-element.119), channel_id=1, source_target_pairs={{0,16},{16,0},{1,17},{17,1},{2,18},{18,2},{3,19},{19,3},{4,20},{20... | collective-permute-start | bytes 3538952 | tf_op jit(solution)/shard_map/ppermute | solution.py:562
  208.4 38.9 %collective-permute-start.6 = (bf16[4,48,3840]{2,1,0:T(8,128)(2,1)}, bf16[4,48,3840]{2,1,0:T(8,128)(2,1)S(1)}, u32[]{:S(2)}, u32[]{:S(2)}) collective-permute-start(bf16[4,48,3840]{2,1,0:T(8,128)(2,1)} %get-tuple-element.121), channel_id=1, source_target_pairs={{0,2},{2,0},{4,6},{6,4},{8,10},{10,8},{12,14},{14,12},{1,3},{3,1},... | collective-permute-start | bytes 4423688 | tf_op jit(solution)/shard_map/ppermute | solution.py:562
  235.1 74.2 %collective-permute-start.3 = (bf16[1024,256]{1,0:T(8,128)(2,1)}, bf16[1024,256]{1,0:T(8,128)(2,1)S(1)}, u32[]{:S(2)}, u32[]{:S(2)}) collective-permute-start(bf16[1024,256]{1,0:T(8,128)(2,1)} %get-tuple-element.117), channel_id=1, source_target_pairs={{0,1},{1,0},{2,3},{3,2},{4,5},{5,4},{6,7},{7,6},{8,9},{9,8},{10,11... | collective-permute-start | bytes 1572872 | tf_op jit(solution)/shard_map/ppermute | solution.py:562
  239.9 25.7 %collective-permute-start.9 = (bf16[4,96,768]{2,1,0:T(8,128)(2,1)}, bf16[4,96,768]{2,1,0:T(8,128)(2,1)S(1)}, u32[]{:S(2)}, u32[]{:S(2)}) collective-permute-start(bf16[4,96,768]{2,1,0:T(8,128)(2,1)} %get-tuple-element.128), channel_id=1, source_target_pairs={{0,2},{2,0},{4,6},{6,4},{8,10},{10,8},{12,14},{14,12},{1,3},{3,1},... | collective-permute-start | bytes 1769480 | tf_op jit(solution)/shard_map/ppermute | solution.py:562
  251.3 19.6 %collective-permute-start.10 = (bf16[4,48,1920]{2,1,0:T(8,128)(2,1)}, bf16[4,48,1920]{2,1,0:T(8,128)(2,1)S(1)}, u32[]{:S(2)}, u32[]{:S(2)}) collective-permute-start(bf16[4,48,1920]{2,1,0:T(8,128)(2,1)} %get-tuple-element.130), channel_id=1, source_target_pairs={{0,16},{16,0},{1,17},{17,1},{2,18},{18,2},{3,19},{19,3},{4,20},{20... | collective-permute-start | bytes 2211848 | tf_op jit(solution)/shard_map/ppermute | solution.py:562
  268.4 19.4 %collective-permute-start.13 = (bf16[2,96,768]{2,1,0:T(8,128)(2,1)}, bf16[2,96,768]{2,1,0:T(8,128)(2,1)S(1)}, u32[]{:S(2)}, u32[]{:S(2)}) collective-permute-start(bf16[2,96,768]{2,1,0:T(8,128)(2,1)} %get-tuple-element.137), channel_id=1, source_target_pairs={{0,4},{2,6},{4,0},{6,2},{8,12},{10,14},{12,8},{14,10},{1,5},{3,7},... | collective-permute-start | bytes 884744 | tf_op jit(solution)/shard_map/ppermute | solution.py:562
  273.9 16.4 %collective-permute-start.14 = (bf16[2,48,1920]{2,1,0:T(8,128)(2,1)}, bf16[2,48,1920]{2,1,0:T(8,128)(2,1)S(1)}, u32[]{:S(2)}, u32[]{:S(2)}) collective-permute-start(bf16[2,48,1920]{2,1,0:T(8,128)(2,1)} %get-tuple-element.139), channel_id=1, source_target_pairs={{0,4},{2,6},{4,0},{6,2},{8,12},{10,14},{12,8},{14,10},{1,5},{3,7},... | collective-permute-start | bytes 1105928 | tf_op jit(solution)/shard_map/ppermute | solution.py:562
  287.8 22.0 %collective-permute-start.4 = (bf16[1024,256]{1,0:T(8,128)(2,1)S(1)}, bf16[1024,256]{1,0:T(8,128)(2,1)S(1)}, u32[]{:S(2)}, u32[]{:S(2)}) collective-permute-start(bf16[1024,256]{1,0:T(8,128)(2,1)S(1)} %copy-done.37), channel_id=1, source_target_pairs={{0,1},{1,0},{2,3},{3,2},{4,5},{5,4},{6,7},{7,6},{8,9},{9,8},{10,11... | collective-permute-start | bytes 1572872 | tf_op jit(solution)/shard_map/ppermute | solution.py:562
  290.3 19.6 %collective-permute-start.7 = (bf16[1024,128]{1,0:T(8,128)(2,1)S(1)}, bf16[1024,128]{1,0:T(8,128)(2,1)S(1)}, u32[]{:S(2)}, u32[]{:S(2)}) collective-permute-start(bf16[1024,128]{1,0:T(8,128)(2,1)S(1)} %copy-done.38), channel_id=1, source_target_pairs={{0,1},{1,0},{2,3},{3,2},{4,5},{5,4},{6,7},{7,6},{8,9},{9,8},{10,11... | collective-permute-start | bytes 786440 | tf_op jit(solution)/shard_map/ppermute | solution.py:562
  292.9 17.4 %collective-permute-start.38 = (bf16[1,96,768]{2,1,0:T(8,128)(2,1)}, bf16[1,96,768]{2,1,0:T(8,128)(2,1)}, u32[]{:S(2)}, u32[]{:S(2)}) collective-permute-start(bf16[1,96,768]{2,1,0:T(8,128)(2,1)} %get-tuple-element.178), channel_id=1, source_target_pairs={{0,8},{2,10},{4,12},{6,14},{8,0},{10,2},{12,4},{14,6},{1,9},{3,11}... | collective-permute-start | bytes 442376 | tf_op jit(solution)/shard_map/ppermute | solution.py:562
  313.7 39.9 %collective-permute-start.39 = (bf16[96,768]{1,0:T(8,128)(2,1)S(1)}, bf16[96,768]{1,0:T(8,128)(2,1)S(1)}, u32[]{:S(2)}, u32[]{:S(2)}) collective-permute-start(bf16[96,768]{1,0:T(8,128)(2,1)S(1)} %fusion.3), channel_id=1, source_target_pairs={{0,16},{16,0},{1,17},{17,1},{2,18},{18,2},{3,19},{19,3},{4,20},{20... | collective-permute-start | bytes 442376 | tf_op jit(solution)/shard_map/ppermute | solution.py:562
  329.4 64.5 %collective-permute-start.37 = (bf16[48,1920]{1,0:T(8,128)(2,1)S(1)}, bf16[48,1920]{1,0:T(8,128)(2,1)S(1)}, u32[]{:S(2)}, u32[]{:S(2)}) collective-permute-start(bf16[48,1920]{1,0:T(8,128)(2,1)S(1)} %fusion.2), channel_id=1, source_target_pairs={{0,16},{16,0},{1,17},{17,1},{2,18},{18,2},{3,19},{19,3},{4,20},{20... | collective-permute-start | bytes 552968 | tf_op jit(solution)/shard_map/ppermute | solution.py:562
  338.6 56.8 %collective-permute-start.30 = (bf16[8,48,1280]{2,1,0:T(8,128)(2,1)}, bf16[8,48,1280]{2,1,0:T(8,128)(2,1)S(1)}, u32[]{:S(2)}, u32[]{:S(2)}) collective-permute-start(bf16[8,48,1280]{2,1,0:T(8,128)(2,1)} %get-tuple-element.168), channel_id=1, source_target_pairs={{0,1},{1,0},{2,3},{3,2},{4,5},{5,4},{6,7},{7,6},{8,9},{9,8},{10,11... | collective-permute-start | bytes 2949128 | tf_op jit(solution)/shard_map/ppermute | solution.py:562
  346.6 110.6 %all-to-all-start.3 = ((bf16[16,64,768]{2,1,0:T(8,128)(2,1)}), bf16[16,64,768]{2,1,0:T(8,128)(2,1)S(1)}, u32[]{:S(2)}, u32[]{:S(2)}) async-start(bf16[16,64,768]{2,1,0:T(8,128)(2,1)} %bitcast.14), calls=%async_computation.3 | async-start | bytes 3145728 | tf_op jit(solution)/shard_map/all_to_all | solution.py:664
  350.6 51.1 %collective-permute-start.24 = (bf16[8,48,1024]{2,1,0:T(8,128)(2,1)}, bf16[8,48,1024]{2,1,0:T(8,128)(2,1)S(1)}, u32[]{:S(2)}, u32[]{:S(2)}) collective-permute-start(bf16[8,48,1024]{2,1,0:T(8,128)(2,1)} %get-tuple-element.158), channel_id=1, source_target_pairs={{0,1},{1,0},{2,3},{3,2},{4,5},{5,4},{6,7},{7,6},{8,9},{9,8},{10,11... | collective-permute-start | bytes 2359304 | tf_op jit(solution)/shard_map/ppermute | solution.py:562
  350.9 41.3 %collective-permute-start.22 = (f32[4,11,384]{2,1,0:T(8,128)S(1)}, f32[4,11,384]{2,1,0:T(8,128)S(1)}, u32[]{:S(2)}, u32[]{:S(2)}) collective-permute-start(f32[4,11,384]{2,1,0:T(8,128)S(1)} %maximum_select_fusion.4), channel_id=1, source_target_pairs={{0,8},{2,10},{4,12},{6,14},{8,0},{10,2},{12,4},{14,6},{1,9},{3,11}... | collective-permute-start | bytes 202760 | tf_op jit(solution)/shard_map/ppermute | solution.py:562
  400.0 20.6 %collective-permute-start.31 = (bf16[4,48,1280]{2,1,0:T(8,128)(2,1)}, bf16[4,48,1280]{2,1,0:T(8,128)(2,1)S(1)}, u32[]{:S(2)}, u32[]{:S(2)}) collective-permute-start(bf16[4,48,1280]{2,1,0:T(8,128)(2,1)} %get-tuple-element.170), channel_id=1, source_target_pairs={{0,2},{2,0},{4,6},{6,4},{8,10},{10,8},{12,14},{14,12},{1,3},{3,1},... | collective-permute-start | bytes 1474568 | tf_op jit(solution)/shard_map/ppermute | solution.py:562
  (61 other events, 380.5 us)

commit v3 on v2

--- a/solution.py
+++ b/solution.py
@@ -17,7 +17,15 @@
 NN = (((1,), (0,)), ((), ()))
 NT = (((1,), (1,)), ((), ()))
 TN = (((0,), (0,)), ((), ()))
-VMEM_LIMIT = 56 << 20
+KEY_CHUNK = 512
+SMALLEST = 2.0**-90
+VM_ATTEND = 48
+VM_BACK = 56
+VM_MLP = 48
+VM_SUM = 56
+COST = 50
+DOWN_TILE = 768
+MLP_BLOCK = 256
 
 
 def mm(a, b, dims=NN):
@@ -33,7 +41,7 @@
     return jax.ShapeDtypeStruct(shape, dtype)
 
 
-def call(kernel, name, grid, ins, outs, scratch=(), flops=0, deps=()):
+def call(kernel, name, grid, ins, outs, scratch=(), flops=0, deps=(), vmem=32):
     given, skipped = len(ins), len(deps)
 
     def body(*refs):
@@ -48,133 +56,136 @@
         out_specs=[spec for a, spec in outs],
         out_shape=[a for a, spec in outs],
         scratch_shapes=list(scratch),
-        compiler_params=pltpu.CompilerParams(vmem_limit_bytes=VMEM_LIMIT),
-        cost_estimate=pl.CostEstimate(flops=flops, bytes_accessed=moved, transcendentals=0),
+        compiler_params=pltpu.CompilerParams(vmem_limit_bytes=vmem << 20),
+        cost_estimate=pl.CostEstimate(flops=flops // COST, bytes_accessed=moved // COST, transcendentals=0),
         name=name,
     )(*[a for a, spec in ins], *deps)
 
 
 def attend_kernel(q_ref, k0, k1, v0, v1, o_ref, full_ref, lse_ref):
+    count = q_ref.shape[0]
+    n = k0.shape[0]
     q = q_ref[...]
-    ones = jnp.ones(v0.shape, BF)
-    val0 = jnp.concatenate([v0[...], ones], 1)
-    val1 = jnp.concatenate([v1[...], ones], 1)
-    outs, logs = [], []
-    for head in range(2):
+    wide_q = q.astype(F32)
+    square_q = (wide_q * wide_q).astype(BF)
+    turned, squares = [v0[...].T, v1[...].T], []
+    for k in (k0, k1):
+        wide_k = k[...].astype(F32)
+        squares.append((wide_k * wide_k).astype(BF))
+    chunk = min(KEY_CHUNK, n)
+
+    def one_head(head, exact):
         qm = of_head(q, head)
-        s0 = mm(qm, k0[...], NT)
-        s1 = mm(qm, k1[...], NT)
-        top = jnp.max(jnp.maximum(s0, s1), axis=1, keepdims=True)
-        p0 = jnp.exp2(s0 - top).astype(BF)
-        p1 = jnp.exp2(s1 - top).astype(BF)
-        both = mm(p0, val0) + mm(p1, val1)
-        total = both[:, 128:]
-        outs.append(both[:, :128] / total)
-        logs.append(top + jnp.log2(total))
-    lane = lax.broadcasted_iota(jnp.int32, outs[0].shape, 1)
-    both = jnp.where(lane < 64, outs[0], outs[1])
-    o_ref[...] = both.astype(BF)
-    full_ref[...] = both
-    turned = jnp.where(lane < 64, logs[0], logs[1]).T
-    lse_ref[0:4, :] = turned[0:4]
-    lse_ref[4:8, :] = turned[64:68]
+        top = None
+        if exact:
+            for k in (k0, k1):
+                for i in range(0, n, chunk):
+                    part = jnp.max(mm(k[i : i + chunk], qm, NT), axis=0, keepdims=True)
+                    top = part if top is None else jnp.maximum(top, part)
+        else:
+            pick = of_head(jnp.ones((8, 128), BF), head)
+            for square in squares:
+                part = jnp.max(mm(pick, square, NT))
+                top = part if top is None else jnp.maximum(top, part)
+            top = jnp.sqrt(mm(pick, square_q, NT)[0:1] * (top * 1.05))
+        out = total = None
+        for k, values in ((k0, turned[0]), (k1, turned[1])):
+            for i in range(0, n, chunk):
+                probs = jnp.exp2(mm(k[i : i + chunk], qm, NT) - top)
+                part = jnp.sum(probs, axis=0, keepdims=True)
+                total = part if total is None else total + part
+                part = mm(values[64 * head : 64 * head + 64, i : i + chunk], probs.astype(BF))
+                out = part if out is None else out + part
+        lse = jnp.broadcast_to(top + jnp.log2(total), (64, count))
+        return out / total, lse, jnp.min(total)
+
+    def run(exact):
+        first, second = one_head(0, exact), one_head(1, exact)
+        out = jnp.concatenate([first[0], second[0]], 0).T
+        o_ref[...] = out.astype(BF)
+        full_ref[...] = out
+        lse_ref[...] = jnp.concatenate([first[1], second[1]], 0).T
+        return jnp.minimum(first[2], second[2])
+
+    least = run(False)
+
+    @pl.when(jnp.logical_not(least >= SMALLEST))
+    def _():
+        run(True)
 
 
 def attend(q, kv_own, kv_peer, frames):
     tokens, width = q.shape
     pairs = width // 128
     n = tokens // frames
-    bq = min(512, n)
-    nb = n // bq
-    qs = pl.BlockSpec((bq, 128), lambda f, p, j: (f * nb + j, p))
-    ks = pl.BlockSpec((n, 128), lambda f, p, j: (f, p))
-    vs = pl.BlockSpec((n, 128), lambda f, p, j: (f, pairs + p))
-    ls = pl.BlockSpec((8, bq), lambda f, p, j: (p, f * nb + j))
+    qs = pl.BlockSpec((n, 128), lambda f, p: (f, p))
+    vs = pl.BlockSpec((n, 128), lambda f, p: (f, pairs + p))
     return call(
         attend_kernel,
         "attend",
-        (frames, pairs, nb),
-        [(q, qs), (kv_own, ks), (kv_peer, ks), (kv_own, vs), (kv_peer, vs)],
+        (frames, pairs),
+        [(q, qs), (kv_own, qs), (kv_peer, qs), (kv_own, vs), (kv_peer, vs)],
         [
             (sds((tokens, width), BF), qs),
             (sds((tokens, width), F32), qs),
-            (sds((pairs * 8, tokens), F32), ls),
+            (sds((tokens, width), F32), qs),
         ],
-        flops=50_000_000_000,
+        flops=30_000_000_000,
+        vmem=VM_ATTEND,
     )
 
 
 def attend_back_kernel(
     q_ref, k0, k1, v0, v1, go_ref, o_ref, lse_ref, dq_ref, dk0, dk1, dv0, dv1, dka, dva
 ):
-    j = pl.program_id(2)
+    n = k0.shape[0]
     q = q_ref[...]
     go = go_ref[...]
-    prod = (go.astype(F32) * o_ref[...]).T
+    turned_q, turned_go = q.T, go.T
+    prod = go.astype(F32) * o_ref[...]
+    qms = [of_head(q, head) for head in range(2)]
+    goms = [of_head(go, head) for head in range(2)]
+    lses = [lse_ref[:, 64 * head : 64 * head + 1] for head in range(2)]
+    deltas = [jnp.sum(of_head(prod, head), axis=1, keepdims=True) for head in range(2)]
+    chunk = min(KEY_CHUNK, n)
     dq = None
     for part, (k, v) in enumerate(((k0, v0), (k1, v1))):
-        keys = k[...]
-        vals = v[...]
-        turned = keys.T
-        acc_v = acc_k = None
-        for head in range(2):
-            qm = of_head(q, head)
-            gom = of_head(go, head)
-            lse = lse_ref[4 * head : 4 * head + 1, :]
-            delta = jnp.sum(prod[64 * head : 64 * head + 64], axis=0, keepdims=True)
-            probs = jnp.exp2(mm(keys, qm, NT) - lse)
-            ds = (probs * (mm(vals, gom, NT) - delta)).astype(BF)
-            probs = probs.astype(BF)
-            a = mm(probs, gom)
-            b = mm(ds, qm)
-            c = mm(of_head(turned, head, 0), ds)
-            dq = c if dq is None else dq + c
-            acc_v = a if acc_v is None else acc_v + a
-            acc_k = b if acc_k is None else acc_k + b
-
-        @pl.when(j == 0)
-        def _():
-            dva[part] = acc_v
-            dka[part] = acc_k
-
-        @pl.when(j > 0)
-        def _():
-            dva[part] += acc_v
-            dka[part] += acc_k
-
-    dq_ref[...] = (dq * SCALING).T.astype(BF)
-
-    @pl.when(j == pl.num_programs(2) - 1)
-    def _():
-        back = SCALING / (SCALING * LOG2E)
-        dk0[...] = (dka[0] * back).astype(BF)
-        dk1[...] = (dka[1] * back).astype(BF)
-        dv0[...] = dva[0].astype(BF)
-        dv1[...] = dva[1].astype(BF)
+        for i in range(0, n, chunk):
+            keys = k[i : i + chunk]
+            vals = v[i : i + chunk]
+            for head in range(2):
+                lanes = slice(64 * head, 64 * head + 64)
+                probs = jnp.exp2(mm(qms[head], keys, NT) - lses[head])
+                ds = (probs * (mm(goms[head], vals, NT) - deltas[head])).astype(BF)
+                dva[part, lanes, i : i + chunk] = mm(turned_go[lanes], probs.astype(BF))
+                dka[part, lanes, i : i + chunk] = mm(turned_q[lanes], ds)
+                term = mm(ds, of_head(keys, head))
+                dq = term if dq is None else dq + term
+    dq_ref[...] = (dq * SCALING).astype(BF)
+    back = 1.0 / LOG2E
+    for part, (dk, dv) in enumerate(((dk0, dv0), (dk1, dv1))):
+        dk[...] = (dka[part].T * back).astype(BF)
+        dv[...] = dva[part].T.astype(BF)
 
 
 def attend_back(q, kv_own, kv_peer, go, att, lse, frames, first, count, deps):
     tokens, width = q.shape
     pairs = width // 128
     n = tokens // frames
-    bq = min(512, n)
-    nb = n // bq
-    qs = pl.BlockSpec((bq, 128), lambda f, p, j: (f * nb + j, first + p))
-    ks = pl.BlockSpec((n, 128), lambda f, p, j: (f, first + p))
-    vs = pl.BlockSpec((n, 128), lambda f, p, j: (f, pairs + first + p))
-    ls = pl.BlockSpec((8, bq), lambda f, p, j: (first + p, f * nb + j))
-    qo = pl.BlockSpec((bq, 128), lambda f, p, j: (f * nb + j, p))
-    ko = pl.BlockSpec((n, 128), lambda f, p, j: (f, p))
-    shape = jax.ShapeDtypeStruct((tokens, 128 * count), BF)
+    qs = pl.BlockSpec((n, 128), lambda f, p: (f, first + p))
+    vs = pl.BlockSpec((n, 128), lambda f, p: (f, pairs + first + p))
+    out = pl.BlockSpec((n, 128), lambda f, p: (f, p))
+    shape = sds((tokens, 128 * count), BF)
     return call(
         attend_back_kernel,
         "attend_back",
-        (frames, count, nb),
-        [(q, qs), (kv_own, ks), (kv_peer, ks), (kv_own, vs), (kv_peer, vs), (go, qs), (att, qs), (lse, ls)],
-        [(shape, qo)] + [(shape, ko)] * 4,
-        [pltpu.VMEM((2, n, 128), F32)] * 2,
-        14_000_000_000 * count,
+        (frames, count),
+        [(q, qs), (kv_own, qs), (kv_peer, qs), (kv_own, vs), (kv_peer, vs), (go, qs), (att, qs), (lse, qs)],
+        [(shape, out)] * 5,
+        [pltpu.VMEM((2, 128, n), F32)] * 2,
+        11_000_000_000 * count,
         deps,
+        VM_BACK,
     )
 
 
@@ -211,7 +222,7 @@
     kv_ref[:, width:] = mm(hidden, wv[...]).astype(BF)
 
 
-def keys_of(x, chan_add, shift, gain, weight, frames):
+def keys_of(x, chan_add, shift, gain, weight, frames, deps):
     count, width = x.shape
     block = 256
     per = count // frames // block
@@ -233,6 +244,7 @@
             (sds((count, 2 * width), BF), rows_of(block, 2 * width)),
         ],
         flops=2_400_000_000,
+        deps=deps,
     )
 
 
@@ -345,7 +357,7 @@
 def mlp(x, chan_add, att, g, rows, up_bias, wo, wu, wd, frames):
     count, width = x.shape
     wide = wu.shape[1]
-    block = 256
+    block = MLP_BLOCK
     per = count // frames // block
     narrow, broad = rows_of(block, width), rows_of(block, wide)
     anywhere = pl.BlockSpec(memory_space=pl.ANY)
@@ -381,6 +393,7 @@
             pltpu.SemaphoreType.DMA((3,)),
         ],
         25_000_000_000,
+        vmem=VM_MLP,
     )
 
 
@@ -392,11 +405,11 @@
     send_ref[...] = scr[:, 1 - core].astype(BF)
 
 
-def down_grad(core, act, g, lon):
+def down_grad(core, act, g, lon, deps):
     count, wide = act.shape
     width = g.shape[1]
     share = wide // lon
-    tile = 384
+    tile = DOWN_TILE
     chips = tile // (2 * share)
     out = sds((lon // 2, share, width), BF)
     spec = pl.BlockSpec((chips, share, width), lambda i: (i, 0, 0))
@@ -408,6 +421,8 @@
         [(out, spec), (out, spec)],
         [pltpu.VMEM((chips, 2, share, width), F32)],
         4_800_000_000,
+        deps,
+        VM_SUM,
     )
 
 
@@ -454,34 +469,41 @@
         [(out, spec), (out, spec)],
         [pltpu.VMEM((width, count), BF), pltpu.VMEM((lon // 2, 2, share, width), F32)],
         6_000_000_000,
-    )
-
-
-def qkv_grad_kernel_of(start, stop):
-    def kernel(core_ref, hid_ref, grad_ref, send_ref, keep_ref, scr):
-        core = core_ref[0]
-        scr[...] = mm(hid_ref[...], grad_ref[:, start:stop], TN).reshape(scr.shape)
-        keep_ref[...] = scr[:, core].astype(BF)
-        send_ref[...] = scr[:, 1 - core].astype(BF)
-
-    return kernel
-
-
-def qkv_grad(core, hidden, grad, start, stop, lon, deps=()):
+        vmem=VM_SUM,
+    )
+
+
+def qkv_grad_kernel(core_ref, hid_ref, grad_ref, send_ref, keep_ref, turned, scr):
+    core = core_ref[0]
+
+    @pl.when(pl.program_id(0) == 0)
+    def _():
+        turned[...] = hid_ref[...].T
+
+    scr[...] = mm(turned[...], grad_ref[...]).reshape(scr.shape)
+    keep_ref[...] = scr[:, core].astype(BF)
+    send_ref[...] = scr[:, 1 - core].astype(BF)
+
+
+def qkv_grad(core, hidden, grad, lon, deps):
     count, width = hidden.shape
-    cols = stop - start
     share = width // lon
-    out = sds((lon // 2, share, cols), BF)
-    spec = whole_of((lon // 2, share, cols))
-    return call(
-        qkv_grad_kernel_of(start, stop),
+    out = sds((lon // 2, share, grad.shape[1]), BF)
+    spec = pl.BlockSpec((lon // 2, share, width), lambda i: (0, 0, i))
+    return call(
+        qkv_grad_kernel,
         "qkv_grad",
-        (1,),
-        [(core, SMALL), (hidden, whole_of((count, width))), (grad, whole_of(grad.shape))],
+        (grad.shape[1] // width,),
+        [
+            (core, SMALL),
+            (hidden, whole_of((count, width))),
+            (grad, pl.BlockSpec((count, width), lambda i: (0, i))),
+        ],
         [(out, spec), (out, spec)],
-        [pltpu.VMEM((lon // 2, 2, share, cols), F32)],
-        1_800_000_000,
+        [pltpu.VMEM((width, count), BF), pltpu.VMEM((lon // 2, 2, share, width), F32)],
+        3_600_000_000,
         deps,
+        VM_SUM,
     )
 
 
@@ -519,7 +541,7 @@
     return kernel
 
 
-def first_back(pieces, x, chan_add, gain, grad_middle, weight, frames):
+def first_back(pieces, x, chan_add, gain, grad_middle, weight, frames, deps):
     count, width = x.shape
     block = 256
     per = count // frames // block
@@ -543,6 +565,8 @@
             (sds((1, width), F32), whole_of((1, width))),
         ],
         flops=3_600_000_000,
+        deps=deps,
+        vmem=VM_SUM,
     )
 
 
@@ -562,94 +586,188 @@
     return lax.ppermute(value, axis, swap_pairs(lax.axis_size(axis), bit))
 
 
-def add_kernel_of(kind):
-    def kernel(mine_ref, kept_ref, got_ref, *outs):
+def cross(value, turn):
+    pairs = []
+    for i in range(8):
+        lat_next = (i & 1) == turn
+        pairs.append((i, i ^ (4 if lat_next else 2)))
+    return lax.ppermute(value, ("lat", "yy", "core"), pairs)
+
+
+def both(kept_ref, got_ref, *at):
+    return (kept_ref[at].astype(F32) + got_ref[at].astype(F32)).astype(BF)
+
+
+def mlp_part(ins, out, at, yy, half):
+    kept_d, got_d, kept_u, got_u = ins
+    rows, width = kept_d.shape[1:]
+    share = kept_u.shape[1]
+    wide = kept_u.shape[2] - width
+
+    @pl.when(half == 0)
+    def _():
+        out[0, at, :rows] = both(kept_d, got_d, yy)
+        out[0, at, rows:] = both(kept_u, got_u, yy, slice(None), slice(wide, None))
+
+    @pl.when(half == 1)
+    def _():
+        for c in range(wide // width):
+            out[0, at, c * share : (c + 1) * share] = both(
+                kept_u, got_u, yy, slice(None), slice(c * width, (c + 1) * width)
+            )
+        out[0, at, rows:] = jnp.zeros((share, width), BF)
+
+
+def qkv_part(ins, out, at, yy, half):
+    kept, got = ins
+    cols = kept.shape[2] // 2
+    for side in range(2):
+
+        @pl.when(half == side)
+        def _():
+            out[0, at] = both(kept, got, yy, slice(None), slice(side * cols, (side + 1) * cols))
+
+
+def first_add(part, ins, rows, cols, deps=()):
+    zed = ins[0].shape[0] // 2
+
+    def kernel(where_ref, *refs):
+        core, mine = where_ref[0], where_ref[1]
+        for which, out in zip((1 - mine, mine), refs[len(ins) :]):
+            for at in range(2):
+                yy = jnp.where(core == 0, at, which)
+                half = jnp.where(core == 0, which, at)
+                part(refs[: len(ins)], out, at, yy, half)
+
+    core = my_bit("core", 0)
+    mine = jnp.where(core == 0, my_bit("lat", 0), my_bit("yy", 0))
+    out = sds((zed, 2, rows, cols), BF)
+    spec = pl.BlockSpec((1, 2, rows, cols), lambda i: (i, 0, 0, 0))
+    return call(
+        kernel,
+        "first_add",
+        (zed,),
+        [(jnp.concatenate([core, mine]), SMALL)]
+        + [(a, pl.BlockSpec((2,) + a.shape[1:], lambda i: (i, 0, 0))) for a in ins],
+        [(out, spec)] * 2,
+        deps=deps,
+        vmem=VM_SUM,
+    )
+
+
+def second_add(kept, got, deps=()):
+    zed, two, rows, cols = kept.shape
+
+    def kernel(mine_ref, kept_ref, got_ref, send_ref, keep_ref):
         mine = mine_ref[0]
-
-        def total(*at):
-            return (kept_ref[at].astype(F32) + got_ref[at].astype(F32)).astype(BF)
-
-        for which, ref in zip((1 - mine, mine), outs):
-            if kind == "lead":
-                ref[0] = total(which)
-            elif kind == "rows":
-                half = ref.shape[1]
-                ref[...] = total(slice(None), pl.ds(pl.multiple_of(which * half, half), half))
-            else:
-                half = ref.shape[2]
-                ref[...] = total(
-                    slice(None), slice(None), pl.ds(pl.multiple_of(which * half, half), half)
-                )
-
-    return kernel
-
-
-def add_split(kept, got, kind, mine, deps=()):
-    lead, rows, cols = kept.shape
-    size = 2 if lead > 1 else 1
-    spec = pl.BlockSpec((size, rows, cols), lambda i: (i, 0, 0))
-    if kind == "lead":
-        part, half = (1, rows, cols), (lead // 2, rows, cols)
-    elif kind == "rows":
-        part, half = (size, rows // 2, cols), (lead, rows // 2, cols)
-    else:
-        part, half = (size, rows, cols // 2), (lead, rows, cols // 2)
-    out = pl.BlockSpec(part, lambda i: (i, 0, 0))
-    return call(
-        add_kernel_of(kind),
-        "add_" + kind,
-        (lead // size,),
+        send_ref[0] = both(kept_ref, got_ref, 0, 1 - mine)
+        keep_ref[0] = both(kept_ref, got_ref, 0, mine)
+
+    mine = jnp.where(my_bit("core", 0) == 0, my_bit("yy", 0), my_bit("lat", 0))
+    spec = pl.BlockSpec((1, 2, rows, cols), lambda i: (i, 0, 0, 0))
+    out = pl.BlockSpec((1, rows, cols), lambda i: (i, 0, 0))
+    return call(
+        kernel,
+        "second_add",
+        (zed,),
         [(mine, SMALL), (kept, spec), (got, spec)],
-        [(sds(half, BF), out)] * 2,
+        [(sds((zed, rows, cols), BF), out)] * 2,
         deps=deps,
-    )
-
-
-class Sum:
-    def __init__(self, send, kept, stages, cut):
-        self.kept, self.stages, self.cut = kept, list(stages), cut
-        self.got = swap(send, "core", 0)
-        self.final = None
-
-    def advance(self, deps=()):
-        if not self.stages:
-            return ()
-        axis, bit = self.stages.pop(0)
-        kind = "lead" if axis == "chip" else self.cut
-        send, self.kept = add_split(self.kept, self.got, kind, my_bit(axis, bit), deps)
-        self.got = swap(send, axis, bit)
-        return (self.kept,)
-
-    def finish(self):
-        while self.stages:
-            self.advance()
-        total = (self.kept.astype(F32) + self.got.astype(F32)).astype(BF)
-        total = total.reshape(total.shape[-2:])
-        lat = lax.axis_size("lat")
-        if lat == 2:
-            other = swap(total, "lat", 0)
-            dim = 0 if self.cut == "rows" else 1
-            total = jnp.where(
-                lax.axis_index("lat") == 1,
-                jnp.concatenate([other, total], dim),
-                jnp.concatenate([total, other], dim),
-            ).astype(F32)
-        elif lat > 1:
-            total = lax.psum(total.astype(F32), "lat")
-        return total.astype(F32)
-
-
-def stages_of(lat_at):
-    chip = [("chip", bit) for bit in range(bits_of(lax.axis_size("chip")))]
-    if lax.axis_size("lat") == 2:
-        chip.insert(lat_at, ("lat", 0))
-    return chip
+        vmem=VM_SUM,
+    )
+
+
+def third_add(kept, got, deps=()):
+    zed, rows, cols = kept.shape
+
+    def kernel(me_ref, kept_ref, got_ref, *outs):
+        for up, out in enumerate(outs):
+            out[...] = both(kept_ref, got_ref, lax.rem(me_ref[0] + up, zed))
+
+    me = lax.axis_index("zed").astype(jnp.int32).reshape(1)
+    return call(
+        kernel,
+        "third_add",
+        (1,),
+        [(me, SMALL), (kept, whole_of(kept.shape)), (got, whole_of(kept.shape))],
+        [(sds((rows, cols), BF), whole_of((rows, cols)))] * zed,
+        deps=deps,
+        vmem=VM_SUM,
+    )
+
+
+def cut_lead(kept, got, bit, deps=()):
+    zed, rows, cols = kept.shape
+
+    def kernel(mine_ref, kept_ref, got_ref, send_ref, keep_ref):
+        mine = mine_ref[0]
+        send_ref[0] = both(kept_ref, got_ref, 1 - mine)
+        keep_ref[0] = both(kept_ref, got_ref, mine)
+
+    spec = pl.BlockSpec((2, rows, cols), lambda i: (i, 0, 0))
+    out = pl.BlockSpec((1, rows, cols), lambda i: (i, 0, 0))
+    return call(
+        kernel,
+        "cut_lead",
+        (zed // 2,),
+        [(my_bit("zed", bit), SMALL), (kept, spec), (got, spec)],
+        [(sds((zed // 2, rows, cols), BF), out)] * 2,
+        deps=deps,
+        vmem=VM_SUM,
+    )
+
+
+def up_zed(value, up):
+    zed = lax.axis_size("zed")
+    return lax.ppermute(value, "zed", [(i, (i + up) % zed) for i in range(zed)])
+
+
+def last_add(parts, deps=()):
+    rows, cols = parts[0].shape
+
+    def kernel(*refs):
+        total = refs[0][...].astype(F32)
+        for ref in refs[1:-1]:
+            total = total + ref[...].astype(F32)
+        refs[-1][...] = total.astype(BF)
+
+    spec = whole_of((rows, cols))
+    return call(
+        kernel,
+        "last_add",
+        (1,),
+        [(a, spec) for a in parts],
+        [(sds((rows, cols), BF), spec)],
+        deps=deps,
+        vmem=VM_SUM,
+    )[0]
+
+
+def halves_of(mine):
+    other = swap(mine, "lat", 0)
+    high = lax.axis_index("lat") == 1
+    return jnp.where(high, other, mine).astype(F32), jnp.where(high, mine, other).astype(F32)
+
+
+def held(value, deps):
+    def kernel(value_ref, out_ref):
+        out_ref[...] = value_ref[...]
+
+    spec = whole_of(value.shape)
+    return call(
+        kernel, "held", (1,), [(value, spec)], [(sds(value.shape, value.dtype), spec)], deps=deps
+    )[0]
+
+
+def plain_sum(kept, got):
+    value = lax.psum_scatter(kept + got, ("zed", "yy"), scatter_dimension=0, tiled=True)[0]
+    return lax.psum(value.astype(F32), "lat")
 
 
 def to_frames(value, chips):
     frames_all, patches, width = value.shape
     frames = frames_all // chips
-    value = lax.all_to_all(value, ("lat", "chip"), 0, 0, tiled=True)
+    value = lax.all_to_all(value, ("lat", "zed", "yy"), 0, 0, tiled=True)
     if frames > 1:
         value = value.reshape(chips, frames, patches, width).swapaxes(0, 1)
     return value.reshape(-1, width)
@@ -661,7 +779,7 @@
     if frames > 1:
         value = value.reshape(frames, chips, -1, width).swapaxes(0, 1)
     value = value.reshape(frames_all, -1, width)
-    return lax.all_to_all(value, ("lat", "chip"), 0, 0, tiled=True)
+    return lax.all_to_all(value, ("lat", "zed", "yy"), 0, 0, tiled=True)
 
 
 def on_device(
@@ -684,21 +802,21 @@
     cotangent,
 ):
     lat = lax.axis_size("lat")
-    chips = lat * lax.axis_size("chip")
-    lon = 2 * lax.axis_size("chip")
+    lon = 4 * lax.axis_size("zed")
+    chips = lat * (lon // 2)
     frames_all, rows_here, cols_here, width = tokens.shape
     frames = frames_all // chips
     leads = lead_embed.shape[0]
     wide = up_weight.shape[1]
     share = width // lon
-    place = (lax.axis_index("chip") * 2) + lax.axis_index("core")
     core = my_bit("core", 0)
 
     x = to_frames(tokens.reshape(frames_all, -1, width), chips)
-    g = to_frames(cotangent.reshape(frames_all, -1, width), chips)
+    flat = cotangent.reshape(frames_all, -1, width)
+    g = to_frames(flat, chips)
     count = x.shape[0]
 
-    first = lax.axis_index(("lat", "chip")) * frames
+    first = lax.axis_index(("lat", "zed", "yy")) * frames
     mask_here = lax.dynamic_slice_in_dim(channel_mask, first, frames, 0).astype(BF)
     lead_here = lax.dynamic_slice_in_dim(lead_index, first, frames, 0)
     lead_onehot = (lead_here[:, None] == jnp.arange(leads, dtype=jnp.int32)[None, :]).astype(BF)
@@ -707,7 +825,7 @@
     gain1 = norm1_gain.astype(F32)[None]
     rows2 = jnp.stack([out_bias, norm2_gain, norm2_bias, down_bias]).astype(F32)
 
-    hidden1, kv_own = keys_of(x, chan_add, shift1, gain1, qkv_weight, frames)
+    hidden1, kv_own = keys_of(x, chan_add, shift1, gain1, qkv_weight, frames, (flat,))
     kv_peer = swap(kv_own, "core", 0)
     queries = queries_of(hidden1, qkv_weight)
     attended, attended32, lse = attend(queries, kv_own, kv_peer, frames)
@@ -725,51 +843,98 @@
         frames,
     )
     out_patch = to_places(result, chips, frames_all)
-    down_sum = Sum(*down_grad(core, activ, g, lon), stages_of(0), "rows")
-    up_sum = Sum(*up_grad(core, hidden2, grad_pre, attended, grad_branch, lon), stages_of(1), "cols")
-
+    up_send, up_kept = up_grad(core, hidden2, grad_pre, attended, grad_branch, lon)
+    up_got = swap(up_send, "core", 0)
+    down_send, down_kept = down_grad(core, activ, g, lon, (up_send,))
+    down_got = swap(down_send, "core", 0)
+
+    staged = lat == 2
+    rows = down_kept.shape[1] + share
+    pieces, pair = [], 0
+    deps = (down_kept,)
+    if staged:
+        sent, kept = first_add(mlp_part, [down_kept, down_got, up_kept, up_got], rows, width)
+        got = cross(sent, 0)
+        deps = (sent,)
     pairs = width // 128
-    plan = [2] + [1] * (pairs - 2)
-    pieces, pair = [], 0
-    marks = ()
-    for size in plan:
-        deps = down_sum.advance(marks) + up_sum.advance(marks)
+    plan = [pairs // 2, (pairs + 1) // 3, pairs - pairs // 2 - (pairs + 1) // 3]
+    for at, size in enumerate(plan):
         dq, dk0, dk1, dv0, dv1 = attend_back(
             queries, kv_own, kv_peer, grad_att, attended32, lse, frames, pair, size, deps
         )
         pieces.append((dq, dk0, dv0, swap(dk1, "core", 0), swap(dv1, "core", 0)))
         pair += size
-        marks = (dq,)
-
+        deps = (dq,)
+        if staged and at == 0:
+            sent, kept = second_add(kept, got, deps)
+            got = cross(sent, 1)
+            deps = (sent, dq)
+        if staged and at == 1:
+            sent, kept = cut_lead(kept, got, 0, deps)
+            got = swap(sent, "zed", 0)
+            deps = (sent, dq)
+        if at == 1:
+            deps = deps + (out_patch,)
+
+    if staged:
+        for bit in range(1, bits_of(lax.axis_size("zed"))):
+            sent, kept = cut_lead(kept, got, bit, deps)
+            got = swap(sent, "zed", bit)
+            deps = (sent,)
+        mlp_parts = [kept[0], got[0]]
     grad_start, grad_qkv, frame_sums, gain_sum = first_back(
-        pieces, x, chan_add, gain1, grad_middle, qkv_weight, frames
+        pieces, x, chan_add, gain1, grad_middle, qkv_weight, frames, deps
     )
     grad_patch = to_places(grad_start, chips, frames_all)
-    middle = 3 * width // 512 * 256
-    first_half = qkv_grad(core, hidden1, grad_qkv, 0, middle, lon)
-    other_half = qkv_grad(core, hidden1, grad_qkv, middle, 3 * width, lon)
-    qkv_a = Sum(*first_half, stages_of(0), "cols")
-    qkv_b = Sum(*other_half, stages_of(1), "cols")
-
-    parts = wide // width
-    early_up = early[4:].reshape(lon, parts, share).swapaxes(0, 1).reshape(parts, width)
+
+    ups = wide // width
+    early_up = early[4:].reshape(lon, ups, share).swapaxes(0, 1).reshape(ups, width)
     late = jnp.concatenate(
         [frame_sums.reshape(2 * frames, width), gain_sum, early[:4], early_up], 0
     )
     late = late.reshape(-1, lon // 2, 2, share)
     mine = core[0]
-    late = lax.dynamic_index_in_dim(late, mine, 2, keepdims=False) + swap(
-        lax.dynamic_index_in_dim(late, 1 - mine, 2, keepdims=False), "core", 0
-    )
+    late_got = swap(lax.dynamic_index_in_dim(late, 1 - mine, 2, keepdims=False), "core", 0)
+    late = lax.dynamic_index_in_dim(late, mine, 2, keepdims=False) + late_got
+
+    deps = (late_got,)
+    qkv_send, qkv_kept = qkv_grad(core, hidden1, grad_qkv, lon, deps)
+    qkv_got = swap(qkv_send, "core", 0)
+
+    zed = lax.axis_size("zed")
+
+    if staged:
+        sent, kept = first_add(qkv_part, [qkv_kept, qkv_got], share, 3 * width // 2)
+        got = cross(sent, 0)
+        sent, kept = second_add(kept, got, (grad_patch, mlp_parts[1]))
+        got = cross(sent, 1)
+        parts = third_add(kept, got)
+        late = held(late, (parts[0],))
+        parts = [parts[0]] + [up_zed(part, up) for up, part in enumerate(parts) if up]
+        halves = halves_of(last_add(mlp_parts, (parts[0],)))
+        sum_down, sum_out = halves[0][: rows - share], halves[0][rows - share :]
+        sum_up = jnp.concatenate(
+            [halves[1][c * share : (c + 1) * share] for c in range(wide // width)], 1
+        )
+        sum_qkv = jnp.concatenate(halves_of(last_add(parts)), 1)
+    else:
+        sum_down = plain_sum(down_kept, down_got)
+        sum_up = plain_sum(up_kept, up_got)
+        sum_up, sum_out = sum_up[:, :wide], sum_up[:, wide:]
+        sum_qkv = plain_sum(qkv_kept, qkv_got)
+
     late = late.reshape(1, late.shape[0], -1)
-    for axis in ("chip", "lat"):
+    for axis in ("yy", "lat"):
         for bit in range(bits_of(lax.axis_size(axis))):
             other = swap(late, axis, bit)
             high = my_bit(axis, bit)[0] == 1
             late = jnp.where(
                 high, jnp.concatenate([other, late], 0), jnp.concatenate([late, other], 0)
             )
-    late = lax.dynamic_slice_in_dim(late, lax.axis_index("chip") * share, share, 2)
+    late = jnp.stack([late] + [up_zed(late, up) for up in range(1, zed)])
+    late = jnp.take(late, (lax.axis_index("zed") - jnp.arange(zed)) % zed, axis=0)
+    late = lax.dynamic_slice_in_dim(late, lax.axis_index(("zed", "yy")) * share, share, 3)
+    late = late.reshape(zed, lat, 2, -1, share).swapaxes(0, 1).reshape(chips, -1, share)
     bias_of = late[:, 0 : 2 * frames : 2].reshape(frames_all, share)
     start_of = late[:, 1 : 2 * frames : 2].reshape(frames_all, share)
     rest = late[:, 2 * frames :].sum(0)
@@ -778,9 +943,6 @@
     sum_lead = jnp.dot(hot.T, bias_of, precision=exact)
     sum_chan = jnp.dot(channel_mask.astype(F32).T, start_of, precision=exact)
 
-    sum_down = down_sum.finish()
-    sum_up = up_sum.finish()
-    sum_qkv = jnp.concatenate([qkv_a.finish(), qkv_b.finish()], 1)
     shape = (frames_all, rows_here, cols_here, width)
     return (
         out_patch.reshape(shape),
@@ -790,11 +952,11 @@
         rest[0],
         bias_of.sum(0),
         sum_qkv,
-        sum_up[:, wide:],
+        sum_out,
         rest[4],
         rest[2],
         rest[3],
-        sum_up[:, :wide],
+        sum_up,
         rest[5:].reshape(-1),
         sum_down,
         rest[1],
@@ -803,9 +965,9 @@
 
 def solution(mesh):
     lat, lon = mesh.shape["lat"], mesh.shape["lon"]
-    fine = Mesh(mesh.devices.reshape(lat, lon // 2, 2), ("lat", "chip", "core"))
-    places = P(None, "lat", ("chip", "core"), None)
-    wide = ("chip", "core")
+    fine = Mesh(mesh.devices.reshape(lat, lon // 4, 2, 2), ("lat", "zed", "yy", "core"))
+    wide = ("zed", "yy", "core")
+    places = P(None, "lat", wide, None)
     return jax.shard_map(
         on_device,
         mesh=fine,

time: 463 us -> 409 us (0.88)
  Pallas kernels: 264 us -> 212 us
  local copies, waits for them, and re-layouts: 27.7 us -> 39.3 us
  waiting for transfers between devices: 99.1 us -> 94.3 us
    pallas_call x30 -> x21, Pallas kernels: 264 us -> 212 us  [call(): pl.pallas_call(body, grid=grid, in_specs=[spec for a, spec in ins] + [any...]
    ppermute x40 -> x17, waiting for transfers between devices: 66.4 us -> 42.6 us  [swap(): return lax.ppermute(value, axis, swap_pairs(lax.axis_size(axis), bit))]
    ppermute x40 -> x17, starting transfers between devices: 31.9 us -> 11 us  [swap(): return lax.ppermute(value, axis, swap_pairs(lax.axis_size(axis), bit))]
    ppermute x0 -> x10, waiting for transfers between devices: none -> 17.9 us  [the longest x4 17.2 us: cross(): return lax.ppermute(value, ('lat', 'yy', 'core'), pairs)]
    ppermute x0 -> x10, starting transfers between devices: none -> 15.7 us  [the longest x6 8.82 us: up_zed(): return lax.ppermute(value, 'zed', [(i, (i + up) % zed) for i in range(zed)])]
    unnamed x85 -> x110, local copies, waits for them, and re-layouts: 13.6 us -> 26.9 us
  transfers between devices with their start and end apart: 44 -> 31, of which waited for: 11 -> 10; matrix products, arithmetic and copies ran while one was open for 4% -> 3% of each run, Pallas kernels for 45% -> 34%
where the time goes in v3:
time: 409 us; the launch traced here: 405 us
  Pallas kernels  212 us (52%)
  waiting for transfers between devices  94.3 us (23%)
  starting transfers between devices  51.8 us (13%)
  local copies, waits for them, and re-layouts  39.3 us (10%)
    pallas_call x21, Pallas kernels, call(): pl.pallas_call(body, grid=grid, in_specs=[spec for a, spec in ins] + [any...  212 us
    ppermute x17, waiting for transfers between devices, swap(): return lax.ppermute(value, axis, swap_pairs(lax.axis_size(axis), bit))  42.6 us
    all_to_all x2, waiting for transfers between devices, to_frames(): value = lax.all_to_all(value, ('lat', 'zed', 'yy'), 0, 0, tiled=True)  33.7 us
    unnamed x110, local copies, waits for them, and re-layouts  26.9 us
    ppermute x4, waiting for transfers between devices, cross(): return lax.ppermute(value, ('lat', 'yy', 'core'), pairs)  17.2 us
    all_to_all x2, starting transfers between devices, to_frames(): value = lax.all_to_all(value, ('lat', 'zed', 'yy'), 0, 0, tiled=True)  13.2 us
    all_to_all x2, starting transfers between devices, to_places(): return lax.all_to_all(value, ('lat', 'zed', 'yy'), 0, 0, tiled=True)  11.9 us
    ppermute x17, starting transfers between devices, swap(): return lax.ppermute(value, axis, swap_pairs(lax.axis_size(axis), bit))  11 us
  transfers between devices with their start and end apart: 31, of which 10 were waited for; matrix products, arithmetic and copies ran while one was open for 3% of the time, Pallas kernels for 34%

profile of v3, /device:TPU:0, one launch (start us, length us, event | category | flops | bytes accessed | tf_op | source)
XLA Modules:
  0.0 405.2 jit_solution(13684836494157499183)
XLA Ops:
  0.7 3.8 reshape.291
  4.4 8.5 %all-to-all-start = ((bf16[16,64,768]{2,1,0:T(8,128)(2,1)}), bf16[16,64,768]{2,1,0:T(8,128)(2,1)S(1)}, u32[]{:S(2)}, u32[]{:S(2)}) async-start(bf16[16,64,768]{2,1,0:T(8,128)(2,1)} %reshape.291), calls=%async_computation | async-start | bytes 3145728 | tf_op jit(solution)/shard_map/all_to_all | solution.py:770
  15.9 33.7 %all-to-all-done = bf16[16,64,768]{2,1,0:T(8,128)(2,1)S(1)} async-done(((bf16[16,64,768]{2,1,0:T(8,128)(2,1)}), bf16[16,64,768]{2,1,0:T(8,128)(2,1)S(1)}, u32[]{:S(2)}, u32[]{:S(2)}) %all-to-all-start) | async-done | bytes 1572896 | tf_op jit(solution)/shard_map/all_to_all | solution.py:770
  55.6 4.3 %keys.1 = (bf16[1024,768]{1,0:T(8,128)(2,1)S(1)}, bf16[1024,1536]{1,0:T(8,128)(2,1)S(1)}) custom-call(bf16[1024,768]{1,0:T(8,128)(2,1)S(1)} %bitcast.62, f32[1,1,768]{2,1,0:T(1,128)S(1)} %convolution_bitcast_fusion.1.refs_1_.refs_16_, f32[1,1,768]{2,1,0:T(1,128)S(1)} %broadcast_in_dim.32.refs_2_, f32[1,768]{1,0:T(1,128)S(1)} %reshape.313.refs_3_.refs_17_, ...), custom_call_target="tpu_custom_call" | custom-call | flops 48000000 | bytes 267571 | tf_op jit(solution)/shard_map/keys/pallas_call | solution.py:52
  61.2 4.7 %all-to-all-start.1 = ((bf16[16,64,768]{2,1,0:T(8,128)(2,1)}), bf16[16,64,768]{2,1,0:T(8,128)(2,1)}, u32[]{:S(2)}, u32[]{:S(2)}) async-start(bf16[16,64,768]{2,1,0:T(8,128)(2,1)} %reshape.294.refs_6_), calls=%async_computation.1 | async-start | bytes 3145728 | tf_op jit(solution)/shard_map/all_to_all | solution.py:770
  71.5 31.3 %attend.1 = (bf16[1024,768]{1,0:T(8,128)(2,1)S(1)}, f32[1024,768]{1,0:T(8,128)}, f32[1024,768]{1,0:T(8,128)}) custom-call(bf16[1024,768]{1,0:T(8,128)(2,1)S(1)} %queries.1.refs_0_, bf16[1024,1536]{1,0:T(8,128)(2,1)} %copy-done.2, bf16[1024,1536]{1,0:T(8,128)(2,1)} %collective-permute-done.refs_2_.refs_4_, bf16[1024,1536]{1,0:T(8,128)(2,1)} %copy-done.2, ...), custom_call_target="tpu_custom_call" | custom-call | flops 600000000 | bytes 440401 | tf_op jit(solution)/shard_map/attend/pallas_call | solution.py:52
  105.2 35.2 %mlp.1 = (bf16[1024,768]{1,0:T(8,128)(2,1)}, bf16[1024,3072]{1,0:T(8,128)(2,1)}, bf16[1024,3072]{1,0:T(8,128)(2,1)}, bf16[1024,768]{1,0:T(8,128)(2,1)S(1)}, f32[...) custom-call(bf16[1024,768]{1,0:T(8,128)(2,1)} %bitcast.60, ...), custom_call_target="tpu_custom_call" | custom-call | flops 500000000 | bytes 748154 | tf_op jit(solution)/shard_map/mlp/pallas_call | solution.py:52
  143.2 12.5 %up_grad.1 = (bf16[8,48,3840]{2,1,0:T(8,128)(2,1)}, bf16[8,48,3840]{2,1,0:T(8,128)(2,1)}) custom-call(s32[1]{0:T(128)} %bitcast.9.refs_0_, bf16[1024,768]{1,0:T(8,128)(2,1)} %copy-done.12, bf16[1024,3072]{1,0:T(8,128)(2,1)} %get-tuple-element.78.refs_2_, bf16[1024,768]{1,0:T(8,128)(2,1)} %copy-done.11, bf16[1024,768]{1,0:T(8,128)(2,1)} %copy-done.13), custom_call_target="tpu_custom_call" | custom-call | flops 120000000 | bytes 338165 | tf_op jit(solution)/shard_map/up_grad/pallas_call | solution.py:52
  156.1 9.4 %down_grad.1 = (bf16[8,192,768]{2,1,0:T(8,128)(2,1)}, bf16[8,192,768]{2,1,0:T(8,128)(2,1)}) custom-call(s32[1]{0:T(128)} %bitcast.9.refs_0_, bf16[1024,3072]{1,0:T(8,128)(2,1)} %get-tuple-element.76.refs_1_, bf16[1024,768]{1,0:T(8,128)(2,1)} %bitcast.6.refs_3_.refs_2_, bf16[8,48,3840]{2,1,0:T(8,128)(2,1)} %get-tuple-element.80.refs_3_), custom_call_target="tpu_custom_call" | custom-call | flops 96000000 | bytes 251658 | tf_op jit(solution)/shard_map/down_grad/pallas_call | solution.py:52
  166.3 4.1 %collective-permute-done.1.refs_2_ = bf16[8,192,768]{2,1,0:T(8,128)(2,1)} collective-permute-done((bf16[8,192,768]{2,1,0:T(8,128)(2,1)}, bf16[8,192,768]{2,1,0:T(8,128)(2,1)}, u32[]{:S(2)}, u32[]{:S(2)}) %collective-permute-start.1) | collective-permute-done | bytes 2359328 | tf_op jit(solution)/shard_map/ppermute | solution.py:586
  172.0 7.2 %first_add.2 = (bf16[4,2,240,768]{3,2,1,0:T(8,128)(2,1)}, bf16[4,2,240,768]{3,2,1,0:T(8,128)(2,1)}) custom-call(s32[2]{0:T(128)} %pad_add_fusion.refs_0_, bf16[8,192,768]{2,1,0:T(8,128)(2,1)} %get-tuple-element.81.refs_1_, bf16[8,192,768]{2,1,0:T(8,128)(2,1)} %collective-permute-done.1.refs_2_, bf16[8,48,3840]{2,1,0:T(8,128)(2,1)} %get-tuple-element.83.refs_3_, ...), custom_call_target="tpu_custom_call" | custom-call | bytes 330301 | tf_op jit(solution)/shard_map/first_add/pallas_call | solution.py:52
  180.9 6.0 %all-to-all-start.2 = ((bf16[16,64,768]{2,1,0:T(8,128)(2,1)}), bf16[16,64,768]{2,1,0:T(8,128)(2,1)S(1)}, u32[]{:S(2)}, u32[]{:S(2)}) async-start(bf16[16,64,768]{2,1,0:T(8,128)(2,1)} %bitcast.8), calls=%async_computation.2 | async-start | bytes 3145728 | tf_op jit(solution)/shard_map/all_to_all | solution.py:782
  186.9 32.3 %attend_back.3 = (bf16[1024,384]{1,0:T(8,128)(2,1)}, bf16[1024,384]{1,0:T(8,128)(2,1)}, bf16[1024,384]{1,0:T(8,128)(2,1)}, bf16[1024,384]{1,0:T(8,128)(2,1)}, bf16[1024,384]{1,0:T(8,128)(2,1)}) custom-call(bf16[1024,768]{1,0:T(8,128)(2,1)} %copy-done.5, bf16[1024,1536]{1,0:T(8,128)(2,1)} %copy-done.2, ...), custom_call_target="tpu_custom_call" | custom-call | flops 660000000 | bytes 519045 | tf_op jit(solution)/shard_map/attend_back/pallas_call | solution.py:52
  219.2 10.2 %collective-permute-done.5.refs_2_ = bf16[4,2,240,768]{3,2,1,0:T(8,128)(2,1)} collective-permute-done((bf16[4,2,240,768]{3,2,1,0:T(8,128)(2,1)}, bf16[4,2,240,768]{3,2,1,0:T(8,128)(2,1)}, u32[]{:S(2)}, u32[]{:S(2)}) %collective-permute-start.5) | collective-permute-done | bytes 2949152 | tf_op jit(solution)/shard_map/ppermute | solution.py:594
  229.4 4.8 %second_add.2 = (bf16[4,240,768]{2,1,0:T(8,128)(2,1)}, bf16[4,240,768]{2,1,0:T(8,128)(2,1)}) custom-call(s32[1]{0:T(128)S(6)} %select_n.123.refs_0_, bf16[4,2,240,768]{3,2,1,0:T(8,128)(2,1)} %get-tuple-element.90.refs_1_, bf16[4,2,240,768]{3,2,1,0:T(8,128)(2,1)} %collective-permute-done.5.refs_2_, bf16[1024,384]{1,0:T(8,128)(2,1)} %get-tuple-element.85.refs_3_.refs_9_.refs_0_), custom_call_target="tpu_custom_call" | custom-call | bytes 176947 | tf_op jit(solution)/shard_map/second_add/pallas_call | solution.py:52
  235.9 22.4 %attend_back.4 = (bf16[1024,256]{1,0:T(8,128)(2,1)}, bf16[1024,256]{1,0:T(8,128)(2,1)}, bf16[1024,256]{1,0:T(8,128)(2,1)}, bf16[1024,256]{1,0:T(8,128)(2,1)}, bf16[1024,256]{1,0:T(8,128)(2,1)}) custom-call(bf16[1024,768]{1,0:T(8,128)(2,1)} %copy-done.5, bf16[1024,1536]{1,0:T(8,128)(2,1)} %copy-done.2, ...), custom_call_target="tpu_custom_call" | custom-call | flops 440000000 | bytes 492830 | tf_op jit(solution)/shard_map/attend_back/pallas_call | solution.py:52
  265.8 12.4 %attend_back.5 = (bf16[1024,128]{1,0:T(8,128)(2,1)}, bf16[1024,128]{1,0:T(8,128)(2,1)}, bf16[1024,128]{1,0:T(8,128)(2,1)}, bf16[1024,128]{1,0:T(8,128)(2,1)}, bf16[1024,128]{1,0:T(8,128)(2,1)}) custom-call(bf16[1024,768]{1,0:T(8,128)(2,1)} %copy-done.5, bf16[1024,1536]{1,0:T(8,128)(2,1)} %copy-done.2, ...), custom_call_target="tpu_custom_call" | custom-call | flops 220000000 | bytes 466616 | tf_op jit(solution)/shard_map/attend_back/pallas_call | solution.py:52
  285.8 11.4 %first_back.1 = (bf16[1024,768]{1,0:T(8,128)(2,1)}, bf16[1024,2304]{1,0:T(8,128)(2,1)}, f32[1,2,768]{2,1,0:T(2,128)}, f32[1,768]{1,0:T(1,128)}) custom-call(bf16[1024,384]{1,0:T(8,128)(2,1)} %get-tuple-element.85.refs_3_.refs_9_.refs_0_, bf16[1024,384]{1,0:T(8,128)(2,1)} %get-tuple-element.86.refs_1_, bf16[1024,384]{1,0:T(8,128)(2,1)} %get-tuple-element.87.refs_2_, ...), custom_call_target="tpu_custom_call" | custom-call | flops 72000000 | bytes 448573 | tf_op jit(solution)/shard_map/first_back/pallas_call | solution.py:52
  297.3 5.9 %all-to-all-start.3 = ((bf16[16,64,768]{2,1,0:T(8,128)(2,1)}), bf16[16,64,768]{2,1,0:T(8,128)(2,1)S(1)}, u32[]{:S(2)}, u32[]{:S(2)}) async-start(bf16[16,64,768]{2,1,0:T(8,128)(2,1)} %bitcast.64), calls=%async_computation.3 | async-start | bytes 3145728 | tf_op jit(solution)/shard_map/all_to_all | solution.py:782
  305.7 8.2 %qkv_grad.1 = (bf16[8,48,2304]{2,1,0:T(8,128)(2,1)}, bf16[8,48,2304]{2,1,0:T(8,128)(2,1)}) custom-call(s32[1]{0:T(128)} %bitcast.9.refs_0_, bf16[1024,768]{1,0:T(8,128)(2,1)} %copy-done.9, bf16[1024,2304]{1,0:T(8,128)(2,1)} %get-tuple-element.111.refs_2_, f32[11,8,48]{2,1,0:T(8,128)} %copy-done.35), custom_call_target="tpu_custom_call" | custom-call | flops 72000000 | bytes 196608 | tf_op jit(solution)/shard_map/qkv_grad/pallas_call | solution.py:52
  314.1 3.7 collective-permute-done.13.refs_2_
  319.1 4.3 %first_add.3 = (bf16[4,2,48,1152]{3,2,1,0:T(8,128)(2,1)}, bf16[4,2,48,1152]{3,2,1,0:T(8,128)(2,1)}) custom-call(s32[2]{0:T(128)} %pad_add_fusion.refs_0_, bf16[8,48,2304]{2,1,0:T(8,128)(2,1)} %get-tuple-element.112.refs_1_, bf16[8,48,2304]{2,1,0:T(8,128)(2,1)} %copy-done.23), custom_call_target="tpu_custom_call" | custom-call | bytes 106168 | tf_op jit(solution)/shard_map/first_add/pallas_call | solution.py:52
  327.8 27.9 %collective-permute-done.15 = bf16[1,240,768]{2,1,0:T(8,128)(2,1)S(1)} collective-permute-done((bf16[1,240,768]{2,1,0:T(8,128)(2,1)S(1)}, bf16[1,240,768]{2,1,0:T(8,128)(2,1)S(1)}, u32[]{:S(2)}, u32[]{:S(2)}) %collective-permute-start.15) | collective-permute-done | bytes 368672 | tf_op jit(solution)/shard_map/ppermute | solution.py:586
  362.1 7.0 %collective-permute-done.16.refs_2_ = bf16[4,48,1152]{2,1,0:T(8,128)(2,1)S(1)} collective-permute-done((bf16[4,48,1152]{2,1,0:T(8,128)(2,1)}, bf16[4,48,1152]{2,1,0:T(8,128)(2,1)S(1)}, u32[]{:S(2)}, u32[]{:S(2)}) %collective-permute-start.16) | collective-permute-done | bytes 442400 | tf_op jit(solution)/shard_map/ppermute | solution.py:594
  (223 shorter events, 92.2 us)
Async XLA Ops:
  4.4 45.2 %all-to-all-start = ((bf16[16,64,768]{2,1,0:T(8,128)(2,1)}), bf16[16,64,768]{2,1,0:T(8,128)(2,1)S(1)}, u32[]{:S(2)}, u32[]{:S(2)}) async-start(bf16[16,64,768]{2,1,0:T(8,128)(2,1)} %reshape.291), calls=%async_computation | async-start | bytes 3145728 | tf_op jit(solution)/shard_map/all_to_all | solution.py:770
  61.1 10.4 %collective-permute-start = (bf16[1024,1536]{1,0:T(8,128)(2,1)S(1)}, bf16[1024,1536]{1,0:T(8,128)(2,1)}, u32[]{:S(2)}, u32[]{:S(2)}) collective-permute-start(bf16[1024,1536]{1,0:T(8,128)(2,1)S(1)} %get-tuple-element.70.refs_1_.refs_3_), channel_id=1, source_target_pairs={{0,1},{1,0},{2,3},{3,2},{4,5},{5,4},{6,7},{7,6},{8,9},{9,8},{10,11... | collective-permute-start | bytes 9437192 | tf_op jit(solution)/shard_map/ppermute | solution.py:586
  61.2 44.0 %all-to-all-start.1 = ((bf16[16,64,768]{2,1,0:T(8,128)(2,1)}), bf16[16,64,768]{2,1,0:T(8,128)(2,1)}, u32[]{:S(2)}, u32[]{:S(2)}) async-start(bf16[16,64,768]{2,1,0:T(8,128)(2,1)} %reshape.294.refs_6_), calls=%async_computation.1 | async-start | bytes 3145728 | tf_op jit(solution)/shard_map/all_to_all | solution.py:770
  155.8 14.7 %collective-permute-start.2 = (bf16[8,48,3840]{2,1,0:T(8,128)(2,1)}, bf16[8,48,3840]{2,1,0:T(8,128)(2,1)S(1)}, u32[]{:S(2)}, u32[]{:S(2)}) collective-permute-start(bf16[8,48,3840]{2,1,0:T(8,128)(2,1)} %get-tuple-element.80.refs_3_), channel_id=1, source_target_pairs={{0,1},{1,0},{2,3},{3,2},{4,5},{5,4},{6,7},{7,6},{8,9},{9,8},{10,11... | collective-permute-start | bytes 8847368 | tf_op jit(solution)/shard_map/ppermute | solution.py:586
  179.2 50.2 %collective-permute-start.5 = (bf16[4,2,240,768]{3,2,1,0:T(8,128)(2,1)}, bf16[4,2,240,768]{3,2,1,0:T(8,128)(2,1)}, u32[]{:S(2)}, u32[]{:S(2)}) collective-permute-start(bf16[4,2,240,768]{3,2,1,0:T(8,128)(2,1)} %get-tuple-element.84.refs_8_), channel_id=1, source_target_pairs={{0,16},{1,3},{2,18},{3,1},{16,0},{17,19},{18,2},{19,17},{4,20},{5,... | collective-permute-start | bytes 8847368 | tf_op jit(solution)/shard_map/ppermute | solution.py:594
  180.9 83.7 %all-to-all-start.2 = ((bf16[16,64,768]{2,1,0:T(8,128)(2,1)}), bf16[16,64,768]{2,1,0:T(8,128)(2,1)S(1)}, u32[]{:S(2)}, u32[]{:S(2)}) async-start(bf16[16,64,768]{2,1,0:T(8,128)(2,1)} %bitcast.8), calls=%async_computation.2 | async-start | bytes 3145728 | tf_op jit(solution)/shard_map/all_to_all | solution.py:782
  234.2 24.1 %collective-permute-start.8 = (bf16[4,240,768]{2,1,0:T(8,128)(2,1)}, bf16[4,240,768]{2,1,0:T(8,128)(2,1)S(1)}, u32[]{:S(2)}, u32[]{:S(2)}) collective-permute-start(bf16[4,240,768]{2,1,0:T(8,128)(2,1)} %get-tuple-element.91.refs_8_), channel_id=1, source_target_pairs={{0,2},{1,17},{2,0},{3,19},{16,18},{17,1},{18,16},{19,3},{4,6},{5,2... | collective-permute-start | bytes 4423688 | tf_op jit(solution)/shard_map/ppermute | solution.py:594
  235.9 42.3 %collective-permute-start.3 = (bf16[1024,384]{1,0:T(8,128)(2,1)}, bf16[1024,384]{1,0:T(8,128)(2,1)}, u32[]{:S(2)}, u32[]{:S(2)}) collective-permute-start(bf16[1024,384]{1,0:T(8,128)(2,1)} %get-tuple-element.88), channel_id=1, source_target_pairs={{0,1},{1,0},{2,3},{3,2},{4,5},{5,4},{6,7},{7,6},{8,9},{9,8},{10,11... | collective-permute-start | bytes 2359304 | tf_op jit(solution)/shard_map/ppermute | solution.py:586
  262.4 19.2 %collective-permute-start.11 = (bf16[2,240,768]{2,1,0:T(8,128)(2,1)}, bf16[2,240,768]{2,1,0:T(8,128)(2,1)S(1)}, u32[]{:S(2)}, u32[]{:S(2)}) collective-permute-start(bf16[2,240,768]{2,1,0:T(8,128)(2,1)} %get-tuple-element.98.refs_8_), channel_id=1, source_target_pairs={{0,4},{4,0},{8,12},{12,8},{1,5},{5,1},{9,13},{13,9},{2,6},{6,2},{1... | collective-permute-start | bytes 2211848 | tf_op jit(solution)/shard_map/ppermute | solution.py:586
  263.9 20.8 %collective-permute-start.4 = (bf16[1024,384]{1,0:T(8,128)(2,1)}, bf16[1024,384]{1,0:T(8,128)(2,1)S(1)}, u32[]{:S(2)}, u32[]{:S(2)}) collective-permute-start(bf16[1024,384]{1,0:T(8,128)(2,1)} %get-tuple-element.89), channel_id=1, source_target_pairs={{0,1},{1,0},{2,3},{3,2},{4,5},{5,4},{6,7},{7,6},{8,9},{9,8},{10,11... | collective-permute-start | bytes 2359304 | tf_op jit(solution)/shard_map/ppermute | solution.py:586
  264.2 20.6 %collective-permute-start.6 = (bf16[1024,256]{1,0:T(8,128)(2,1)}, bf16[1024,256]{1,0:T(8,128)(2,1)}, u32[]{:S(2)}, u32[]{:S(2)}) collective-permute-start(bf16[1024,256]{1,0:T(8,128)(2,1)} %get-tuple-element.95), channel_id=1, source_target_pairs={{0,1},{1,0},{2,3},{3,2},{4,5},{5,4},{6,7},{7,6},{8,9},{9,8},{10,11... | collective-permute-start | bytes 1572872 | tf_op jit(solution)/shard_map/ppermute | solution.py:586
  264.4 20.3 %collective-permute-start.7 = (bf16[1024,256]{1,0:T(8,128)(2,1)}, bf16[1024,256]{1,0:T(8,128)(2,1)}, u32[]{:S(2)}, u32[]{:S(2)}) collective-permute-start(bf16[1024,256]{1,0:T(8,128)(2,1)} %get-tuple-element.96), channel_id=1, source_target_pairs={{0,1},{1,0},{2,3},{3,2},{4,5},{5,4},{6,7},{7,6},{8,9},{9,8},{10,11... | collective-permute-start | bytes 1572872 | tf_op jit(solution)/shard_map/ppermute | solution.py:586
  297.3 58.4 %all-to-all-start.3 = ((bf16[16,64,768]{2,1,0:T(8,128)(2,1)}), bf16[16,64,768]{2,1,0:T(8,128)(2,1)S(1)}, u32[]{:S(2)}, u32[]{:S(2)}) async-start(bf16[16,64,768]{2,1,0:T(8,128)(2,1)} %bitcast.64), calls=%async_computation.3 | async-start | bytes 3145728 | tf_op jit(solution)/shard_map/all_to_all | solution.py:782
  323.4 32.3 %collective-permute-start.14 = (bf16[4,2,48,1152]{3,2,1,0:T(8,128)(2,1)}, bf16[4,2,48,1152]{3,2,1,0:T(8,128)(2,1)}, u32[]{:S(2)}, u32[]{:S(2)}) collective-permute-start(bf16[4,2,48,1152]{3,2,1,0:T(8,128)(2,1)} %get-tuple-element.115), channel_id=1, source_target_pairs={{0,16},{1,3},{2,18},{3,1},{16,0},{17,19},{18,2},{19,17},{4,20},{5,... | collective-permute-start | bytes 2654216 | tf_op jit(solution)/shard_map/ppermute | solution.py:594
  325.4 30.3 %collective-permute-start.15 = (bf16[1,240,768]{2,1,0:T(8,128)(2,1)S(1)}, bf16[1,240,768]{2,1,0:T(8,128)(2,1)S(1)}, u32[]{:S(2)}, u32[]{:S(2)}) collective-permute-start(bf16[1,240,768]{2,1,0:T(8,128)(2,1)S(1)} %copy-done.32), channel_id=1, source_target_pairs={{0,8},{4,12},{8,0},{12,4},{1,9},{5,13},{9,1},{13,5},{2,10},{6,14},... | collective-permute-start | bytes 1105928 | tf_op jit(solution)/shard_map/ppermute | solution.py:586
  360.6 8.5 %collective-permute-start.16 = (bf16[4,48,1152]{2,1,0:T(8,128)(2,1)}, bf16[4,48,1152]{2,1,0:T(8,128)(2,1)S(1)}, u32[]{:S(2)}, u32[]{:S(2)}) collective-permute-start(bf16[4,48,1152]{2,1,0:T(8,128)(2,1)} %get-tuple-element.117), channel_id=1, source_target_pairs={{0,2},{1,17},{2,0},{3,19},{16,18},{17,1},{18,16},{19,3},{4,6},{5,2... | collective-permute-start | bytes 1327112 | tf_op jit(solution)/shard_map/ppermute | solution.py:594
  372.8 10.1 %collective-permute-start.17 = (f32[1,11,384]{2,1,0:T(8,128)S(1)}, f32[1,11,384]{2,1,0:T(8,128)S(1)}, u32[]{:S(2)}, u32[]{:S(2)}) collective-permute-start(f32[1,11,384]{2,1,0:T(8,128)S(1)} %reshape.307), channel_id=1, source_target_pairs={{0,2},{2,0},{1,3},{3,1},{4,6},{6,4},{5,7},{7,5},{8,10},{10,8},{9,1... | collective-permute-start | bytes 50696 | tf_op jit(solution)/shard_map/ppermute | solution.py:586
  379.0 10.2 %collective-permute-start.22 = (bf16[48,1152]{1,0:T(8,128)(2,1)S(1)}, bf16[48,1152]{1,0:T(8,128)(2,1)S(1)}, u32[]{:S(2)}, u32[]{:S(2)}) collective-permute-start(bf16[48,1152]{1,0:T(8,128)(2,1)S(1)} %copy-done.53), channel_id=1, source_target_pairs={{0,4},{4,8},{8,12},{12,0},{1,5},{5,9},{9,13},{13,1},{2,6},{6,10},{... | collective-permute-start | bytes 331784 | tf_op jit(solution)/shard_map/ppermute | solution.py:722
  379.0 13.0 %collective-permute-start.23 = (bf16[48,1152]{1,0:T(8,128)(2,1)S(1)}, bf16[48,1152]{1,0:T(8,128)(2,1)S(1)}, u32[]{:S(2)}, u32[]{:S(2)}) collective-permute-start(bf16[48,1152]{1,0:T(8,128)(2,1)S(1)} %copy-done.52), channel_id=1, source_target_pairs={{0,8},{4,12},{8,0},{12,4},{1,9},{5,13},{9,1},{13,5},{2,10},{6,14},... | collective-permute-start | bytes 331784 | tf_op jit(solution)/shard_map/ppermute | solution.py:722
  381.0 12.6 %collective-permute-start.24 = (bf16[48,1152]{1,0:T(8,128)(2,1)S(1)}, bf16[48,1152]{1,0:T(8,128)(2,1)S(1)}, u32[]{:S(2)}, u32[]{:S(2)}) collective-permute-start(bf16[48,1152]{1,0:T(8,128)(2,1)S(1)} %copy-done.51), channel_id=1, source_target_pairs={{0,12},{4,0},{8,4},{12,8},{1,13},{5,1},{9,5},{13,9},{2,14},{6,2},{... | collective-permute-start | bytes 331784 | tf_op jit(solution)/shard_map/ppermute | solution.py:722
  387.1 9.5 %collective-permute-start.19 = (f32[4,11,384]{2,1,0:T(8,128)S(1)}, f32[4,11,384]{2,1,0:T(8,128)S(1)}, u32[]{:S(2)}, u32[]{:S(2)}) collective-permute-start(f32[4,11,384]{2,1,0:T(8,128)S(1)} %maximum_select_fusion.1), channel_id=1, source_target_pairs={{0,4},{4,8},{8,12},{12,0},{1,5},{5,9},{9,13},{13,1},{2,6},{6,10},{... | collective-permute-start | bytes 202760 | tf_op jit(solution)/shard_map/ppermute | solution.py:722
  387.6 9.6 %collective-permute-start.20 = (f32[4,11,384]{2,1,0:T(8,128)S(1)}, f32[4,11,384]{2,1,0:T(8,128)S(1)}, u32[]{:S(2)}, u32[]{:S(2)}) collective-permute-start(f32[4,11,384]{2,1,0:T(8,128)S(1)} %maximum_select_fusion.1), channel_id=1, source_target_pairs={{0,8},{4,12},{8,0},{12,4},{1,9},{5,13},{9,1},{13,5},{2,10},{6,14},... | collective-permute-start | bytes 202760 | tf_op jit(solution)/shard_map/ppermute | solution.py:722
  389.2 8.1 %collective-permute-start.21 = (f32[4,11,384]{2,1,0:T(8,128)S(1)}, f32[4,11,384]{2,1,0:T(8,128)S(1)}, u32[]{:S(2)}, u32[]{:S(2)}) collective-permute-start(f32[4,11,384]{2,1,0:T(8,128)S(1)} %maximum_select_fusion.1), channel_id=1, source_target_pairs={{0,12},{4,0},{8,4},{12,8},{1,13},{5,1},{9,5},{13,9},{2,14},{6,2},{... | collective-permute-start | bytes 202760 | tf_op jit(solution)/shard_map/ppermute | solution.py:722
  392.1 10.3 %collective-permute-start.26 = (bf16[240,768]{1,0:T(8,128)(2,1)}, bf16[240,768]{1,0:T(8,128)(2,1)S(1)}, u32[]{:S(2)}, u32[]{:S(2)}) collective-permute-start(bf16[240,768]{1,0:T(8,128)(2,1)} %last_add.3), channel_id=1, source_target_pairs={{0,16},{16,0},{1,17},{17,1},{2,18},{18,2},{3,19},{19,3},{4,20},{20... | collective-permute-start | bytes 1105928 | tf_op jit(solution)/shard_map/ppermute | solution.py:586
  (62 other events, 305.1 us)

commit v4 on v3

--- a/solution.py
+++ b/solution.py
@@ -21,11 +21,13 @@
 SMALLEST = 2.0**-90
 VM_ATTEND = 48
 VM_BACK = 56
-VM_MLP = 48
+VM_MLP = 62
 VM_SUM = 56
+VM_QKV = 32
 COST = 50
 DOWN_TILE = 768
-MLP_BLOCK = 256
+MLP_BLOCK = 512
+MLP_SPLIT = 1
 
 
 def mm(a, b, dims=NN):
@@ -213,56 +215,41 @@
 SMALL = pl.BlockSpec(memory_space=pltpu.SMEM)
 
 
-def key_kernel(x_ref, chan_ref, shift_ref, gain_ref, wk, wv, h_ref, kv_ref):
+def qkv_kernel(x_ref, chan_ref, shift_ref, gain_ref, w, h_ref, kv_ref, q_ref):
     width = x_ref.shape[1]
     normed, inverse = normed_of(x_ref[...].astype(F32) + chan_ref[0])
     hidden = (normed * gain_ref[...] + shift_ref[0]).astype(BF)
     h_ref[...] = hidden
-    kv_ref[:, :width] = mm(hidden, wk[...]).astype(BF)
-    kv_ref[:, width:] = mm(hidden, wv[...]).astype(BF)
-
-
-def keys_of(x, chan_add, shift, gain, weight, frames, deps):
+    kv_ref[...] = mm(hidden, w[:, width:]).astype(BF)
+    q_ref[...] = (mm(hidden, w[:, :width]) * (SCALING * LOG2E)).astype(BF)
+
+
+def qkv_of(x, chan_add, shift, gain, weight, frames, deps):
     count, width = x.shape
     block = 256
     per = count // frames // block
     frame = pl.BlockSpec((1, 1, width), lambda i: (i // per, 0, 0))
-    return call(
-        key_kernel,
-        "keys",
+    narrow = rows_of(block, width)
+    return call(
+        qkv_kernel,
+        "qkv",
         (count // block,),
         [
-            (x, rows_of(block, width)),
+            (x, narrow),
             (chan_add, frame),
             (shift, frame),
             (gain, whole_of((1, width))),
-            (weight, pl.BlockSpec((width, width), lambda i: (0, 1))),
-            (weight, pl.BlockSpec((width, width), lambda i: (0, 2))),
+            (weight, whole_of(weight.shape)),
         ],
         [
-            (sds((count, width), BF), rows_of(block, width)),
+            (sds((count, width), BF), narrow),
             (sds((count, 2 * width), BF), rows_of(block, 2 * width)),
+            (sds((count, width), BF), narrow),
         ],
-        flops=2_400_000_000,
+        flops=3_600_000_000,
         deps=deps,
-    )
-
-
-def query_kernel(h_ref, w, q_ref):
-    q_ref[...] = (mm(h_ref[...], w[...]) * (SCALING * LOG2E)).astype(BF)
-
-
-def queries_of(hidden, weight):
-    count, width = hidden.shape
-    block = 256
-    return call(
-        query_kernel,
-        "queries",
-        (count // block,),
-        [(hidden, rows_of(block, width)), (weight, pl.BlockSpec((width, width), lambda i: (0, 0)))],
-        [(sds((count, width), BF), rows_of(block, width))],
-        flops=1_200_000_000,
-    )[0]
+        vmem=VM_QKV,
+    )
 
 
 ROOT = math.sqrt(2 / math.pi)
@@ -302,7 +289,6 @@
 ):
     step = pl.program_id(0)
     width = x_ref.shape[1]
-    chunks = wu.shape[1] // width
     copies = [
         pltpu.make_async_copy(wo_any, wo, sems.at[0]),
         pltpu.make_async_copy(wu_any, wu, sems.at[1]),
@@ -330,17 +316,30 @@
 
     result = middle + down_bias
     grad_hidden = None
-    for c in range(chunks):
-        cols = pl.ds(c * width, width)
-        act, slope = gelu_both(mm(hidden, wu[:, cols]) + up_bias_ref[:, cols])
+    part = width // MLP_SPLIT
+    spans = [pl.ds(i * part, part) for i in range(wu.shape[1] // part)]
+
+    def products(cols):
+        return mm(hidden, wu[:, cols]), mm(g, wd[cols, :], NT)
+
+    ready = products(spans[0])
+    for i, cols in enumerate(spans):
+        pre, back = ready
+        if i + 1 < len(spans):
+            ready = products(spans[i + 1])
+        act, slope = gelu_both(pre + up_bias_ref[:, cols])
         act = act.astype(BF)
         act_ref[:, cols] = act
-        grad_pre = (mm(g, wd[cols, :], NT) * slope).astype(BF)
+        grad_pre = (back * slope).astype(BF)
         gpre_ref[:, cols] = grad_pre
-        sums_ref[4 + c : 5 + c] += jnp.sum(grad_pre.astype(F32), axis=0, keepdims=True)
+        at = i % MLP_SPLIT * part
+        row = 4 + i // MLP_SPLIT
+        sums_ref[row : row + 1, at : at + part] += jnp.sum(
+            grad_pre.astype(F32), axis=0, keepdims=True
+        )
         result = result + mm(act, wd[cols, :])
-        part = mm(grad_pre, wu[:, cols], NT)
-        grad_hidden = part if grad_hidden is None else grad_hidden + part
+        term = mm(grad_pre, wu[:, cols], NT)
+        grad_hidden = term if grad_hidden is None else grad_hidden + term
     res_ref[...] = result.astype(BF)
     g = g.astype(F32)
     sums_ref[0:1] += jnp.sum(g, axis=0, keepdims=True)
@@ -473,34 +472,61 @@
     )
 
 
-def qkv_grad_kernel(core_ref, hid_ref, grad_ref, send_ref, keep_ref, turned, scr):
+def fill_part(out, pieces, part):
+    at = 0
+    for dq, dk0, dv0, got_k, got_v in pieces:
+        size = dq.shape[1]
+        if part == 0:
+            out[:, at : at + size] = dq[...]
+        elif part == 1:
+            out[:, at : at + size] = dk0[...] + got_k[...]
+        else:
+            out[:, at : at + size] = dv0[...] + got_v[...]
+        at += size
+
+
+def groups_of(refs):
+    return [refs[i : i + 5] for i in range(0, len(refs), 5)]
+
+
+def qkv_grad_kernel(core_ref, hid_ref, *refs):
+    pieces = groups_of(refs[:-5])
+    send_ref, keep_ref, turned, grad, scr = refs[-5:]
     core = core_ref[0]
-
-    @pl.when(pl.program_id(0) == 0)
+    step = pl.program_id(0)
+
+    @pl.when(step == 0)
     def _():
         turned[...] = hid_ref[...].T
 
-    scr[...] = mm(turned[...], grad_ref[...]).reshape(scr.shape)
+    for part in range(3):
+
+        @pl.when(step == part)
+        def _():
+            fill_part(grad, pieces, part)
+
+    scr[...] = mm(turned[...], grad[...]).reshape(scr.shape)
     keep_ref[...] = scr[:, core].astype(BF)
     send_ref[...] = scr[:, 1 - core].astype(BF)
 
 
-def qkv_grad(core, hidden, grad, lon, deps):
+def qkv_grad(core, hidden, pieces, lon, deps):
     count, width = hidden.shape
     share = width // lon
-    out = sds((lon // 2, share, grad.shape[1]), BF)
+    out = sds((lon // 2, share, 3 * width), BF)
     spec = pl.BlockSpec((lon // 2, share, width), lambda i: (0, 0, i))
     return call(
         qkv_grad_kernel,
         "qkv_grad",
-        (grad.shape[1] // width,),
+        (3,),
+        [(core, SMALL), (hidden, whole_of((count, width)))]
+        + [(a, whole_of(a.shape)) for group in pieces for a in group],
+        [(out, spec), (out, spec)],
         [
-            (core, SMALL),
-            (hidden, whole_of((count, width))),
-            (grad, pl.BlockSpec((count, width), lambda i: (0, i))),
+            pltpu.VMEM((width, count), BF),
+            pltpu.VMEM((count, width), BF),
+            pltpu.VMEM((lon // 2, 2, share, width), F32),
         ],
-        [(out, spec), (out, spec)],
-        [pltpu.VMEM((width, count), BF), pltpu.VMEM((lon // 2, 2, share, width), F32)],
         3_600_000_000,
         deps,
         VM_SUM,
@@ -509,18 +535,12 @@
 
 def first_back_kernel_of(groups, frame_blocks):
     def kernel(*refs):
-        ins = refs[: 5 * groups]
-        x_ref, chan_ref, gain_ref, mid_ref, w, patch_ref, qkv_ref, frame_ref, gain_sum = refs[5 * groups :]
+        pieces = groups_of(refs[: 5 * groups])
+        x_ref, chan_ref, gain_ref, mid_ref, w, patch_ref, frame_ref, gain_sum, qkv_ref = refs[5 * groups :]
         step = pl.program_id(0)
         width = x_ref.shape[1]
-        at = 0
-        for c in range(groups):
-            dq, dk0, dv0, got_k, got_v = ins[5 * c : 5 * c + 5]
-            size = dq.shape[1]
-            qkv_ref[:, pl.ds(at, size)] = dq[...]
-            qkv_ref[:, pl.ds(width + at, size)] = dk0[...] + got_k[...]
-            qkv_ref[:, pl.ds(2 * width + at, size)] = dv0[...] + got_v[...]
-            at += size
+        for part in range(3):
+            fill_part(qkv_ref.at[:, part * width : (part + 1) * width], pieces, part)
         grad_hidden = mm(qkv_ref[...], w[...], NT)
         normed, inverse = normed_of(x_ref[...].astype(F32) + chan_ref[0])
         grad_start = mid_ref[...] + norm_back(grad_hidden * gain_ref[...], normed, inverse)
@@ -560,13 +580,13 @@
         ],
         [
             (sds((count, width), BF), rows_of(block, width)),
-            (sds((count, 3 * width), BF), rows_of(block, 3 * width)),
             (sds((frames, 2, width), F32), pl.BlockSpec((1, 2, width), lambda i: (i // per, 0, 0))),
             (sds((1, width), F32), whole_of((1, width))),
         ],
-        flops=3_600_000_000,
-        deps=deps,
-        vmem=VM_SUM,
+        [pltpu.VMEM((block, 3 * width), BF)],
+        3_600_000_000,
+        deps,
+        VM_SUM,
     )
 
 
@@ -594,6 +614,9 @@
     return lax.ppermute(value, ("lat", "yy", "core"), pairs)
 
 
+EVERY = slice(None)
+
+
 def both(kept_ref, got_ref, *at):
     return (kept_ref[at].astype(F32) + got_ref[at].astype(F32)).astype(BF)
 
@@ -607,15 +630,15 @@
     @pl.when(half == 0)
     def _():
         out[0, at, :rows] = both(kept_d, got_d, yy)
-        out[0, at, rows:] = both(kept_u, got_u, yy, slice(None), slice(wide, None))
+        out[0, at, rows:] = both(kept_u, got_u, yy, slice(0, share // 2), slice(wide, None))
 
     @pl.when(half == 1)
     def _():
         for c in range(wide // width):
             out[0, at, c * share : (c + 1) * share] = both(
-                kept_u, got_u, yy, slice(None), slice(c * width, (c + 1) * width)
+                kept_u, got_u, yy, EVERY, slice(c * width, (c + 1) * width)
             )
-        out[0, at, rows:] = jnp.zeros((share, width), BF)
+        out[0, at, rows:] = both(kept_u, got_u, yy, slice(share // 2, None), slice(wide, None))
 
 
 def qkv_part(ins, out, at, yy, half):
@@ -741,6 +764,26 @@
         deps=deps,
         vmem=VM_SUM,
     )[0]
+
+
+def add_and_pass(kept, got, passed):
+    rows, cols = kept.shape
+
+    def kernel(kept_ref, got_ref, passed_ref, out_ref, same_ref):
+        out_ref[...] = both(kept_ref, got_ref, Ellipsis)
+
+    spec = whole_of((rows, cols))
+    anywhere = pl.BlockSpec(memory_space=pl.ANY)
+    return pl.pallas_call(
+        kernel,
+        grid=(1,),
+        in_specs=[spec, spec, anywhere],
+        out_specs=[spec, anywhere],
+        out_shape=[sds((rows, cols), BF), sds(passed.shape, passed.dtype)],
+        input_output_aliases={2: 1},
+        compiler_params=pltpu.CompilerParams(vmem_limit_bytes=VM_SUM << 20),
+        name="add_and_pass",
+    )(kept, got, passed)
 
 
 def halves_of(mine):
@@ -825,9 +868,8 @@
     gain1 = norm1_gain.astype(F32)[None]
     rows2 = jnp.stack([out_bias, norm2_gain, norm2_bias, down_bias]).astype(F32)
 
-    hidden1, kv_own = keys_of(x, chan_add, shift1, gain1, qkv_weight, frames, (flat,))
+    hidden1, kv_own, queries = qkv_of(x, chan_add, shift1, gain1, qkv_weight, frames, (flat,))
     kv_peer = swap(kv_own, "core", 0)
-    queries = queries_of(hidden1, qkv_weight)
     attended, attended32, lse = attend(queries, kv_own, kv_peer, frames)
 
     result, activ, grad_pre, hidden2, grad_middle, grad_branch, grad_att, early = mlp(
@@ -849,7 +891,7 @@
     down_got = swap(down_send, "core", 0)
 
     staged = lat == 2
-    rows = down_kept.shape[1] + share
+    rows = down_kept.shape[1] + share // 2
     pieces, pair = [], 0
     deps = (down_kept,)
     if staged:
@@ -882,9 +924,11 @@
             got = swap(sent, "zed", bit)
             deps = (sent,)
         mlp_parts = [kept[0], got[0]]
-    grad_start, grad_qkv, frame_sums, gain_sum = first_back(
+    grad_start, frame_sums, gain_sum = first_back(
         pieces, x, chan_add, gain1, grad_middle, qkv_weight, frames, deps
     )
+    if staged:
+        mlp_sum, grad_start = add_and_pass(*mlp_parts, grad_start)
     grad_patch = to_places(grad_start, chips, frames_all)
 
     ups = wide // width
@@ -898,7 +942,7 @@
     late = lax.dynamic_index_in_dim(late, mine, 2, keepdims=False) + late_got
 
     deps = (late_got,)
-    qkv_send, qkv_kept = qkv_grad(core, hidden1, grad_qkv, lon, deps)
+    qkv_send, qkv_kept = qkv_grad(core, hidden1, pieces, lon, deps)
     qkv_got = swap(qkv_send, "core", 0)
 
     zed = lax.axis_size("zed")
@@ -906,13 +950,16 @@
     if staged:
         sent, kept = first_add(qkv_part, [qkv_kept, qkv_got], share, 3 * width // 2)
         got = cross(sent, 0)
-        sent, kept = second_add(kept, got, (grad_patch, mlp_parts[1]))
+        sent, kept = second_add(kept, got, (grad_patch,))
         got = cross(sent, 1)
         parts = third_add(kept, got)
-        late = held(late, (parts[0],))
+        late = held(late.reshape(late.shape[0], -1), (sent,))
+        deps = (parts[0],)
         parts = [parts[0]] + [up_zed(part, up) for up, part in enumerate(parts) if up]
-        halves = halves_of(last_add(mlp_parts, (parts[0],)))
-        sum_down, sum_out = halves[0][: rows - share], halves[0][rows - share :]
+        halves = halves_of(held(mlp_sum, (parts[0],)))
+        tall = wide // lon
+        sum_down = halves[0][:tall]
+        sum_out = jnp.concatenate([half[tall:] for half in halves], 0)
         sum_up = jnp.concatenate(
             [halves[1][c * share : (c + 1) * share] for c in range(wide // width)], 1
         )
@@ -931,6 +978,8 @@
             late = jnp.where(
                 high, jnp.concatenate([other, late], 0), jnp.concatenate([late, other], 0)
             )
+    if staged:
+        late = held(late, deps)
     late = jnp.stack([late] + [up_zed(late, up) for up in range(1, zed)])
     late = jnp.take(late, (lax.axis_index("zed") - jnp.arange(zed)) % zed, axis=0)
     late = lax.dynamic_slice_in_dim(late, lax.axis_index(("zed", "yy")) * share, share, 3)

time: 409 us -> 401 us (0.980)
  waiting for transfers between devices: 94.3 us -> 84.3 us
    ppermute x17, waiting for transfers between devices: 42.6 us -> 25.3 us  [swap(): return lax.ppermute(value, axis, swap_pairs(lax.axis_size(axis), bit))]
    ppermute x4, waiting for transfers between devices: 17.2 us -> 23.8 us  [cross(): return lax.ppermute(value, ('lat', 'yy', 'core'), pairs)]
    unnamed x110 -> x100, local copies, waits for them, and re-layouts: 26.9 us -> 25.7 us
  transfers between devices with their start and end apart: 31 -> 31, of which waited for: 10 -> 14; matrix products, arithmetic and copies ran while one was open for 3% -> 4% of each run, Pallas kernels for 34% -> 36%
where the time goes in v4:
time: 401 us; the launch traced here: 397 us
  Pallas kernels  214 us (53%)
  waiting for transfers between devices  84.3 us (21%)
  starting transfers between devices  49.8 us (12%)
  local copies, waits for them, and re-layouts  37.4 us (9%)
  other arithmetic  6.93 us (2%)
    pallas_call x21, Pallas kernels, call(): pl.pallas_call(body, grid=grid, in_specs=[spec for a, spec in ins] + [any...  212 us
    all_to_all x2, waiting for transfers between devices, to_frames(): value = lax.all_to_all(value, ('lat', 'zed', 'yy'), 0, 0, tiled=True)  35.2 us
    unnamed x100, local copies, waits for them, and re-layouts  25.7 us
    ppermute x17, waiting for transfers between devices, swap(): return lax.ppermute(value, axis, swap_pairs(lax.axis_size(axis), bit))  25.3 us
    ppermute x4, waiting for transfers between devices, cross(): return lax.ppermute(value, ('lat', 'yy', 'core'), pairs)  23.8 us
    all_to_all x2, starting transfers between devices, to_frames(): value = lax.all_to_all(value, ('lat', 'zed', 'yy'), 0, 0, tiled=True)  13.2 us
    ppermute x17, starting transfers between devices, swap(): return lax.ppermute(value, axis, swap_pairs(lax.axis_size(axis), bit))  10.8 us
    all_to_all x2, starting transfers between devices, to_places(): return lax.all_to_all(value, ('lat', 'zed', 'yy'), 0, 0, tiled=True)  10.2 us
  transfers between devices with their start and end apart: 31, of which 14 were waited for; matrix products, arithmetic and copies ran while one was open for 4% of the time, Pallas kernels for 36%

profile of v4, /device:TPU:0, one launch (start us, length us, event | category | flops | bytes accessed | tf_op | source)
XLA Modules:
  0.0 396.7 jit_solution(7379997672688416850)
XLA Ops:
  0.7 3.8 reshape.185
  4.4 8.5 %all-to-all-start = ((bf16[16,64,768]{2,1,0:T(8,128)(2,1)}), bf16[16,64,768]{2,1,0:T(8,128)(2,1)S(1)}, u32[]{:S(2)}, u32[]{:S(2)}) async-start(bf16[16,64,768]{2,1,0:T(8,128)(2,1)} %reshape.185), calls=%async_computation | async-start | bytes 3145728 | tf_op jit(solution)/shard_map/all_to_all | solution.py:813
  15.9 33.7 %all-to-all-done = bf16[16,64,768]{2,1,0:T(8,128)(2,1)S(1)} async-done(((bf16[16,64,768]{2,1,0:T(8,128)(2,1)}), bf16[16,64,768]{2,1,0:T(8,128)(2,1)S(1)}, u32[]{:S(2)}, u32[]{:S(2)}) %all-to-all-start) | async-done | bytes 1572896 | tf_op jit(solution)/shard_map/all_to_all | solution.py:813
  55.6 5.3 %qkv.1 = (bf16[1024,768]{1,0:T(8,128)(2,1)S(1)}, bf16[1024,1536]{1,0:T(8,128)(2,1)S(1)}, bf16[1024,768]{1,0:T(8,128)(2,1)S(1)}) custom-call(bf16[1024,768]{1,0:T(8,128)(2,1)S(1)} %bitcast.61, f32[1,1,768]{2,1,0:T(1,128)S(1)} %convolution_bitcast_fusion.1.refs_1_.refs_16_, f32[1,1,768]{2,1,0:T(1,128)S(1)} %broadcast_in_dim.32.refs_2_, ...), custom_call_target="tpu_custom_call" | custom-call | flops 72000000 | bytes 228249 | tf_op jit(solution)/shard_map/qkv/pallas_call | solution.py:54
  65.4 4.7 %all-to-all-start.1 = ((bf16[16,64,768]{2,1,0:T(8,128)(2,1)}), bf16[16,64,768]{2,1,0:T(8,128)(2,1)}, u32[]{:S(2)}, u32[]{:S(2)}) async-start(bf16[16,64,768]{2,1,0:T(8,128)(2,1)} %reshape.188.refs_5_), calls=%async_computation.1 | async-start | bytes 3145728 | tf_op jit(solution)/shard_map/all_to_all | solution.py:813
  72.8 31.2 %attend.1 = (bf16[1024,768]{1,0:T(8,128)(2,1)S(1)}, f32[1024,768]{1,0:T(8,128)}, f32[1024,768]{1,0:T(8,128)}) custom-call(bf16[1024,768]{1,0:T(8,128)(2,1)S(1)} %copy-done.4, bf16[1024,1536]{1,0:T(8,128)(2,1)} %copy-done.2, bf16[1024,1536]{1,0:T(8,128)(2,1)} %collective-permute-done.refs_2_.refs_4_, bf16[1024,1536]{1,0:T(8,128)(2,1)} %copy-done.2, ...), custom_call_target="tpu_custom_call" | custom-call | flops 600000000 | bytes 440401 | tf_op jit(solution)/shard_map/attend/pallas_call | solution.py:54
  106.6 37.3 %mlp.1 = (bf16[1024,768]{1,0:T(8,128)(2,1)}, bf16[1024,3072]{1,0:T(8,128)(2,1)}, bf16[1024,3072]{1,0:T(8,128)(2,1)}, bf16[1024,768]{1,0:T(8,128)(2,1)}, f32[1024...) custom-call(bf16[1024,768]{1,0:T(8,128)(2,1)} %bitcast.59, ...), custom_call_target="tpu_custom_call" | custom-call | flops 500000000 | bytes 748154 | tf_op jit(solution)/shard_map/mlp/pallas_call | solution.py:54
  143.9 12.5 %up_grad.1 = (bf16[8,48,3840]{2,1,0:T(8,128)(2,1)}, bf16[8,48,3840]{2,1,0:T(8,128)(2,1)}) custom-call(s32[1]{0:T(128)} %bitcast.11.refs_0_, bf16[1024,768]{1,0:T(8,128)(2,1)} %get-tuple-element.76.refs_1_, bf16[1024,3072]{1,0:T(8,128)(2,1)} %get-tuple-element.77.refs_2_, bf16[1024,768]{1,0:T(8,128)(2,1)} %copy-done.9, ...), custom_call_target="tpu_custom_call" | custom-call | flops 120000000 | bytes 338165 | tf_op jit(solution)/shard_map/up_grad/pallas_call | solution.py:54
  156.4 9.4 %down_grad.1 = (bf16[8,192,768]{2,1,0:T(8,128)(2,1)}, bf16[8,192,768]{2,1,0:T(8,128)(2,1)}) custom-call(s32[1]{0:T(128)} %bitcast.11.refs_0_, bf16[1024,3072]{1,0:T(8,128)(2,1)} %get-tuple-element.75.refs_1_, bf16[1024,768]{1,0:T(8,128)(2,1)} %bitcast.6.refs_3_.refs_2_, bf16[8,48,3840]{2,1,0:T(8,128)(2,1)} %get-tuple-element.79.refs_3_), custom_call_target="tpu_custom_call" | custom-call | flops 96000000 | bytes 251658 | tf_op jit(solution)/shard_map/down_grad/pallas_call | solution.py:54
  166.9 3.9 collective-permute-done.1.refs_2_
  172.4 7.1 %first_add.2 = (bf16[4,2,216,768]{3,2,1,0:T(8,128)(2,1)}, bf16[4,2,216,768]{3,2,1,0:T(8,128)(2,1)}) custom-call(s32[2]{0:T(128)} %pad_add_fusion.refs_0_, bf16[8,192,768]{2,1,0:T(8,128)(2,1)} %get-tuple-element.80.refs_1_, bf16[8,192,768]{2,1,0:T(8,128)(2,1)} %collective-permute-done.1.refs_2_, bf16[8,48,3840]{2,1,0:T(8,128)(2,1)} %get-tuple-element.82.refs_3_, ...), custom_call_target="tpu_custom_call" | custom-call | bytes 318505 | tf_op jit(solution)/shard_map/first_add/pallas_call | solution.py:54
  180.9 4.6 %all-to-all-start.2 = ((bf16[16,64,768]{2,1,0:T(8,128)(2,1)}), bf16[16,64,768]{2,1,0:T(8,128)(2,1)S(1)}, u32[]{:S(2)}, u32[]{:S(2)}) async-start(bf16[16,64,768]{2,1,0:T(8,128)(2,1)} %bitcast.66), calls=%async_computation.2 | async-start | bytes 3145728 | tf_op jit(solution)/shard_map/all_to_all | solution.py:825
  185.6 32.3 %attend_back.3 = (bf16[1024,384]{1,0:T(8,128)(2,1)}, bf16[1024,384]{1,0:T(8,128)(2,1)}, bf16[1024,384]{1,0:T(8,128)(2,1)}, bf16[1024,384]{1,0:T(8,128)(2,1)}, bf16[1024,384]{1,0:T(8,128)(2,1)}) custom-call(bf16[1024,768]{1,0:T(8,128)(2,1)} %copy-done.3, bf16[1024,1536]{1,0:T(8,128)(2,1)} %copy-done.2, ...), custom_call_target="tpu_custom_call" | custom-call | flops 660000000 | bytes 519045 | tf_op jit(solution)/shard_map/attend_back/pallas_call | solution.py:54
  217.8 8.7 %collective-permute-done.3.refs_2_ = bf16[4,2,216,768]{3,2,1,0:T(8,128)(2,1)} collective-permute-done((bf16[4,2,216,768]{3,2,1,0:T(8,128)(2,1)}, bf16[4,2,216,768]{3,2,1,0:T(8,128)(2,1)}, u32[]{:S(2)}, u32[]{:S(2)}) %collective-permute-start.3) | collective-permute-done | bytes 2654240 | tf_op jit(solution)/shard_map/ppermute | solution.py:614
  226.5 4.6 %second_add.2 = (bf16[4,216,768]{2,1,0:T(8,128)(2,1)}, bf16[4,216,768]{2,1,0:T(8,128)(2,1)}) custom-call(s32[1]{0:T(128)S(6)} %select_n.102.refs_0_, bf16[4,2,216,768]{3,2,1,0:T(8,128)(2,1)} %get-tuple-element.83.refs_1_, bf16[4,2,216,768]{3,2,1,0:T(8,128)(2,1)} %collective-permute-done.3.refs_2_, ...), custom_call_target="tpu_custom_call" | custom-call | bytes 159252 | tf_op jit(solution)/shard_map/second_add/pallas_call | solution.py:54
  232.2 22.5 %attend_back.4 = (bf16[1024,256]{1,0:T(8,128)(2,1)}, bf16[1024,256]{1,0:T(8,128)(2,1)}, bf16[1024,256]{1,0:T(8,128)(2,1)}, bf16[1024,256]{1,0:T(8,128)(2,1)}, bf16[1024,256]{1,0:T(8,128)(2,1)}) custom-call(bf16[1024,768]{1,0:T(8,128)(2,1)} %copy-done.3, bf16[1024,1536]{1,0:T(8,128)(2,1)} %copy-done.2, ...), custom_call_target="tpu_custom_call" | custom-call | flops 440000000 | bytes 492830 | tf_op jit(solution)/shard_map/attend_back/pallas_call | solution.py:54
  261.1 12.4 %attend_back.5 = (bf16[1024,128]{1,0:T(8,128)(2,1)}, bf16[1024,128]{1,0:T(8,128)(2,1)}, bf16[1024,128]{1,0:T(8,128)(2,1)}, bf16[1024,128]{1,0:T(8,128)(2,1)}, bf16[1024,128]{1,0:T(8,128)(2,1)}) custom-call(bf16[1024,768]{1,0:T(8,128)(2,1)} %copy-done.3, bf16[1024,1536]{1,0:T(8,128)(2,1)} %copy-done.2, ...), custom_call_target="tpu_custom_call" | custom-call | flops 220000000 | bytes 466616 | tf_op jit(solution)/shard_map/attend_back/pallas_call | solution.py:54
  282.2 10.6 %first_back.1 = (bf16[1024,768]{1,0:T(8,128)(2,1)}, f32[1,2,768]{2,1,0:T(2,128)}, f32[1,768]{1,0:T(1,128)}) custom-call(bf16[1024,384]{1,0:T(8,128)(2,1)} %get-tuple-element.88.refs_3_.refs_9_.refs_0_.refs_2_, bf16[1024,384]{1,0:T(8,128)(2,1)} %get-tuple-element.97.refs_1_.refs_3_, bf16[1024,384]{1,0:T(8,128)(2,1)} %get-tuple-element.98.refs_2_.refs_4_, ...), custom_call_target="tpu_custom_call" | custom-call | flops 72000000 | bytes 354201 | tf_op jit(solution)/shard_map/first_back/pallas_call | solution.py:54
  297.2 5.5 %all-to-all-start.3 = ((bf16[16,64,768]{2,1,0:T(8,128)(2,1)}), bf16[16,64,768]{2,1,0:T(8,128)(2,1)S(1)}, u32[]{:S(2)}, u32[]{:S(2)}) async-start(bf16[16,64,768]{2,1,0:T(8,128)(2,1)} %bitcast.65), calls=%async_computation.3 | async-start | bytes 3145728 | tf_op jit(solution)/shard_map/all_to_all | solution.py:825
  305.3 10.3 %qkv_grad.1 = (bf16[8,48,2304]{2,1,0:T(8,128)(2,1)}, bf16[8,48,2304]{2,1,0:T(8,128)(2,1)}) custom-call(s32[1]{0:T(128)} %bitcast.11.refs_0_, bf16[1024,768]{1,0:T(8,128)(2,1)} %copy-done.10, bf16[1024,384]{1,0:T(8,128)(2,1)} %get-tuple-element.88.refs_3_.refs_9_.refs_0_.refs_2_, bf16[1024,384]{1,0:T(8,128)(2,1)} %get-tuple-element.97.refs_1_.refs_3_, ...), custom_call_target="tpu_custom_call" | custom-call | flops 72000000 | bytes 259522 | tf_op jit(solution)/shard_map/qkv_grad/pallas_call | solution.py:54
  320.7 4.2 %first_add.3 = (bf16[4,2,48,1152]{3,2,1,0:T(8,128)(2,1)}, bf16[4,2,48,1152]{3,2,1,0:T(8,128)(2,1)}) custom-call(s32[2]{0:T(128)} %pad_add_fusion.refs_0_, bf16[8,48,2304]{2,1,0:T(8,128)(2,1)} %get-tuple-element.116.refs_1_, bf16[8,48,2304]{2,1,0:T(8,128)(2,1)} %copy-done.23), custom_call_target="tpu_custom_call" | custom-call | bytes 106168 | tf_op jit(solution)/shard_map/first_add/pallas_call | solution.py:54
  327.1 15.2 %collective-permute-done.15.refs_2_ = bf16[4,2,48,1152]{3,2,1,0:T(8,128)(2,1)S(1)} collective-permute-done((bf16[4,2,48,1152]{3,2,1,0:T(8,128)(2,1)}, bf16[4,2,48,1152]{3,2,1,0:T(8,128)(2,1)S(1)}, u32[]{:S(2)}, u32[]{:S(2)}) %collective-permute-start.15) | collective-permute-done | bytes 884768 | tf_op jit(solution)/shard_map/ppermute | solution.py:614
  351.1 6.0 %collective-permute-done.16 = f32[1,11,384]{2,1,0:T(8,128)S(1)} collective-permute-done((f32[1,11,384]{2,1,0:T(8,128)S(1)}, f32[1,11,384]{2,1,0:T(8,128)S(1)}, u32[]{:S(2)}, u32[]{:S(2)}) %collective-permute-start.16) | collective-permute-done | bytes 16928 | tf_op jit(solution)/shard_map/ppermute | solution.py:606
  375.5 4.0 collective-permute-start.24
  (214 shorter events, 97.1 us)
Async XLA Ops:
  4.4 45.2 %all-to-all-start = ((bf16[16,64,768]{2,1,0:T(8,128)(2,1)}), bf16[16,64,768]{2,1,0:T(8,128)(2,1)S(1)}, u32[]{:S(2)}, u32[]{:S(2)}) async-start(bf16[16,64,768]{2,1,0:T(8,128)(2,1)} %reshape.185), calls=%async_computation | async-start | bytes 3145728 | tf_op jit(solution)/shard_map/all_to_all | solution.py:813
  63.8 7.6 %collective-permute-start = (bf16[1024,1536]{1,0:T(8,128)(2,1)S(1)}, bf16[1024,1536]{1,0:T(8,128)(2,1)}, u32[]{:S(2)}, u32[]{:S(2)}) collective-permute-start(bf16[1024,1536]{1,0:T(8,128)(2,1)S(1)} %get-tuple-element.72.refs_1_.refs_3_), channel_id=1, source_target_pairs={{0,1},{1,0},{2,3},{3,2},{4,5},{5,4},{6,7},{7,6},{8,9},{9,8},{10,11... | collective-permute-start | bytes 9437192 | tf_op jit(solution)/shard_map/ppermute | solution.py:606
  65.4 41.2 %all-to-all-start.1 = ((bf16[16,64,768]{2,1,0:T(8,128)(2,1)}), bf16[16,64,768]{2,1,0:T(8,128)(2,1)}, u32[]{:S(2)}, u32[]{:S(2)}) async-start(bf16[16,64,768]{2,1,0:T(8,128)(2,1)} %reshape.188.refs_5_), calls=%async_computation.1 | async-start | bytes 3145728 | tf_op jit(solution)/shard_map/all_to_all | solution.py:813
  156.4 14.4 %collective-permute-start.2 = (bf16[8,48,3840]{2,1,0:T(8,128)(2,1)}, bf16[8,48,3840]{2,1,0:T(8,128)(2,1)S(1)}, u32[]{:S(2)}, u32[]{:S(2)}) collective-permute-start(bf16[8,48,3840]{2,1,0:T(8,128)(2,1)} %get-tuple-element.79.refs_3_), channel_id=1, source_target_pairs={{0,1},{1,0},{2,3},{3,2},{4,5},{5,4},{6,7},{7,6},{8,9},{9,8},{10,11... | collective-permute-start | bytes 8847368 | tf_op jit(solution)/shard_map/ppermute | solution.py:606
  179.5 47.1 %collective-permute-start.3 = (bf16[4,2,216,768]{3,2,1,0:T(8,128)(2,1)}, bf16[4,2,216,768]{3,2,1,0:T(8,128)(2,1)}, u32[]{:S(2)}, u32[]{:S(2)}) collective-permute-start(bf16[4,2,216,768]{3,2,1,0:T(8,128)(2,1)} %get-tuple-element.84.refs_8_), channel_id=1, source_target_pairs={{0,16},{1,3},{2,18},{3,1},{16,0},{17,19},{18,2},{19,17},{4,20},{5,... | collective-permute-start | bytes 7962632 | tf_op jit(solution)/shard_map/ppermute | solution.py:614
  180.9 79.1 %all-to-all-start.2 = ((bf16[16,64,768]{2,1,0:T(8,128)(2,1)}), bf16[16,64,768]{2,1,0:T(8,128)(2,1)S(1)}, u32[]{:S(2)}, u32[]{:S(2)}) async-start(bf16[16,64,768]{2,1,0:T(8,128)(2,1)} %bitcast.66), calls=%async_computation.2 | async-start | bytes 3145728 | tf_op jit(solution)/shard_map/all_to_all | solution.py:825
  231.1 23.6 %collective-permute-start.4 = (bf16[4,216,768]{2,1,0:T(8,128)(2,1)}, bf16[4,216,768]{2,1,0:T(8,128)(2,1)}, u32[]{:S(2)}, u32[]{:S(2)}) collective-permute-start(bf16[4,216,768]{2,1,0:T(8,128)(2,1)} %get-tuple-element.90.refs_8_), channel_id=1, source_target_pairs={{0,2},{1,17},{2,0},{3,19},{16,18},{17,1},{18,16},{19,3},{4,6},{5,2... | collective-permute-start | bytes 3981320 | tf_op jit(solution)/shard_map/ppermute | solution.py:614
  231.7 47.8 %collective-permute-start.7 = (bf16[1024,384]{1,0:T(8,128)(2,1)}, bf16[1024,384]{1,0:T(8,128)(2,1)S(1)}, u32[]{:S(2)}, u32[]{:S(2)}) collective-permute-start(bf16[1024,384]{1,0:T(8,128)(2,1)} %get-tuple-element.99), channel_id=1, source_target_pairs={{0,1},{1,0},{2,3},{3,2},{4,5},{5,4},{6,7},{7,6},{8,9},{9,8},{10,11... | collective-permute-start | bytes 2359304 | tf_op jit(solution)/shard_map/ppermute | solution.py:606
  231.8 47.7 %collective-permute-start.8 = (bf16[1024,384]{1,0:T(8,128)(2,1)}, bf16[1024,384]{1,0:T(8,128)(2,1)S(1)}, u32[]{:S(2)}, u32[]{:S(2)}) collective-permute-start(bf16[1024,384]{1,0:T(8,128)(2,1)} %get-tuple-element.100), channel_id=1, source_target_pairs={{0,1},{1,0},{2,3},{3,2},{4,5},{5,4},{6,7},{7,6},{8,9},{9,8},{10,11... | collective-permute-start | bytes 2359304 | tf_op jit(solution)/shard_map/ppermute | solution.py:606
  257.8 17.4 %collective-permute-start.5 = (bf16[2,216,768]{2,1,0:T(8,128)(2,1)}, bf16[2,216,768]{2,1,0:T(8,128)(2,1)}, u32[]{:S(2)}, u32[]{:S(2)}) collective-permute-start(bf16[2,216,768]{2,1,0:T(8,128)(2,1)} %get-tuple-element.93.refs_8_), channel_id=1, source_target_pairs={{0,4},{4,0},{8,12},{12,8},{1,5},{5,1},{9,13},{13,9},{2,6},{6,2},{1... | collective-permute-start | bytes 1990664 | tf_op jit(solution)/shard_map/ppermute | solution.py:606
  259.5 20.7 %collective-permute-start.10 = (bf16[1024,256]{1,0:T(8,128)(2,1)}, bf16[1024,256]{1,0:T(8,128)(2,1)}, u32[]{:S(2)}, u32[]{:S(2)}) collective-permute-start(bf16[1024,256]{1,0:T(8,128)(2,1)} %get-tuple-element.104), channel_id=1, source_target_pairs={{0,1},{1,0},{2,3},{3,2},{4,5},{5,4},{6,7},{7,6},{8,9},{9,8},{10,11... | collective-permute-start | bytes 1572872 | tf_op jit(solution)/shard_map/ppermute | solution.py:606
  259.5 20.7 %collective-permute-start.9 = (bf16[1024,256]{1,0:T(8,128)(2,1)}, bf16[1024,256]{1,0:T(8,128)(2,1)}, u32[]{:S(2)}, u32[]{:S(2)}) collective-permute-start(bf16[1024,256]{1,0:T(8,128)(2,1)} %get-tuple-element.103), channel_id=1, source_target_pairs={{0,1},{1,0},{2,3},{3,2},{4,5},{5,4},{6,7},{7,6},{8,9},{9,8},{10,11... | collective-permute-start | bytes 1572872 | tf_op jit(solution)/shard_map/ppermute | solution.py:606
  277.3 17.2 %collective-permute-start.6 = (bf16[1,216,768]{2,1,0:T(8,128)(2,1)}, bf16[1,216,768]{2,1,0:T(8,128)(2,1)S(1)}, u32[]{:S(2)}, u32[]{:S(2)}) collective-permute-start(bf16[1,216,768]{2,1,0:T(8,128)(2,1)} %get-tuple-element.96.refs_20_), channel_id=1, source_target_pairs={{0,8},{4,12},{8,0},{12,4},{1,9},{5,13},{9,1},{13,5},{2,10},{6,14},... | collective-permute-start | bytes 995336 | tf_op jit(solution)/shard_map/ppermute | solution.py:606
  297.2 45.1 %all-to-all-start.3 = ((bf16[16,64,768]{2,1,0:T(8,128)(2,1)}), bf16[16,64,768]{2,1,0:T(8,128)(2,1)S(1)}, u32[]{:S(2)}, u32[]{:S(2)}) async-start(bf16[16,64,768]{2,1,0:T(8,128)(2,1)} %bitcast.65), calls=%async_computation.3 | async-start | bytes 3145728 | tf_op jit(solution)/shard_map/all_to_all | solution.py:825
  325.0 17.3 %collective-permute-start.15 = (bf16[4,2,48,1152]{3,2,1,0:T(8,128)(2,1)}, bf16[4,2,48,1152]{3,2,1,0:T(8,128)(2,1)S(1)}, u32[]{:S(2)}, u32[]{:S(2)}) collective-permute-start(bf16[4,2,48,1152]{3,2,1,0:T(8,128)(2,1)} %get-tuple-element.119), channel_id=1, source_target_pairs={{0,16},{1,3},{2,18},{3,1},{16,0},{17,19},{18,2},{19,17},{4,20},{5,... | collective-permute-start | bytes 2654216 | tf_op jit(solution)/shard_map/ppermute | solution.py:614
  348.0 13.2 %collective-permute-start.18 = (bf16[4,48,1152]{2,1,0:T(8,128)(2,1)}, bf16[4,48,1152]{2,1,0:T(8,128)(2,1)S(1)}, u32[]{:S(2)}, u32[]{:S(2)}) collective-permute-start(bf16[4,48,1152]{2,1,0:T(8,128)(2,1)} %get-tuple-element.120.refs_1_), channel_id=1, source_target_pairs={{0,2},{1,17},{2,0},{3,19},{16,18},{17,1},{18,16},{19,3},{4,6},{5,2... | collective-permute-start | bytes 1327112 | tf_op jit(solution)/shard_map/ppermute | solution.py:614
  350.9 6.1 %collective-permute-start.16 = (f32[1,11,384]{2,1,0:T(8,128)S(1)}, f32[1,11,384]{2,1,0:T(8,128)S(1)}, u32[]{:S(2)}, u32[]{:S(2)}) collective-permute-start(f32[1,11,384]{2,1,0:T(8,128)S(1)} %bitcast.63), channel_id=1, source_target_pairs={{0,2},{2,0},{1,3},{3,1},{4,6},{6,4},{5,7},{7,5},{8,10},{10,8},{9,1... | collective-permute-start | bytes 50696 | tf_op jit(solution)/shard_map/ppermute | solution.py:606
  364.8 9.4 %collective-permute-start.19 = (f32[4,11,384]{2,1,0:T(8,128)S(1)}, f32[4,11,384]{2,1,0:T(8,128)S(1)}, u32[]{:S(2)}, u32[]{:S(2)}) collective-permute-start(f32[4,11,384]{2,1,0:T(8,128)S(1)} %held.4), channel_id=1, source_target_pairs={{0,4},{4,8},{8,12},{12,0},{1,5},{5,9},{9,13},{13,1},{2,6},{6,10},{... | collective-permute-start | bytes 202760 | tf_op jit(solution)/shard_map/ppermute | solution.py:745
  365.0 10.6 %collective-permute-start.20 = (f32[4,11,384]{2,1,0:T(8,128)S(1)}, f32[4,11,384]{2,1,0:T(8,128)}, u32[]{:S(2)}, u32[]{:S(2)}) collective-permute-start(f32[4,11,384]{2,1,0:T(8,128)S(1)} %held.4), channel_id=1, source_target_pairs={{0,8},{4,12},{8,0},{12,4},{1,9},{5,13},{9,1},{13,5},{2,10},{6,14},... | collective-permute-start | bytes 202760 | tf_op jit(solution)/shard_map/ppermute | solution.py:745
  367.4 12.0 %collective-permute-start.21 = (f32[4,11,384]{2,1,0:T(8,128)S(1)}, f32[4,11,384]{2,1,0:T(8,128)}, u32[]{:S(2)}, u32[]{:S(2)}) collective-permute-start(f32[4,11,384]{2,1,0:T(8,128)S(1)} %held.4), channel_id=1, source_target_pairs={{0,12},{4,0},{8,4},{12,8},{1,13},{5,1},{9,5},{13,9},{2,14},{6,2},{... | collective-permute-start | bytes 202760 | tf_op jit(solution)/shard_map/ppermute | solution.py:745
  372.1 21.8 %collective-permute-start.26 = (bf16[216,768]{1,0:T(8,128)(2,1)S(1)}, bf16[216,768]{1,0:T(8,128)(2,1)S(1)}, u32[]{:S(2)}, u32[]{:S(2)}) collective-permute-start(bf16[216,768]{1,0:T(8,128)(2,1)S(1)} %held.5), channel_id=1, source_target_pairs={{0,16},{16,0},{1,17},{17,1},{2,18},{18,2},{3,19},{19,3},{4,20},{20... | collective-permute-start | bytes 995336 | tf_op jit(solution)/shard_map/ppermute | solution.py:606
  373.7 10.5 %collective-permute-start.22 = (bf16[48,1152]{1,0:T(8,128)(2,1)}, bf16[48,1152]{1,0:T(8,128)(2,1)S(1)}, u32[]{:S(2)}, u32[]{:S(2)}) collective-permute-start(bf16[48,1152]{1,0:T(8,128)(2,1)} %get-tuple-element.123), channel_id=1, source_target_pairs={{0,4},{4,8},{8,12},{12,0},{1,5},{5,9},{9,13},{13,1},{2,6},{6,10},{... | collective-permute-start | bytes 331784 | tf_op jit(solution)/shard_map/ppermute | solution.py:745
  374.2 9.9 %collective-permute-start.23 = (bf16[48,1152]{1,0:T(8,128)(2,1)}, bf16[48,1152]{1,0:T(8,128)(2,1)S(1)}, u32[]{:S(2)}, u32[]{:S(2)}) collective-permute-start(bf16[48,1152]{1,0:T(8,128)(2,1)} %get-tuple-element.124), channel_id=1, source_target_pairs={{0,8},{4,12},{8,0},{12,4},{1,9},{5,13},{9,1},{13,5},{2,10},{6,14},... | collective-permute-start | bytes 331784 | tf_op jit(solution)/shard_map/ppermute | solution.py:745
  375.5 8.7 %collective-permute-start.24 = (bf16[48,1152]{1,0:T(8,128)(2,1)}, bf16[48,1152]{1,0:T(8,128)(2,1)S(1)}, u32[]{:S(2)}, u32[]{:S(2)}) collective-permute-start(bf16[48,1152]{1,0:T(8,128)(2,1)} %get-tuple-element.125), channel_id=1, source_target_pairs={{0,12},{4,0},{8,4},{12,8},{1,13},{5,1},{9,5},{13,9},{2,14},{6,2},{... | collective-permute-start | bytes 331784 | tf_op jit(solution)/shard_map/ppermute | solution.py:745
  (57 other events, 251.1 us)

commit v5 on v4

--- a/solution.py
+++ b/solution.py
@@ -19,14 +19,14 @@
 TN = (((0,), (0,)), ((), ()))
 KEY_CHUNK = 512
 SMALLEST = 2.0**-90
-VM_ATTEND = 48
-VM_BACK = 56
+VM_ATTEND = 62
+VM_BACK = 62
 VM_MLP = 62
-VM_SUM = 56
-VM_QKV = 32
+VM_SUM = 62
+VM_QKV = 62
 COST = 50
 DOWN_TILE = 768
-MLP_BLOCK = 512
+MLP_BLOCK = 256
 MLP_SPLIT = 1
 
 
@@ -96,10 +96,10 @@
                 probs = jnp.exp2(mm(k[i : i + chunk], qm, NT) - top)
                 part = jnp.sum(probs, axis=0, keepdims=True)
                 total = part if total is None else total + part
-                part = mm(values[64 * head : 64 * head + 64, i : i + chunk], probs.astype(BF))
+                part = mm(values[:, i : i + chunk], probs.astype(BF))
                 out = part if out is None else out + part
         lse = jnp.broadcast_to(top + jnp.log2(total), (64, count))
-        return out / total, lse, jnp.min(total)
+        return out[64 * head : 64 * head + 64] / total, lse, jnp.min(total)
 
     def run(exact):
         first, second = one_head(0, exact), one_head(1, exact)
@@ -159,8 +159,8 @@
                 lanes = slice(64 * head, 64 * head + 64)
                 probs = jnp.exp2(mm(qms[head], keys, NT) - lses[head])
                 ds = (probs * (mm(goms[head], vals, NT) - deltas[head])).astype(BF)
-                dva[part, lanes, i : i + chunk] = mm(turned_go[lanes], probs.astype(BF))
-                dka[part, lanes, i : i + chunk] = mm(turned_q[lanes], ds)
+                dva[part, lanes, i : i + chunk] = mm(turned_go, probs.astype(BF))[lanes]
+                dka[part, lanes, i : i + chunk] = mm(turned_q, ds)[lanes]
                 term = mm(ds, of_head(keys, head))
                 dq = term if dq is None else dq + term
     dq_ref[...] = (dq * SCALING).astype(BF)
@@ -786,10 +786,54 @@
     )(kept, got, passed)
 
 
-def halves_of(mine):
-    other = swap(mine, "lat", 0)
-    high = lax.axis_index("lat") == 1
-    return jnp.where(high, other, mine).astype(F32), jnp.where(high, mine, other).astype(F32)
+def spread(mine, other, shapes, fill, deps=()):
+    def kernel(high_ref, mine_ref, other_ref, *outs):
+        @pl.when(high_ref[0] == 0)
+        def _():
+            fill(mine_ref, other_ref, outs)
+
+        @pl.when(high_ref[0] == 1)
+        def _():
+            fill(other_ref, mine_ref, outs)
+
+    spec = whole_of(mine.shape)
+    return call(
+        kernel,
+        "spread",
+        (1,),
+        [(my_bit("lat", 0), SMALL), (mine, spec), (other, spec)],
+        [(sds(shape, F32), whole_of(shape)) for shape in shapes],
+        deps=deps,
+        vmem=VM_SUM,
+    )
+
+
+def fill_qkv(low, high, outs):
+    cols = low.shape[1]
+    outs[0][:, :cols] = low[...].astype(F32)
+    outs[0][:, cols:] = high[...].astype(F32)
+
+
+def fill_mlp(low, high, outs):
+    down, up, out = outs
+    tall, share, width = down.shape[0], up.shape[0], down.shape[1]
+    down[...] = low[:tall].astype(F32)
+    for c in range(up.shape[1] // width):
+        up[:, c * width : (c + 1) * width] = high[c * share : (c + 1) * share].astype(F32)
+    out[: share // 2] = low[tall:].astype(F32)
+    out[share // 2 :] = high[tall:].astype(F32)
+
+
+def beside(value):
+    value = value[None]
+    for axis in ("yy", "lat"):
+        for bit in range(bits_of(lax.axis_size(axis))):
+            other = swap(value, axis, bit)
+            high = my_bit(axis, bit)[0] == 1
+            value = jnp.where(
+                high, jnp.concatenate([other, value], 0), jnp.concatenate([value, other], 0)
+            )
+    return value
 
 
 def held(value, deps):
@@ -950,36 +994,27 @@
     if staged:
         sent, kept = first_add(qkv_part, [qkv_kept, qkv_got], share, 3 * width // 2)
         got = cross(sent, 0)
-        sent, kept = second_add(kept, got, (grad_patch,))
+        late = beside(held(late.reshape(late.shape[0], -1), (sent,)))
+        sent, kept = second_add(kept, got, (grad_patch, late))
         got = cross(sent, 1)
         parts = third_add(kept, got)
-        late = held(late.reshape(late.shape[0], -1), (sent,))
         deps = (parts[0],)
         parts = [parts[0]] + [up_zed(part, up) for up, part in enumerate(parts) if up]
-        halves = halves_of(held(mlp_sum, (parts[0],)))
+        mlp_sum = held(mlp_sum, deps)
+        late = held(late, deps)
         tall = wide // lon
-        sum_down = halves[0][:tall]
-        sum_out = jnp.concatenate([half[tall:] for half in halves], 0)
-        sum_up = jnp.concatenate(
-            [halves[1][c * share : (c + 1) * share] for c in range(wide // width)], 1
+        sum_down, sum_up, sum_out = spread(
+            mlp_sum, swap(mlp_sum, "lat", 0), [(tall, width), (share, wide), (share, width)], fill_mlp
         )
-        sum_qkv = jnp.concatenate(halves_of(last_add(parts)), 1)
+        total = last_add(parts)
+        sum_qkv = spread(total, swap(total, "lat", 0), [(share, 3 * width)], fill_qkv)[0]
     else:
         sum_down = plain_sum(down_kept, down_got)
         sum_up = plain_sum(up_kept, up_got)
         sum_up, sum_out = sum_up[:, :wide], sum_up[:, wide:]
         sum_qkv = plain_sum(qkv_kept, qkv_got)
-
-    late = late.reshape(1, late.shape[0], -1)
-    for axis in ("yy", "lat"):
-        for bit in range(bits_of(lax.axis_size(axis))):
-            other = swap(late, axis, bit)
-            high = my_bit(axis, bit)[0] == 1
-            late = jnp.where(
-                high, jnp.concatenate([other, late], 0), jnp.concatenate([late, other], 0)
-            )
-    if staged:
-        late = held(late, deps)
+        late = beside(late.reshape(late.shape[0], -1))
+
     late = jnp.stack([late] + [up_zed(late, up) for up in range(1, zed)])
     late = jnp.take(late, (lax.axis_index("zed") - jnp.arange(zed)) % zed, axis=0)
     late = lax.dynamic_slice_in_dim(late, lax.axis_index(("zed", "yy")) * share, share, 3)

time: 401 us -> 393 us (0.980)
  local copies, waits for them, and re-layouts: 37.4 us -> 29.3 us
    unnamed x100 -> x84, local copies, waits for them, and re-layouts: 25.7 us -> 12.4 us
    ppermute x17, waiting for transfers between devices: 25.3 us -> 32.1 us  [swap(): return lax.ppermute(value, axis, swap_pairs(lax.axis_size(axis), bit))]
    ppermute x4, waiting for transfers between devices: 23.8 us -> 18 us  [cross(): return lax.ppermute(value, ('lat', 'yy', 'core'), pairs)]
    pallas_call x21 -> x23, Pallas kernels: 212 us -> 215 us  [call(): pl.pallas_call(body, grid=grid, in_specs=[spec for a, spec in ins] + [any...]
  transfers between devices with their start and end apart: 31 -> 31, of which waited for: 14 -> 16; matrix products, arithmetic and copies ran while one was open for 4% -> 5% of each run, Pallas kernels for 36% -> 36%
where the time goes in v5:
time: 393 us; the launch traced here: 389 us
  Pallas kernels  217 us (55%)
  waiting for transfers between devices  88.1 us (22%)
  starting transfers between devices  46.5 us (12%)
  local copies, waits for them, and re-layouts  29.3 us (7%)
    pallas_call x23, Pallas kernels, call(): pl.pallas_call(body, grid=grid, in_specs=[spec for a, spec in ins] + [any...  215 us
    all_to_all x2, waiting for transfers between devices, to_frames(): value = lax.all_to_all(value, ('lat', 'zed', 'yy'), 0, 0, tiled=True)  34.9 us
    ppermute x17, waiting for transfers between devices, swap(): return lax.ppermute(value, axis, swap_pairs(lax.axis_size(axis), bit))  32.1 us
    ppermute x4, waiting for transfers between devices, cross(): return lax.ppermute(value, ('lat', 'yy', 'core'), pairs)  18 us
    all_to_all x2, starting transfers between devices, to_frames(): value = lax.all_to_all(value, ('lat', 'zed', 'yy'), 0, 0, tiled=True)  12.5 us
    unnamed x84, local copies, waits for them, and re-layouts  12.4 us
    ppermute x17, starting transfers between devices, swap(): return lax.ppermute(value, axis, swap_pairs(lax.axis_size(axis), bit))  10.8 us
    ppermute x6, starting transfers between devices, up_zed(): return lax.ppermute(value, 'zed', [(i, (i + up) % zed) for i in range(zed)])  8.81 us
  transfers between devices with their start and end apart: 31, of which 16 were waited for; matrix products, arithmetic and copies ran while one was open for 5% of the time, Pallas kernels for 36%

profile of v5, /device:TPU:0, one launch (start us, length us, event | category | flops | bytes accessed | tf_op | source)
XLA Modules:
  0.0 388.7 jit_solution(1811829741765605182)
XLA Ops:
  4.4 8.5 %all-to-all-start = ((bf16[16,64,768]{2,1,0:T(8,128)(2,1)}), bf16[16,64,768]{2,1,0:T(8,128)(2,1)S(1)}, u32[]{:S(2)}, u32[]{:S(2)}) async-start(bf16[16,64,768]{2,1,0:T(8,128)(2,1)} %reshape.184), calls=%async_computation | async-start | bytes 3145728 | tf_op jit(solution)/shard_map/all_to_all | solution.py:857
  19.9 29.6 %all-to-all-done = bf16[16,64,768]{2,1,0:T(8,128)(2,1)S(1)} async-done(((bf16[16,64,768]{2,1,0:T(8,128)(2,1)}), bf16[16,64,768]{2,1,0:T(8,128)(2,1)S(1)}, u32[]{:S(2)}, u32[]{:S(2)}) %all-to-all-start) | async-done | bytes 1572896 | tf_op jit(solution)/shard_map/all_to_all | solution.py:857
  50.7 8.3 %qkv.1 = (bf16[1024,768]{1,0:T(8,128)(2,1)}, bf16[1024,1536]{1,0:T(8,128)(2,1)}, bf16[1024,768]{1,0:T(8,128)(2,1)}) custom-call(bf16[1024,768]{1,0:T(8,128)(2,1)} %bitcast.62, f32[1,1,768]{2,1,0:T(1,128)} %convolution_bitcast_fusion.1.refs_1_.refs_16_, f32[1,1,768]{2,1,0:T(1,128)} %broadcast_in_dim.35.refs_2_, f32[1,768]{1,0:T(1,128)} %reshape.206.refs_3_.refs_17_, ...), custom_call_target="tpu_custom_call" | custom-call | flops 72000000 | bytes 228249 | tf_op jit(solution)/shard_map/qkv/pallas_call | solution.py:54
  59.1 4.1 %all-to-all-start.1 = ((bf16[16,64,768]{2,1,0:T(8,128)(2,1)}), bf16[16,64,768]{2,1,0:T(8,128)(2,1)S(1)}, u32[]{:S(2)}, u32[]{:S(2)}) async-start(bf16[16,64,768]{2,1,0:T(8,128)(2,1)} %reshape.187.refs_5_), calls=%async_computation.1 | async-start | bytes 3145728 | tf_op jit(solution)/shard_map/all_to_all | solution.py:857
  65.1 29.9 %attend.1 = (bf16[1024,768]{1,0:T(8,128)(2,1)}, f32[1024,768]{1,0:T(8,128)}, f32[1024,768]{1,0:T(8,128)}) custom-call(bf16[1024,768]{1,0:T(8,128)(2,1)} %get-tuple-element.74.refs_0_, bf16[1024,1536]{1,0:T(8,128)(2,1)} %get-tuple-element.75.refs_1_.refs_3_, bf16[1024,1536]{1,0:T(8,128)(2,1)} %collective-permute-done.refs_2_.refs_4_, ...), custom_call_target="tpu_custom_call" | custom-call | flops 600000000 | bytes 440401 | tf_op jit(solution)/shard_map/attend/pallas_call | solution.py:54
  95.0 5.2 %all-to-all-done.1 = bf16[16,64,768]{2,1,0:T(8,128)(2,1)S(1)} async-done(((bf16[16,64,768]{2,1,0:T(8,128)(2,1)}), bf16[16,64,768]{2,1,0:T(8,128)(2,1)S(1)}, u32[]{:S(2)}, u32[]{:S(2)}) %all-to-all-start.1) | async-done | bytes 1572896 | tf_op jit(solution)/shard_map/all_to_all | solution.py:857
  101.4 37.7 %mlp.1 = (bf16[1024,768]{1,0:T(8,128)(2,1)}, bf16[1024,3072]{1,0:T(8,128)(2,1)}, bf16[1024,3072]{1,0:T(8,128)(2,1)}, bf16[1024,768]{1,0:T(8,128)(2,1)}, f32[1024...) custom-call(bf16[1024,768]{1,0:T(8,128)(2,1)} %bitcast.63, ...), custom_call_target="tpu_custom_call" | custom-call | flops 500000000 | bytes 748154 | tf_op jit(solution)/shard_map/mlp/pallas_call | solution.py:54
  139.1 12.6 %up_grad.1 = (bf16[8,48,3840]{2,1,0:T(8,128)(2,1)}, bf16[8,48,3840]{2,1,0:T(8,128)(2,1)}) custom-call(s32[1]{0:T(128)} %bitcast.11.refs_0_, bf16[1024,768]{1,0:T(8,128)(2,1)} %get-tuple-element.79.refs_1_, bf16[1024,3072]{1,0:T(8,128)(2,1)} %get-tuple-element.80.refs_2_, bf16[1024,768]{1,0:T(8,128)(2,1)} %get-tuple-element.76.refs_2_.refs_3_, ...), custom_call_target="tpu_custom_call" | custom-call | flops 120000000 | bytes 338165 | tf_op jit(solution)/shard_map/up_grad/pallas_call | solution.py:54
  151.7 9.4 %down_grad.1 = (bf16[8,192,768]{2,1,0:T(8,128)(2,1)}, bf16[8,192,768]{2,1,0:T(8,128)(2,1)}) custom-call(s32[1]{0:T(128)} %bitcast.11.refs_0_, bf16[1024,3072]{1,0:T(8,128)(2,1)} %get-tuple-element.78.refs_1_, bf16[1024,768]{1,0:T(8,128)(2,1)} %bitcast.66, bf16[8,48,3840]{2,1,0:T(8,128)(2,1)} %get-tuple-element.82.refs_3_), custom_call_target="tpu_custom_call" | custom-call | flops 96000000 | bytes 251658 | tf_op jit(solution)/shard_map/down_grad/pallas_call | solution.py:54
  162.1 3.9 %collective-permute-done.1.refs_2_ = bf16[8,192,768]{2,1,0:T(8,128)(2,1)} collective-permute-done((bf16[8,192,768]{2,1,0:T(8,128)(2,1)}, bf16[8,192,768]{2,1,0:T(8,128)(2,1)}, u32[]{:S(2)}, u32[]{:S(2)}) %collective-permute-start.1) | collective-permute-done | bytes 2359328 | tf_op jit(solution)/shard_map/ppermute | solution.py:606
  166.1 7.5 %first_add.2 = (bf16[4,2,216,768]{3,2,1,0:T(8,128)(2,1)}, bf16[4,2,216,768]{3,2,1,0:T(8,128)(2,1)}) custom-call(s32[2]{0:T(128)} %pad_add_fusion.refs_0_, bf16[8,192,768]{2,1,0:T(8,128)(2,1)} %get-tuple-element.83.refs_1_, bf16[8,192,768]{2,1,0:T(8,128)(2,1)} %collective-permute-done.1.refs_2_, bf16[8,48,3840]{2,1,0:T(8,128)(2,1)} %get-tuple-element.85.refs_3_, ...), custom_call_target="tpu_custom_call" | custom-call | bytes 318505 | tf_op jit(solution)/shard_map/first_add/pallas_call | solution.py:54
  179.0 30.4 %attend_back.3 = (bf16[1024,384]{1,0:T(8,128)(2,1)}, bf16[1024,384]{1,0:T(8,128)(2,1)}, bf16[1024,384]{1,0:T(8,128)(2,1)}, bf16[1024,384]{1,0:T(8,128)(2,1)}, bf16[1024,384]{1,0:T(8,128)(2,1)}) custom-call(bf16[1024,768]{1,0:T(8,128)(2,1)} %get-tuple-element.74.refs_0_, bf16[1024,1536]{1,0:T(8,128)(2,1)} %get-tuple-element.75.refs_1_.refs_3_, ...), custom_call_target="tpu_custom_call" | custom-call | flops 660000000 | bytes 519045 | tf_op jit(solution)/shard_map/attend_back/pallas_call | solution.py:54
  209.4 11.3 %collective-permute-done.3.refs_2_ = bf16[4,2,216,768]{3,2,1,0:T(8,128)(2,1)} collective-permute-done((bf16[4,2,216,768]{3,2,1,0:T(8,128)(2,1)}, bf16[4,2,216,768]{3,2,1,0:T(8,128)(2,1)}, u32[]{:S(2)}, u32[]{:S(2)}) %collective-permute-start.3) | collective-permute-done | bytes 2654240 | tf_op jit(solution)/shard_map/ppermute | solution.py:614
  220.7 4.5 %second_add.2 = (bf16[4,216,768]{2,1,0:T(8,128)(2,1)}, bf16[4,216,768]{2,1,0:T(8,128)(2,1)}) custom-call(s32[1]{0:T(128)S(6)} %select_n.78.refs_0_, bf16[4,2,216,768]{3,2,1,0:T(8,128)(2,1)} %get-tuple-element.86.refs_1_, bf16[4,2,216,768]{3,2,1,0:T(8,128)(2,1)} %collective-permute-done.3.refs_2_, ...), custom_call_target="tpu_custom_call" | custom-call | bytes 159252 | tf_op jit(solution)/shard_map/second_add/pallas_call | solution.py:54
  226.3 21.2 %attend_back.4 = (bf16[1024,256]{1,0:T(8,128)(2,1)}, bf16[1024,256]{1,0:T(8,128)(2,1)}, bf16[1024,256]{1,0:T(8,128)(2,1)}, bf16[1024,256]{1,0:T(8,128)(2,1)}, bf16[1024,256]{1,0:T(8,128)(2,1)}) custom-call(bf16[1024,768]{1,0:T(8,128)(2,1)} %get-tuple-element.74.refs_0_, bf16[1024,1536]{1,0:T(8,128)(2,1)} %get-tuple-element.75.refs_1_.refs_3_, ...), custom_call_target="tpu_custom_call" | custom-call | flops 440000000 | bytes 492830 | tf_op jit(solution)/shard_map/attend_back/pallas_call | solution.py:54
  254.0 11.9 %attend_back.5 = (bf16[1024,128]{1,0:T(8,128)(2,1)}, bf16[1024,128]{1,0:T(8,128)(2,1)}, bf16[1024,128]{1,0:T(8,128)(2,1)}, bf16[1024,128]{1,0:T(8,128)(2,1)}, bf16[1024,128]{1,0:T(8,128)(2,1)}) custom-call(bf16[1024,768]{1,0:T(8,128)(2,1)} %get-tuple-element.74.refs_0_, bf16[1024,1536]{1,0:T(8,128)(2,1)} %get-tuple-element.75.refs_1_.refs_3_, ...), custom_call_target="tpu_custom_call" | custom-call | flops 220000000 | bytes 466616 | tf_op jit(solution)/shard_map/attend_back/pallas_call | solution.py:54
  275.0 10.6 %first_back.1 = (bf16[1024,768]{1,0:T(8,128)(2,1)}, f32[1,2,768]{2,1,0:T(2,128)}, f32[1,768]{1,0:T(1,128)}) custom-call(bf16[1024,384]{1,0:T(8,128)(2,1)} %get-tuple-element.91.refs_3_.refs_9_.refs_0_.refs_2_, bf16[1024,384]{1,0:T(8,128)(2,1)} %get-tuple-element.100.refs_1_.refs_3_, bf16[1024,384]{1,0:T(8,128)(2,1)} %get-tuple-element.101.refs_2_.refs_4_, ...), custom_call_target="tpu_custom_call" | custom-call | flops 72000000 | bytes 354201 | tf_op jit(solution)/shard_map/first_back/pallas_call | solution.py:54
  290.3 4.5 %all-to-all-start.3 = ((bf16[16,64,768]{2,1,0:T(8,128)(2,1)}), bf16[16,64,768]{2,1,0:T(8,128)(2,1)S(1)}, u32[]{:S(2)}, u32[]{:S(2)}) async-start(bf16[16,64,768]{2,1,0:T(8,128)(2,1)} %bitcast.67), calls=%async_computation.3 | async-start | bytes 3145728 | tf_op jit(solution)/shard_map/all_to_all | solution.py:869
  297.3 10.3 %qkv_grad.1 = (bf16[8,48,2304]{2,1,0:T(8,128)(2,1)}, bf16[8,48,2304]{2,1,0:T(8,128)(2,1)}) custom-call(s32[1]{0:T(128)} %bitcast.11.refs_0_, bf16[1024,768]{1,0:T(8,128)(2,1)} %get-tuple-element.118.refs_1_, bf16[1024,384]{1,0:T(8,128)(2,1)} %get-tuple-element.91.refs_3_.refs_9_.refs_0_.refs_2_, bf16[1024,384]{1,0:T(8,128)(2,1)} %get-tuple-element.100.refs_1_.refs_3_, ...), custom_call_target="tpu_custom_call" | custom-call | flops 72000000 | bytes 259522 | tf_op jit(solution)/shard_map/qkv_grad/pallas_call | solution.py:54
  311.7 4.2 %first_add.3 = (bf16[4,2,48,1152]{3,2,1,0:T(8,128)(2,1)}, bf16[4,2,48,1152]{3,2,1,0:T(8,128)(2,1)}) custom-call(s32[2]{0:T(128)} %pad_add_fusion.refs_0_, bf16[8,48,2304]{2,1,0:T(8,128)(2,1)} %get-tuple-element.119.refs_1_, bf16[8,48,2304]{2,1,0:T(8,128)(2,1)} %collective-permute-done.14.refs_2_), custom_call_target="tpu_custom_call" | custom-call | bytes 106168 | tf_op jit(solution)/shard_map/first_add/pallas_call | solution.py:54
  323.4 10.1 %collective-permute-done.16 = f32[2,11,384]{2,1,0:T(8,128)S(1)} collective-permute-done((f32[2,11,384]{2,1,0:T(8,128)S(1)}, f32[2,11,384]{2,1,0:T(8,128)S(1)}, u32[]{:S(2)}, u32[]{:S(2)}) %collective-permute-start.16) | collective-permute-done | bytes 33824 | tf_op jit(solution)/shard_map/ppermute | solution.py:606
  341.8 6.7 %collective-permute-done.18.refs_2_ = bf16[4,48,1152]{2,1,0:T(8,128)(2,1)} collective-permute-done((bf16[4,48,1152]{2,1,0:T(8,128)(2,1)}, bf16[4,48,1152]{2,1,0:T(8,128)(2,1)}, u32[]{:S(2)}, u32[]{:S(2)}) %collective-permute-start.18) | collective-permute-done | bytes 442400 | tf_op jit(solution)/shard_map/ppermute | solution.py:614
  356.9 3.9 %reshape.197 = bf16[16,16,4,768]{3,2,1,0:T(4,128)(2,1)} reshape(bf16[16,64,768]{2,1,0:T(8,128)(2,1)} %copy-done.11) | data formatting | bytes 3145728 | tf_op jit(solution)/shard_map/reshape | solution.py:1033
  378.9 4.2 %collective-permute-done.25.refs_2_ = bf16[48,1152]{1,0:T(8,128)(2,1)S(1)} collective-permute-done((bf16[48,1152]{1,0:T(8,128)(2,1)}, bf16[48,1152]{1,0:T(8,128)(2,1)S(1)}, u32[]{:S(2)}, u32[]{:S(2)}) %collective-permute-start.25) | collective-permute-done | bytes 110624 | tf_op jit(solution)/shard_map/ppermute | solution.py:606
  (191 shorter events, 96.8 us)
Async XLA Ops:
  4.4 45.2 %all-to-all-start = ((bf16[16,64,768]{2,1,0:T(8,128)(2,1)}), bf16[16,64,768]{2,1,0:T(8,128)(2,1)S(1)}, u32[]{:S(2)}, u32[]{:S(2)}) async-start(bf16[16,64,768]{2,1,0:T(8,128)(2,1)} %reshape.184), calls=%async_computation | async-start | bytes 3145728 | tf_op jit(solution)/shard_map/all_to_all | solution.py:857
  59.1 6.1 %collective-permute-start = (bf16[1024,1536]{1,0:T(8,128)(2,1)}, bf16[1024,1536]{1,0:T(8,128)(2,1)}, u32[]{:S(2)}, u32[]{:S(2)}) collective-permute-start(bf16[1024,1536]{1,0:T(8,128)(2,1)} %get-tuple-element.75.refs_1_.refs_3_), channel_id=1, source_target_pairs={{0,1},{1,0},{2,3},{3,2},{4,5},{5,4},{6,7},{7,6},{8,9},{9,8},{10,11... | collective-permute-start | bytes 9437192 | tf_op jit(solution)/shard_map/ppermute | solution.py:606
  59.1 41.1 %all-to-all-start.1 = ((bf16[16,64,768]{2,1,0:T(8,128)(2,1)}), bf16[16,64,768]{2,1,0:T(8,128)(2,1)S(1)}, u32[]{:S(2)}, u32[]{:S(2)}) async-start(bf16[16,64,768]{2,1,0:T(8,128)(2,1)} %reshape.187.refs_5_), calls=%async_computation.1 | async-start | bytes 3145728 | tf_op jit(solution)/shard_map/all_to_all | solution.py:857
  151.7 14.4 %collective-permute-start.2 = (bf16[8,48,3840]{2,1,0:T(8,128)(2,1)}, bf16[8,48,3840]{2,1,0:T(8,128)(2,1)}, u32[]{:S(2)}, u32[]{:S(2)}) collective-permute-start(bf16[8,48,3840]{2,1,0:T(8,128)(2,1)} %get-tuple-element.82.refs_3_), channel_id=1, source_target_pairs={{0,1},{1,0},{2,3},{3,2},{4,5},{5,4},{6,7},{7,6},{8,9},{9,8},{10,11... | collective-permute-start | bytes 8847368 | tf_op jit(solution)/shard_map/ppermute | solution.py:606
  173.5 47.1 %collective-permute-start.3 = (bf16[4,2,216,768]{3,2,1,0:T(8,128)(2,1)}, bf16[4,2,216,768]{3,2,1,0:T(8,128)(2,1)}, u32[]{:S(2)}, u32[]{:S(2)}) collective-permute-start(bf16[4,2,216,768]{3,2,1,0:T(8,128)(2,1)} %get-tuple-element.87.refs_8_), channel_id=1, source_target_pairs={{0,16},{1,3},{2,18},{3,1},{16,0},{17,19},{18,2},{19,17},{4,20},{5,... | collective-permute-start | bytes 7962632 | tf_op jit(solution)/shard_map/ppermute | solution.py:614
  175.1 77.8 %all-to-all-start.2 = ((bf16[16,64,768]{2,1,0:T(8,128)(2,1)}), bf16[16,64,768]{2,1,0:T(8,128)(2,1)S(1)}, u32[]{:S(2)}, u32[]{:S(2)}) async-start(bf16[16,64,768]{2,1,0:T(8,128)(2,1)} %bitcast.68), calls=%async_computation.2 | async-start | bytes 3145728 | tf_op jit(solution)/shard_map/all_to_all | solution.py:869
  225.2 22.3 %collective-permute-start.4 = (bf16[4,216,768]{2,1,0:T(8,128)(2,1)}, bf16[4,216,768]{2,1,0:T(8,128)(2,1)}, u32[]{:S(2)}, u32[]{:S(2)}) collective-permute-start(bf16[4,216,768]{2,1,0:T(8,128)(2,1)} %get-tuple-element.93.refs_8_), channel_id=1, source_target_pairs={{0,2},{1,17},{2,0},{3,19},{16,18},{17,1},{18,16},{19,3},{4,6},{5,2... | collective-permute-start | bytes 3981320 | tf_op jit(solution)/shard_map/ppermute | solution.py:614
  225.8 46.5 %collective-permute-start.7 = (bf16[1024,384]{1,0:T(8,128)(2,1)}, bf16[1024,384]{1,0:T(8,128)(2,1)}, u32[]{:S(2)}, u32[]{:S(2)}) collective-permute-start(bf16[1024,384]{1,0:T(8,128)(2,1)} %get-tuple-element.102), channel_id=1, source_target_pairs={{0,1},{1,0},{2,3},{3,2},{4,5},{5,4},{6,7},{7,6},{8,9},{9,8},{10,11... | collective-permute-start | bytes 2359304 | tf_op jit(solution)/shard_map/ppermute | solution.py:606
  225.9 46.4 %collective-permute-start.8 = (bf16[1024,384]{1,0:T(8,128)(2,1)}, bf16[1024,384]{1,0:T(8,128)(2,1)}, u32[]{:S(2)}, u32[]{:S(2)}) collective-permute-start(bf16[1024,384]{1,0:T(8,128)(2,1)} %get-tuple-element.103), channel_id=1, source_target_pairs={{0,1},{1,0},{2,3},{3,2},{4,5},{5,4},{6,7},{7,6},{8,9},{9,8},{10,11... | collective-permute-start | bytes 2359304 | tf_op jit(solution)/shard_map/ppermute | solution.py:606
  250.4 17.6 %collective-permute-start.5 = (bf16[2,216,768]{2,1,0:T(8,128)(2,1)}, bf16[2,216,768]{2,1,0:T(8,128)(2,1)}, u32[]{:S(2)}, u32[]{:S(2)}) collective-permute-start(bf16[2,216,768]{2,1,0:T(8,128)(2,1)} %get-tuple-element.96.refs_8_), channel_id=1, source_target_pairs={{0,4},{4,0},{8,12},{12,8},{1,5},{5,1},{9,13},{13,9},{2,6},{6,2},{1... | collective-permute-start | bytes 1990664 | tf_op jit(solution)/shard_map/ppermute | solution.py:606
  252.4 20.5 %collective-permute-start.10 = (bf16[1024,256]{1,0:T(8,128)(2,1)}, bf16[1024,256]{1,0:T(8,128)(2,1)}, u32[]{:S(2)}, u32[]{:S(2)}) collective-permute-start(bf16[1024,256]{1,0:T(8,128)(2,1)} %get-tuple-element.107), channel_id=1, source_target_pairs={{0,1},{1,0},{2,3},{3,2},{4,5},{5,4},{6,7},{7,6},{8,9},{9,8},{10,11... | collective-permute-start | bytes 1572872 | tf_op jit(solution)/shard_map/ppermute | solution.py:606
  252.4 20.5 %collective-permute-start.9 = (bf16[1024,256]{1,0:T(8,128)(2,1)}, bf16[1024,256]{1,0:T(8,128)(2,1)}, u32[]{:S(2)}, u32[]{:S(2)}) collective-permute-start(bf16[1024,256]{1,0:T(8,128)(2,1)} %get-tuple-element.106), channel_id=1, source_target_pairs={{0,1},{1,0},{2,3},{3,2},{4,5},{5,4},{6,7},{7,6},{8,9},{9,8},{10,11... | collective-permute-start | bytes 1572872 | tf_op jit(solution)/shard_map/ppermute | solution.py:606
  270.2 17.5 %collective-permute-start.6 = (bf16[1,216,768]{2,1,0:T(8,128)(2,1)}, bf16[1,216,768]{2,1,0:T(8,128)(2,1)S(1)}, u32[]{:S(2)}, u32[]{:S(2)}) collective-permute-start(bf16[1,216,768]{2,1,0:T(8,128)(2,1)} %get-tuple-element.99.refs_20_), channel_id=1, source_target_pairs={{0,8},{4,12},{8,0},{12,4},{1,9},{5,13},{9,1},{13,5},{2,10},{6,14},... | collective-permute-start | bytes 995336 | tf_op jit(solution)/shard_map/ppermute | solution.py:606
  290.3 43.9 %all-to-all-start.3 = ((bf16[16,64,768]{2,1,0:T(8,128)(2,1)}), bf16[16,64,768]{2,1,0:T(8,128)(2,1)S(1)}, u32[]{:S(2)}, u32[]{:S(2)}) async-start(bf16[16,64,768]{2,1,0:T(8,128)(2,1)} %bitcast.67), calls=%async_computation.3 | async-start | bytes 3145728 | tf_op jit(solution)/shard_map/all_to_all | solution.py:869
  315.9 18.3 %collective-permute-start.17 = (bf16[4,2,48,1152]{3,2,1,0:T(8,128)(2,1)}, bf16[4,2,48,1152]{3,2,1,0:T(8,128)(2,1)S(1)}, u32[]{:S(2)}, u32[]{:S(2)}) collective-permute-start(bf16[4,2,48,1152]{3,2,1,0:T(8,128)(2,1)} %get-tuple-element.121.refs_1_), channel_id=1, source_target_pairs={{0,16},{1,3},{2,18},{3,1},{16,0},{17,19},{18,2},{19,17},{4,20},{5,... | collective-permute-start | bytes 2654216 | tf_op jit(solution)/shard_map/ppermute | solution.py:614
  323.4 10.2 %collective-permute-start.16 = (f32[2,11,384]{2,1,0:T(8,128)S(1)}, f32[2,11,384]{2,1,0:T(8,128)S(1)}, u32[]{:S(2)}, u32[]{:S(2)}) collective-permute-start(f32[2,11,384]{2,1,0:T(8,128)S(1)} %maximum_select_fusion.1), channel_id=1, source_target_pairs={{0,16},{16,0},{1,17},{17,1},{2,18},{18,2},{3,19},{19,3},{4,20},{20... | collective-permute-start | bytes 101384 | tf_op jit(solution)/shard_map/ppermute | solution.py:606
  339.9 8.6 %collective-permute-start.18 = (bf16[4,48,1152]{2,1,0:T(8,128)(2,1)}, bf16[4,48,1152]{2,1,0:T(8,128)(2,1)}, u32[]{:S(2)}, u32[]{:S(2)}) collective-permute-start(bf16[4,48,1152]{2,1,0:T(8,128)(2,1)} %get-tuple-element.124), channel_id=1, source_target_pairs={{0,2},{1,17},{2,0},{3,19},{16,18},{17,1},{18,16},{19,3},{4,6},{5,2... | collective-permute-start | bytes 1327112 | tf_op jit(solution)/shard_map/ppermute | solution.py:614
  351.4 11.6 %collective-permute-start.19 = (f32[4,11,384]{2,1,0:T(8,128)S(1)}, f32[4,11,384]{2,1,0:T(8,128)S(1)}, u32[]{:S(2)}, u32[]{:S(2)}) collective-permute-start(f32[4,11,384]{2,1,0:T(8,128)S(1)} %held.4), channel_id=1, source_target_pairs={{0,4},{4,8},{8,12},{12,0},{1,5},{5,9},{9,13},{13,1},{2,6},{6,10},{... | collective-permute-start | bytes 202760 | tf_op jit(solution)/shard_map/ppermute | solution.py:745
  351.7 12.6 %collective-permute-start.20 = (f32[4,11,384]{2,1,0:T(8,128)S(1)}, f32[4,11,384]{2,1,0:T(8,128)S(1)}, u32[]{:S(2)}, u32[]{:S(2)}) collective-permute-start(f32[4,11,384]{2,1,0:T(8,128)S(1)} %held.4), channel_id=1, source_target_pairs={{0,8},{4,12},{8,0},{12,4},{1,9},{5,13},{9,1},{13,5},{2,10},{6,14},... | collective-permute-start | bytes 202760 | tf_op jit(solution)/shard_map/ppermute | solution.py:745
  354.5 12.6 %collective-permute-start.21 = (f32[4,11,384]{2,1,0:T(8,128)S(1)}, f32[4,11,384]{2,1,0:T(8,128)S(1)}, u32[]{:S(2)}, u32[]{:S(2)}) collective-permute-start(f32[4,11,384]{2,1,0:T(8,128)S(1)} %held.4), channel_id=1, source_target_pairs={{0,12},{4,0},{8,4},{12,8},{1,13},{5,1},{9,5},{13,9},{2,14},{6,2},{... | collective-permute-start | bytes 202760 | tf_op jit(solution)/shard_map/ppermute | solution.py:745
  360.9 24.6 %collective-permute-start.26 = (bf16[216,768]{1,0:T(8,128)(2,1)S(1)}, bf16[216,768]{1,0:T(8,128)(2,1)S(1)}, u32[]{:S(2)}, u32[]{:S(2)}) collective-permute-start(bf16[216,768]{1,0:T(8,128)(2,1)S(1)} %held.5.refs_1_), channel_id=1, source_target_pairs={{0,16},{16,0},{1,17},{17,1},{2,18},{18,2},{3,19},{19,3},{4,20},{20... | collective-permute-start | bytes 995336 | tf_op jit(solution)/shard_map/ppermute | solution.py:606
  362.4 8.4 %collective-permute-start.22 = (bf16[48,1152]{1,0:T(8,128)(2,1)S(1)}, bf16[48,1152]{1,0:T(8,128)(2,1)S(1)}, u32[]{:S(2)}, u32[]{:S(2)}) collective-permute-start(bf16[48,1152]{1,0:T(8,128)(2,1)S(1)} %copy-done.40), channel_id=1, source_target_pairs={{0,4},{4,8},{8,12},{12,0},{1,5},{5,9},{9,13},{13,1},{2,6},{6,10},{... | collective-permute-start | bytes 331784 | tf_op jit(solution)/shard_map/ppermute | solution.py:745
  363.0 11.1 %collective-permute-start.23 = (bf16[48,1152]{1,0:T(8,128)(2,1)S(1)}, bf16[48,1152]{1,0:T(8,128)(2,1)S(1)}, u32[]{:S(2)}, u32[]{:S(2)}) collective-permute-start(bf16[48,1152]{1,0:T(8,128)(2,1)S(1)} %copy-done.39), channel_id=1, source_target_pairs={{0,8},{4,12},{8,0},{12,4},{1,9},{5,13},{9,1},{13,5},{2,10},{6,14},... | collective-permute-start | bytes 331784 | tf_op jit(solution)/shard_map/ppermute | solution.py:745
  364.3 9.8 %collective-permute-start.24 = (bf16[48,1152]{1,0:T(8,128)(2,1)S(1)}, bf16[48,1152]{1,0:T(8,128)(2,1)S(1)}, u32[]{:S(2)}, u32[]{:S(2)}) collective-permute-start(bf16[48,1152]{1,0:T(8,128)(2,1)S(1)} %copy-done.38), channel_id=1, source_target_pairs={{0,12},{4,0},{8,4},{12,8},{1,13},{5,1},{9,5},{13,9},{2,14},{6,2},{... | collective-permute-start | bytes 331784 | tf_op jit(solution)/shard_map/ppermute | solution.py:745
  (49 other events, 255.0 us)

commit v6 on v5

--- a/solution.py
+++ b/solution.py
@@ -959,14 +959,12 @@
             sent, kept = cut_lead(kept, got, 0, deps)
             got = swap(sent, "zed", 0)
             deps = (sent, dq)
-        if at == 1:
-            deps = deps + (out_patch,)
 
     if staged:
         for bit in range(1, bits_of(lax.axis_size("zed"))):
             sent, kept = cut_lead(kept, got, bit, deps)
             got = swap(sent, "zed", bit)
-            deps = (sent,)
+            deps = (sent, out_patch)
         mlp_parts = [kept[0], got[0]]
     grad_start, frame_sums, gain_sum = first_back(
         pieces, x, chan_add, gain1, grad_middle, qkv_weight, frames, deps
@@ -1006,7 +1004,7 @@
         sum_down, sum_up, sum_out = spread(
             mlp_sum, swap(mlp_sum, "lat", 0), [(tall, width), (share, wide), (share, width)], fill_mlp
         )
-        total = last_add(parts)
+        total = last_add(parts, (sum_down,))
         sum_qkv = spread(total, swap(total, "lat", 0), [(share, 3 * width)], fill_qkv)[0]
     else:
         sum_down = plain_sum(down_kept, down_got)

time: 393 us -> 389 us (0.990)
    unnamed x84 -> x76, local copies, waits for them, and re-layouts: 12.4 us -> 9.4 us
where the time goes in v6:
time: 389 us; the launch traced here: 385 us
  Pallas kernels  217 us (56%)
  waiting for transfers between devices  87.3 us (22%)
  starting transfers between devices  46.5 us (12%)
  local copies, waits for them, and re-layouts  26.3 us (7%)
    pallas_call x23, Pallas kernels, call(): pl.pallas_call(body, grid=grid, in_specs=[spec for a, spec in ins] + [any...  215 us
    all_to_all x2, waiting for transfers between devices, to_frames(): value = lax.all_to_all(value, ('lat', 'zed', 'yy'), 0, 0, tiled=True)  35 us
    ppermute x17, waiting for transfers between devices, swap(): return lax.ppermute(value, axis, swap_pairs(lax.axis_size(axis), bit))  34 us
    ppermute x4, waiting for transfers between devices, cross(): return lax.ppermute(value, ('lat', 'yy', 'core'), pairs)  18 us
    all_to_all x2, starting transfers between devices, to_frames(): value = lax.all_to_all(value, ('lat', 'zed', 'yy'), 0, 0, tiled=True)  12.5 us
    ppermute x17, starting transfers between devices, swap(): return lax.ppermute(value, axis, swap_pairs(lax.axis_size(axis), bit))  10.8 us
    unnamed x76, local copies, waits for them, and re-layouts  9.4 us
    ppermute x6, starting transfers between devices, up_zed(): return lax.ppermute(value, 'zed', [(i, (i + up) % zed) for i in range(zed)])  8.82 us
  transfers between devices with their start and end apart: 31, of which 16 were waited for; matrix products, arithmetic and copies ran while one was open for 5% of the time, Pallas kernels for 36%

profile of v6, /device:TPU:0, one launch (start us, length us, event | category | flops | bytes accessed | tf_op | source)
XLA Modules:
  0.0 384.6 jit_solution(2312184368961382240)
XLA Ops:
  4.4 8.5 %all-to-all-start = ((bf16[16,64,768]{2,1,0:T(8,128)(2,1)}), bf16[16,64,768]{2,1,0:T(8,128)(2,1)S(1)}, u32[]{:S(2)}, u32[]{:S(2)}) async-start(bf16[16,64,768]{2,1,0:T(8,128)(2,1)} %reshape.184), calls=%async_computation | async-start | bytes 3145728 | tf_op jit(solution)/shard_map/all_to_all | solution.py:857
  19.9 29.7 %all-to-all-done = bf16[16,64,768]{2,1,0:T(8,128)(2,1)S(1)} async-done(((bf16[16,64,768]{2,1,0:T(8,128)(2,1)}), bf16[16,64,768]{2,1,0:T(8,128)(2,1)S(1)}, u32[]{:S(2)}, u32[]{:S(2)}) %all-to-all-start) | async-done | bytes 1572896 | tf_op jit(solution)/shard_map/all_to_all | solution.py:857
  50.7 8.3 %qkv.1 = (bf16[1024,768]{1,0:T(8,128)(2,1)}, bf16[1024,1536]{1,0:T(8,128)(2,1)}, bf16[1024,768]{1,0:T(8,128)(2,1)}) custom-call(bf16[1024,768]{1,0:T(8,128)(2,1)} %bitcast.62, f32[1,1,768]{2,1,0:T(1,128)} %convolution_bitcast_fusion.1.refs_1_.refs_16_, f32[1,1,768]{2,1,0:T(1,128)} %broadcast_in_dim.35.refs_2_, f32[1,768]{1,0:T(1,128)} %reshape.206.refs_3_.refs_17_, ...), custom_call_target="tpu_custom_call" | custom-call | flops 72000000 | bytes 228249 | tf_op jit(solution)/shard_map/qkv/pallas_call | solution.py:54
  59.1 4.1 %all-to-all-start.1 = ((bf16[16,64,768]{2,1,0:T(8,128)(2,1)}), bf16[16,64,768]{2,1,0:T(8,128)(2,1)S(1)}, u32[]{:S(2)}, u32[]{:S(2)}) async-start(bf16[16,64,768]{2,1,0:T(8,128)(2,1)} %reshape.187.refs_5_), calls=%async_computation.1 | async-start | bytes 3145728 | tf_op jit(solution)/shard_map/all_to_all | solution.py:857
  65.1 29.8 %attend.1 = (bf16[1024,768]{1,0:T(8,128)(2,1)}, f32[1024,768]{1,0:T(8,128)}, f32[1024,768]{1,0:T(8,128)}) custom-call(bf16[1024,768]{1,0:T(8,128)(2,1)} %get-tuple-element.74.refs_0_, bf16[1024,1536]{1,0:T(8,128)(2,1)} %get-tuple-element.75.refs_1_.refs_3_, bf16[1024,1536]{1,0:T(8,128)(2,1)} %collective-permute-done.refs_2_.refs_4_, ...), custom_call_target="tpu_custom_call" | custom-call | flops 600000000 | bytes 440401 | tf_op jit(solution)/shard_map/attend/pallas_call | solution.py:54
  94.9 5.4 %all-to-all-done.1 = bf16[16,64,768]{2,1,0:T(8,128)(2,1)S(1)} async-done(((bf16[16,64,768]{2,1,0:T(8,128)(2,1)}), bf16[16,64,768]{2,1,0:T(8,128)(2,1)S(1)}, u32[]{:S(2)}, u32[]{:S(2)}) %all-to-all-start.1) | async-done | bytes 1572896 | tf_op jit(solution)/shard_map/all_to_all | solution.py:857
  101.4 37.7 %mlp.1 = (bf16[1024,768]{1,0:T(8,128)(2,1)}, bf16[1024,3072]{1,0:T(8,128)(2,1)}, bf16[1024,3072]{1,0:T(8,128)(2,1)}, bf16[1024,768]{1,0:T(8,128)(2,1)}, f32[1024...) custom-call(bf16[1024,768]{1,0:T(8,128)(2,1)} %bitcast.63, ...), custom_call_target="tpu_custom_call" | custom-call | flops 500000000 | bytes 748154 | tf_op jit(solution)/shard_map/mlp/pallas_call | solution.py:54
  139.1 12.5 %up_grad.1 = (bf16[8,48,3840]{2,1,0:T(8,128)(2,1)}, bf16[8,48,3840]{2,1,0:T(8,128)(2,1)}) custom-call(s32[1]{0:T(128)} %bitcast.11.refs_0_, bf16[1024,768]{1,0:T(8,128)(2,1)} %get-tuple-element.79.refs_1_, bf16[1024,3072]{1,0:T(8,128)(2,1)} %get-tuple-element.80.refs_2_, bf16[1024,768]{1,0:T(8,128)(2,1)} %get-tuple-element.76.refs_2_.refs_3_, ...), custom_call_target="tpu_custom_call" | custom-call | flops 120000000 | bytes 338165 | tf_op jit(solution)/shard_map/up_grad/pallas_call | solution.py:54
  151.7 9.4 %down_grad.1 = (bf16[8,192,768]{2,1,0:T(8,128)(2,1)}, bf16[8,192,768]{2,1,0:T(8,128)(2,1)}) custom-call(s32[1]{0:T(128)} %bitcast.11.refs_0_, bf16[1024,3072]{1,0:T(8,128)(2,1)} %get-tuple-element.78.refs_1_, bf16[1024,768]{1,0:T(8,128)(2,1)} %bitcast.66, bf16[8,48,3840]{2,1,0:T(8,128)(2,1)} %get-tuple-element.82.refs_3_), custom_call_target="tpu_custom_call" | custom-call | flops 96000000 | bytes 251658 | tf_op jit(solution)/shard_map/down_grad/pallas_call | solution.py:54
  162.1 3.9 %collective-permute-done.1.refs_2_ = bf16[8,192,768]{2,1,0:T(8,128)(2,1)} collective-permute-done((bf16[8,192,768]{2,1,0:T(8,128)(2,1)}, bf16[8,192,768]{2,1,0:T(8,128)(2,1)}, u32[]{:S(2)}, u32[]{:S(2)}) %collective-permute-start.1) | collective-permute-done | bytes 2359328 | tf_op jit(solution)/shard_map/ppermute | solution.py:606
  166.0 7.5 %first_add.2 = (bf16[4,2,216,768]{3,2,1,0:T(8,128)(2,1)}, bf16[4,2,216,768]{3,2,1,0:T(8,128)(2,1)}) custom-call(s32[2]{0:T(128)} %pad_add_fusion.refs_0_, bf16[8,192,768]{2,1,0:T(8,128)(2,1)} %get-tuple-element.83.refs_1_, bf16[8,192,768]{2,1,0:T(8,128)(2,1)} %collective-permute-done.1.refs_2_, bf16[8,48,3840]{2,1,0:T(8,128)(2,1)} %get-tuple-element.85.refs_3_, ...), custom_call_target="tpu_custom_call" | custom-call | bytes 318505 | tf_op jit(solution)/shard_map/first_add/pallas_call | solution.py:54
  178.9 30.4 %attend_back.3 = (bf16[1024,384]{1,0:T(8,128)(2,1)}, bf16[1024,384]{1,0:T(8,128)(2,1)}, bf16[1024,384]{1,0:T(8,128)(2,1)}, bf16[1024,384]{1,0:T(8,128)(2,1)}, bf16[1024,384]{1,0:T(8,128)(2,1)}) custom-call(bf16[1024,768]{1,0:T(8,128)(2,1)} %get-tuple-element.74.refs_0_, bf16[1024,1536]{1,0:T(8,128)(2,1)} %get-tuple-element.75.refs_1_.refs_3_, ...), custom_call_target="tpu_custom_call" | custom-call | flops 660000000 | bytes 519045 | tf_op jit(solution)/shard_map/attend_back/pallas_call | solution.py:54
  209.4 11.3 %collective-permute-done.3.refs_2_ = bf16[4,2,216,768]{3,2,1,0:T(8,128)(2,1)} collective-permute-done((bf16[4,2,216,768]{3,2,1,0:T(8,128)(2,1)}, bf16[4,2,216,768]{3,2,1,0:T(8,128)(2,1)}, u32[]{:S(2)}, u32[]{:S(2)}) %collective-permute-start.3) | collective-permute-done | bytes 2654240 | tf_op jit(solution)/shard_map/ppermute | solution.py:614
  220.6 4.5 %second_add.2 = (bf16[4,216,768]{2,1,0:T(8,128)(2,1)}, bf16[4,216,768]{2,1,0:T(8,128)(2,1)}) custom-call(s32[1]{0:T(128)S(6)} %select_n.78.refs_0_, bf16[4,2,216,768]{3,2,1,0:T(8,128)(2,1)} %get-tuple-element.86.refs_1_, bf16[4,2,216,768]{3,2,1,0:T(8,128)(2,1)} %collective-permute-done.3.refs_2_, ...), custom_call_target="tpu_custom_call" | custom-call | bytes 159252 | tf_op jit(solution)/shard_map/second_add/pallas_call | solution.py:54
  226.2 21.2 %attend_back.4 = (bf16[1024,256]{1,0:T(8,128)(2,1)}, bf16[1024,256]{1,0:T(8,128)(2,1)}, bf16[1024,256]{1,0:T(8,128)(2,1)}, bf16[1024,256]{1,0:T(8,128)(2,1)}, bf16[1024,256]{1,0:T(8,128)(2,1)}) custom-call(bf16[1024,768]{1,0:T(8,128)(2,1)} %get-tuple-element.74.refs_0_, bf16[1024,1536]{1,0:T(8,128)(2,1)} %get-tuple-element.75.refs_1_.refs_3_, ...), custom_call_target="tpu_custom_call" | custom-call | flops 440000000 | bytes 492830 | tf_op jit(solution)/shard_map/attend_back/pallas_call | solution.py:54
  252.8 11.8 %attend_back.5 = (bf16[1024,128]{1,0:T(8,128)(2,1)}, bf16[1024,128]{1,0:T(8,128)(2,1)}, bf16[1024,128]{1,0:T(8,128)(2,1)}, bf16[1024,128]{1,0:T(8,128)(2,1)}, bf16[1024,128]{1,0:T(8,128)(2,1)}) custom-call(bf16[1024,768]{1,0:T(8,128)(2,1)} %get-tuple-element.74.refs_0_, bf16[1024,1536]{1,0:T(8,128)(2,1)} %get-tuple-element.75.refs_1_.refs_3_, ...), custom_call_target="tpu_custom_call" | custom-call | flops 220000000 | bytes 466616 | tf_op jit(solution)/shard_map/attend_back/pallas_call | solution.py:54
  274.7 10.6 %first_back.1 = (bf16[1024,768]{1,0:T(8,128)(2,1)}, f32[1,2,768]{2,1,0:T(2,128)}, f32[1,768]{1,0:T(1,128)}) custom-call(bf16[1024,384]{1,0:T(8,128)(2,1)} %get-tuple-element.91.refs_3_.refs_9_.refs_0_.refs_2_, bf16[1024,384]{1,0:T(8,128)(2,1)} %get-tuple-element.100.refs_1_.refs_3_, bf16[1024,384]{1,0:T(8,128)(2,1)} %get-tuple-element.101.refs_2_.refs_4_, ...), custom_call_target="tpu_custom_call" | custom-call | flops 72000000 | bytes 354201 | tf_op jit(solution)/shard_map/first_back/pallas_call | solution.py:54
  289.7 4.4 %all-to-all-start.3 = ((bf16[16,64,768]{2,1,0:T(8,128)(2,1)}), bf16[16,64,768]{2,1,0:T(8,128)(2,1)S(1)}, u32[]{:S(2)}, u32[]{:S(2)}) async-start(bf16[16,64,768]{2,1,0:T(8,128)(2,1)} %bitcast.67), calls=%async_computation.3 | async-start | bytes 3145728 | tf_op jit(solution)/shard_map/all_to_all | solution.py:869
  296.6 10.3 %qkv_grad.1 = (bf16[8,48,2304]{2,1,0:T(8,128)(2,1)}, bf16[8,48,2304]{2,1,0:T(8,128)(2,1)}) custom-call(s32[1]{0:T(128)} %bitcast.11.refs_0_, bf16[1024,768]{1,0:T(8,128)(2,1)} %get-tuple-element.118.refs_1_, bf16[1024,384]{1,0:T(8,128)(2,1)} %get-tuple-element.91.refs_3_.refs_9_.refs_0_.refs_2_, bf16[1024,384]{1,0:T(8,128)(2,1)} %get-tuple-element.100.refs_1_.refs_3_, ...), custom_call_target="tpu_custom_call" | custom-call | flops 72000000 | bytes 259522 | tf_op jit(solution)/shard_map/qkv_grad/pallas_call | solution.py:54
  311.0 4.2 %first_add.3 = (bf16[4,2,48,1152]{3,2,1,0:T(8,128)(2,1)}, bf16[4,2,48,1152]{3,2,1,0:T(8,128)(2,1)}) custom-call(s32[2]{0:T(128)} %pad_add_fusion.refs_0_, bf16[8,48,2304]{2,1,0:T(8,128)(2,1)} %get-tuple-element.119.refs_1_, bf16[8,48,2304]{2,1,0:T(8,128)(2,1)} %collective-permute-done.14.refs_2_), custom_call_target="tpu_custom_call" | custom-call | bytes 106168 | tf_op jit(solution)/shard_map/first_add/pallas_call | solution.py:54
  322.8 10.1 %collective-permute-done.16 = f32[2,11,384]{2,1,0:T(8,128)S(1)} collective-permute-done((f32[2,11,384]{2,1,0:T(8,128)S(1)}, f32[2,11,384]{2,1,0:T(8,128)S(1)}, u32[]{:S(2)}, u32[]{:S(2)}) %collective-permute-start.16) | collective-permute-done | bytes 33824 | tf_op jit(solution)/shard_map/ppermute | solution.py:606
  341.2 6.7 %collective-permute-done.18.refs_2_ = bf16[4,48,1152]{2,1,0:T(8,128)(2,1)} collective-permute-done((bf16[4,48,1152]{2,1,0:T(8,128)(2,1)}, bf16[4,48,1152]{2,1,0:T(8,128)(2,1)}, u32[]{:S(2)}, u32[]{:S(2)}) %collective-permute-start.18) | collective-permute-done | bytes 442400 | tf_op jit(solution)/shard_map/ppermute | solution.py:614
  356.3 3.9 %reshape.197 = bf16[16,16,4,768]{3,2,1,0:T(4,128)(2,1)} reshape(bf16[16,64,768]{2,1,0:T(8,128)(2,1)} %copy-done.11) | data formatting | bytes 3145728 | tf_op jit(solution)/shard_map/reshape | solution.py:1031
  377.7 4.3 %collective-permute-done.26.refs_2_ = bf16[48,1152]{1,0:T(8,128)(2,1)S(1)} collective-permute-done((bf16[48,1152]{1,0:T(8,128)(2,1)}, bf16[48,1152]{1,0:T(8,128)(2,1)S(1)}, u32[]{:S(2)}, u32[]{:S(2)}) %collective-permute-start.26) | collective-permute-done | bytes 110624 | tf_op jit(solution)/shard_map/ppermute | solution.py:606
  (183 shorter events, 92.7 us)
Async XLA Ops:
  4.4 45.2 %all-to-all-start = ((bf16[16,64,768]{2,1,0:T(8,128)(2,1)}), bf16[16,64,768]{2,1,0:T(8,128)(2,1)S(1)}, u32[]{:S(2)}, u32[]{:S(2)}) async-start(bf16[16,64,768]{2,1,0:T(8,128)(2,1)} %reshape.184), calls=%async_computation | async-start | bytes 3145728 | tf_op jit(solution)/shard_map/all_to_all | solution.py:857
  59.1 41.1 %all-to-all-start.1 = ((bf16[16,64,768]{2,1,0:T(8,128)(2,1)}), bf16[16,64,768]{2,1,0:T(8,128)(2,1)S(1)}, u32[]{:S(2)}, u32[]{:S(2)}) async-start(bf16[16,64,768]{2,1,0:T(8,128)(2,1)} %reshape.187.refs_5_), calls=%async_computation.1 | async-start | bytes 3145728 | tf_op jit(solution)/shard_map/all_to_all | solution.py:857
  151.6 14.4 %collective-permute-start.2 = (bf16[8,48,3840]{2,1,0:T(8,128)(2,1)}, bf16[8,48,3840]{2,1,0:T(8,128)(2,1)}, u32[]{:S(2)}, u32[]{:S(2)}) collective-permute-start(bf16[8,48,3840]{2,1,0:T(8,128)(2,1)} %get-tuple-element.82.refs_3_), channel_id=1, source_target_pairs={{0,1},{1,0},{2,3},{3,2},{4,5},{5,4},{6,7},{7,6},{8,9},{9,8},{10,11... | collective-permute-start | bytes 8847368 | tf_op jit(solution)/shard_map/ppermute | solution.py:606
  173.5 47.1 %collective-permute-start.3 = (bf16[4,2,216,768]{3,2,1,0:T(8,128)(2,1)}, bf16[4,2,216,768]{3,2,1,0:T(8,128)(2,1)}, u32[]{:S(2)}, u32[]{:S(2)}) collective-permute-start(bf16[4,2,216,768]{3,2,1,0:T(8,128)(2,1)} %get-tuple-element.87.refs_8_), channel_id=1, source_target_pairs={{0,16},{1,3},{2,18},{3,1},{16,0},{17,19},{18,2},{19,17},{4,20},{5,... | collective-permute-start | bytes 7962632 | tf_op jit(solution)/shard_map/ppermute | solution.py:614
  175.0 97.8 %all-to-all-start.2 = ((bf16[16,64,768]{2,1,0:T(8,128)(2,1)}), bf16[16,64,768]{2,1,0:T(8,128)(2,1)S(1)}, u32[]{:S(2)}, u32[]{:S(2)}) async-start(bf16[16,64,768]{2,1,0:T(8,128)(2,1)} %bitcast.68), calls=%async_computation.2 | async-start | bytes 3145728 | tf_op jit(solution)/shard_map/all_to_all | solution.py:869
  225.2 22.3 %collective-permute-start.4 = (bf16[4,216,768]{2,1,0:T(8,128)(2,1)}, bf16[4,216,768]{2,1,0:T(8,128)(2,1)}, u32[]{:S(2)}, u32[]{:S(2)}) collective-permute-start(bf16[4,216,768]{2,1,0:T(8,128)(2,1)} %get-tuple-element.93.refs_8_), channel_id=1, source_target_pairs={{0,2},{1,17},{2,0},{3,19},{16,18},{17,1},{18,16},{19,3},{4,6},{5,2... | collective-permute-start | bytes 3981320 | tf_op jit(solution)/shard_map/ppermute | solution.py:614
  225.7 46.6 %collective-permute-start.7 = (bf16[1024,384]{1,0:T(8,128)(2,1)}, bf16[1024,384]{1,0:T(8,128)(2,1)}, u32[]{:S(2)}, u32[]{:S(2)}) collective-permute-start(bf16[1024,384]{1,0:T(8,128)(2,1)} %get-tuple-element.102), channel_id=1, source_target_pairs={{0,1},{1,0},{2,3},{3,2},{4,5},{5,4},{6,7},{7,6},{8,9},{9,8},{10,11... | collective-permute-start | bytes 2359304 | tf_op jit(solution)/shard_map/ppermute | solution.py:606
  225.9 46.4 %collective-permute-start.8 = (bf16[1024,384]{1,0:T(8,128)(2,1)}, bf16[1024,384]{1,0:T(8,128)(2,1)}, u32[]{:S(2)}, u32[]{:S(2)}) collective-permute-start(bf16[1024,384]{1,0:T(8,128)(2,1)} %get-tuple-element.103), channel_id=1, source_target_pairs={{0,1},{1,0},{2,3},{3,2},{4,5},{5,4},{6,7},{7,6},{8,9},{9,8},{10,11... | collective-permute-start | bytes 2359304 | tf_op jit(solution)/shard_map/ppermute | solution.py:606
  250.3 17.6 %collective-permute-start.5 = (bf16[2,216,768]{2,1,0:T(8,128)(2,1)}, bf16[2,216,768]{2,1,0:T(8,128)(2,1)}, u32[]{:S(2)}, u32[]{:S(2)}) collective-permute-start(bf16[2,216,768]{2,1,0:T(8,128)(2,1)} %get-tuple-element.96.refs_8_), channel_id=1, source_target_pairs={{0,4},{4,0},{8,12},{12,8},{1,5},{5,1},{9,13},{13,9},{2,6},{6,2},{1... | collective-permute-start | bytes 1990664 | tf_op jit(solution)/shard_map/ppermute | solution.py:606
  252.3 20.5 %collective-permute-start.10 = (bf16[1024,256]{1,0:T(8,128)(2,1)}, bf16[1024,256]{1,0:T(8,128)(2,1)}, u32[]{:S(2)}, u32[]{:S(2)}) collective-permute-start(bf16[1024,256]{1,0:T(8,128)(2,1)} %get-tuple-element.107), channel_id=1, source_target_pairs={{0,1},{1,0},{2,3},{3,2},{4,5},{5,4},{6,7},{7,6},{8,9},{9,8},{10,11... | collective-permute-start | bytes 1572872 | tf_op jit(solution)/shard_map/ppermute | solution.py:606
  252.3 20.5 %collective-permute-start.9 = (bf16[1024,256]{1,0:T(8,128)(2,1)}, bf16[1024,256]{1,0:T(8,128)(2,1)}, u32[]{:S(2)}, u32[]{:S(2)}) collective-permute-start(bf16[1024,256]{1,0:T(8,128)(2,1)} %get-tuple-element.106), channel_id=1, source_target_pairs={{0,1},{1,0},{2,3},{3,2},{4,5},{5,4},{6,7},{7,6},{8,9},{9,8},{10,11... | collective-permute-start | bytes 1572872 | tf_op jit(solution)/shard_map/ppermute | solution.py:606
  270.2 17.6 %collective-permute-start.6 = (bf16[1,216,768]{2,1,0:T(8,128)(2,1)}, bf16[1,216,768]{2,1,0:T(8,128)(2,1)}, u32[]{:S(2)}, u32[]{:S(2)}) collective-permute-start(bf16[1,216,768]{2,1,0:T(8,128)(2,1)} %get-tuple-element.99.refs_20_), channel_id=1, source_target_pairs={{0,8},{4,12},{8,0},{12,4},{1,9},{5,13},{9,1},{13,5},{2,10},{6,14},... | collective-permute-start | bytes 995336 | tf_op jit(solution)/shard_map/ppermute | solution.py:606
  289.7 43.9 %all-to-all-start.3 = ((bf16[16,64,768]{2,1,0:T(8,128)(2,1)}), bf16[16,64,768]{2,1,0:T(8,128)(2,1)S(1)}, u32[]{:S(2)}, u32[]{:S(2)}) async-start(bf16[16,64,768]{2,1,0:T(8,128)(2,1)} %bitcast.67), calls=%async_computation.3 | async-start | bytes 3145728 | tf_op jit(solution)/shard_map/all_to_all | solution.py:869
  315.2 18.3 %collective-permute-start.17 = (bf16[4,2,48,1152]{3,2,1,0:T(8,128)(2,1)}, bf16[4,2,48,1152]{3,2,1,0:T(8,128)(2,1)S(1)}, u32[]{:S(2)}, u32[]{:S(2)}) collective-permute-start(bf16[4,2,48,1152]{3,2,1,0:T(8,128)(2,1)} %get-tuple-element.121.refs_1_), channel_id=1, source_target_pairs={{0,16},{1,3},{2,18},{3,1},{16,0},{17,19},{18,2},{19,17},{4,20},{5,... | collective-permute-start | bytes 2654216 | tf_op jit(solution)/shard_map/ppermute | solution.py:614
  322.7 10.2 %collective-permute-start.16 = (f32[2,11,384]{2,1,0:T(8,128)S(1)}, f32[2,11,384]{2,1,0:T(8,128)S(1)}, u32[]{:S(2)}, u32[]{:S(2)}) collective-permute-start(f32[2,11,384]{2,1,0:T(8,128)S(1)} %maximum_select_fusion.1), channel_id=1, source_target_pairs={{0,16},{16,0},{1,17},{17,1},{2,18},{18,2},{3,19},{19,3},{4,20},{20... | collective-permute-start | bytes 101384 | tf_op jit(solution)/shard_map/ppermute | solution.py:606
  339.3 8.6 %collective-permute-start.18 = (bf16[4,48,1152]{2,1,0:T(8,128)(2,1)}, bf16[4,48,1152]{2,1,0:T(8,128)(2,1)}, u32[]{:S(2)}, u32[]{:S(2)}) collective-permute-start(bf16[4,48,1152]{2,1,0:T(8,128)(2,1)} %get-tuple-element.124), channel_id=1, source_target_pairs={{0,2},{1,17},{2,0},{3,19},{16,18},{17,1},{18,16},{19,3},{4,6},{5,2... | collective-permute-start | bytes 1327112 | tf_op jit(solution)/shard_map/ppermute | solution.py:614
  350.7 11.6 %collective-permute-start.19 = (f32[4,11,384]{2,1,0:T(8,128)S(1)}, f32[4,11,384]{2,1,0:T(8,128)S(1)}, u32[]{:S(2)}, u32[]{:S(2)}) collective-permute-start(f32[4,11,384]{2,1,0:T(8,128)S(1)} %held.4), channel_id=1, source_target_pairs={{0,4},{4,8},{8,12},{12,0},{1,5},{5,9},{9,13},{13,1},{2,6},{6,10},{... | collective-permute-start | bytes 202760 | tf_op jit(solution)/shard_map/ppermute | solution.py:745
  351.0 12.6 %collective-permute-start.20 = (f32[4,11,384]{2,1,0:T(8,128)S(1)}, f32[4,11,384]{2,1,0:T(8,128)S(1)}, u32[]{:S(2)}, u32[]{:S(2)}) collective-permute-start(f32[4,11,384]{2,1,0:T(8,128)S(1)} %held.4), channel_id=1, source_target_pairs={{0,8},{4,12},{8,0},{12,4},{1,9},{5,13},{9,1},{13,5},{2,10},{6,14},... | collective-permute-start | bytes 202760 | tf_op jit(solution)/shard_map/ppermute | solution.py:745
  353.8 12.6 %collective-permute-start.21 = (f32[4,11,384]{2,1,0:T(8,128)S(1)}, f32[4,11,384]{2,1,0:T(8,128)S(1)}, u32[]{:S(2)}, u32[]{:S(2)}) collective-permute-start(f32[4,11,384]{2,1,0:T(8,128)S(1)} %held.4), channel_id=1, source_target_pairs={{0,12},{4,0},{8,4},{12,8},{1,13},{5,1},{9,5},{13,9},{2,14},{6,2},{... | collective-permute-start | bytes 202760 | tf_op jit(solution)/shard_map/ppermute | solution.py:745
  360.3 10.0 %collective-permute-start.25 = (bf16[216,768]{1,0:T(8,128)(2,1)S(1)}, bf16[216,768]{1,0:T(8,128)(2,1)S(1)}, u32[]{:S(2)}, u32[]{:S(2)}) collective-permute-start(bf16[216,768]{1,0:T(8,128)(2,1)S(1)} %held.5.refs_1_), channel_id=1, source_target_pairs={{0,16},{16,0},{1,17},{17,1},{2,18},{18,2},{3,19},{19,3},{4,20},{20... | collective-permute-start | bytes 995336 | tf_op jit(solution)/shard_map/ppermute | solution.py:606
  361.8 11.4 %collective-permute-start.22 = (bf16[48,1152]{1,0:T(8,128)(2,1)S(1)}, bf16[48,1152]{1,0:T(8,128)(2,1)S(1)}, u32[]{:S(2)}, u32[]{:S(2)}) collective-permute-start(bf16[48,1152]{1,0:T(8,128)(2,1)S(1)} %copy-done.36), channel_id=1, source_target_pairs={{0,4},{4,8},{8,12},{12,0},{1,5},{5,9},{9,13},{13,1},{2,6},{6,10},{... | collective-permute-start | bytes 331784 | tf_op jit(solution)/shard_map/ppermute | solution.py:745
  362.4 11.1 %collective-permute-start.23 = (bf16[48,1152]{1,0:T(8,128)(2,1)S(1)}, bf16[48,1152]{1,0:T(8,128)(2,1)S(1)}, u32[]{:S(2)}, u32[]{:S(2)}) collective-permute-start(bf16[48,1152]{1,0:T(8,128)(2,1)S(1)} %copy-done.35), channel_id=1, source_target_pairs={{0,8},{4,12},{8,0},{12,4},{1,9},{5,13},{9,1},{13,5},{2,10},{6,14},... | collective-permute-start | bytes 331784 | tf_op jit(solution)/shard_map/ppermute | solution.py:745
  363.6 9.8 %collective-permute-start.24 = (bf16[48,1152]{1,0:T(8,128)(2,1)S(1)}, bf16[48,1152]{1,0:T(8,128)(2,1)S(1)}, u32[]{:S(2)}, u32[]{:S(2)}) collective-permute-start(bf16[48,1152]{1,0:T(8,128)(2,1)S(1)} %copy-done.34), channel_id=1, source_target_pairs={{0,12},{4,0},{8,4},{12,8},{1,13},{5,1},{9,5},{13,9},{2,14},{6,2},{... | collective-permute-start | bytes 331784 | tf_op jit(solution)/shard_map/ppermute | solution.py:745
  375.9 6.1 %collective-permute-start.26 = (bf16[48,1152]{1,0:T(8,128)(2,1)}, bf16[48,1152]{1,0:T(8,128)(2,1)S(1)}, u32[]{:S(2)}, u32[]{:S(2)}) collective-permute-start(bf16[48,1152]{1,0:T(8,128)(2,1)} %last_add.1.refs_1_), channel_id=1, source_target_pairs={{0,16},{16,0},{1,17},{17,1},{2,18},{18,2},{3,19},{19,3},{4,20},{20... | collective-permute-start | bytes 331784 | tf_op jit(solution)/shard_map/ppermute | solution.py:606
  (45 other events, 220.7 us)

commit v7 on v6

--- a/solution.py
+++ b/solution.py
@@ -26,7 +26,7 @@
 VM_QKV = 62
 COST = 50
 DOWN_TILE = 768
-MLP_BLOCK = 256
+MLP_BLOCK = 512
 MLP_SPLIT = 1
 
 
@@ -943,7 +943,7 @@
         got = cross(sent, 0)
         deps = (sent,)
     pairs = width // 128
-    plan = [pairs // 2, (pairs + 1) // 3, pairs - pairs // 2 - (pairs + 1) // 3]
+    plan = [pairs - 2, 1, 1]
     for at, size in enumerate(plan):
         dq, dk0, dk1, dv0, dv1 = attend_back(
             queries, kv_own, kv_peer, grad_att, attended32, lse, frames, pair, size, deps

time: 389 us -> 383 us (0.985)
  waiting for transfers between devices: 87.3 us -> 81.5 us
    ppermute x4, waiting for transfers between devices: 18 us -> 13.9 us  [cross(): return lax.ppermute(value, ('lat', 'yy', 'core'), pairs)]
  transfers between devices with their start and end apart: 31 -> 31, of which waited for: 16 -> 18; matrix products, arithmetic and copies ran while one was open for 5% -> 5% of each run, Pallas kernels for 36% -> 37%
where the time goes in v7:
time: 383 us; the launch traced here: 378 us
  Pallas kernels  216 us (56%)
  waiting for transfers between devices  81.5 us (21%)
  starting transfers between devices  46.9 us (12%)
  local copies, waits for them, and re-layouts  26.1 us (7%)
    pallas_call x23, Pallas kernels, call(): pl.pallas_call(body, grid=grid, in_specs=[spec for a, spec in ins] + [any...  214 us
    all_to_all x2, waiting for transfers between devices, to_frames(): value = lax.all_to_all(value, ('lat', 'zed', 'yy'), 0, 0, tiled=True)  35.2 us
    ppermute x17, waiting for transfers between devices, swap(): return lax.ppermute(value, axis, swap_pairs(lax.axis_size(axis), bit))  32.4 us
    ppermute x4, waiting for transfers between devices, cross(): return lax.ppermute(value, ('lat', 'yy', 'core'), pairs)  13.9 us
    all_to_all x2, starting transfers between devices, to_frames(): value = lax.all_to_all(value, ('lat', 'zed', 'yy'), 0, 0, tiled=True)  12.7 us
    ppermute x17, starting transfers between devices, swap(): return lax.ppermute(value, axis, swap_pairs(lax.axis_size(axis), bit))  9.87 us
    all_to_all x2, starting transfers between devices, to_places(): return lax.all_to_all(value, ('lat', 'zed', 'yy'), 0, 0, tiled=True)  9.45 us
    unnamed x76, local copies, waits for them, and re-layouts  9.2 us
  transfers between devices with their start and end apart: 31, of which 18 were waited for; matrix products, arithmetic and copies ran while one was open for 5% of the time, Pallas kernels for 37%

profile of v7, /device:TPU:0, one launch (start us, length us, event | category | flops | bytes accessed | tf_op | source)
XLA Modules:
  0.0 378.2 jit_solution(17626927912937644905)
XLA Ops:
  4.4 8.5 %all-to-all-start = ((bf16[16,64,768]{2,1,0:T(8,128)(2,1)}), bf16[16,64,768]{2,1,0:T(8,128)(2,1)S(1)}, u32[]{:S(2)}, u32[]{:S(2)}) async-start(bf16[16,64,768]{2,1,0:T(8,128)(2,1)} %reshape.184), calls=%async_computation | async-start | bytes 3145728 | tf_op jit(solution)/shard_map/all_to_all | solution.py:857
  19.9 29.7 %all-to-all-done = bf16[16,64,768]{2,1,0:T(8,128)(2,1)S(1)} async-done(((bf16[16,64,768]{2,1,0:T(8,128)(2,1)}), bf16[16,64,768]{2,1,0:T(8,128)(2,1)S(1)}, u32[]{:S(2)}, u32[]{:S(2)}) %all-to-all-start) | async-done | bytes 1572896 | tf_op jit(solution)/shard_map/all_to_all | solution.py:857
  50.7 8.3 %qkv.1 = (bf16[1024,768]{1,0:T(8,128)(2,1)}, bf16[1024,1536]{1,0:T(8,128)(2,1)}, bf16[1024,768]{1,0:T(8,128)(2,1)}) custom-call(bf16[1024,768]{1,0:T(8,128)(2,1)} %bitcast.62, f32[1,1,768]{2,1,0:T(1,128)} %convolution_bitcast_fusion.1.refs_1_.refs_16_, f32[1,1,768]{2,1,0:T(1,128)} %broadcast_in_dim.35.refs_2_, f32[1,768]{1,0:T(1,128)} %reshape.206.refs_3_.refs_17_, ...), custom_call_target="tpu_custom_call" | custom-call | flops 72000000 | bytes 228249 | tf_op jit(solution)/shard_map/qkv/pallas_call | solution.py:54
  59.1 4.2 %all-to-all-start.1 = ((bf16[16,64,768]{2,1,0:T(8,128)(2,1)}), bf16[16,64,768]{2,1,0:T(8,128)(2,1)S(1)}, u32[]{:S(2)}, u32[]{:S(2)}) async-start(bf16[16,64,768]{2,1,0:T(8,128)(2,1)} %reshape.187.refs_5_), calls=%async_computation.1 | async-start | bytes 3145728 | tf_op jit(solution)/shard_map/all_to_all | solution.py:857
  65.1 29.8 %attend.1 = (bf16[1024,768]{1,0:T(8,128)(2,1)}, f32[1024,768]{1,0:T(8,128)}, f32[1024,768]{1,0:T(8,128)}) custom-call(bf16[1024,768]{1,0:T(8,128)(2,1)} %get-tuple-element.74.refs_0_, bf16[1024,1536]{1,0:T(8,128)(2,1)} %get-tuple-element.75.refs_1_.refs_3_, bf16[1024,1536]{1,0:T(8,128)(2,1)} %collective-permute-done.refs_2_.refs_4_, ...), custom_call_target="tpu_custom_call" | custom-call | flops 600000000 | bytes 440401 | tf_op jit(solution)/shard_map/attend/pallas_call | solution.py:54
  94.9 5.5 %all-to-all-done.1 = bf16[16,64,768]{2,1,0:T(8,128)(2,1)S(1)} async-done(((bf16[16,64,768]{2,1,0:T(8,128)(2,1)}), bf16[16,64,768]{2,1,0:T(8,128)(2,1)S(1)}, u32[]{:S(2)}, u32[]{:S(2)}) %all-to-all-start.1) | async-done | bytes 1572896 | tf_op jit(solution)/shard_map/all_to_all | solution.py:857
  101.5 37.4 %mlp.1 = (bf16[1024,768]{1,0:T(8,128)(2,1)}, bf16[1024,3072]{1,0:T(8,128)(2,1)}, bf16[1024,3072]{1,0:T(8,128)(2,1)}, bf16[1024,768]{1,0:T(8,128)(2,1)}, f32[1024...) custom-call(bf16[1024,768]{1,0:T(8,128)(2,1)} %bitcast.63, ...), custom_call_target="tpu_custom_call" | custom-call | flops 500000000 | bytes 748154 | tf_op jit(solution)/shard_map/mlp/pallas_call | solution.py:54
  138.9 12.5 %up_grad.1 = (bf16[8,48,3840]{2,1,0:T(8,128)(2,1)}, bf16[8,48,3840]{2,1,0:T(8,128)(2,1)}) custom-call(s32[1]{0:T(128)} %bitcast.11.refs_0_, bf16[1024,768]{1,0:T(8,128)(2,1)} %get-tuple-element.79.refs_1_, bf16[1024,3072]{1,0:T(8,128)(2,1)} %get-tuple-element.80.refs_2_, bf16[1024,768]{1,0:T(8,128)(2,1)} %get-tuple-element.76.refs_2_.refs_3_, ...), custom_call_target="tpu_custom_call" | custom-call | flops 120000000 | bytes 338165 | tf_op jit(solution)/shard_map/up_grad/pallas_call | solution.py:54
  151.4 9.4 %down_grad.1 = (bf16[8,192,768]{2,1,0:T(8,128)(2,1)}, bf16[8,192,768]{2,1,0:T(8,128)(2,1)}) custom-call(s32[1]{0:T(128)} %bitcast.11.refs_0_, bf16[1024,3072]{1,0:T(8,128)(2,1)} %get-tuple-element.78.refs_1_, bf16[1024,768]{1,0:T(8,128)(2,1)} %bitcast.66, bf16[8,48,3840]{2,1,0:T(8,128)(2,1)} %get-tuple-element.82.refs_3_), custom_call_target="tpu_custom_call" | custom-call | flops 96000000 | bytes 251658 | tf_op jit(solution)/shard_map/down_grad/pallas_call | solution.py:54
  161.9 3.9 %collective-permute-done.1.refs_2_ = bf16[8,192,768]{2,1,0:T(8,128)(2,1)} collective-permute-done((bf16[8,192,768]{2,1,0:T(8,128)(2,1)}, bf16[8,192,768]{2,1,0:T(8,128)(2,1)}, u32[]{:S(2)}, u32[]{:S(2)}) %collective-permute-start.1) | collective-permute-done | bytes 2359328 | tf_op jit(solution)/shard_map/ppermute | solution.py:606
  165.8 7.1 %first_add.2 = (bf16[4,2,216,768]{3,2,1,0:T(8,128)(2,1)}, bf16[4,2,216,768]{3,2,1,0:T(8,128)(2,1)}) custom-call(s32[2]{0:T(128)} %pad_add_fusion.refs_0_, bf16[8,192,768]{2,1,0:T(8,128)(2,1)} %get-tuple-element.83.refs_1_, bf16[8,192,768]{2,1,0:T(8,128)(2,1)} %collective-permute-done.1.refs_2_, bf16[8,48,3840]{2,1,0:T(8,128)(2,1)} %get-tuple-element.85.refs_3_, ...), custom_call_target="tpu_custom_call" | custom-call | bytes 318505 | tf_op jit(solution)/shard_map/first_add/pallas_call | solution.py:54
  178.2 39.7 %attend_back.3 = (bf16[1024,512]{1,0:T(8,128)(2,1)}, bf16[1024,512]{1,0:T(8,128)(2,1)}, bf16[1024,512]{1,0:T(8,128)(2,1)}, bf16[1024,512]{1,0:T(8,128)(2,1)}, bf16[1024,512]{1,0:T(8,128)(2,1)}) custom-call(bf16[1024,768]{1,0:T(8,128)(2,1)} %get-tuple-element.74.refs_0_, bf16[1024,1536]{1,0:T(8,128)(2,1)} %get-tuple-element.75.refs_1_.refs_3_, ...), custom_call_target="tpu_custom_call" | custom-call | flops 880000000 | bytes 545259 | tf_op jit(solution)/shard_map/attend_back/pallas_call | solution.py:54
  219.9 4.8 %second_add.2 = (bf16[4,216,768]{2,1,0:T(8,128)(2,1)}, bf16[4,216,768]{2,1,0:T(8,128)(2,1)}) custom-call(s32[1]{0:T(128)S(6)} %select_n.78.refs_0_, bf16[4,2,216,768]{3,2,1,0:T(8,128)(2,1)} %get-tuple-element.86.refs_1_, bf16[4,2,216,768]{3,2,1,0:T(8,128)(2,1)} %collective-permute-done.3.refs_2_, ...), custom_call_target="tpu_custom_call" | custom-call | bytes 159252 | tf_op jit(solution)/shard_map/second_add/pallas_call | solution.py:54
  225.8 11.7 %attend_back.4 = (bf16[1024,128]{1,0:T(8,128)(2,1)}, bf16[1024,128]{1,0:T(8,128)(2,1)}, bf16[1024,128]{1,0:T(8,128)(2,1)}, bf16[1024,128]{1,0:T(8,128)(2,1)}, bf16[1024,128]{1,0:T(8,128)(2,1)}) custom-call(bf16[1024,768]{1,0:T(8,128)(2,1)} %get-tuple-element.74.refs_0_, bf16[1024,1536]{1,0:T(8,128)(2,1)} %get-tuple-element.75.refs_1_.refs_3_, ...), custom_call_target="tpu_custom_call" | custom-call | flops 220000000 | bytes 466616 | tf_op jit(solution)/shard_map/attend_back/pallas_call | solution.py:54
  237.6 5.3 %collective-permute-done.4.refs_2_ = bf16[4,216,768]{2,1,0:T(8,128)(2,1)} collective-permute-done((bf16[4,216,768]{2,1,0:T(8,128)(2,1)}, bf16[4,216,768]{2,1,0:T(8,128)(2,1)}, u32[]{:S(2)}, u32[]{:S(2)}) %collective-permute-start.4) | collective-permute-done | bytes 1327136 | tf_op jit(solution)/shard_map/ppermute | solution.py:614
  247.9 11.8 %attend_back.5 = (bf16[1024,128]{1,0:T(8,128)(2,1)}, bf16[1024,128]{1,0:T(8,128)(2,1)}, bf16[1024,128]{1,0:T(8,128)(2,1)}, bf16[1024,128]{1,0:T(8,128)(2,1)}, bf16[1024,128]{1,0:T(8,128)(2,1)}) custom-call(bf16[1024,768]{1,0:T(8,128)(2,1)} %get-tuple-element.74.refs_0_, bf16[1024,1536]{1,0:T(8,128)(2,1)} %get-tuple-element.75.refs_1_.refs_3_, ...), custom_call_target="tpu_custom_call" | custom-call | flops 220000000 | bytes 466616 | tf_op jit(solution)/shard_map/attend_back/pallas_call | solution.py:54
  268.3 10.5 %first_back.1 = (bf16[1024,768]{1,0:T(8,128)(2,1)}, f32[1,2,768]{2,1,0:T(2,128)}, f32[1,768]{1,0:T(1,128)}) custom-call(bf16[1024,512]{1,0:T(8,128)(2,1)} %get-tuple-element.91.refs_3_.refs_9_.refs_0_.refs_2_, bf16[1024,512]{1,0:T(8,128)(2,1)} %get-tuple-element.100.refs_1_.refs_3_, bf16[1024,512]{1,0:T(8,128)(2,1)} %get-tuple-element.101.refs_2_.refs_4_, ...), custom_call_target="tpu_custom_call" | custom-call | flops 72000000 | bytes 354201 | tf_op jit(solution)/shard_map/first_back/pallas_call | solution.py:54
  282.0 5.5 %all-to-all-start.3 = ((bf16[16,64,768]{2,1,0:T(8,128)(2,1)}), bf16[16,64,768]{2,1,0:T(8,128)(2,1)S(1)}, u32[]{:S(2)}, u32[]{:S(2)}) async-start(bf16[16,64,768]{2,1,0:T(8,128)(2,1)} %bitcast.67), calls=%async_computation.3 | async-start | bytes 3145728 | tf_op jit(solution)/shard_map/all_to_all | solution.py:869
  290.1 10.4 %qkv_grad.1 = (bf16[8,48,2304]{2,1,0:T(8,128)(2,1)}, bf16[8,48,2304]{2,1,0:T(8,128)(2,1)}) custom-call(s32[1]{0:T(128)} %bitcast.11.refs_0_, bf16[1024,768]{1,0:T(8,128)(2,1)} %get-tuple-element.118.refs_1_, bf16[1024,512]{1,0:T(8,128)(2,1)} %get-tuple-element.91.refs_3_.refs_9_.refs_0_.refs_2_, bf16[1024,512]{1,0:T(8,128)(2,1)} %get-tuple-element.100.refs_1_.refs_3_, ...), custom_call_target="tpu_custom_call" | custom-call | flops 72000000 | bytes 259522 | tf_op jit(solution)/shard_map/qkv_grad/pallas_call | solution.py:54
  304.5 4.2 %first_add.3 = (bf16[4,2,48,1152]{3,2,1,0:T(8,128)(2,1)}, bf16[4,2,48,1152]{3,2,1,0:T(8,128)(2,1)}) custom-call(s32[2]{0:T(128)} %pad_add_fusion.refs_0_, bf16[8,48,2304]{2,1,0:T(8,128)(2,1)} %get-tuple-element.119.refs_1_, bf16[8,48,2304]{2,1,0:T(8,128)(2,1)} %collective-permute-done.14.refs_2_), custom_call_target="tpu_custom_call" | custom-call | bytes 106168 | tf_op jit(solution)/shard_map/first_add/pallas_call | solution.py:54
  316.4 10.3 %collective-permute-done.16 = f32[2,11,384]{2,1,0:T(8,128)S(1)} collective-permute-done((f32[2,11,384]{2,1,0:T(8,128)S(1)}, f32[2,11,384]{2,1,0:T(8,128)S(1)}, u32[]{:S(2)}, u32[]{:S(2)}) %collective-permute-start.16) | collective-permute-done | bytes 33824 | tf_op jit(solution)/shard_map/ppermute | solution.py:606
  335.1 6.6 %collective-permute-done.18.refs_2_ = bf16[4,48,1152]{2,1,0:T(8,128)(2,1)} collective-permute-done((bf16[4,48,1152]{2,1,0:T(8,128)(2,1)}, bf16[4,48,1152]{2,1,0:T(8,128)(2,1)}, u32[]{:S(2)}, u32[]{:S(2)}) %collective-permute-start.18) | collective-permute-done | bytes 442400 | tf_op jit(solution)/shard_map/ppermute | solution.py:614
  349.8 3.9 %reshape.197 = bf16[16,16,4,768]{3,2,1,0:T(4,128)(2,1)} reshape(bf16[16,64,768]{2,1,0:T(8,128)(2,1)} %copy-done.11) | data formatting | bytes 3145728 | tf_op jit(solution)/shard_map/reshape | solution.py:1031
  371.3 4.4 %collective-permute-done.26.refs_2_ = bf16[48,1152]{1,0:T(8,128)(2,1)S(1)} collective-permute-done((bf16[48,1152]{1,0:T(8,128)(2,1)}, bf16[48,1152]{1,0:T(8,128)(2,1)S(1)}, u32[]{:S(2)}, u32[]{:S(2)}) %collective-permute-start.26) | collective-permute-done | bytes 110624 | tf_op jit(solution)/shard_map/ppermute | solution.py:606
  (183 shorter events, 91.6 us)
Async XLA Ops:
  4.4 45.2 %all-to-all-start = ((bf16[16,64,768]{2,1,0:T(8,128)(2,1)}), bf16[16,64,768]{2,1,0:T(8,128)(2,1)S(1)}, u32[]{:S(2)}, u32[]{:S(2)}) async-start(bf16[16,64,768]{2,1,0:T(8,128)(2,1)} %reshape.184), calls=%async_computation | async-start | bytes 3145728 | tf_op jit(solution)/shard_map/all_to_all | solution.py:857
  59.1 6.1 %collective-permute-start = (bf16[1024,1536]{1,0:T(8,128)(2,1)}, bf16[1024,1536]{1,0:T(8,128)(2,1)}, u32[]{:S(2)}, u32[]{:S(2)}) collective-permute-start(bf16[1024,1536]{1,0:T(8,128)(2,1)} %get-tuple-element.75.refs_1_.refs_3_), channel_id=1, source_target_pairs={{0,1},{1,0},{2,3},{3,2},{4,5},{5,4},{6,7},{7,6},{8,9},{9,8},{10,11... | collective-permute-start | bytes 9437192 | tf_op jit(solution)/shard_map/ppermute | solution.py:606
  59.1 41.2 %all-to-all-start.1 = ((bf16[16,64,768]{2,1,0:T(8,128)(2,1)}), bf16[16,64,768]{2,1,0:T(8,128)(2,1)S(1)}, u32[]{:S(2)}, u32[]{:S(2)}) async-start(bf16[16,64,768]{2,1,0:T(8,128)(2,1)} %reshape.187.refs_5_), calls=%async_computation.1 | async-start | bytes 3145728 | tf_op jit(solution)/shard_map/all_to_all | solution.py:857
  151.4 14.4 %collective-permute-start.2 = (bf16[8,48,3840]{2,1,0:T(8,128)(2,1)}, bf16[8,48,3840]{2,1,0:T(8,128)(2,1)}, u32[]{:S(2)}, u32[]{:S(2)}) collective-permute-start(bf16[8,48,3840]{2,1,0:T(8,128)(2,1)} %get-tuple-element.82.refs_3_), channel_id=1, source_target_pairs={{0,1},{1,0},{2,3},{3,2},{4,5},{5,4},{6,7},{7,6},{8,9},{9,8},{10,11... | collective-permute-start | bytes 8847368 | tf_op jit(solution)/shard_map/ppermute | solution.py:606
  160.8 5.0 %collective-permute-start.1 = (bf16[8,192,768]{2,1,0:T(8,128)(2,1)}, bf16[8,192,768]{2,1,0:T(8,128)(2,1)}, u32[]{:S(2)}, u32[]{:S(2)}) collective-permute-start(bf16[8,192,768]{2,1,0:T(8,128)(2,1)} %get-tuple-element.84), channel_id=1, source_target_pairs={{0,1},{1,0},{2,3},{3,2},{4,5},{5,4},{6,7},{7,6},{8,9},{9,8},{10,11... | collective-permute-start | bytes 7077896 | tf_op jit(solution)/shard_map/ppermute | solution.py:606
  172.9 47.1 %collective-permute-start.3 = (bf16[4,2,216,768]{3,2,1,0:T(8,128)(2,1)}, bf16[4,2,216,768]{3,2,1,0:T(8,128)(2,1)}, u32[]{:S(2)}, u32[]{:S(2)}) collective-permute-start(bf16[4,2,216,768]{3,2,1,0:T(8,128)(2,1)} %get-tuple-element.87.refs_8_), channel_id=1, source_target_pairs={{0,16},{1,3},{2,18},{3,1},{16,0},{17,19},{18,2},{19,17},{4,20},{5,... | collective-permute-start | bytes 7962632 | tf_op jit(solution)/shard_map/ppermute | solution.py:614
  174.3 92.0 %all-to-all-start.2 = ((bf16[16,64,768]{2,1,0:T(8,128)(2,1)}), bf16[16,64,768]{2,1,0:T(8,128)(2,1)S(1)}, u32[]{:S(2)}, u32[]{:S(2)}) async-start(bf16[16,64,768]{2,1,0:T(8,128)(2,1)} %bitcast.68), calls=%async_computation.2 | async-start | bytes 3145728 | tf_op jit(solution)/shard_map/all_to_all | solution.py:869
  224.7 18.2 %collective-permute-start.4 = (bf16[4,216,768]{2,1,0:T(8,128)(2,1)}, bf16[4,216,768]{2,1,0:T(8,128)(2,1)}, u32[]{:S(2)}, u32[]{:S(2)}) collective-permute-start(bf16[4,216,768]{2,1,0:T(8,128)(2,1)} %get-tuple-element.93.refs_8_), channel_id=1, source_target_pairs={{0,2},{1,17},{2,0},{3,19},{16,18},{17,1},{18,16},{19,3},{4,6},{5,2... | collective-permute-start | bytes 3981320 | tf_op jit(solution)/shard_map/ppermute | solution.py:614
  225.3 40.5 %collective-permute-start.7 = (bf16[1024,512]{1,0:T(8,128)(2,1)}, bf16[1024,512]{1,0:T(8,128)(2,1)}, u32[]{:S(2)}, u32[]{:S(2)}) collective-permute-start(bf16[1024,512]{1,0:T(8,128)(2,1)} %get-tuple-element.102), channel_id=1, source_target_pairs={{0,1},{1,0},{2,3},{3,2},{4,5},{5,4},{6,7},{7,6},{8,9},{9,8},{10,11... | collective-permute-start | bytes 3145736 | tf_op jit(solution)/shard_map/ppermute | solution.py:606
  225.5 40.3 %collective-permute-start.8 = (bf16[1024,512]{1,0:T(8,128)(2,1)}, bf16[1024,512]{1,0:T(8,128)(2,1)}, u32[]{:S(2)}, u32[]{:S(2)}) collective-permute-start(bf16[1024,512]{1,0:T(8,128)(2,1)} %get-tuple-element.103), channel_id=1, source_target_pairs={{0,1},{1,0},{2,3},{3,2},{4,5},{5,4},{6,7},{7,6},{8,9},{9,8},{10,11... | collective-permute-start | bytes 3145736 | tf_op jit(solution)/shard_map/ppermute | solution.py:606
  245.9 16.1 %collective-permute-start.5 = (bf16[2,216,768]{2,1,0:T(8,128)(2,1)}, bf16[2,216,768]{2,1,0:T(8,128)(2,1)}, u32[]{:S(2)}, u32[]{:S(2)}) collective-permute-start(bf16[2,216,768]{2,1,0:T(8,128)(2,1)} %get-tuple-element.96.refs_8_), channel_id=1, source_target_pairs={{0,4},{4,0},{8,12},{12,8},{1,5},{5,1},{9,13},{13,9},{2,6},{6,2},{1... | collective-permute-start | bytes 1990664 | tf_op jit(solution)/shard_map/ppermute | solution.py:606
  264.1 16.0 %collective-permute-start.6 = (bf16[1,216,768]{2,1,0:T(8,128)(2,1)}, bf16[1,216,768]{2,1,0:T(8,128)(2,1)}, u32[]{:S(2)}, u32[]{:S(2)}) collective-permute-start(bf16[1,216,768]{2,1,0:T(8,128)(2,1)} %get-tuple-element.99.refs_20_), channel_id=1, source_target_pairs={{0,8},{4,12},{8,0},{12,4},{1,9},{5,13},{9,1},{13,5},{2,10},{6,14},... | collective-permute-start | bytes 995336 | tf_op jit(solution)/shard_map/ppermute | solution.py:606
  282.0 45.4 %all-to-all-start.3 = ((bf16[16,64,768]{2,1,0:T(8,128)(2,1)}), bf16[16,64,768]{2,1,0:T(8,128)(2,1)S(1)}, u32[]{:S(2)}, u32[]{:S(2)}) async-start(bf16[16,64,768]{2,1,0:T(8,128)(2,1)} %bitcast.67), calls=%async_computation.3 | async-start | bytes 3145728 | tf_op jit(solution)/shard_map/all_to_all | solution.py:869
  308.7 18.6 %collective-permute-start.17 = (bf16[4,2,48,1152]{3,2,1,0:T(8,128)(2,1)}, bf16[4,2,48,1152]{3,2,1,0:T(8,128)(2,1)S(1)}, u32[]{:S(2)}, u32[]{:S(2)}) collective-permute-start(bf16[4,2,48,1152]{3,2,1,0:T(8,128)(2,1)} %get-tuple-element.121.refs_1_), channel_id=1, source_target_pairs={{0,16},{1,3},{2,18},{3,1},{16,0},{17,19},{18,2},{19,17},{4,20},{5,... | collective-permute-start | bytes 2654216 | tf_op jit(solution)/shard_map/ppermute | solution.py:614
  316.2 10.5 %collective-permute-start.16 = (f32[2,11,384]{2,1,0:T(8,128)S(1)}, f32[2,11,384]{2,1,0:T(8,128)S(1)}, u32[]{:S(2)}, u32[]{:S(2)}) collective-permute-start(f32[2,11,384]{2,1,0:T(8,128)S(1)} %maximum_select_fusion.1), channel_id=1, source_target_pairs={{0,16},{16,0},{1,17},{17,1},{2,18},{18,2},{3,19},{19,3},{4,20},{20... | collective-permute-start | bytes 101384 | tf_op jit(solution)/shard_map/ppermute | solution.py:606
  333.1 8.6 %collective-permute-start.18 = (bf16[4,48,1152]{2,1,0:T(8,128)(2,1)}, bf16[4,48,1152]{2,1,0:T(8,128)(2,1)}, u32[]{:S(2)}, u32[]{:S(2)}) collective-permute-start(bf16[4,48,1152]{2,1,0:T(8,128)(2,1)} %get-tuple-element.124), channel_id=1, source_target_pairs={{0,2},{1,17},{2,0},{3,19},{16,18},{17,1},{18,16},{19,3},{4,6},{5,2... | collective-permute-start | bytes 1327112 | tf_op jit(solution)/shard_map/ppermute | solution.py:614
  344.6 11.6 %collective-permute-start.19 = (f32[4,11,384]{2,1,0:T(8,128)S(1)}, f32[4,11,384]{2,1,0:T(8,128)S(1)}, u32[]{:S(2)}, u32[]{:S(2)}) collective-permute-start(f32[4,11,384]{2,1,0:T(8,128)S(1)} %held.4), channel_id=1, source_target_pairs={{0,4},{4,8},{8,12},{12,0},{1,5},{5,9},{9,13},{13,1},{2,6},{6,10},{... | collective-permute-start | bytes 202760 | tf_op jit(solution)/shard_map/ppermute | solution.py:745
  344.6 13.1 %collective-permute-start.20 = (f32[4,11,384]{2,1,0:T(8,128)S(1)}, f32[4,11,384]{2,1,0:T(8,128)S(1)}, u32[]{:S(2)}, u32[]{:S(2)}) collective-permute-start(f32[4,11,384]{2,1,0:T(8,128)S(1)} %held.4), channel_id=1, source_target_pairs={{0,8},{4,12},{8,0},{12,4},{1,9},{5,13},{9,1},{13,5},{2,10},{6,14},... | collective-permute-start | bytes 202760 | tf_op jit(solution)/shard_map/ppermute | solution.py:745
  347.6 13.0 %collective-permute-start.21 = (f32[4,11,384]{2,1,0:T(8,128)S(1)}, f32[4,11,384]{2,1,0:T(8,128)S(1)}, u32[]{:S(2)}, u32[]{:S(2)}) collective-permute-start(f32[4,11,384]{2,1,0:T(8,128)S(1)} %held.4), channel_id=1, source_target_pairs={{0,12},{4,0},{8,4},{12,8},{1,13},{5,1},{9,5},{13,9},{2,14},{6,2},{... | collective-permute-start | bytes 202760 | tf_op jit(solution)/shard_map/ppermute | solution.py:745
  353.8 10.5 %collective-permute-start.25 = (bf16[216,768]{1,0:T(8,128)(2,1)S(1)}, bf16[216,768]{1,0:T(8,128)(2,1)S(1)}, u32[]{:S(2)}, u32[]{:S(2)}) collective-permute-start(bf16[216,768]{1,0:T(8,128)(2,1)S(1)} %held.5.refs_1_), channel_id=1, source_target_pairs={{0,16},{16,0},{1,17},{17,1},{2,18},{18,2},{3,19},{19,3},{4,20},{20... | collective-permute-start | bytes 995336 | tf_op jit(solution)/shard_map/ppermute | solution.py:606
  355.6 11.7 %collective-permute-start.22 = (bf16[48,1152]{1,0:T(8,128)(2,1)S(1)}, bf16[48,1152]{1,0:T(8,128)(2,1)S(1)}, u32[]{:S(2)}, u32[]{:S(2)}) collective-permute-start(bf16[48,1152]{1,0:T(8,128)(2,1)S(1)} %copy-done.36), channel_id=1, source_target_pairs={{0,4},{4,8},{8,12},{12,0},{1,5},{5,9},{9,13},{13,1},{2,6},{6,10},{... | collective-permute-start | bytes 331784 | tf_op jit(solution)/shard_map/ppermute | solution.py:745
  356.2 11.1 %collective-permute-start.23 = (bf16[48,1152]{1,0:T(8,128)(2,1)S(1)}, bf16[48,1152]{1,0:T(8,128)(2,1)S(1)}, u32[]{:S(2)}, u32[]{:S(2)}) collective-permute-start(bf16[48,1152]{1,0:T(8,128)(2,1)S(1)} %copy-done.35), channel_id=1, source_target_pairs={{0,8},{4,12},{8,0},{12,4},{1,9},{5,13},{9,1},{13,5},{2,10},{6,14},... | collective-permute-start | bytes 331784 | tf_op jit(solution)/shard_map/ppermute | solution.py:745
  357.7 9.6 %collective-permute-start.24 = (bf16[48,1152]{1,0:T(8,128)(2,1)S(1)}, bf16[48,1152]{1,0:T(8,128)(2,1)S(1)}, u32[]{:S(2)}, u32[]{:S(2)}) collective-permute-start(bf16[48,1152]{1,0:T(8,128)(2,1)S(1)} %copy-done.34), channel_id=1, source_target_pairs={{0,12},{4,0},{8,4},{12,8},{1,13},{5,1},{9,5},{13,9},{2,14},{6,2},{... | collective-permute-start | bytes 331784 | tf_op jit(solution)/shard_map/ppermute | solution.py:745
  369.8 5.9 %collective-permute-start.26 = (bf16[48,1152]{1,0:T(8,128)(2,1)}, bf16[48,1152]{1,0:T(8,128)(2,1)S(1)}, u32[]{:S(2)}, u32[]{:S(2)}) collective-permute-start(bf16[48,1152]{1,0:T(8,128)(2,1)} %last_add.1.refs_1_), channel_id=1, source_target_pairs={{0,16},{16,0},{1,17},{17,1},{2,18},{18,2},{3,19},{19,3},{4,20},{20... | collective-permute-start | bytes 331784 | tf_op jit(solution)/shard_map/ppermute | solution.py:606
  (45 other events, 220.0 us)

commit v8 on v7

--- a/solution.py
+++ b/solution.py
@@ -766,24 +766,21 @@
     )[0]
 
 
-def add_and_pass(kept, got, passed):
-    rows, cols = kept.shape
-
-    def kernel(kept_ref, got_ref, passed_ref, out_ref, same_ref):
-        out_ref[...] = both(kept_ref, got_ref, Ellipsis)
-
-    spec = whole_of((rows, cols))
+def passed_after(value, deps):
+    def kernel(*refs):
+        pass
+
     anywhere = pl.BlockSpec(memory_space=pl.ANY)
     return pl.pallas_call(
         kernel,
         grid=(1,),
-        in_specs=[spec, spec, anywhere],
-        out_specs=[spec, anywhere],
-        out_shape=[sds((rows, cols), BF), sds(passed.shape, passed.dtype)],
-        input_output_aliases={2: 1},
+        in_specs=[anywhere] * (1 + len(deps)),
+        out_specs=anywhere,
+        out_shape=sds(value.shape, value.dtype),
+        input_output_aliases={0: 0},
         compiler_params=pltpu.CompilerParams(vmem_limit_bytes=VM_SUM << 20),
-        name="add_and_pass",
-    )(kept, got, passed)
+        name="passed_after",
+    )(value, *deps)
 
 
 def spread(mine, other, shapes, fill, deps=()):
@@ -970,7 +967,8 @@
         pieces, x, chan_add, gain1, grad_middle, qkv_weight, frames, deps
     )
     if staged:
-        mlp_sum, grad_start = add_and_pass(*mlp_parts, grad_start)
+        grad_start = passed_after(grad_start, (mlp_parts[1],))
+        mlp_sum = last_add(mlp_parts, (grad_start,))
     grad_patch = to_places(grad_start, chips, frames_all)
 
     ups = wide // width

time: 383 us -> 381 us (level)
    pallas_call x23 -> x24, Pallas kernels: 214 us -> 216 us  [call(): pl.pallas_call(body, grid=grid, in_specs=[spec for a, spec in ins] + [any...]
    unnamed x76 -> x72, local copies, waits for them, and re-layouts: 9.2 us -> 9.97 us
  transfers between devices with their start and end apart: 31 -> 31, of which waited for: 18 -> 19; matrix products, arithmetic and copies ran while one was open for 5% -> 5% of each run, Pallas kernels for 37% -> 38%
where the time goes in v8:
time: 381 us; the launch traced here: 377 us
  Pallas kernels  216 us (57%)
  waiting for transfers between devices  81.9 us (21%)
  starting transfers between devices  46.8 us (12%)
  local copies, waits for them, and re-layouts  24.3 us (6%)
    pallas_call x24, Pallas kernels, call(): pl.pallas_call(body, grid=grid, in_specs=[spec for a, spec in ins] + [any...  216 us
    all_to_all x2, waiting for transfers between devices, to_frames(): value = lax.all_to_all(value, ('lat', 'zed', 'yy'), 0, 0, tiled=True)  35.1 us
    ppermute x17, waiting for transfers between devices, swap(): return lax.ppermute(value, axis, swap_pairs(lax.axis_size(axis), bit))  32.6 us
    ppermute x4, waiting for transfers between devices, cross(): return lax.ppermute(value, ('lat', 'yy', 'core'), pairs)  13.9 us
    all_to_all x2, starting transfers between devices, to_frames(): value = lax.all_to_all(value, ('lat', 'zed', 'yy'), 0, 0, tiled=True)  12.7 us
    unnamed x72, local copies, waits for them, and re-layouts  9.97 us
    ppermute x17, starting transfers between devices, swap(): return lax.ppermute(value, axis, swap_pairs(lax.axis_size(axis), bit))  9.86 us
    all_to_all x2, starting transfers between devices, to_places(): return lax.all_to_all(value, ('lat', 'zed', 'yy'), 0, 0, tiled=True)  9.44 us
  transfers between devices with their start and end apart: 31, of which 19 were waited for; matrix products, arithmetic and copies ran while one was open for 5% of the time, Pallas kernels for 38%

profile of v8, /device:TPU:0, one launch (start us, length us, event | category | flops | bytes accessed | tf_op | source)
XLA Modules:
  0.0 376.9 jit_solution(4288012017986774644)
XLA Ops:
  4.4 8.5 %all-to-all-start = ((bf16[16,64,768]{2,1,0:T(8,128)(2,1)}), bf16[16,64,768]{2,1,0:T(8,128)(2,1)S(1)}, u32[]{:S(2)}, u32[]{:S(2)}) async-start(bf16[16,64,768]{2,1,0:T(8,128)(2,1)} %reshape.184), calls=%async_computation | async-start | bytes 3145728 | tf_op jit(solution)/shard_map/all_to_all | solution.py:854
  19.9 29.7 %all-to-all-done = bf16[16,64,768]{2,1,0:T(8,128)(2,1)S(1)} async-done(((bf16[16,64,768]{2,1,0:T(8,128)(2,1)}), bf16[16,64,768]{2,1,0:T(8,128)(2,1)S(1)}, u32[]{:S(2)}, u32[]{:S(2)}) %all-to-all-start) | async-done | bytes 1572896 | tf_op jit(solution)/shard_map/all_to_all | solution.py:854
  50.7 8.3 %qkv.1 = (bf16[1024,768]{1,0:T(8,128)(2,1)}, bf16[1024,1536]{1,0:T(8,128)(2,1)}, bf16[1024,768]{1,0:T(8,128)(2,1)}) custom-call(bf16[1024,768]{1,0:T(8,128)(2,1)} %bitcast.62, f32[1,1,768]{2,1,0:T(1,128)} %convolution_bitcast_fusion.1.refs_1_.refs_16_, f32[1,1,768]{2,1,0:T(1,128)} %broadcast_in_dim.35.refs_2_, f32[1,768]{1,0:T(1,128)} %reshape.206.refs_3_.refs_17_, ...), custom_call_target="tpu_custom_call" | custom-call | flops 72000000 | bytes 228249 | tf_op jit(solution)/shard_map/qkv/pallas_call | solution.py:54
  59.2 4.2 %all-to-all-start.1 = ((bf16[16,64,768]{2,1,0:T(8,128)(2,1)}), bf16[16,64,768]{2,1,0:T(8,128)(2,1)S(1)}, u32[]{:S(2)}, u32[]{:S(2)}) async-start(bf16[16,64,768]{2,1,0:T(8,128)(2,1)} %reshape.187.refs_5_), calls=%async_computation.1 | async-start | bytes 3145728 | tf_op jit(solution)/shard_map/all_to_all | solution.py:854
  65.1 29.8 %attend.1 = (bf16[1024,768]{1,0:T(8,128)(2,1)}, f32[1024,768]{1,0:T(8,128)}, f32[1024,768]{1,0:T(8,128)}) custom-call(bf16[1024,768]{1,0:T(8,128)(2,1)} %get-tuple-element.72.refs_0_, bf16[1024,1536]{1,0:T(8,128)(2,1)} %get-tuple-element.73.refs_1_.refs_3_, bf16[1024,1536]{1,0:T(8,128)(2,1)} %collective-permute-done.refs_2_.refs_4_, ...), custom_call_target="tpu_custom_call" | custom-call | flops 600000000 | bytes 440401 | tf_op jit(solution)/shard_map/attend/pallas_call | solution.py:54
  94.9 5.5 %all-to-all-done.1 = bf16[16,64,768]{2,1,0:T(8,128)(2,1)S(1)} async-done(((bf16[16,64,768]{2,1,0:T(8,128)(2,1)}), bf16[16,64,768]{2,1,0:T(8,128)(2,1)S(1)}, u32[]{:S(2)}, u32[]{:S(2)}) %all-to-all-start.1) | async-done | bytes 1572896 | tf_op jit(solution)/shard_map/all_to_all | solution.py:854
  101.5 37.4 %mlp.1 = (bf16[1024,768]{1,0:T(8,128)(2,1)}, bf16[1024,3072]{1,0:T(8,128)(2,1)}, bf16[1024,3072]{1,0:T(8,128)(2,1)}, bf16[1024,768]{1,0:T(8,128)(2,1)}, f32[1024...) custom-call(bf16[1024,768]{1,0:T(8,128)(2,1)} %bitcast.63, ...), custom_call_target="tpu_custom_call" | custom-call | flops 500000000 | bytes 748154 | tf_op jit(solution)/shard_map/mlp/pallas_call | solution.py:54
  138.9 12.5 %up_grad.1 = (bf16[8,48,3840]{2,1,0:T(8,128)(2,1)}, bf16[8,48,3840]{2,1,0:T(8,128)(2,1)}) custom-call(s32[1]{0:T(128)} %bitcast.9.refs_0_, bf16[1024,768]{1,0:T(8,128)(2,1)} %get-tuple-element.80.refs_1_, bf16[1024,3072]{1,0:T(8,128)(2,1)} %get-tuple-element.81.refs_2_, bf16[1024,768]{1,0:T(8,128)(2,1)} %get-tuple-element.74.refs_2_.refs_3_, ...), custom_call_target="tpu_custom_call" | custom-call | flops 120000000 | bytes 338165 | tf_op jit(solution)/shard_map/up_grad/pallas_call | solution.py:54
  151.4 9.4 %down_grad.1 = (bf16[8,192,768]{2,1,0:T(8,128)(2,1)}, bf16[8,192,768]{2,1,0:T(8,128)(2,1)}) custom-call(s32[1]{0:T(128)} %bitcast.9.refs_0_, bf16[1024,3072]{1,0:T(8,128)(2,1)} %get-tuple-element.79.refs_1_, bf16[1024,768]{1,0:T(8,128)(2,1)} %bitcast.67, bf16[8,48,3840]{2,1,0:T(8,128)(2,1)} %get-tuple-element.83.refs_3_), custom_call_target="tpu_custom_call" | custom-call | flops 96000000 | bytes 251658 | tf_op jit(solution)/shard_map/down_grad/pallas_call | solution.py:54
  161.9 3.9 %collective-permute-done.1.refs_2_ = bf16[8,192,768]{2,1,0:T(8,128)(2,1)} collective-permute-done((bf16[8,192,768]{2,1,0:T(8,128)(2,1)}, bf16[8,192,768]{2,1,0:T(8,128)(2,1)}, u32[]{:S(2)}, u32[]{:S(2)}) %collective-permute-start.1) | collective-permute-done | bytes 2359328 | tf_op jit(solution)/shard_map/ppermute | solution.py:606
  165.8 7.0 %first_add.2 = (bf16[4,2,216,768]{3,2,1,0:T(8,128)(2,1)}, bf16[4,2,216,768]{3,2,1,0:T(8,128)(2,1)}) custom-call(s32[2]{0:T(128)} %pad_add_fusion.refs_0_, bf16[8,192,768]{2,1,0:T(8,128)(2,1)} %get-tuple-element.84.refs_1_, bf16[8,192,768]{2,1,0:T(8,128)(2,1)} %collective-permute-done.1.refs_2_, bf16[8,48,3840]{2,1,0:T(8,128)(2,1)} %get-tuple-element.86.refs_3_, ...), custom_call_target="tpu_custom_call" | custom-call | bytes 318505 | tf_op jit(solution)/shard_map/first_add/pallas_call | solution.py:54
  174.3 3.9 %all-to-all-start.2 = ((bf16[16,64,768]{2,1,0:T(8,128)(2,1)}), bf16[16,64,768]{2,1,0:T(8,128)(2,1)S(1)}, u32[]{:S(2)}, u32[]{:S(2)}) async-start(bf16[16,64,768]{2,1,0:T(8,128)(2,1)} %bitcast.68), calls=%async_computation.2 | async-start | bytes 3145728 | tf_op jit(solution)/shard_map/all_to_all | solution.py:866
  178.2 39.7 %attend_back.3 = (bf16[1024,512]{1,0:T(8,128)(2,1)}, bf16[1024,512]{1,0:T(8,128)(2,1)}, bf16[1024,512]{1,0:T(8,128)(2,1)}, bf16[1024,512]{1,0:T(8,128)(2,1)}, bf16[1024,512]{1,0:T(8,128)(2,1)}) custom-call(bf16[1024,768]{1,0:T(8,128)(2,1)} %get-tuple-element.72.refs_0_, bf16[1024,1536]{1,0:T(8,128)(2,1)} %get-tuple-element.73.refs_1_.refs_3_, ...), custom_call_target="tpu_custom_call" | custom-call | flops 880000000 | bytes 545259 | tf_op jit(solution)/shard_map/attend_back/pallas_call | solution.py:54
  219.9 4.8 %second_add.2 = (bf16[4,216,768]{2,1,0:T(8,128)(2,1)}, bf16[4,216,768]{2,1,0:T(8,128)(2,1)}) custom-call(s32[1]{0:T(128)S(6)} %select_n.79.refs_0_, bf16[4,2,216,768]{3,2,1,0:T(8,128)(2,1)} %get-tuple-element.93.refs_1_, bf16[4,2,216,768]{3,2,1,0:T(8,128)(2,1)} %collective-permute-done.5.refs_2_, ...), custom_call_target="tpu_custom_call" | custom-call | bytes 159252 | tf_op jit(solution)/shard_map/second_add/pallas_call | solution.py:54
  225.8 11.7 %attend_back.4 = (bf16[1024,128]{1,0:T(8,128)(2,1)}, bf16[1024,128]{1,0:T(8,128)(2,1)}, bf16[1024,128]{1,0:T(8,128)(2,1)}, bf16[1024,128]{1,0:T(8,128)(2,1)}, bf16[1024,128]{1,0:T(8,128)(2,1)}) custom-call(bf16[1024,768]{1,0:T(8,128)(2,1)} %get-tuple-element.72.refs_0_, bf16[1024,1536]{1,0:T(8,128)(2,1)} %get-tuple-element.73.refs_1_.refs_3_, ...), custom_call_target="tpu_custom_call" | custom-call | flops 220000000 | bytes 466616 | tf_op jit(solution)/shard_map/attend_back/pallas_call | solution.py:54
  237.6 5.3 %collective-permute-done.8.refs_2_ = bf16[4,216,768]{2,1,0:T(8,128)(2,1)} collective-permute-done((bf16[4,216,768]{2,1,0:T(8,128)(2,1)}, bf16[4,216,768]{2,1,0:T(8,128)(2,1)}, u32[]{:S(2)}, u32[]{:S(2)}) %collective-permute-start.8) | collective-permute-done | bytes 1327136 | tf_op jit(solution)/shard_map/ppermute | solution.py:614
  247.9 11.7 %attend_back.5 = (bf16[1024,128]{1,0:T(8,128)(2,1)}, bf16[1024,128]{1,0:T(8,128)(2,1)}, bf16[1024,128]{1,0:T(8,128)(2,1)}, bf16[1024,128]{1,0:T(8,128)(2,1)}, bf16[1024,128]{1,0:T(8,128)(2,1)}) custom-call(bf16[1024,768]{1,0:T(8,128)(2,1)} %get-tuple-element.72.refs_0_, bf16[1024,1536]{1,0:T(8,128)(2,1)} %get-tuple-element.73.refs_1_.refs_3_, ...), custom_call_target="tpu_custom_call" | custom-call | flops 220000000 | bytes 466616 | tf_op jit(solution)/shard_map/attend_back/pallas_call | solution.py:54
  268.3 10.5 %first_back.1 = (bf16[1024,768]{1,0:T(8,128)(2,1)}, f32[1,2,768]{2,1,0:T(2,128)}, f32[1,768]{1,0:T(1,128)}) custom-call(bf16[1024,512]{1,0:T(8,128)(2,1)} %get-tuple-element.88.refs_3_.refs_9_.refs_0_.refs_2_, bf16[1024,512]{1,0:T(8,128)(2,1)} %get-tuple-element.89.refs_1_.refs_3_, bf16[1024,512]{1,0:T(8,128)(2,1)} %get-tuple-element.90.refs_2_.refs_4_, ...), custom_call_target="tpu_custom_call" | custom-call | flops 72000000 | bytes 354201 | tf_op jit(solution)/shard_map/first_back/pallas_call | solution.py:54
  280.8 5.5 %all-to-all-start.3 = ((bf16[16,64,768]{2,1,0:T(8,128)(2,1)}), bf16[16,64,768]{2,1,0:T(8,128)(2,1)S(1)}, u32[]{:S(2)}, u32[]{:S(2)}) async-start(bf16[16,64,768]{2,1,0:T(8,128)(2,1)} %bitcast.65), calls=%async_computation.3 | async-start | bytes 3145728 | tf_op jit(solution)/shard_map/all_to_all | solution.py:866
  288.8 10.4 %qkv_grad.1 = (bf16[8,48,2304]{2,1,0:T(8,128)(2,1)}, bf16[8,48,2304]{2,1,0:T(8,128)(2,1)}) custom-call(s32[1]{0:T(128)} %bitcast.9.refs_0_, bf16[1024,768]{1,0:T(8,128)(2,1)} %get-tuple-element.114.refs_1_, bf16[1024,512]{1,0:T(8,128)(2,1)} %get-tuple-element.88.refs_3_.refs_9_.refs_0_.refs_2_, bf16[1024,512]{1,0:T(8,128)(2,1)} %get-tuple-element.89.refs_1_.refs_3_, ...), custom_call_target="tpu_custom_call" | custom-call | flops 72000000 | bytes 259522 | tf_op jit(solution)/shard_map/qkv_grad/pallas_call | solution.py:54
  303.2 4.2 %first_add.3 = (bf16[4,2,48,1152]{3,2,1,0:T(8,128)(2,1)}, bf16[4,2,48,1152]{3,2,1,0:T(8,128)(2,1)}) custom-call(s32[2]{0:T(128)} %pad_add_fusion.refs_0_, bf16[8,48,2304]{2,1,0:T(8,128)(2,1)} %get-tuple-element.115.refs_1_, bf16[8,48,2304]{2,1,0:T(8,128)(2,1)} %collective-permute-done.14.refs_2_), custom_call_target="tpu_custom_call" | custom-call | bytes 106168 | tf_op jit(solution)/shard_map/first_add/pallas_call | solution.py:54
  315.1 10.3 %collective-permute-done.16 = f32[2,11,384]{2,1,0:T(8,128)S(1)} collective-permute-done((f32[2,11,384]{2,1,0:T(8,128)S(1)}, f32[2,11,384]{2,1,0:T(8,128)S(1)}, u32[]{:S(2)}, u32[]{:S(2)}) %collective-permute-start.16) | collective-permute-done | bytes 33824 | tf_op jit(solution)/shard_map/ppermute | solution.py:606
  333.9 6.6 %collective-permute-done.18.refs_2_ = bf16[4,48,1152]{2,1,0:T(8,128)(2,1)} collective-permute-done((bf16[4,48,1152]{2,1,0:T(8,128)(2,1)}, bf16[4,48,1152]{2,1,0:T(8,128)(2,1)}, u32[]{:S(2)}, u32[]{:S(2)}) %collective-permute-start.18) | collective-permute-done | bytes 442400 | tf_op jit(solution)/shard_map/ppermute | solution.py:614
  369.7 4.6 %collective-permute-done.26.refs_2_ = bf16[48,1152]{1,0:T(8,128)(2,1)S(1)} collective-permute-done((bf16[48,1152]{1,0:T(8,128)(2,1)}, bf16[48,1152]{1,0:T(8,128)(2,1)S(1)}, u32[]{:S(2)}, u32[]{:S(2)}) %collective-permute-start.26) | collective-permute-done | bytes 110624 | tf_op jit(solution)/shard_map/ppermute | solution.py:606
  (180 shorter events, 90.1 us)
Async XLA Ops:
  4.4 45.2 %all-to-all-start = ((bf16[16,64,768]{2,1,0:T(8,128)(2,1)}), bf16[16,64,768]{2,1,0:T(8,128)(2,1)S(1)}, u32[]{:S(2)}, u32[]{:S(2)}) async-start(bf16[16,64,768]{2,1,0:T(8,128)(2,1)} %reshape.184), calls=%async_computation | async-start | bytes 3145728 | tf_op jit(solution)/shard_map/all_to_all | solution.py:854
  59.1 6.1 %collective-permute-start = (bf16[1024,1536]{1,0:T(8,128)(2,1)}, bf16[1024,1536]{1,0:T(8,128)(2,1)}, u32[]{:S(2)}, u32[]{:S(2)}) collective-permute-start(bf16[1024,1536]{1,0:T(8,128)(2,1)} %get-tuple-element.73.refs_1_.refs_3_), channel_id=1, source_target_pairs={{0,1},{1,0},{2,3},{3,2},{4,5},{5,4},{6,7},{7,6},{8,9},{9,8},{10,11... | collective-permute-start | bytes 9437192 | tf_op jit(solution)/shard_map/ppermute | solution.py:606
  59.2 41.2 %all-to-all-start.1 = ((bf16[16,64,768]{2,1,0:T(8,128)(2,1)}), bf16[16,64,768]{2,1,0:T(8,128)(2,1)S(1)}, u32[]{:S(2)}, u32[]{:S(2)}) async-start(bf16[16,64,768]{2,1,0:T(8,128)(2,1)} %reshape.187.refs_5_), calls=%async_computation.1 | async-start | bytes 3145728 | tf_op jit(solution)/shard_map/all_to_all | solution.py:854
  151.4 14.4 %collective-permute-start.2 = (bf16[8,48,3840]{2,1,0:T(8,128)(2,1)}, bf16[8,48,3840]{2,1,0:T(8,128)(2,1)}, u32[]{:S(2)}, u32[]{:S(2)}) collective-permute-start(bf16[8,48,3840]{2,1,0:T(8,128)(2,1)} %get-tuple-element.83.refs_3_), channel_id=1, source_target_pairs={{0,1},{1,0},{2,3},{3,2},{4,5},{5,4},{6,7},{7,6},{8,9},{9,8},{10,11... | collective-permute-start | bytes 8847368 | tf_op jit(solution)/shard_map/ppermute | solution.py:606
  160.8 5.0 %collective-permute-start.1 = (bf16[8,192,768]{2,1,0:T(8,128)(2,1)}, bf16[8,192,768]{2,1,0:T(8,128)(2,1)}, u32[]{:S(2)}, u32[]{:S(2)}) collective-permute-start(bf16[8,192,768]{2,1,0:T(8,128)(2,1)} %get-tuple-element.85), channel_id=1, source_target_pairs={{0,1},{1,0},{2,3},{3,2},{4,5},{5,4},{6,7},{7,6},{8,9},{9,8},{10,11... | collective-permute-start | bytes 7077896 | tf_op jit(solution)/shard_map/ppermute | solution.py:606
  172.9 47.1 %collective-permute-start.5 = (bf16[4,2,216,768]{3,2,1,0:T(8,128)(2,1)}, bf16[4,2,216,768]{3,2,1,0:T(8,128)(2,1)}, u32[]{:S(2)}, u32[]{:S(2)}) collective-permute-start(bf16[4,2,216,768]{3,2,1,0:T(8,128)(2,1)} %get-tuple-element.87.refs_8_), channel_id=1, source_target_pairs={{0,16},{1,3},{2,18},{3,1},{16,0},{17,19},{18,2},{19,17},{4,20},{5,... | collective-permute-start | bytes 7962632 | tf_op jit(solution)/shard_map/ppermute | solution.py:614
  174.3 92.0 %all-to-all-start.2 = ((bf16[16,64,768]{2,1,0:T(8,128)(2,1)}), bf16[16,64,768]{2,1,0:T(8,128)(2,1)S(1)}, u32[]{:S(2)}, u32[]{:S(2)}) async-start(bf16[16,64,768]{2,1,0:T(8,128)(2,1)} %bitcast.68), calls=%async_computation.2 | async-start | bytes 3145728 | tf_op jit(solution)/shard_map/all_to_all | solution.py:866
  224.7 18.2 %collective-permute-start.8 = (bf16[4,216,768]{2,1,0:T(8,128)(2,1)}, bf16[4,216,768]{2,1,0:T(8,128)(2,1)}, u32[]{:S(2)}, u32[]{:S(2)}) collective-permute-start(bf16[4,216,768]{2,1,0:T(8,128)(2,1)} %get-tuple-element.94.refs_8_), channel_id=1, source_target_pairs={{0,2},{1,17},{2,0},{3,19},{16,18},{17,1},{18,16},{19,3},{4,6},{5,2... | collective-permute-start | bytes 3981320 | tf_op jit(solution)/shard_map/ppermute | solution.py:614
  225.3 40.5 %collective-permute-start.3 = (bf16[1024,512]{1,0:T(8,128)(2,1)}, bf16[1024,512]{1,0:T(8,128)(2,1)}, u32[]{:S(2)}, u32[]{:S(2)}) collective-permute-start(bf16[1024,512]{1,0:T(8,128)(2,1)} %get-tuple-element.91), channel_id=1, source_target_pairs={{0,1},{1,0},{2,3},{3,2},{4,5},{5,4},{6,7},{7,6},{8,9},{9,8},{10,11... | collective-permute-start | bytes 3145736 | tf_op jit(solution)/shard_map/ppermute | solution.py:606
  225.5 40.3 %collective-permute-start.4 = (bf16[1024,512]{1,0:T(8,128)(2,1)}, bf16[1024,512]{1,0:T(8,128)(2,1)}, u32[]{:S(2)}, u32[]{:S(2)}) collective-permute-start(bf16[1024,512]{1,0:T(8,128)(2,1)} %get-tuple-element.92), channel_id=1, source_target_pairs={{0,1},{1,0},{2,3},{3,2},{4,5},{5,4},{6,7},{7,6},{8,9},{9,8},{10,11... | collective-permute-start | bytes 3145736 | tf_op jit(solution)/shard_map/ppermute | solution.py:606
  245.9 16.1 %collective-permute-start.11 = (bf16[2,216,768]{2,1,0:T(8,128)(2,1)}, bf16[2,216,768]{2,1,0:T(8,128)(2,1)}, u32[]{:S(2)}, u32[]{:S(2)}) collective-permute-start(bf16[2,216,768]{2,1,0:T(8,128)(2,1)} %get-tuple-element.101.refs_8_), channel_id=1, source_target_pairs={{0,4},{4,0},{8,12},{12,8},{1,5},{5,1},{9,13},{13,9},{2,6},{6,2},{1... | collective-permute-start | bytes 1990664 | tf_op jit(solution)/shard_map/ppermute | solution.py:606
  264.1 15.9 %collective-permute-start.12 = (bf16[1,216,768]{2,1,0:T(8,128)(2,1)}, bf16[1,216,768]{2,1,0:T(8,128)(2,1)S(1)}, u32[]{:S(2)}, u32[]{:S(2)}) collective-permute-start(bf16[1,216,768]{2,1,0:T(8,128)(2,1)} %get-tuple-element.109.refs_20_), channel_id=1, source_target_pairs={{0,8},{4,12},{8,0},{12,4},{1,9},{5,13},{9,1},{13,5},{2,10},{6,14},... | collective-permute-start | bytes 995336 | tf_op jit(solution)/shard_map/ppermute | solution.py:606
  280.8 45.4 %all-to-all-start.3 = ((bf16[16,64,768]{2,1,0:T(8,128)(2,1)}), bf16[16,64,768]{2,1,0:T(8,128)(2,1)S(1)}, u32[]{:S(2)}, u32[]{:S(2)}) async-start(bf16[16,64,768]{2,1,0:T(8,128)(2,1)} %bitcast.65), calls=%async_computation.3 | async-start | bytes 3145728 | tf_op jit(solution)/shard_map/all_to_all | solution.py:866
  307.5 18.6 %collective-permute-start.17 = (bf16[4,2,48,1152]{3,2,1,0:T(8,128)(2,1)}, bf16[4,2,48,1152]{3,2,1,0:T(8,128)(2,1)S(1)}, u32[]{:S(2)}, u32[]{:S(2)}) collective-permute-start(bf16[4,2,48,1152]{3,2,1,0:T(8,128)(2,1)} %get-tuple-element.117.refs_1_), channel_id=1, source_target_pairs={{0,16},{1,3},{2,18},{3,1},{16,0},{17,19},{18,2},{19,17},{4,20},{5,... | collective-permute-start | bytes 2654216 | tf_op jit(solution)/shard_map/ppermute | solution.py:614
  315.0 10.5 %collective-permute-start.16 = (f32[2,11,384]{2,1,0:T(8,128)S(1)}, f32[2,11,384]{2,1,0:T(8,128)S(1)}, u32[]{:S(2)}, u32[]{:S(2)}) collective-permute-start(f32[2,11,384]{2,1,0:T(8,128)S(1)} %maximum_select_fusion.1), channel_id=1, source_target_pairs={{0,16},{16,0},{1,17},{17,1},{2,18},{18,2},{3,19},{19,3},{4,20},{20... | collective-permute-start | bytes 101384 | tf_op jit(solution)/shard_map/ppermute | solution.py:606
  331.9 8.6 %collective-permute-start.18 = (bf16[4,48,1152]{2,1,0:T(8,128)(2,1)}, bf16[4,48,1152]{2,1,0:T(8,128)(2,1)}, u32[]{:S(2)}, u32[]{:S(2)}) collective-permute-start(bf16[4,48,1152]{2,1,0:T(8,128)(2,1)} %get-tuple-element.120), channel_id=1, source_target_pairs={{0,2},{1,17},{2,0},{3,19},{16,18},{17,1},{18,16},{19,3},{4,6},{5,2... | collective-permute-start | bytes 1327112 | tf_op jit(solution)/shard_map/ppermute | solution.py:614
  343.4 11.0 %collective-permute-start.19 = (f32[4,11,384]{2,1,0:T(8,128)S(1)}, f32[4,11,384]{2,1,0:T(8,128)S(1)}, u32[]{:S(2)}, u32[]{:S(2)}) collective-permute-start(f32[4,11,384]{2,1,0:T(8,128)S(1)} %held.4), channel_id=1, source_target_pairs={{0,4},{4,8},{8,12},{12,0},{1,5},{5,9},{9,13},{13,1},{2,6},{6,10},{... | collective-permute-start | bytes 202760 | tf_op jit(solution)/shard_map/ppermute | solution.py:745
  343.5 12.4 %collective-permute-start.20 = (f32[4,11,384]{2,1,0:T(8,128)S(1)}, f32[4,11,384]{2,1,0:T(8,128)S(1)}, u32[]{:S(2)}, u32[]{:S(2)}) collective-permute-start(f32[4,11,384]{2,1,0:T(8,128)S(1)} %held.4), channel_id=1, source_target_pairs={{0,8},{4,12},{8,0},{12,4},{1,9},{5,13},{9,1},{13,5},{2,10},{6,14},... | collective-permute-start | bytes 202760 | tf_op jit(solution)/shard_map/ppermute | solution.py:745
  346.4 12.4 %collective-permute-start.21 = (f32[4,11,384]{2,1,0:T(8,128)S(1)}, f32[4,11,384]{2,1,0:T(8,128)S(1)}, u32[]{:S(2)}, u32[]{:S(2)}) collective-permute-start(f32[4,11,384]{2,1,0:T(8,128)S(1)} %held.4), channel_id=1, source_target_pairs={{0,12},{4,0},{8,4},{12,8},{1,13},{5,1},{9,5},{13,9},{2,14},{6,2},{... | collective-permute-start | bytes 202760 | tf_op jit(solution)/shard_map/ppermute | solution.py:745
  352.0 10.5 %collective-permute-start.25 = (bf16[216,768]{1,0:T(8,128)(2,1)S(1)}, bf16[216,768]{1,0:T(8,128)(2,1)S(1)}, u32[]{:S(2)}, u32[]{:S(2)}) collective-permute-start(bf16[216,768]{1,0:T(8,128)(2,1)S(1)} %held.5.refs_1_), channel_id=1, source_target_pairs={{0,16},{16,0},{1,17},{17,1},{2,18},{18,2},{3,19},{19,3},{4,20},{20... | collective-permute-start | bytes 995336 | tf_op jit(solution)/shard_map/ppermute | solution.py:606
  353.8 11.7 %collective-permute-start.22 = (bf16[48,1152]{1,0:T(8,128)(2,1)}, bf16[48,1152]{1,0:T(8,128)(2,1)S(1)}, u32[]{:S(2)}, u32[]{:S(2)}) collective-permute-start(bf16[48,1152]{1,0:T(8,128)(2,1)} %get-tuple-element.122), channel_id=1, source_target_pairs={{0,4},{4,8},{8,12},{12,0},{1,5},{5,9},{9,13},{13,1},{2,6},{6,10},{... | collective-permute-start | bytes 331784 | tf_op jit(solution)/shard_map/ppermute | solution.py:745
  354.4 11.3 %collective-permute-start.23 = (bf16[48,1152]{1,0:T(8,128)(2,1)}, bf16[48,1152]{1,0:T(8,128)(2,1)S(1)}, u32[]{:S(2)}, u32[]{:S(2)}) collective-permute-start(bf16[48,1152]{1,0:T(8,128)(2,1)} %get-tuple-element.123), channel_id=1, source_target_pairs={{0,8},{4,12},{8,0},{12,4},{1,9},{5,13},{9,1},{13,5},{2,10},{6,14},... | collective-permute-start | bytes 331784 | tf_op jit(solution)/shard_map/ppermute | solution.py:745
  355.9 9.9 %collective-permute-start.24 = (bf16[48,1152]{1,0:T(8,128)(2,1)}, bf16[48,1152]{1,0:T(8,128)(2,1)S(1)}, u32[]{:S(2)}, u32[]{:S(2)}) collective-permute-start(bf16[48,1152]{1,0:T(8,128)(2,1)} %get-tuple-element.124), channel_id=1, source_target_pairs={{0,12},{4,0},{8,4},{12,8},{1,13},{5,1},{9,5},{13,9},{2,14},{6,2},{... | collective-permute-start | bytes 331784 | tf_op jit(solution)/shard_map/ppermute | solution.py:745
  368.2 6.1 %collective-permute-start.26 = (bf16[48,1152]{1,0:T(8,128)(2,1)}, bf16[48,1152]{1,0:T(8,128)(2,1)S(1)}, u32[]{:S(2)}, u32[]{:S(2)}) collective-permute-start(bf16[48,1152]{1,0:T(8,128)(2,1)} %last_add.3.refs_1_), channel_id=1, source_target_pairs={{0,16},{16,0},{1,17},{17,1},{2,18},{18,2},{3,19},{19,3},{4,20},{20... | collective-permute-start | bytes 331784 | tf_op jit(solution)/shard_map/ppermute | solution.py:606
  (43 other events, 196.8 us)
